TPU v7x, 32 devices: a whole 2x2x4 slice. The times are simulated.
32 devices in a mesh: phase: 4 (over z), vox: 8 (over y, x, core).
Axes of the slice: x: 2, y: 2, z: 4, core: 2. Of those that a mesh axis runs over, the one named last changes fastest.
Arguments:
- influence: float32 [4, 16384, 1536], P('phase', 'vox'), may hold values from -0.15625 to 0.15625
- weights: float32 [1536, 128], P(('phase', 'vox')), may hold values from 0.5 to 2
- warp_tiles: float32 [64, 128, 128], replicated, may hold values from -0.5 to 0.5
- owners: int32 [4, 128, 1], P('phase', 'vox'), may hold values from 0 to 7; in each aligned block of 16 rows (0 to 15, 16 to 31, ..., all dimensions but the last counted through in order) at most 2 rows name the same one
- owner_slot: int32 [4, 128], P('phase', 'vox'), may hold values from 0 to 15
- tile_index: int32 [4, 128], P('phase', 'vox'), may hold values from 0 to 63
- structure: int32 [16384], P('vox'), may hold values from 0 to 7
- prescribed: float32 [8, 128], replicated, may hold values from 0 to 3
- importance: float32 [8], replicated, may hold values from 0.25 to 4
- step_size: float32 [128], replicated, may hold values from 0.02 to 0.08
Outputs:
- new_weights: float32 [1536, 128], P(('phase', 'vox'))
- dose_field: float32 [16384, 128], P('vox')
Inputs may be any that keep to these rules, and one draw needn't show every extreme that they name: `owners`: for each phase and each device of vox, at most 2 of that device's 16 blocks name one owner, and some device reaches 2.
All inputs are finite; a program needn't handle non-finite values.
Results may differ from a plain program's by a relative error of at most 0.00023.
Values sent between devices are 32-bit elements; how exact they have to be, the bound alone decides.
No kernel may reach another device: no remote copies, remote signals or barrier semaphores. Data moves between devices by JAX's collectives and lax.ppermute only.
A program may use at most 128 MiB of HBM per device.

v0:
```python
import jax
import jax.numpy as jnp
from jax import lax
from jax.sharding import PartitionSpec as P

CAP = 2
NSTRUCT = 8
ITERS = 2


def per_device(
    influence,
    weights,
    warp_tiles,
    owners,
    owner_slot,
    tile_index,
    structure,
    prescribed,
    importance,
    step_size,
):
    highest = lax.Precision.HIGHEST
    matrix = influence[0]
    vox_rows = matrix.shape[0]
    block_rows = warp_tiles.shape[1]
    plans = weights.shape[1]
    local_blocks = vox_rows // block_rows
    vox_count = lax.axis_size("vox")
    slots_all = vox_count * CAP
    targets = owners[0, :, 0]
    my_slots = owner_slot[0]
    my_tiles = tile_index[0]
    positions_i = jnp.arange(local_blocks, dtype=jnp.int32)
    earlier = (targets[:, None] == targets[None, :]) & (positions_i[None, :] < positions_i[:, None])
    order_in_owner = jnp.sum(earlier.astype(jnp.int32), axis=1)
    position = targets * CAP + order_in_owner
    chosen_mask = jnp.arange(slots_all, dtype=jnp.int32)[:, None] == position[None, :]
    selector = chosen_mask.astype(jnp.float32)
    slot_sent = jnp.sum(jnp.where(chosen_mask, my_slots[None, :] + 1, 0), axis=1) - 1
    own_tiles = warp_tiles[my_tiles]
    member = (structure[:, None] == jnp.arange(NSTRUCT, dtype=jnp.int32)[None, :]).astype(
        jnp.float32
    )
    target_dose = jnp.dot(member, prescribed, precision=highest, preferred_element_type=jnp.float32)
    voxel_weight = jnp.dot(
        member, importance[:, None], precision=highest, preferred_element_type=jnp.float32
    )
    new_weights = weights
    dose_field = jnp.zeros((vox_rows, plans), jnp.float32)
    for iteration in range(ITERS):
        phase_dose = jnp.dot(
            matrix,
            lax.all_gather(new_weights, ("phase", "vox"), axis=0, tiled=True),
            precision=highest,
            preferred_element_type=jnp.float32,
        )
        blocks = phase_dose.reshape(local_blocks, block_rows, plans)
        warped = jnp.einsum("kab,kbp->kap", own_tiles, blocks, precision=highest)
        outgoing = jnp.dot(
            selector,
            warped.reshape(local_blocks, block_rows * plans),
            precision=highest,
            preferred_element_type=jnp.float32,
        )
        outgoing = outgoing.reshape(vox_count, CAP, block_rows * plans)
        labels_out = slot_sent.reshape(vox_count, CAP, 1)
        incoming, info = (
            lax.all_to_all(outgoing, "vox", split_axis=0, concat_axis=0, tiled=True),
            lax.all_to_all(labels_out, "vox", split_axis=0, concat_axis=0, tiled=True),
        )
        received_slot = info.reshape(slots_all)
        warped_in = incoming.reshape(slots_all, block_rows, plans)
        placing = (
            jnp.arange(local_blocks, dtype=jnp.int32)[:, None] == received_slot[None, :]
        ).astype(jnp.float32)
        partial_dose = jnp.dot(
            placing,
            warped_in.reshape(slots_all, block_rows * plans),
            precision=highest,
            preferred_element_type=jnp.float32,
        )
        partial_dose = partial_dose.reshape(vox_rows, plans)
        dose_field = lax.psum(partial_dose, "phase")
        adjoint = voxel_weight * (dose_field - target_dose)
        adjoint_rows = adjoint.reshape(local_blocks, block_rows * plans)
        back_slots = jnp.dot(
            placing.T, adjoint_rows, precision=highest, preferred_element_type=jnp.float32
        )
        returned = lax.all_to_all(
            back_slots.reshape(vox_count, CAP, block_rows * plans),
            "vox",
            split_axis=0,
            concat_axis=0,
            tiled=True,
        )
        pulled = jnp.dot(
            selector.T,
            returned.reshape(slots_all, block_rows * plans),
            precision=highest,
            preferred_element_type=jnp.float32,
        )
        local_adjoint = jnp.einsum(
            "kab,kap->kbp",
            own_tiles,
            pulled.reshape(local_blocks, block_rows, plans),
            precision=highest,
        )
        phase_adjoint = local_adjoint.reshape(vox_rows, plans)
        gradient = lax.psum_scatter(
            lax.dot_general(
                matrix,
                phase_adjoint,
                (((0,), (0,)), ((), ())),
                precision=highest,
                preferred_element_type=jnp.float32,
            ),
            ("phase", "vox"),
            scatter_dimension=0,
            tiled=True,
        )
        new_weights = jnp.maximum(new_weights - step_size[None, :] * gradient, 0.0)
    return (new_weights, dose_field)


def solution(mesh):
    in_specs = (
        P("phase", "vox", None),
        P(("phase", "vox"), None),
        P(),
        P("phase", "vox", None),
        P("phase", "vox"),
        P("phase", "vox"),
        P("vox"),
        P(),
        P(),
        P(),
    )
    out_specs = (P(("phase", "vox"), None), P("vox", None))
    return jax.shard_map(
        per_device, mesh=mesh, in_specs=in_specs, out_specs=out_specs, check_vma=False
    )
```

profile of v0, /device:TPU:0, one launch (start us, length us, event | category | flops | bytes accessed | tf_op | source)
XLA Modules:
  0.0 564.1 jit_solution(15706269789195181886)
XLA Ops:
  7.2 0.9 convert_reduce_fusion
  8.1 0.7 multiply_add_fusion.1
  8.8 0.7 add_bitcast_fusion
  9.4 0.1 select_reduce_fusion
  9.5 0.7 sub.18
  10.2 5.2 all-to-all-start
  15.4 0.7 fusion.53
  16.0 44.6 %all_gather.6 = f32[1536,128]{1,0:T(8,128)S(1)} all-gather(f32[48,128]{1,0:T(8,128)} %param.11), channel_id=1, replica_groups=mesh['phase'=4,'vox'=8] {'phase','vox'}, dimensions={0}, use_global_device_ids=true | all-gather | bytes 811008 | tf_op jit(solution)/shard_map/all_gather | solution.py:54
  60.7 2.8 gather_fusion
  63.5 12.9 %fusion.27 = f32[16,128,128]{2,1,0:T(8,128)S(1)} fusion(f32[16,128,1536]{2,1,0:T(8,128)} %bitcast.79, f32[1536,128]{1,0:T(8,128)S(1)} %all_gather.6), kind=kOutput, calls=%fused_computation.25 | convolution fusion | flops 4831838208 | bytes 14417920 | tf_op jit(solution)/shard_map/dot_general | solution.py:52
  76.4 1.2 fusion.55
  77.6 0.2 reshape.196
  77.8 0.6 fusion.33
  78.4 1.8 copy.61
  80.2 3.6 all-to-all-start.1
  83.8 0.5 broadcast.109
  84.3 0.7 reduce.3
  85.1 14.0 %all-to-all-done.1 = f32[8,2,16384]{2,1,0:T(2,128)S(1)} async-done(((f32[8,2,16384]{2,1,0:T(2,128)}), f32[8,2,16384]{2,1,0:T(2,128)S(1)}, u32[]{:S(2)}, u32[]{:S(2)}) %all-to-all-start.1) | async-done | bytes 1048608 | tf_op jit(solution)/shard_map/all_to_all | solution.py:69
  99.1 0.7 reshape_reshape.6
  99.8 0.6 fusion.36
  100.4 1.1 reshape.175
  101.6 0.2 reduce-scatter.7.cloned.1.call-start
  101.8 0.7 fusion.26
  102.6 47.3 %all-reduce.3.cloned.1.call-done = f32[2048,128]{1,0:T(8,128)} async-done(((f32[2048,128]{1,0:T(8,128)}), f32[2048,128]{1,0:T(8,128)}) %all-reduce.3.cloned.1.call-update) | async-done | bytes 1048592 | tf_op jit(solution)/shard_map/psum | solution.py:84
  149.9 2.8 subtract_multiply_fusion.1
  152.7 1.4 reshape.197
  154.1 0.6 fusion.51
  154.7 0.8 copy.63
  155.6 18.9 %all_to_all.26 = f32[8,2,16384]{2,1,0:T(2,128)} all-to-all(f32[8,2,16384]{2,1,0:T(2,128)S(1)} %copy.63), channel_id=1, replica_groups=mesh['phase'=4,'vox'=8] {'vox'}, dimensions={0} | all-to-all | bytes 2097152 | tf_op jit(solution)/shard_map/all_to_all | solution.py:90
  174.5 2.0 reshape.177
  176.4 0.6 fusion.18
  177.1 2.1 fusion.23
  179.2 10.1 %fusion.6 = f32[1536,128]{0,1:T(8,128)S(1)} fusion(f32[2048,128]{1,0:T(8,128)S(1)} %bitcast.81, f32[1,2048,1536]{2,1,0:T(8,128)} %param.10), kind=kOutput, calls=%fused_computation.7 | convolution fusion | flops 4831838208 | bytes 14417920 | tf_op jit(solution)/shard_map/dot_general | solution.py:111
  189.3 1.1 copy.80
  190.6 0.1 copy.67
  190.7 93.1 %reduce-scatter.7.cloned.1.call-done = f32[48,128]{1,0:T(8,128)} async-done(((f32[1536,128]{1,0:T(8,128)}), f32[48,128]{1,0:T(8,128)}) %reduce-scatter.7.cloned.1.call-update) | async-done | bytes 24592
  283.7 0.8 copy.81
  284.7 42.0 %all_gather.7 = f32[1536,128]{1,0:T(8,128)S(1)} all-gather(f32[48,128]{1,0:T(8,128)S(1)} %copy.68), channel_id=1, replica_groups=mesh['phase'=4,'vox'=8] {'phase','vox'}, dimensions={0}, use_global_device_ids=true | all-gather | bytes 811008 | tf_op jit(solution)/shard_map/all_gather | solution.py:54
  326.7 16.1 %fusion.9 = f32[2048,128]{0,1:T(8,128)S(1)} fusion(f32[1536,128]{1,0:T(8,128)S(1)} %all_gather.7, f32[1,2048,1536]{2,1,0:T(8,128)} %param.10), kind=kOutput, calls=%fused_computation.8 | convolution fusion | flops 4831838208 | bytes 14417920 | tf_op jit(solution)/shard_map/dot_general | solution.py:52
  342.8 1.3 copy.79
  344.1 2.4 fusion.56
  346.5 1.2 reshape.199
  347.7 1.8 fusion.31
  349.5 0.8 copy.70
  350.3 18.5 %all_to_all.27 = f32[8,2,16384]{2,1,0:T(2,128)} all-to-all(f32[8,2,16384]{2,1,0:T(2,128)S(1)} %copy.70), channel_id=1, replica_groups=mesh['phase'=4,'vox'=8] {'vox'}, dimensions={0} | all-to-all | bytes 2097152 | tf_op jit(solution)/shard_map/all_to_all | solution.py:69
  368.8 1.9 reshape_reshape.7
  370.7 1.6 fusion.35
  372.3 2.4 reshape.181
  374.8 0.3 reduce-scatter.9.cloned.1.call-start
  375.1 48.0 %all-reduce.5.cloned.1.call-done = f32[2048,128]{1,0:T(8,128)} async-done(((f32[2048,128]{1,0:T(8,128)}), f32[2048,128]{1,0:T(8,128)}) %all-reduce.5.cloned.1.call-update) | async-done | bytes 1048592 | tf_op jit(solution)/shard_map/psum | solution.py:84
  423.0 1.6 subtract_multiply_fusion
  424.7 0.2 reshape.200
  424.9 0.6 fusion.49
  425.5 0.8 copy.72
  426.3 18.9 %all_to_all.28 = f32[8,2,16384]{2,1,0:T(2,128)} all-to-all(f32[8,2,16384]{2,1,0:T(2,128)S(1)} %copy.72), channel_id=1, replica_groups=mesh['phase'=4,'vox'=8] {'vox'}, dimensions={0} | all-to-all | bytes 2097152 | tf_op jit(solution)/shard_map/all_to_all | solution.py:90
  445.2 2.0 reshape.183
  447.3 0.6 fusion.15
  447.9 2.1 fusion.21
  450.0 10.1 %fusion.12 = f32[1536,128]{0,1:T(8,128)S(1)} fusion(f32[2048,128]{1,0:T(8,128)S(1)} %bitcast.80, f32[1,2048,1536]{2,1,0:T(8,128)} %param.10), kind=kOutput, calls=%fused_computation.9 | convolution fusion | flops 4831838208 | bytes 14417920 | tf_op jit(solution)/shard_map/dot_general | solution.py:111
  460.2 1.1 copy.82
  461.4 93.2 %reduce-scatter.9.cloned.1.call-done = f32[48,128]{1,0:T(8,128)} async-done(((f32[1536,128]{1,0:T(8,128)}), f32[48,128]{1,0:T(8,128)}) %reduce-scatter.9.cloned.1.call-update) | async-done | bytes 24592
  554.5 0.8 copy.83
  555.5 0.7 copy.76
  556.2 1.0 copy.104
  (28 shorter events, 0.6 us)
Async XLA Ops:
  7.2 142.8 %copy-start = (f32[8,128]{1,0:T(8,128)S(1)}, f32[8,128]{1,0:T(8,128)}, u32[]{:S(2)}) copy-start(f32[8,128]{1,0:T(8,128)} %param.17) | copy-start | bytes 12292
  10.2 70.0 %all-to-all-start = ((s32[8,2,1]{1,2,0:T(1,128)}), s32[8,2,1]{1,2,0:T(1,128)S(1)}, u32[]{:S(2)}, u32[]{:S(2)}) async-start(s32[8,2,1]{1,2,0:T(1,128)} %bitcast.5), calls=%async_computation | async-start | bytes 8192 | tf_op jit(solution)/shard_map/all_to_all | solution.py:70
  76.4 25.4 %copy-start.3 = (s32[2048]{0:T(1024)S(1)}, s32[2048]{0:T(1024)}, u32[]{:S(2)}) copy-start(s32[2048]{0:T(1024)} %param.16) | copy-start | bytes 24580
  76.4 25.4 %copy-start.5 = (f32[8]{0:T(128)S(1)}, f32[8]{0:T(128)}, u32[]{:S(2)}) copy-start(f32[8]{0:T(128)} %param.18) | copy-start | bytes 100
  80.2 18.9 %all-to-all-start.1 = ((f32[8,2,16384]{2,1,0:T(2,128)}), f32[8,2,16384]{2,1,0:T(2,128)S(1)}, u32[]{:S(2)}, u32[]{:S(2)}) async-start(f32[8,2,16384]{2,1,0:T(2,128)} %copy.61), calls=%async_computation.1 | async-start | bytes 2097152 | tf_op jit(solution)/shard_map/all_to_all | solution.py:69
  83.8 66.2 %all-reduce.3.cloned.1.call-start = ((), (), s32[]{:S(2)}) async-start(), calls=%async_computation.7 | async-start | bytes 2097152 | tf_op jit(solution)/shard_map/psum | solution.py:84
  101.6 182.2 %reduce-scatter.7.cloned.1.call-start = ((), (), s32[]{:S(2)}) async-start(), calls=%async_computation.9 | async-start | bytes 811008
  174.5 16.1 %copy-start.2 = (f32[48,128]{1,0:T(8,128)S(1)}, f32[48,128]{1,0:T(8,128)}, u32[]{:S(2)}) copy-start(f32[48,128]{1,0:T(8,128)} %param.11) | copy-start | bytes 73732
  174.5 110.1 %copy-start.4 = (f32[128]{0:T(128)S(1)}, f32[128]{0:T(128)}, u32[]{:S(2)}) copy-start(f32[128]{0:T(128)} %param.19) | copy-start | bytes 1540
  190.5 232.5 %all-reduce.5.cloned.1.call-start = ((), (), s32[]{:S(2)}) async-start(), calls=%async_computation.8 | async-start | bytes 2097152 | tf_op jit(solution)/shard_map/psum | solution.py:84
  374.8 179.8 %reduce-scatter.9.cloned.1.call-start = ((), (), s32[]{:S(2)}) async-start(), calls=%async_computation.10 | async-start | bytes 811008
  445.2 110.9 %copy-start.1 = (f32[2048,128]{1,0:T(8,128)S(1)}, f32[2048,128]{1,0:T(8,128)}, u32[]{:S(2)}) copy-start(f32[2048,128]{1,0:T(8,128)} %all-reduce.5.cloned.1.call-done) | copy-start | bytes 3145732
Sparse Core Ops, SparseCore 0:
  101.7 48.1 all-reduce.2
  190.6 93.0 reduce-scatter.6
  374.9 48.1 all-reduce.4
  461.5 93.0 reduce-scatter.8
where the time goes:
time: 573 us; the launch traced here: 564 us
  waiting for transfers between devices  296 us (52%)
  blocking collectives  143 us (25%)
  matrix products  67.7 us (12%)
  local copies, waits for them, and re-layouts  28.5 us (5%)
  between operations  14.5 us (3%)
  starting transfers between devices  9.32 us (2%)
    unnamed x6, waiting for transfers between devices  186 us
    psum x2, waiting for transfers between devices, per_device(): dose_field = lax.psum(partial_dose, 'phase')  95.3 us
    all_gather x2, blocking collectives, per_device(): lax.all_gather(new_weights, ('phase', 'vox'), axis=0, tiled=True)  86.6 us
    all_to_all x2, blocking collectives, per_device(): lax.all_to_all(back_slots.reshape(vox_count, CAP, block_rows * plans), 'v...  37.8 us
    dot_general x2, matrix products, per_device(): jnp.dot(matrix, lax.all_gather(new_weights, ('phase', 'vox'), axis=0, til...  29 us
    dot_general x2, matrix products, per_device(): lax.dot_general(matrix, phase_adjoint, (((0,), (0,)), ((), ())), precisio...  20.3 us
    all_to_all x1, blocking collectives, per_device(): lax.all_to_all(outgoing, 'vox', split_axis=0, concat_axis=0, tiled=True)  18.5 us
    all_to_all x1, waiting for transfers between devices, per_device(): lax.all_to_all(outgoing, 'vox', split_axis=0, concat_axis=0, tiled=True)  14 us
  transfers between devices with their start and end apart: 6, of which 5 were waited for; matrix products, arithmetic and copies ran while one was open for 4% of the time, Pallas kernels for 0%

commit v1 on v0

v1 whole, which is shorter than its diff:
```python
import jax
import jax.numpy as jnp
from jax import lax
from jax.sharding import PartitionSpec as P

CAP = 2
NSTRUCT = 8
ITERS = 2
VOX = "vox"
PHASE = "phase"
LABEL_ROWS = 8


def swap(x, axis, mask):
    count = lax.axis_size(axis)
    return lax.ppermute(x, axis, [(i, i ^ mask) for i in range(count)])


def spread(x, axis, masks):
    return [x] + [swap(x, axis, m) for m in masks]


def core_count():
    return min(2, lax.axis_size(VOX))


def gather_weights(shard, extra):
    phases, vox = lax.axis_size(PHASE), lax.axis_size(VOX)
    by_phase = jnp.concatenate(spread(shard, PHASE, range(1, phases)), axis=0)
    if extra is not None:
        by_phase = jnp.concatenate([by_phase, extra], axis=0)
    cores = core_count()
    by_chip = jnp.stack(spread(by_phase, VOX, range(cores, vox, cores)))
    both = jnp.stack(spread(by_chip, VOX, range(1, cores)), axis=1)
    both = both.reshape(vox, by_phase.shape[0], shard.shape[1])
    rows = phases * shard.shape[0]
    return both[:, :rows].reshape(vox, phases, *shard.shape), both[:, rows:]


def scatter_sum(parts):
    vox, phases = parts.shape[:2]
    cores = core_count()
    split = parts.reshape(vox // cores, cores, phases, *parts.shape[2:])
    chips = split[:, 0]
    for m in range(1, cores):
        chips = chips + swap(split[:, m], VOX, m)
    mine = chips[0]
    for m in range(1, vox // cores):
        mine = mine + swap(chips[m], VOX, m * cores)
    total = mine[0]
    for m in range(1, phases):
        total = total + swap(mine[m], PHASE, m)
    return total


def phase_sum(x):
    phases = lax.axis_size(PHASE)
    if phases == 1:
        return x
    z = lax.axis_index(PHASE)
    which = (z ^ (z >> 1)) & 1
    half = x.shape[0] // 2
    keep = lax.dynamic_slice_in_dim(x, which * half, half)
    give = lax.dynamic_slice_in_dim(x, (1 - which) * half, half)
    keep = keep + swap(give, PHASE, 1)
    span = 4
    while span <= phases:
        keep = keep + swap(keep, PHASE, span - 1)
        span *= 2
    other = swap(keep, PHASE, 1)
    low = jnp.where(which == 0, keep, other)
    high = jnp.where(which == 0, other, keep)
    return jnp.concatenate([low, high], axis=0)


def exchange(x):
    return jnp.stack([x[0]] + [swap(x[m], VOX, m) for m in range(1, x.shape[0])])


def per_device(
    influence,
    weights,
    warp_tiles,
    owners,
    owner_slot,
    tile_index,
    structure,
    prescribed,
    importance,
    step_size,
):
    highest = lax.Precision.HIGHEST
    high = lax.Precision.HIGH
    matrix = influence[0]
    vox_rows, spots = matrix.shape
    block_rows = warp_tiles.shape[1]
    plans = weights.shape[1]
    local_blocks = vox_rows // block_rows
    vox_count = lax.axis_size(VOX)
    phases = lax.axis_size(PHASE)
    me_vox = lax.axis_index(VOX)
    me_phase = lax.axis_index(PHASE)
    slots_all = vox_count * CAP
    targets = owners[0, :, 0]
    my_slots = owner_slot[0]
    my_tiles = tile_index[0]

    def orders(names):
        before = jnp.tril(jnp.ones((local_blocks, local_blocks), jnp.int32), -1)
        same = (names[..., :, None] == names[..., None, :]).astype(jnp.int32)
        return jnp.sum(same * before, axis=-1)

    position = (targets ^ me_vox) * CAP + orders(targets)
    chosen_mask = jnp.arange(slots_all, dtype=jnp.int32)[:, None] == position[None, :]
    source = jnp.sum(
        jnp.where(chosen_mask, jnp.arange(1, local_blocks + 1, dtype=jnp.int32)[None, :], 0), axis=1
    )
    labels = jnp.zeros((LABEL_ROWS, plans), jnp.float32)
    labels = labels.at[0, :local_blocks].set(targets.astype(jnp.float32))
    labels = labels.at[1, :local_blocks].set(my_slots.astype(jnp.float32))

    own_tiles = warp_tiles[my_tiles]
    member = (structure[:, None] == jnp.arange(NSTRUCT, dtype=jnp.int32)[None, :]).astype(
        jnp.float32
    )
    target_dose = jnp.dot(member, prescribed, precision=highest, preferred_element_type=jnp.float32)
    voxel_weight = jnp.dot(
        member, importance[:, None], precision=highest, preferred_element_type=jnp.float32
    )
    place_vox = jnp.arange(vox_count) ^ me_vox
    place_phase = jnp.arange(phases) ^ me_phase

    new_weights = weights
    dose_field = jnp.zeros((vox_rows, plans), jnp.float32)
    for iteration in range(ITERS):
        pieces, infos = gather_weights(new_weights, labels if iteration == 0 else None)
        if iteration == 0:
            names = infos[:, 0, :local_blocks].astype(jnp.int32)
            slots = infos[:, 1, :local_blocks].astype(jnp.int32)
            order = jnp.where(names == me_vox, orders(names), -1)
            hit = order[:, None, :] == jnp.arange(CAP, dtype=jnp.int32)[None, :, None]
            received = jnp.sum(jnp.where(hit, slots[:, None, :] + 1, 0), axis=-1).reshape(slots_all) - 1
        whole = pieces[place_vox][:, place_phase]
        whole = whole.transpose(1, 0, 2, 3).reshape(spots, plans)
        phase_dose = jnp.dot(matrix, whole, precision=high, preferred_element_type=jnp.float32)
        blocks = phase_dose.reshape(local_blocks, block_rows, plans)
        warped = jnp.einsum("kab,kbp->kap", own_tiles, blocks, precision=high)
        padded = jnp.concatenate([jnp.zeros_like(warped[:1]), warped], axis=0)
        outgoing = padded[source].reshape(vox_count, CAP, block_rows, plans)
        incoming = exchange(outgoing).reshape(slots_all, block_rows, plans)
        partial_dose = (
            jnp.zeros((local_blocks + 1, block_rows, plans), jnp.float32).at[received].add(incoming)
        )[:local_blocks]
        field = phase_sum(partial_dose)
        dose_field = field.reshape(vox_rows, plans)
        adjoint = (voxel_weight * (dose_field - target_dose)).reshape(local_blocks, block_rows, plans)
        back = adjoint[jnp.maximum(received, 0)].reshape(vox_count, CAP, block_rows, plans)
        returned = exchange(back).reshape(slots_all, block_rows, plans)
        pulled = returned[position]
        local_adjoint = jnp.einsum("kab,kap->kbp", own_tiles, pulled, precision=high)
        gradient = lax.dot_general(
            matrix,
            local_adjoint.reshape(vox_rows, plans),
            (((0,), (0,)), ((), ())),
            precision=high,
            preferred_element_type=jnp.float32,
        )
        parts = gradient.reshape(phases, vox_count, spots // (phases * vox_count), plans)
        parts = parts[place_phase][:, place_vox].transpose(1, 0, 2, 3)
        total = scatter_sum(parts)
        new_weights = jnp.maximum(new_weights - step_size[None, :] * total, 0.0)
    return (new_weights, dose_field)


def solution(mesh):
    in_specs = (
        P("phase", "vox", None),
        P(("phase", "vox"), None),
        P(),
        P("phase", "vox", None),
        P("phase", "vox"),
        P("phase", "vox"),
        P("vox"),
        P(),
        P(),
        P(),
    )
    out_specs = (P(("phase", "vox"), None), P("vox", None))
    return jax.shard_map(
        per_device, mesh=mesh, in_specs=in_specs, out_specs=out_specs, check_vma=False
    )
```

time: 573 us -> 324 us (0.57); the launches traced: 564 us -> 324 us
  waiting for transfers between devices: 296 us -> 151 us
  blocking collectives: 143 us -> 0 us
  starting transfers between devices: 9.32 us -> 85.7 us
  matrix products: 67.7 us -> 39.9 us
  between operations: 14.5 us -> 1.7 us
  other arithmetic: 5.53 us -> 11.3 us
    unnamed x6 -> x0, waiting for transfers between devices: 186 us -> none
    ppermute x0 -> x62, waiting for transfers between devices: none -> 151 us  [swap(): return lax.ppermute(x, axis, [(i, i ^ mask) for i in range(count)])]
    psum x2 -> x0, waiting for transfers between devices: 95.3 us -> none  [per_device(): dose_field = lax.psum(partial_dose, 'phase')]
    all_gather x2 -> x0, blocking collectives: 86.6 us -> none  [per_device(): lax.all_gather(new_weights, ('phase', 'vox'), axis=0, tiled=True)]
    ppermute x0 -> x62, starting transfers between devices: none -> 85.7 us  [swap(): return lax.ppermute(x, axis, [(i, i ^ mask) for i in range(count)])]
    all_to_all x3 -> x0, blocking collectives: 56.3 us -> none  [the longest x2 37.8 us: per_device(): lax.all_to_all(back_slots.reshape(vox_count, CAP, block_rows * plans), 'v...]
    dot_general x16 -> x8, matrix products: 64.2 us -> 37.3 us  [the longest x2 19.3 us: per_device(): jnp.dot(matrix, whole, precision=high, preferred_element_type=jnp.float32)]
    gather x0 -> x14, local copies, waits for them, and re-layouts: none -> 18 us  [the longest x4 5.59 us: per_device(): parts = parts[place_phase][:, place_vox].transpose(1, 0, 2, 3)]
  transfers between devices with their start and end apart: 6 -> 62, of which waited for: 5 -> 41; matrix products, arithmetic and copies ran while one was open for 4% -> 3% of each run, Pallas kernels for 0% -> 0%
where the time goes in v1:
time: 324 us
  waiting for transfers between devices  151 us (47%)
  starting transfers between devices  85.7 us (26%)
  matrix products  39.9 us (12%)
  local copies, waits for them, and re-layouts  33.7 us (10%)
  other arithmetic  11.3 us (3%)
    ppermute x62, waiting for transfers between devices, swap(): return lax.ppermute(x, axis, [(i, i ^ mask) for i in range(count)])  151 us
    ppermute x62, starting transfers between devices, swap(): return lax.ppermute(x, axis, [(i, i ^ mask) for i in range(count)])  85.7 us
    dot_general x2, matrix products, per_device(): jnp.dot(matrix, whole, precision=high, preferred_element_type=jnp.float32)  19.3 us
    dot_general x2, matrix products, per_device(): lax.dot_general(matrix, local_adjoint.reshape(vox_rows, plans), (((0,), (...  13.5 us
  transfers between devices with their start and end apart: 62, of which 41 were waited for; matrix products, arithmetic and copies ran while one was open for 3% of the time, Pallas kernels for 0%

profile of v1, /device:TPU:0, one launch (start us, length us, event | category | flops | bytes accessed | tf_op | source)
XLA Modules:
  0.0 323.6 jit_solution(14624292716612605565)
XLA Ops:
  0.6 5.1 %collective-permute-start.2 = (f32[48,128]{1,0:T(8,128)}, f32[48,128]{1,0:T(8,128)S(1)}, u32[]{:S(2)}, u32[]{:S(2)}) collective-permute-start(f32[48,128]{1,0:T(8,128)} %param.15), channel_id=1, source_target_pairs={{0,24},{8,16},{16,8},{24,0},{1,25},{9,17},{17,9},{25,1},{2,26},{10... | collective-permute-start | bytes 73736 | tf_op jit(solution)/shard_map/ppermute | solution.py:16
  11.0 2.7 collective-permute-start.5
  14.6 2.8 gather_fusion
  19.1 1.7 collective-permute-done.6
  23.8 9.7 %fusion.8 = f32[2048,128]{0,1:T(8,128)S(1)} fusion(f32[1536,128]{1,0:T(8,128)S(1)} %bitcast.288, f32[1,2048,1536]{2,1,0:T(8,128)} %param.14), kind=kOutput, calls=%fused_computation.25 | convolution fusion | flops 2415919104 | bytes 14417920 | tf_op jit(solution)/shard_map/dot_general | solution.py:145
  38.8 1.4 collective-permute-start.12
  42.1 1.4 collective-permute-done.7
  44.5 5.5 %collective-permute-done.8 = f32[2,128,128]{2,1,0:T(8,128)S(1)} collective-permute-done((f32[2,128,128]{2,1,0:T(8,128)}, f32[2,128,128]{2,1,0:T(8,128)S(1)}, u32[]{:S(2)}, u32[]{:S(2)}) %collective-permute-start.8) | collective-permute-done | bytes 131104 | tf_op jit(solution)/shard_map/ppermute | solution.py:16
  50.0 6.0 %collective-permute-done.9 = f32[2,128,128]{2,1,0:T(8,128)S(1)} collective-permute-done((f32[2,128,128]{2,1,0:T(8,128)}, f32[2,128,128]{2,1,0:T(8,128)S(1)}, u32[]{:S(2)}, u32[]{:S(2)}) %collective-permute-start.9) | collective-permute-done | bytes 131104 | tf_op jit(solution)/shard_map/ppermute | solution.py:16
  56.2 1.6 scatter_fusion
  59.3 12.7 %collective-permute-done.14 = f32[8,128,128]{2,1,0:T(8,128)S(1)} collective-permute-done((f32[8,128,128]{2,1,0:T(8,128)S(1)}, f32[8,128,128]{2,1,0:T(8,128)S(1)}, u32[]{:S(2)}, u32[]{:S(2)}) %collective-permute-start.14) | collective-permute-done | bytes 524320 | tf_op jit(solution)/shard_map/ppermute | solution.py:16
  72.0 3.7 %collective-permute-start.15 = (f32[8,128,128]{2,1,0:T(8,128)S(1)}, f32[8,128,128]{2,1,0:T(8,128)S(1)}, u32[]{:S(2)}, u32[]{:S(2)}) collective-permute-start(f32[8,128,128]{2,1,0:T(8,128)S(1)} %dynamic-slice_add_fusion.1), channel_id=1, source_target_pairs={{0,24},{8,16},{16,8},{24,0},{1,25},{9,17},{17,9},{25,1},{2,26},{10... | collective-permute-start | bytes 1572872 | tf_op jit(solution)/shard_map/ppermute | solution.py:16
  75.7 11.5 %collective-permute-done.15 = f32[8,128,128]{2,1,0:T(8,128)S(1)} collective-permute-done((f32[8,128,128]{2,1,0:T(8,128)S(1)}, f32[8,128,128]{2,1,0:T(8,128)S(1)}, u32[]{:S(2)}, u32[]{:S(2)}) %collective-permute-start.15) | collective-permute-done | bytes 524320 | tf_op jit(solution)/shard_map/ppermute | solution.py:16
  87.3 10.9 %collective-permute-start.16 = (f32[8,128,128]{2,1,0:T(8,128)S(1)}, f32[8,128,128]{2,1,0:T(8,128)S(1)}, u32[]{:S(2)}, u32[]{:S(2)}) collective-permute-start(f32[8,128,128]{2,1,0:T(8,128)S(1)} %add.229), channel_id=1, source_target_pairs={{0,8},{8,0},{16,24},{24,16},{1,9},{9,1},{17,25},{25,17},{2,10},{10... | collective-permute-start | bytes 1572872 | tf_op jit(solution)/shard_map/ppermute | solution.py:16
  99.0 10.4 %collective-permute-done.16 = f32[8,128,128]{2,1,0:T(8,128)S(1)} collective-permute-done((f32[8,128,128]{2,1,0:T(8,128)S(1)}, f32[8,128,128]{2,1,0:T(8,128)S(1)}, u32[]{:S(2)}, u32[]{:S(2)}) %collective-permute-start.16) | collective-permute-done | bytes 524320 | tf_op jit(solution)/shard_map/ppermute | solution.py:16
  109.6 1.8 fusion.20
  111.4 1.8 gather_fusion.4
  115.2 2.5 collective-permute-start.20
  119.7 5.0 %collective-permute-done.18 = f32[2,128,128]{2,1,0:T(8,128)S(1)} collective-permute-done((f32[2,128,128]{2,1,0:T(8,128)S(1)}, f32[2,128,128]{2,1,0:T(8,128)S(1)}, u32[]{:S(2)}, u32[]{:S(2)}) %collective-permute-start.18) | collective-permute-done | bytes 131104 | tf_op jit(solution)/shard_map/ppermute | solution.py:16
  124.7 5.3 %collective-permute-done.19 = f32[2,128,128]{2,1,0:T(8,128)S(1)} collective-permute-done((f32[2,128,128]{2,1,0:T(8,128)S(1)}, f32[2,128,128]{2,1,0:T(8,128)S(1)}, u32[]{:S(2)}, u32[]{:S(2)}) %collective-permute-start.19) | collective-permute-done | bytes 131104 | tf_op jit(solution)/shard_map/ppermute | solution.py:16
  131.1 1.8 gather_fusion.5
  134.0 6.8 %fusion.11 = f32[1536,128]{0,1:T(8,128)S(1)} fusion(f32[2048,128]{1,0:T(8,128)S(1)} %bitcast.279, f32[1,2048,1536]{2,1,0:T(8,128)} %param.14), kind=kOutput, calls=%fused_computation.26 | convolution fusion | flops 2415919104 | bytes 14417920 | tf_op jit(solution)/shard_map/dot_general | solution.py:161
  142.0 2.7 gather_fusion.6
  144.6 1.7 gather_fusion.7
  146.5 1.7 collective-permute-done.24
  150.2 1.6 collective-permute-start.26
  151.8 2.1 collective-permute-done.25
  156.7 1.7 collective-permute-start.28
  158.4 2.2 collective-permute-start.30
  160.6 3.4 %collective-permute-done.30 = f32[48,128]{1,0:T(8,128)S(1)} collective-permute-done((f32[48,128]{1,0:T(8,128)S(1)}, f32[48,128]{1,0:T(8,128)S(1)}, u32[]{:S(2)}, u32[]{:S(2)}) %collective-permute-start.30) | collective-permute-done | bytes 24608 | tf_op jit(solution)/shard_map/ppermute | solution.py:16
  164.0 1.6 collective-permute-done.29
  165.6 1.4 collective-permute-start.33
  167.0 3.0 collective-permute-start.31
  172.1 1.6 collective-permute-start.35
  176.8 1.5 collective-permute-done.34
  178.3 2.0 collective-permute-done.36
  180.4 1.7 collective-permute-done.37
  182.2 1.5 gather_fusion.8
  183.7 2.7 gather_fusion.9
  186.4 9.6 %fusion.14 = f32[2048,128]{0,1:T(8,128)S(1)} fusion(f32[1536,128]{1,0:T(8,128)} %bitcast.289, f32[1,2048,1536]{2,1,0:T(8,128)} %param.14), kind=kOutput, calls=%fused_computation.27 | convolution fusion | flops 2415919104 | bytes 14417920 | tf_op jit(solution)/shard_map/dot_general | solution.py:145
  197.3 1.8 fusion.70
  199.3 1.6 gather_fusion.10
  203.0 1.9 collective-permute-start.43
  205.1 1.5 collective-permute-start.41
  208.9 4.7 %collective-permute-done.39 = f32[2,128,128]{2,1,0:T(8,128)S(1)} collective-permute-done((f32[2,128,128]{2,1,0:T(8,128)S(1)}, f32[2,128,128]{2,1,0:T(8,128)S(1)}, u32[]{:S(2)}, u32[]{:S(2)}) %collective-permute-start.39) | collective-permute-done | bytes 131104 | tf_op jit(solution)/shard_map/ppermute | solution.py:16
  213.9 5.2 %collective-permute-done.40 = f32[2,128,128]{2,1,0:T(8,128)S(1)} collective-permute-done((f32[2,128,128]{2,1,0:T(8,128)S(1)}, f32[2,128,128]{2,1,0:T(8,128)S(1)}, u32[]{:S(2)}, u32[]{:S(2)}) %collective-permute-start.40) | collective-permute-done | bytes 131104 | tf_op jit(solution)/shard_map/ppermute | solution.py:16
  220.3 2.8 scatter_fusion.1
  223.3 1.8 collective-permute-start.45
  225.1 11.9 %collective-permute-done.45 = f32[8,128,128]{2,1,0:T(8,128)S(1)} collective-permute-done((f32[8,128,128]{2,1,0:T(8,128)S(1)}, f32[8,128,128]{2,1,0:T(8,128)S(1)}, u32[]{:S(2)}, u32[]{:S(2)}) %collective-permute-start.45) | collective-permute-done | bytes 524320 | tf_op jit(solution)/shard_map/ppermute | solution.py:16
  237.1 2.1 collective-permute-start.46
  239.3 12.7 %collective-permute-done.46 = f32[8,128,128]{2,1,0:T(8,128)S(1)} collective-permute-done((f32[8,128,128]{2,1,0:T(8,128)S(1)}, f32[8,128,128]{2,1,0:T(8,128)S(1)}, u32[]{:S(2)}, u32[]{:S(2)}) %collective-permute-start.46) | collective-permute-done | bytes 524320 | tf_op jit(solution)/shard_map/ppermute | solution.py:16
  252.0 11.1 %collective-permute-start.47 = (f32[8,128,128]{2,1,0:T(8,128)S(1)}, f32[8,128,128]{2,1,0:T(8,128)S(1)}, u32[]{:S(2)}, u32[]{:S(2)}) collective-permute-start(f32[8,128,128]{2,1,0:T(8,128)S(1)} %add.241), channel_id=1, source_target_pairs={{0,8},{8,0},{16,24},{24,16},{1,9},{9,1},{17,25},{25,17},{2,10},{10... | collective-permute-start | bytes 1572872 | tf_op jit(solution)/shard_map/ppermute | solution.py:16
  263.1 11.4 %collective-permute-done.47 = f32[8,128,128]{2,1,0:T(8,128)S(1)} collective-permute-done((f32[8,128,128]{2,1,0:T(8,128)S(1)}, f32[8,128,128]{2,1,0:T(8,128)S(1)}, u32[]{:S(2)}, u32[]{:S(2)}) %collective-permute-start.47) | collective-permute-done | bytes 524320 | tf_op jit(solution)/shard_map/ppermute | solution.py:16
  277.4 1.8 collective-permute-start.53
  279.2 1.9 collective-permute-start.52
  283.4 5.0 %collective-permute-done.49 = f32[2,128,128]{2,1,0:T(8,128)S(1)} collective-permute-done((f32[2,128,128]{2,1,0:T(8,128)S(1)}, f32[2,128,128]{2,1,0:T(8,128)S(1)}, u32[]{:S(2)}, u32[]{:S(2)}) %collective-permute-start.49) | collective-permute-done | bytes 131104 | tf_op jit(solution)/shard_map/ppermute | solution.py:16
  288.6 5.4 %collective-permute-done.50 = f32[2,128,128]{2,1,0:T(8,128)S(1)} collective-permute-done((f32[2,128,128]{2,1,0:T(8,128)S(1)}, f32[2,128,128]{2,1,0:T(8,128)S(1)}, u32[]{:S(2)}, u32[]{:S(2)}) %collective-permute-start.50) | collective-permute-done | bytes 131104 | tf_op jit(solution)/shard_map/ppermute | solution.py:16
  295.9 6.7 %fusion.17 = f32[1536,128]{0,1:T(8,128)S(1)} fusion(f32[2048,128]{1,0:T(8,128)S(1)} %bitcast.278, f32[1,2048,1536]{2,1,0:T(8,128)} %param.14), kind=kOutput, calls=%fused_computation.28 | convolution fusion | flops 2415919104 | bytes 14417920 | tf_op jit(solution)/shard_map/dot_general | solution.py:161
  304.1 1.7 collective-permute-done.55
  306.9 1.8 collective-permute-start.58
  309.5 2.0 collective-permute-done.56
  311.5 2.2 collective-permute-done.58
  315.0 1.8 collective-permute-start.59
  318.9 3.6 %collective-permute-done.61 = f32[48,128]{1,0:T(8,128)S(1)} collective-permute-done((f32[48,128]{1,0:T(8,128)S(1)}, f32[48,128]{1,0:T(8,128)S(1)}, u32[]{:S(2)}, u32[]{:S(2)}) %collective-permute-start.61) | collective-permute-done | bytes 24608 | tf_op jit(solution)/shard_map/ppermute | solution.py:16
  (220 shorter events, 61.6 us)
Async XLA Ops:
  0.6 108.9 %copy-start = (f32[8,128]{1,0:T(8,128)S(1)}, f32[8,128]{1,0:T(8,128)}, u32[]{:S(2)}) copy-start(f32[8,128]{1,0:T(8,128)} %param.21) | copy-start | bytes 12292
  0.6 10.4 %collective-permute-start.2 = (f32[48,128]{1,0:T(8,128)}, f32[48,128]{1,0:T(8,128)S(1)}, u32[]{:S(2)}, u32[]{:S(2)}) collective-permute-start(f32[48,128]{1,0:T(8,128)} %param.15), channel_id=1, source_target_pairs={{0,24},{8,16},{16,8},{24,0},{1,25},{9,17},{17,9},{25,1},{2,26},{10... | collective-permute-start | bytes 73736 | tf_op jit(solution)/shard_map/ppermute | solution.py:16
  5.8 5.2 %collective-permute-start.1 = (f32[48,128]{1,0:T(8,128)}, f32[48,128]{1,0:T(8,128)S(1)}, u32[]{:S(2)}, u32[]{:S(2)}) collective-permute-start(f32[48,128]{1,0:T(8,128)} %param.15), channel_id=1, source_target_pairs={{0,16},{8,24},{16,0},{24,8},{1,17},{9,25},{17,1},{25,9},{2,18},{10... | collective-permute-start | bytes 73736 | tf_op jit(solution)/shard_map/ppermute | solution.py:16
  5.8 5.2 %collective-permute-start = (f32[48,128]{1,0:T(8,128)}, f32[48,128]{1,0:T(8,128)S(1)}, u32[]{:S(2)}, u32[]{:S(2)}) collective-permute-start(f32[48,128]{1,0:T(8,128)} %param.15), channel_id=1, source_target_pairs={{0,8},{8,0},{16,24},{24,16},{1,9},{9,1},{17,25},{25,17},{2,10},{10... | collective-permute-start | bytes 73736 | tf_op jit(solution)/shard_map/ppermute | solution.py:16
  11.0 6.4 %collective-permute-start.5 = (f32[200,128]{1,0:T(8,128)S(1)}, f32[200,128]{1,0:T(8,128)S(1)}, u32[]{:S(2)}, u32[]{:S(2)}) collective-permute-start(f32[200,128]{1,0:T(8,128)S(1)} %constant_dynamic-update-slice_fusion), channel_id=1, source_target_pairs={{0,6},{1,7},{2,4},{3,5},{4,2},{5,3},{6,0},{7,1},{8,14},{9,15},{10,... | collective-permute-start | bytes 307208 | tf_op jit(solution)/shard_map/ppermute | solution.py:16
  13.7 4.7 %collective-permute-start.4 = (f32[200,128]{1,0:T(8,128)S(1)}, f32[200,128]{1,0:T(8,128)S(1)}, u32[]{:S(2)}, u32[]{:S(2)}) collective-permute-start(f32[200,128]{1,0:T(8,128)S(1)} %constant_dynamic-update-slice_fusion), channel_id=1, source_target_pairs={{0,4},{1,5},{2,6},{3,7},{4,0},{5,1},{6,2},{7,3},{8,12},{9,13},{10,... | collective-permute-start | bytes 307208 | tf_op jit(solution)/shard_map/ppermute | solution.py:16
  14.2 4.7 %collective-permute-start.3 = (f32[200,128]{1,0:T(8,128)S(1)}, f32[200,128]{1,0:T(8,128)S(1)}, u32[]{:S(2)}, u32[]{:S(2)}) collective-permute-start(f32[200,128]{1,0:T(8,128)S(1)} %constant_dynamic-update-slice_fusion), channel_id=1, source_target_pairs={{0,2},{1,3},{2,0},{3,1},{4,6},{5,7},{6,4},{7,5},{8,10},{9,11},{10,... | collective-permute-start | bytes 307208 | tf_op jit(solution)/shard_map/ppermute | solution.py:16
  18.9 1.8 collective-permute-start.6
  37.6 18.5 %collective-permute-start.13 = (f32[2,128,128]{2,1,0:T(8,128)S(1)}, f32[2,128,128]{2,1,0:T(8,128)S(1)}, u32[]{:S(2)}, u32[]{:S(2)}) collective-permute-start(f32[2,128,128]{2,1,0:T(8,128)S(1)} %get-tuple-element.51), channel_id=1, source_target_pairs={{0,7},{1,6},{2,5},{3,4},{4,3},{5,2},{6,1},{7,0},{8,15},{9,14},{10,... | collective-permute-start | bytes 393224 | tf_op jit(solution)/shard_map/ppermute | solution.py:16
  38.8 17.2 %collective-permute-start.12 = (f32[2,128,128]{2,1,0:T(8,128)S(1)}, f32[2,128,128]{2,1,0:T(8,128)S(1)}, u32[]{:S(2)}, u32[]{:S(2)}) collective-permute-start(f32[2,128,128]{2,1,0:T(8,128)S(1)} %get-tuple-element.52), channel_id=1, source_target_pairs={{0,6},{1,7},{2,4},{3,5},{4,2},{5,3},{6,0},{7,1},{8,14},{9,15},{10,... | collective-permute-start | bytes 393224 | tf_op jit(solution)/shard_map/ppermute | solution.py:16
  40.3 15.8 %collective-permute-start.11 = (f32[2,128,128]{2,1,0:T(8,128)}, f32[2,128,128]{2,1,0:T(8,128)S(1)}, u32[]{:S(2)}, u32[]{:S(2)}) collective-permute-start(f32[2,128,128]{2,1,0:T(8,128)} %get-tuple-element.53), channel_id=1, source_target_pairs={{0,5},{1,4},{2,7},{3,6},{4,1},{5,0},{6,3},{7,2},{8,13},{9,12},{10,... | collective-permute-start | bytes 393224 | tf_op jit(solution)/shard_map/ppermute | solution.py:16
  41.5 14.5 %collective-permute-start.10 = (f32[2,128,128]{2,1,0:T(8,128)}, f32[2,128,128]{2,1,0:T(8,128)S(1)}, u32[]{:S(2)}, u32[]{:S(2)}) collective-permute-start(f32[2,128,128]{2,1,0:T(8,128)} %get-tuple-element.54), channel_id=1, source_target_pairs={{0,4},{1,5},{2,6},{3,7},{4,0},{5,1},{6,2},{7,3},{8,12},{9,13},{10,... | collective-permute-start | bytes 393224 | tf_op jit(solution)/shard_map/ppermute | solution.py:16
  42.0 1.6 collective-permute-start.7
  43.5 6.5 %collective-permute-start.8 = (f32[2,128,128]{2,1,0:T(8,128)}, f32[2,128,128]{2,1,0:T(8,128)S(1)}, u32[]{:S(2)}, u32[]{:S(2)}) collective-permute-start(f32[2,128,128]{2,1,0:T(8,128)} %get-tuple-element.56), channel_id=1, source_target_pairs={{0,2},{1,3},{2,0},{3,1},{4,6},{5,7},{6,4},{7,5},{8,10},{9,11},{10,... | collective-permute-start | bytes 393224 | tf_op jit(solution)/shard_map/ppermute | solution.py:16
  50.0 6.0 %collective-permute-start.9 = (f32[2,128,128]{2,1,0:T(8,128)}, f32[2,128,128]{2,1,0:T(8,128)S(1)}, u32[]{:S(2)}, u32[]{:S(2)}) collective-permute-start(f32[2,128,128]{2,1,0:T(8,128)} %get-tuple-element.55), channel_id=1, source_target_pairs={{0,3},{1,2},{2,1},{3,0},{4,7},{5,6},{6,5},{7,4},{8,11},{9,10},{10,... | collective-permute-start | bytes 393224 | tf_op jit(solution)/shard_map/ppermute | solution.py:16
  56.2 42.0 %copy-start.7 = (s32[2048]{0:T(1024)S(1)}, s32[2048]{0:T(1024)}, u32[]{:S(2)}) copy-start(s32[2048]{0:T(1024)} %param.20) | copy-start | bytes 24580
  58.0 14.0 %collective-permute-start.14 = (f32[8,128,128]{2,1,0:T(8,128)S(1)}, f32[8,128,128]{2,1,0:T(8,128)S(1)}, u32[]{:S(2)}, u32[]{:S(2)}) collective-permute-start(f32[8,128,128]{2,1,0:T(8,128)S(1)} %constant_dynamic-slice_fusion), channel_id=1, source_target_pairs={{0,8},{8,0},{16,24},{24,16},{1,9},{9,1},{17,25},{25,17},{2,10},{10... | collective-permute-start | bytes 1572872 | tf_op jit(solution)/shard_map/ppermute | solution.py:16
  72.0 15.1 %collective-permute-start.15 = (f32[8,128,128]{2,1,0:T(8,128)S(1)}, f32[8,128,128]{2,1,0:T(8,128)S(1)}, u32[]{:S(2)}, u32[]{:S(2)}) collective-permute-start(f32[8,128,128]{2,1,0:T(8,128)S(1)} %dynamic-slice_add_fusion.1), channel_id=1, source_target_pairs={{0,24},{8,16},{16,8},{24,0},{1,25},{9,17},{17,9},{25,1},{2,26},{10... | collective-permute-start | bytes 1572872 | tf_op jit(solution)/shard_map/ppermute | solution.py:16
  87.3 22.1 %collective-permute-start.16 = (f32[8,128,128]{2,1,0:T(8,128)S(1)}, f32[8,128,128]{2,1,0:T(8,128)S(1)}, u32[]{:S(2)}, u32[]{:S(2)}) collective-permute-start(f32[8,128,128]{2,1,0:T(8,128)S(1)} %add.229), channel_id=1, source_target_pairs={{0,8},{8,0},{16,24},{24,16},{1,9},{9,1},{17,25},{25,17},{2,10},{10... | collective-permute-start | bytes 1572872 | tf_op jit(solution)/shard_map/ppermute | solution.py:16
  113.3 16.8 %collective-permute-start.23 = (f32[2,128,128]{2,1,0:T(8,128)S(1)}, f32[2,128,128]{2,1,0:T(8,128)S(1)}, u32[]{:S(2)}, u32[]{:S(2)}) collective-permute-start(f32[2,128,128]{2,1,0:T(8,128)S(1)} %get-tuple-element.42), channel_id=1, source_target_pairs={{0,7},{1,6},{2,5},{3,4},{4,3},{5,2},{6,1},{7,0},{8,15},{9,14},{10,... | collective-permute-start | bytes 393224 | tf_op jit(solution)/shard_map/ppermute | solution.py:16
  113.4 16.7 %collective-permute-start.22 = (f32[2,128,128]{2,1,0:T(8,128)S(1)}, f32[2,128,128]{2,1,0:T(8,128)S(1)}, u32[]{:S(2)}, u32[]{:S(2)}) collective-permute-start(f32[2,128,128]{2,1,0:T(8,128)S(1)} %get-tuple-element.43), channel_id=1, source_target_pairs={{0,6},{1,7},{2,4},{3,5},{4,2},{5,3},{6,0},{7,1},{8,14},{9,15},{10,... | collective-permute-start | bytes 393224 | tf_op jit(solution)/shard_map/ppermute | solution.py:16
  114.4 15.7 %collective-permute-start.21 = (f32[2,128,128]{2,1,0:T(8,128)S(1)}, f32[2,128,128]{2,1,0:T(8,128)S(1)}, u32[]{:S(2)}, u32[]{:S(2)}) collective-permute-start(f32[2,128,128]{2,1,0:T(8,128)S(1)} %get-tuple-element.44), channel_id=1, source_target_pairs={{0,5},{1,4},{2,7},{3,6},{4,1},{5,0},{6,3},{7,2},{8,13},{9,12},{10,... | collective-permute-start | bytes 393224 | tf_op jit(solution)/shard_map/ppermute | solution.py:16
  115.2 14.8 %collective-permute-start.20 = (f32[2,128,128]{2,1,0:T(8,128)S(1)}, f32[2,128,128]{2,1,0:T(8,128)S(1)}, u32[]{:S(2)}, u32[]{:S(2)}) collective-permute-start(f32[2,128,128]{2,1,0:T(8,128)S(1)} %get-tuple-element.45), channel_id=1, source_target_pairs={{0,4},{1,5},{2,6},{3,7},{4,0},{5,1},{6,2},{7,3},{8,12},{9,13},{10,... | collective-permute-start | bytes 393224 | tf_op jit(solution)/shard_map/ppermute | solution.py:16
  117.8 1.3 collective-permute-start.17
  119.1 5.6 %collective-permute-start.18 = (f32[2,128,128]{2,1,0:T(8,128)S(1)}, f32[2,128,128]{2,1,0:T(8,128)S(1)}, u32[]{:S(2)}, u32[]{:S(2)}) collective-permute-start(f32[2,128,128]{2,1,0:T(8,128)S(1)} %get-tuple-element.47), channel_id=1, source_target_pairs={{0,2},{1,3},{2,0},{3,1},{4,6},{5,7},{6,4},{7,5},{8,10},{9,11},{10,... | collective-permute-start | bytes 393224 | tf_op jit(solution)/shard_map/ppermute | solution.py:16
  124.7 5.3 %collective-permute-start.19 = (f32[2,128,128]{2,1,0:T(8,128)S(1)}, f32[2,128,128]{2,1,0:T(8,128)S(1)}, u32[]{:S(2)}, u32[]{:S(2)}) collective-permute-start(f32[2,128,128]{2,1,0:T(8,128)S(1)} %get-tuple-element.46), channel_id=1, source_target_pairs={{0,3},{1,2},{2,1},{3,0},{4,7},{5,6},{6,5},{7,4},{8,11},{9,10},{10,... | collective-permute-start | bytes 393224 | tf_op jit(solution)/shard_map/ppermute | solution.py:16
  146.4 1.8 collective-permute-start.24
  148.3 5.7 %collective-permute-start.25 = (f32[4,48,128]{2,1,0:T(8,128)S(1)}, f32[4,48,128]{2,1,0:T(8,128)S(1)}, u32[]{:S(2)}, u32[]{:S(2)}) collective-permute-start(f32[4,48,128]{2,1,0:T(8,128)S(1)} %get-tuple-element.67), channel_id=1, source_target_pairs={{0,2},{1,3},{2,0},{3,1},{4,6},{5,7},{6,4},{7,5},{8,10},{9,11},{10,... | collective-permute-start | bytes 294920 | tf_op jit(solution)/shard_map/ppermute | solution.py:16
  149.4 5.8 %collective-permute-start.27 = (f32[4,48,128]{2,1,0:T(8,128)S(1)}, f32[4,48,128]{2,1,0:T(8,128)S(1)}, u32[]{:S(2)}, u32[]{:S(2)}) collective-permute-start(f32[4,48,128]{2,1,0:T(8,128)S(1)} %get-tuple-element.68), channel_id=1, source_target_pairs={{0,6},{1,7},{2,4},{3,5},{4,2},{5,3},{6,0},{7,1},{8,14},{9,15},{10,... | collective-permute-start | bytes 294920 | tf_op jit(solution)/shard_map/ppermute | solution.py:16
  150.2 6.4 %collective-permute-start.26 = (f32[4,48,128]{2,1,0:T(8,128)S(1)}, f32[4,48,128]{2,1,0:T(8,128)S(1)}, u32[]{:S(2)}, u32[]{:S(2)}) collective-permute-start(f32[4,48,128]{2,1,0:T(8,128)S(1)} %get-tuple-element.69), channel_id=1, source_target_pairs={{0,4},{1,5},{2,6},{3,7},{4,0},{5,1},{6,2},{7,3},{8,12},{9,13},{10,... | collective-permute-start | bytes 294920 | tf_op jit(solution)/shard_map/ppermute | solution.py:16
  156.7 4.0 %collective-permute-start.28 = (f32[48,128]{1,0:T(8,128)S(1)}, f32[48,128]{1,0:T(8,128)S(1)}, u32[]{:S(2)}, u32[]{:S(2)}) collective-permute-start(f32[48,128]{1,0:T(8,128)S(1)} %get-tuple-element.75), channel_id=1, source_target_pairs={{0,8},{8,0},{16,24},{24,16},{1,9},{9,1},{17,25},{25,17},{2,10},{10... | collective-permute-start | bytes 73736 | tf_op jit(solution)/shard_map/ppermute | solution.py:16
  158.4 5.6 %collective-permute-start.30 = (f32[48,128]{1,0:T(8,128)S(1)}, f32[48,128]{1,0:T(8,128)S(1)}, u32[]{:S(2)}, u32[]{:S(2)}) collective-permute-start(f32[48,128]{1,0:T(8,128)S(1)} %get-tuple-element.76), channel_id=1, source_target_pairs={{0,24},{8,16},{16,8},{24,0},{1,25},{9,17},{17,9},{25,1},{2,26},{10... | collective-permute-start | bytes 73736 | tf_op jit(solution)/shard_map/ppermute | solution.py:16
  160.6 5.0 %collective-permute-start.29 = (f32[48,128]{1,0:T(8,128)S(1)}, f32[48,128]{1,0:T(8,128)S(1)}, u32[]{:S(2)}, u32[]{:S(2)}) collective-permute-start(f32[48,128]{1,0:T(8,128)S(1)} %get-tuple-element.77), channel_id=1, source_target_pairs={{0,16},{8,24},{16,0},{24,8},{1,17},{9,25},{17,1},{25,9},{2,18},{10... | collective-permute-start | bytes 73736 | tf_op jit(solution)/shard_map/ppermute | solution.py:16
  165.6 5.7 %collective-permute-start.33 = (f32[48,128]{1,0:T(8,128)S(1)}, f32[48,128]{1,0:T(8,128)S(1)}, u32[]{:S(2)}, u32[]{:S(2)}) collective-permute-start(f32[48,128]{1,0:T(8,128)S(1)} %fusion.48), channel_id=1, source_target_pairs={{0,24},{8,16},{16,8},{24,0},{1,25},{9,17},{17,9},{25,1},{2,26},{10... | collective-permute-start | bytes 73736 | tf_op jit(solution)/shard_map/ppermute | solution.py:16
  167.0 4.8 %collective-permute-start.32 = (f32[48,128]{1,0:T(8,128)S(1)}, f32[48,128]{1,0:T(8,128)S(1)}, u32[]{:S(2)}, u32[]{:S(2)}) collective-permute-start(f32[48,128]{1,0:T(8,128)S(1)} %fusion.48), channel_id=1, source_target_pairs={{0,16},{8,24},{16,0},{24,8},{1,17},{9,25},{17,1},{25,9},{2,18},{10... | collective-permute-start | bytes 73736 | tf_op jit(solution)/shard_map/ppermute | solution.py:16
  167.0 5.1 %collective-permute-start.31 = (f32[48,128]{1,0:T(8,128)S(1)}, f32[48,128]{1,0:T(8,128)S(1)}, u32[]{:S(2)}, u32[]{:S(2)}) collective-permute-start(f32[48,128]{1,0:T(8,128)S(1)} %fusion.48), channel_id=1, source_target_pairs={{0,8},{8,0},{16,24},{24,16},{1,9},{9,1},{17,25},{25,17},{2,10},{10... | collective-permute-start | bytes 73736 | tf_op jit(solution)/shard_map/ppermute | solution.py:16
  172.1 4.7 %collective-permute-start.35 = (f32[192,128]{1,0:T(8,128)S(1)}, f32[192,128]{1,0:T(8,128)S(1)}, u32[]{:S(2)}, u32[]{:S(2)}) collective-permute-start(f32[192,128]{1,0:T(8,128)S(1)} %get-tuple-element.74), channel_id=1, source_target_pairs={{0,4},{1,5},{2,6},{3,7},{4,0},{5,1},{6,2},{7,3},{8,12},{9,13},{10,... | collective-permute-start | bytes 294920 | tf_op jit(solution)/shard_map/ppermute | solution.py:16
  173.7 4.6 %collective-permute-start.34 = (f32[192,128]{1,0:T(8,128)S(1)}, f32[192,128]{1,0:T(8,128)S(1)}, u32[]{:S(2)}, u32[]{:S(2)}) collective-permute-start(f32[192,128]{1,0:T(8,128)S(1)} %get-tuple-element.74), channel_id=1, source_target_pairs={{0,2},{1,3},{2,0},{3,1},{4,6},{5,7},{6,4},{7,5},{8,10},{9,11},{10,... | collective-permute-start | bytes 294920 | tf_op jit(solution)/shard_map/ppermute | solution.py:16
  174.8 5.5 %collective-permute-start.36 = (f32[192,128]{1,0:T(8,128)S(1)}, f32[192,128]{1,0:T(8,128)S(1)}, u32[]{:S(2)}, u32[]{:S(2)}) collective-permute-start(f32[192,128]{1,0:T(8,128)S(1)} %get-tuple-element.74), channel_id=1, source_target_pairs={{0,6},{1,7},{2,4},{3,5},{4,2},{5,3},{6,0},{7,1},{8,14},{9,15},{10,... | collective-permute-start | bytes 294920 | tf_op jit(solution)/shard_map/ppermute | solution.py:16
  180.3 1.8 collective-permute-start.37
  202.2 17.0 %collective-permute-start.44 = (f32[2,128,128]{2,1,0:T(8,128)S(1)}, f32[2,128,128]{2,1,0:T(8,128)S(1)}, u32[]{:S(2)}, u32[]{:S(2)}) collective-permute-start(f32[2,128,128]{2,1,0:T(8,128)S(1)} %get-tuple-element.35), channel_id=1, source_target_pairs={{0,7},{1,6},{2,5},{3,4},{4,3},{5,2},{6,1},{7,0},{8,15},{9,14},{10,... | collective-permute-start | bytes 393224 | tf_op jit(solution)/shard_map/ppermute | solution.py:16
  203.0 16.2 %collective-permute-start.43 = (f32[2,128,128]{2,1,0:T(8,128)S(1)}, f32[2,128,128]{2,1,0:T(8,128)S(1)}, u32[]{:S(2)}, u32[]{:S(2)}) collective-permute-start(f32[2,128,128]{2,1,0:T(8,128)S(1)} %get-tuple-element.36), channel_id=1, source_target_pairs={{0,6},{1,7},{2,4},{3,5},{4,2},{5,3},{6,0},{7,1},{8,14},{9,15},{10,... | collective-permute-start | bytes 393224 | tf_op jit(solution)/shard_map/ppermute | solution.py:16
  204.9 14.2 %collective-permute-start.42 = (f32[2,128,128]{2,1,0:T(8,128)S(1)}, f32[2,128,128]{2,1,0:T(8,128)S(1)}, u32[]{:S(2)}, u32[]{:S(2)}) collective-permute-start(f32[2,128,128]{2,1,0:T(8,128)S(1)} %get-tuple-element.37), channel_id=1, source_target_pairs={{0,5},{1,4},{2,7},{3,6},{4,1},{5,0},{6,3},{7,2},{8,13},{9,12},{10,... | collective-permute-start | bytes 393224 | tf_op jit(solution)/shard_map/ppermute | solution.py:16
  205.1 14.0 %collective-permute-start.41 = (f32[2,128,128]{2,1,0:T(8,128)S(1)}, f32[2,128,128]{2,1,0:T(8,128)S(1)}, u32[]{:S(2)}, u32[]{:S(2)}) collective-permute-start(f32[2,128,128]{2,1,0:T(8,128)S(1)} %get-tuple-element.38), channel_id=1, source_target_pairs={{0,4},{1,5},{2,6},{3,7},{4,0},{5,1},{6,2},{7,3},{8,12},{9,13},{10,... | collective-permute-start | bytes 393224 | tf_op jit(solution)/shard_map/ppermute | solution.py:16
  206.6 1.3 collective-permute-start.38
  208.0 5.7 %collective-permute-start.39 = (f32[2,128,128]{2,1,0:T(8,128)S(1)}, f32[2,128,128]{2,1,0:T(8,128)S(1)}, u32[]{:S(2)}, u32[]{:S(2)}) collective-permute-start(f32[2,128,128]{2,1,0:T(8,128)S(1)} %get-tuple-element.40), channel_id=1, source_target_pairs={{0,2},{1,3},{2,0},{3,1},{4,6},{5,7},{6,4},{7,5},{8,10},{9,11},{10,... | collective-permute-start | bytes 393224 | tf_op jit(solution)/shard_map/ppermute | solution.py:16
  213.7 5.4 %collective-permute-start.40 = (f32[2,128,128]{2,1,0:T(8,128)S(1)}, f32[2,128,128]{2,1,0:T(8,128)S(1)}, u32[]{:S(2)}, u32[]{:S(2)}) collective-permute-start(f32[2,128,128]{2,1,0:T(8,128)S(1)} %get-tuple-element.39), channel_id=1, source_target_pairs={{0,3},{1,2},{2,1},{3,0},{4,7},{5,6},{6,5},{7,4},{8,11},{9,10},{10,... | collective-permute-start | bytes 393224 | tf_op jit(solution)/shard_map/ppermute | solution.py:16
  223.3 13.8 %collective-permute-start.45 = (f32[8,128,128]{2,1,0:T(8,128)S(1)}, f32[8,128,128]{2,1,0:T(8,128)S(1)}, u32[]{:S(2)}, u32[]{:S(2)}) collective-permute-start(f32[8,128,128]{2,1,0:T(8,128)S(1)} %constant_dynamic-slice_fusion.1), channel_id=1, source_target_pairs={{0,8},{8,0},{16,24},{24,16},{1,9},{9,1},{17,25},{25,17},{2,10},{10... | collective-permute-start | bytes 1572872 | tf_op jit(solution)/shard_map/ppermute | solution.py:16
  237.1 14.8 %collective-permute-start.46 = (f32[8,128,128]{2,1,0:T(8,128)S(1)}, f32[8,128,128]{2,1,0:T(8,128)S(1)}, u32[]{:S(2)}, u32[]{:S(2)}) collective-permute-start(f32[8,128,128]{2,1,0:T(8,128)S(1)} %dynamic-slice_add_fusion), channel_id=1, source_target_pairs={{0,24},{8,16},{16,8},{24,0},{1,25},{9,17},{17,9},{25,1},{2,26},{10... | collective-permute-start | bytes 1572872 | tf_op jit(solution)/shard_map/ppermute | solution.py:16
  252.0 22.4 %collective-permute-start.47 = (f32[8,128,128]{2,1,0:T(8,128)S(1)}, f32[8,128,128]{2,1,0:T(8,128)S(1)}, u32[]{:S(2)}, u32[]{:S(2)}) collective-permute-start(f32[8,128,128]{2,1,0:T(8,128)S(1)} %add.241), channel_id=1, source_target_pairs={{0,8},{8,0},{16,24},{24,16},{1,9},{9,1},{17,25},{25,17},{2,10},{10... | collective-permute-start | bytes 1572872 | tf_op jit(solution)/shard_map/ppermute | solution.py:16
  276.3 17.9 %collective-permute-start.54 = (f32[2,128,128]{2,1,0:T(8,128)S(1)}, f32[2,128,128]{2,1,0:T(8,128)S(1)}, u32[]{:S(2)}, u32[]{:S(2)}) collective-permute-start(f32[2,128,128]{2,1,0:T(8,128)S(1)} %get-tuple-element.26), channel_id=1, source_target_pairs={{0,7},{1,6},{2,5},{3,4},{4,3},{5,2},{6,1},{7,0},{8,15},{9,14},{10,... | collective-permute-start | bytes 393224 | tf_op jit(solution)/shard_map/ppermute | solution.py:16
  277.4 16.8 %collective-permute-start.53 = (f32[2,128,128]{2,1,0:T(8,128)S(1)}, f32[2,128,128]{2,1,0:T(8,128)S(1)}, u32[]{:S(2)}, u32[]{:S(2)}) collective-permute-start(f32[2,128,128]{2,1,0:T(8,128)S(1)} %get-tuple-element.27), channel_id=1, source_target_pairs={{0,6},{1,7},{2,4},{3,5},{4,2},{5,3},{6,0},{7,1},{8,14},{9,15},{10,... | collective-permute-start | bytes 393224 | tf_op jit(solution)/shard_map/ppermute | solution.py:16
  279.2 14.9 %collective-permute-start.52 = (f32[2,128,128]{2,1,0:T(8,128)S(1)}, f32[2,128,128]{2,1,0:T(8,128)S(1)}, u32[]{:S(2)}, u32[]{:S(2)}) collective-permute-start(f32[2,128,128]{2,1,0:T(8,128)S(1)} %get-tuple-element.28), channel_id=1, source_target_pairs={{0,5},{1,4},{2,7},{3,6},{4,1},{5,0},{6,3},{7,2},{8,13},{9,12},{10,... | collective-permute-start | bytes 393224 | tf_op jit(solution)/shard_map/ppermute | solution.py:16
  281.1 13.0 %collective-permute-start.51 = (f32[2,128,128]{2,1,0:T(8,128)S(1)}, f32[2,128,128]{2,1,0:T(8,128)S(1)}, u32[]{:S(2)}, u32[]{:S(2)}) collective-permute-start(f32[2,128,128]{2,1,0:T(8,128)S(1)} %get-tuple-element.29), channel_id=1, source_target_pairs={{0,4},{1,5},{2,6},{3,7},{4,0},{5,1},{6,2},{7,3},{8,12},{9,13},{10,... | collective-permute-start | bytes 393224 | tf_op jit(solution)/shard_map/ppermute | solution.py:16
  281.1 1.3 collective-permute-start.48
  282.4 6.0 %collective-permute-start.49 = (f32[2,128,128]{2,1,0:T(8,128)S(1)}, f32[2,128,128]{2,1,0:T(8,128)S(1)}, u32[]{:S(2)}, u32[]{:S(2)}) collective-permute-start(f32[2,128,128]{2,1,0:T(8,128)S(1)} %get-tuple-element.31), channel_id=1, source_target_pairs={{0,2},{1,3},{2,0},{3,1},{4,6},{5,7},{6,4},{7,5},{8,10},{9,11},{10,... | collective-permute-start | bytes 393224 | tf_op jit(solution)/shard_map/ppermute | solution.py:16
  288.4 5.6 %collective-permute-start.50 = (f32[2,128,128]{2,1,0:T(8,128)S(1)}, f32[2,128,128]{2,1,0:T(8,128)S(1)}, u32[]{:S(2)}, u32[]{:S(2)}) collective-permute-start(f32[2,128,128]{2,1,0:T(8,128)S(1)} %get-tuple-element.30), channel_id=1, source_target_pairs={{0,3},{1,2},{2,1},{3,0},{4,7},{5,6},{6,5},{7,4},{8,11},{9,10},{10,... | collective-permute-start | bytes 393224 | tf_op jit(solution)/shard_map/ppermute | solution.py:16
  304.0 1.8 collective-permute-start.55
  305.9 5.6 %collective-permute-start.56 = (f32[4,48,128]{2,1,0:T(8,128)S(1)}, f32[4,48,128]{2,1,0:T(8,128)S(1)}, u32[]{:S(2)}, u32[]{:S(2)}) collective-permute-start(f32[4,48,128]{2,1,0:T(8,128)S(1)} %get-tuple-element.62), channel_id=1, source_target_pairs={{0,2},{1,3},{2,0},{3,1},{4,6},{5,7},{6,4},{7,5},{8,10},{9,11},{10,... | collective-permute-start | bytes 294920 | tf_op jit(solution)/shard_map/ppermute | solution.py:16
  306.9 6.8 %collective-permute-start.58 = (f32[4,48,128]{2,1,0:T(8,128)S(1)}, f32[4,48,128]{2,1,0:T(8,128)S(1)}, u32[]{:S(2)}, u32[]{:S(2)}) collective-permute-start(f32[4,48,128]{2,1,0:T(8,128)S(1)} %get-tuple-element.63), channel_id=1, source_target_pairs={{0,6},{1,7},{2,4},{3,5},{4,2},{5,3},{6,0},{7,1},{8,14},{9,15},{10,... | collective-permute-start | bytes 294920 | tf_op jit(solution)/shard_map/ppermute | solution.py:16
  308.7 6.3 %collective-permute-start.57 = (f32[4,48,128]{2,1,0:T(8,128)S(1)}, f32[4,48,128]{2,1,0:T(8,128)S(1)}, u32[]{:S(2)}, u32[]{:S(2)}) collective-permute-start(f32[4,48,128]{2,1,0:T(8,128)S(1)} %get-tuple-element.64), channel_id=1, source_target_pairs={{0,4},{1,5},{2,6},{3,7},{4,0},{5,1},{6,2},{7,3},{8,12},{9,13},{10,... | collective-permute-start | bytes 294920 | tf_op jit(solution)/shard_map/ppermute | solution.py:16
  315.0 3.9 %collective-permute-start.59 = (f32[48,128]{1,0:T(8,128)S(1)}, f32[48,128]{1,0:T(8,128)S(1)}, u32[]{:S(2)}, u32[]{:S(2)}) collective-permute-start(f32[48,128]{1,0:T(8,128)S(1)} %get-tuple-element.70), channel_id=1, source_target_pairs={{0,8},{8,0},{16,24},{24,16},{1,9},{9,1},{17,25},{25,17},{2,10},{10... | collective-permute-start | bytes 73736 | tf_op jit(solution)/shard_map/ppermute | solution.py:16
  316.8 5.7 %collective-permute-start.61 = (f32[48,128]{1,0:T(8,128)S(1)}, f32[48,128]{1,0:T(8,128)S(1)}, u32[]{:S(2)}, u32[]{:S(2)}) collective-permute-start(f32[48,128]{1,0:T(8,128)S(1)} %get-tuple-element.71), channel_id=1, source_target_pairs={{0,24},{8,16},{16,8},{24,0},{1,25},{9,17},{17,9},{25,1},{2,26},{10... | collective-permute-start | bytes 73736 | tf_op jit(solution)/shard_map/ppermute | solution.py:16
  317.7 5.3 %collective-permute-start.60 = (f32[48,128]{1,0:T(8,128)S(1)}, f32[48,128]{1,0:T(8,128)S(1)}, u32[]{:S(2)}, u32[]{:S(2)}) collective-permute-start(f32[48,128]{1,0:T(8,128)S(1)} %get-tuple-element.72), channel_id=1, source_target_pairs={{0,16},{8,24},{16,0},{24,8},{1,17},{9,25},{17,1},{25,9},{2,18},{10... | collective-permute-start | bytes 73736 | tf_op jit(solution)/shard_map/ppermute | solution.py:16
  (9 other events, 165.0 us)

commit v2 on v1

v2 whole, which is shorter than its diff:
```python
import functools

import jax
import jax.numpy as jnp
from jax import lax
from jax.experimental import pallas as pl
from jax.experimental.pallas import tpu as pltpu
from jax.sharding import PartitionSpec as P

CAP = 2
NSTRUCT = 8
ITERS = 2
CHUNKS = 2
VOX = "vox"
PHASE = "phase"
LABEL_ROWS = 16
F32 = jnp.float32
BF16 = jnp.bfloat16
LARGE = 28 << 20
SMALL = 8 << 20


def swap(x, axis, mask):
    count = lax.axis_size(axis)
    return lax.ppermute(x, axis, [(i, i ^ mask) for i in range(count)])


def spread(x, axis, masks):
    return [x] + [swap(x, axis, m) for m in masks]


def core_count():
    return min(2, lax.axis_size(VOX))


def halves(x, axis):
    big = x.astype(BF16)
    small = (x - big.astype(F32)).astype(BF16)
    return jnp.concatenate([big, small], axis=axis)


def product(left, right):
    rows, cols = left.shape[0], right.shape[1]
    full = jnp.dot(halves(left, 0), halves(right, 1), preferred_element_type=F32)
    return full[:rows, :cols] + (full[:rows, cols:] + full[rows:, :cols])


def split_pieces(me_ref, out, pieces, rows, vox, phases):
    cores = len(pieces)
    for c, ref in enumerate(pieces):
        for k in range(vox // cores):
            for p in range(phases):
                v = me_ref[0] ^ (k * cores + c)
                at = ((me_ref[1] ^ p) * vox + v) * rows
                out[pl.ds(pl.multiple_of(at, rows), rows), :] = halves(
                    ref[k, p * rows : (p + 1) * rows, :], 1
                )


def forward_body(
    dims, source_ref, valid_ref, tile_ref, me_ref, *refs
):
    vox, phases, rows, pieces_n, chunks = dims
    blocks, tiles = refs[:CAP], refs[CAP : 2 * CAP]
    pieces = refs[2 * CAP : 2 * CAP + pieces_n]
    outs = refs[2 * CAP + pieces_n : -1]
    terms = refs[-1]
    step = pl.program_id(0)
    height = blocks[0].shape[0]
    plans = terms.shape[1] // 2

    @pl.when(step == 0)
    def _():
        if len(pieces[0].shape) == 2:
            terms[...] = halves(pieces[0][...], 1)
        else:
            split_pieces(me_ref, terms, pieces, rows, vox, phases)

    rows_now = jnp.concatenate([b[...] for b in blocks], axis=0)
    full = jnp.dot(halves(rows_now, 0), terms[...], preferred_element_type=F32)
    n = rows_now.shape[0]
    dose = full[:n, :plans] + (full[:n, plans:] + full[n:, :plans])
    part = height // chunks
    for j in range(CAP):
        warped = product(tiles[j][0], dose[j * height : (j + 1) * height])
        warped = jnp.where(valid_ref[step * CAP + j] > 0, warped, 0.0)
        for m in range(vox):

            @pl.when(step == m)
            def _():
                for h in range(chunks):
                    outs[h * vox + m][j] = warped[h * part : (h + 1) * part]


def block_specs(height, spots, tile_shape):
    specs = []
    for j in range(CAP):
        specs.append(
            pl.BlockSpec((height, spots), lambda m, s, v, t, e, j=j: (s[m * CAP + j], 0))
        )
    for j in range(CAP):
        specs.append(
            pl.BlockSpec((1, *tile_shape), lambda m, s, v, t, e, j=j: (t[m * CAP + j], 0, 0))
        )
    return specs


def whole(shape):
    return pl.BlockSpec(shape, lambda *_: (0,) * len(shape))


def forward(scalars, matrix, warp_tiles, pieces, rows, vox, phases):
    height = warp_tiles.shape[1]
    spots = matrix.shape[1]
    plans = pieces[0].shape[-1]
    out = jax.ShapeDtypeStruct((CAP, height // CHUNKS, plans), F32)
    flops = 2 * matrix.size * plans * 4
    return pl.pallas_call(
        functools.partial(forward_body, (vox, phases, rows, len(pieces), CHUNKS)),
        grid_spec=pltpu.PrefetchScalarGridSpec(
            num_scalar_prefetch=4,
            grid=(vox,),
            in_specs=block_specs(height, spots, warp_tiles.shape[1:])
            + [whole(p.shape) for p in pieces],
            out_specs=[whole(out.shape)] * (vox * CHUNKS),
            scratch_shapes=[pltpu.VMEM((spots, 2 * plans), BF16)],
        ),
        out_shape=[out] * (vox * CHUNKS),
        compiler_params=pltpu.CompilerParams(
            vmem_limit_bytes=LARGE, dimension_semantics=("arbitrary",)
        ),
        cost_estimate=pl.CostEstimate(
            flops=flops, bytes_accessed=matrix.size * 4, transcendentals=0
        ),
        name="dose_and_warp",
    )(*scalars, *([matrix] * CAP), *([warp_tiles] * CAP), *pieces)


def gradient_body(dims, source_ref, valid_ref, tile_ref, me_ref, *refs):
    vox, phases, rows, cores, chunks = dims
    blocks, tiles = refs[:CAP], refs[CAP : 2 * CAP]
    returned = refs[2 * CAP : 2 * CAP + vox * chunks]
    outs = refs[2 * CAP + vox * chunks : -3]
    adjoint, total, turned = refs[-3:]
    step = pl.program_id(0)
    plans = adjoint.shape[-1]
    part = adjoint.shape[1] // chunks

    @pl.when(step == 0)
    def _():
        total[...] = jnp.zeros_like(total)

    for m in range(vox):

        @pl.when(step == m)
        def _():
            for h in range(chunks):
                adjoint[:, h * part : (h + 1) * part, :] = returned[h * vox + m][...]

    columns = []
    for j in range(CAP):
        pulled = product(adjoint[j].T, tiles[j][0])
        columns.append(jnp.where(valid_ref[step * CAP + j] > 0, pulled, 0.0))
    left = halves(jnp.concatenate(columns, axis=1), 0)
    rows_now = jnp.concatenate([b[...] for b in blocks], axis=0)
    big = rows_now.astype(BF16)
    small = (rows_now - big.astype(F32)).astype(BF16)
    first = jnp.dot(left, big, preferred_element_type=F32)
    second = jnp.dot(left[:plans], small, preferred_element_type=F32)
    total[...] += first[:plans] + (first[plans:] + second)

    @pl.when(step == vox - 1)
    def _():
        spots = total.shape[1]
        if len(outs[0].shape) == 2:
            for i in range(spots // plans):
                outs[0][i * plans : (i + 1) * plans, :] = total[:, i * plans : (i + 1) * plans].T
        else:
            for i in range(spots // plans):
                turned[i * plans : (i + 1) * plans, :] = total[:, i * plans : (i + 1) * plans].T
            for c in range(cores):
                for k in range(vox // cores):
                    for p in range(phases):
                        v = me_ref[0] ^ (k * cores + c)
                        at = ((me_ref[1] ^ p) * vox + v) * rows
                        outs[c][k, p] = turned[pl.ds(pl.multiple_of(at, rows), rows), :]


def gradient_parts(scalars, matrix, warp_tiles, returned, rows, vox, phases):
    height = warp_tiles.shape[1]
    spots = matrix.shape[1]
    plans = returned[0].shape[-1]
    cores = core_count()
    if rows % 8 == 0:
        outs = [jax.ShapeDtypeStruct((vox // cores, phases, rows, plans), F32)] * cores
    else:
        outs = [jax.ShapeDtypeStruct((spots, plans), F32)]
    return pl.pallas_call(
        functools.partial(gradient_body, (vox, phases, rows, cores, CHUNKS)),
        grid_spec=pltpu.PrefetchScalarGridSpec(
            num_scalar_prefetch=4,
            grid=(vox,),
            in_specs=block_specs(height, spots, warp_tiles.shape[1:])
            + [whole(p.shape) for p in returned],
            out_specs=[whole(o.shape) for o in outs],
            scratch_shapes=[
                pltpu.VMEM((CAP, height, plans), F32),
                pltpu.VMEM((plans, spots), F32),
                pltpu.VMEM((spots, plans), F32),
            ],
        ),
        out_shape=outs,
        compiler_params=pltpu.CompilerParams(
            vmem_limit_bytes=LARGE, dimension_semantics=("arbitrary",)
        ),
        cost_estimate=pl.CostEstimate(
            flops=2 * matrix.size * plans * 4, bytes_accessed=matrix.size * 4, transcendentals=0
        ),
        name="warp_back_and_gradient",
    )(*scalars, *([matrix] * CAP), *([warp_tiles] * CAP), *returned)


def place_body(vox, which_ref, slot_ref, *refs):
    incoming, (give, keep, total) = refs[:vox], refs[vox:]
    total[...] = jnp.zeros_like(total)
    for m in range(vox):
        for j in range(CAP):
            slot = slot_ref[m * CAP + j]

            @pl.when(slot >= 0)
            def _():
                total[slot] += incoming[m][j]

    half = keep.shape[0]
    which = which_ref[0]
    keep[...] = total[pl.ds(which * half, half)]
    give[...] = total[pl.ds((1 - which) * half, half)]


def place(which, slots, incoming, blocks):
    vox = len(incoming)
    _, height, plans = incoming[0].shape
    half = jax.ShapeDtypeStruct((blocks // 2, height, plans), F32)
    smem = pl.BlockSpec(memory_space=pltpu.SMEM)
    vmem = pl.BlockSpec(memory_space=pltpu.VMEM)
    return pl.pallas_call(
        functools.partial(place_body, vox),
        in_specs=[smem, smem] + [vmem] * vox,
        out_specs=[vmem, vmem],
        out_shape=[half, half],
        scratch_shapes=[pltpu.VMEM((blocks, height, plans), F32)],
        compiler_params=pltpu.CompilerParams(vmem_limit_bytes=SMALL),
        name="place_blocks",
    )(which, slots, *incoming)


def pull_body(vox, with_dose, which_ref, slot_ref, mine, other, goal, scale, *refs):
    half = mine.shape[0]
    which = which_ref[0]
    field = refs[-1]
    field[pl.ds(which * half, half)] = mine[...]
    field[pl.ds((1 - which) * half, half)] = other[...]
    for m in range(vox):
        for j in range(CAP):
            slot = jnp.maximum(slot_ref[m * CAP + j], 0)
            refs[m][j] = scale[slot] * (field[slot] - goal[slot])
    if with_dose:
        refs[vox][...] = field[...]


def pull(which, slots, mine, other, goal, scale, vox, with_dose):
    half, height, plans = mine.shape
    smem = pl.BlockSpec(memory_space=pltpu.SMEM)
    vmem = pl.BlockSpec(memory_space=pltpu.VMEM)
    outs = [jax.ShapeDtypeStruct((CAP, height, plans), F32)] * vox
    if with_dose:
        outs = outs + [jax.ShapeDtypeStruct((2 * half, height, plans), F32)]
    return pl.pallas_call(
        functools.partial(pull_body, vox, with_dose),
        in_specs=[smem, smem] + [vmem] * 4,
        out_specs=[vmem] * len(outs),
        out_shape=outs,
        scratch_shapes=[pltpu.VMEM((2 * half, height, plans), F32)],
        compiler_params=pltpu.CompilerParams(vmem_limit_bytes=SMALL),
        name="adjoint_blocks",
    )(which, slots, mine, other, goal, scale)


def gather_weights(shard, extra):
    phases, vox = lax.axis_size(PHASE), lax.axis_size(VOX)
    by_phase = spread(shard, PHASE, range(1, phases))
    if extra is not None:
        by_phase.append(extra)
    by_phase = jnp.concatenate(by_phase, axis=0)
    cores = core_count()
    by_chip = jnp.stack(spread(by_phase, VOX, range(cores, vox, cores)))
    return spread(by_chip, VOX, range(1, cores))


def scatter_sum(parts):
    cores = len(parts)
    chips = parts[0]
    for m in range(1, cores):
        chips = chips + swap(parts[m], VOX, m)
    mine = chips[0]
    for m in range(1, chips.shape[0]):
        mine = mine + swap(chips[m], VOX, m * cores)
    total = mine[0]
    for m in range(1, mine.shape[0]):
        total = total + swap(mine[m], PHASE, m)
    return total


def exchange(pieces):
    return [pieces[0]] + [swap(pieces[m], VOX, m) for m in range(1, len(pieces))]


def phase_halves(give, keep):
    phases = lax.axis_size(PHASE)
    if phases == 1:
        return keep, give
    keep = keep + swap(give, PHASE, 1)
    span = 4
    while span <= phases:
        keep = keep + swap(keep, PHASE, span - 1)
        span *= 2
    return keep, swap(keep, PHASE, 1)


def per_device(
    influence,
    weights,
    warp_tiles,
    owners,
    owner_slot,
    tile_index,
    structure,
    prescribed,
    importance,
    step_size,
):
    highest = lax.Precision.HIGHEST
    matrix = influence[0]
    vox_rows, spots = matrix.shape
    block_rows = warp_tiles.shape[1]
    rows, plans = weights.shape
    local_blocks = vox_rows // block_rows
    vox = lax.axis_size(VOX)
    phases = lax.axis_size(PHASE)
    cores = core_count()
    me_vox = lax.axis_index(VOX)
    me_phase = lax.axis_index(PHASE)
    slots_all = vox * CAP
    part = block_rows // CHUNKS
    targets = owners[0, :, 0]
    which = ((me_phase ^ (me_phase >> 1)) & 1).astype(jnp.int32).reshape(1)

    def orders(names):
        before = jnp.tril(jnp.ones((local_blocks, local_blocks), jnp.int32), -1)
        same = (names[..., :, None] == names[..., None, :]).astype(jnp.int32)
        return jnp.sum(same * before, axis=-1)

    position = (targets ^ me_vox) * CAP + orders(targets)
    chosen_mask = jnp.arange(slots_all, dtype=jnp.int32)[:, None] == position[None, :]
    positions_i = jnp.arange(local_blocks, dtype=jnp.int32)
    source = jnp.sum(jnp.where(chosen_mask, positions_i[None, :], 0), axis=1)
    valid = jnp.sum(chosen_mask.astype(jnp.int32), axis=1)
    tiles = jnp.sum(jnp.where(chosen_mask, tile_index[0][None, :], 0), axis=1)
    me = jnp.stack([me_vox, me_phase]).astype(jnp.int32)
    scalars = (source, valid, tiles, me)
    labels = jnp.zeros((LABEL_ROWS, plans), F32)
    labels = labels.at[0, :local_blocks].set(targets.astype(F32))
    labels = labels.at[1, :local_blocks].set(owner_slot[0].astype(F32))

    member = (structure[:, None] == jnp.arange(NSTRUCT, dtype=jnp.int32)[None, :]).astype(F32)
    target_dose = jnp.dot(member, prescribed, precision=highest, preferred_element_type=F32)
    voxel_weight = jnp.dot(
        member, importance[:, None], precision=highest, preferred_element_type=F32
    )
    voxel_weight = jnp.broadcast_to(voxel_weight, target_dose.shape)
    goals = target_dose.reshape(local_blocks, CHUNKS, part, plans)
    scales = voxel_weight.reshape(local_blocks, CHUNKS, part, plans)
    goals = [goals[:, h] for h in range(CHUNKS)]
    scales = [scales[:, h] for h in range(CHUNKS)]

    new_weights = weights
    received = None
    for iteration in range(ITERS):
        last = iteration == ITERS - 1
        pieces = gather_weights(new_weights, labels if iteration == 0 else None)
        if iteration == 0:
            infos = jnp.stack(pieces, axis=1).reshape(vox, -1, plans)[:, phases * rows :]
            names = infos[:, 0, :local_blocks].astype(jnp.int32)
            slots = infos[:, 1, :local_blocks].astype(jnp.int32)
            order = jnp.where(names == me_vox, orders(names), -1)
            hit = order[:, None, :] == jnp.arange(CAP, dtype=jnp.int32)[None, :, None]
            received = jnp.sum(jnp.where(hit, slots[:, None, :] + 1, 0), axis=-1)
            received = received.reshape(slots_all) - 1
        if rows % 16:
            every = jnp.stack(pieces, axis=1).reshape(vox, -1, plans)[:, : phases * rows]
            every = every.reshape(vox, phases, rows, plans)
            every = every[jnp.arange(vox) ^ me_vox][:, jnp.arange(phases) ^ me_phase]
            pieces = [every.transpose(1, 0, 2, 3).reshape(spots, plans)]
        outgoing = forward(scalars, matrix, warp_tiles, pieces, rows, vox, phases)
        returned, dose = [], []
        incoming = [exchange(outgoing[h * vox : (h + 1) * vox]) for h in range(CHUNKS)]
        for h in range(CHUNKS):
            give, keep = place(which, received, incoming[h], local_blocks)
            mine, other = phase_halves(give, keep)
            back = pull(which, received, mine, other, goals[h], scales[h], vox, last)
            returned += exchange(back[:vox])
            dose += back[vox:]
        parts = gradient_parts(scalars, matrix, warp_tiles, returned, rows, vox, phases)
        if rows % 8:
            parts = parts[0].reshape(phases, vox, rows, plans)
            parts = parts[jnp.arange(phases) ^ me_phase][:, jnp.arange(vox) ^ me_vox]
            parts = parts.transpose(1, 0, 2, 3).reshape(vox // cores, cores, phases, rows, plans)
            parts = [parts[:, c] for c in range(cores)]
        total = scatter_sum(parts)
        new_weights = jnp.maximum(new_weights - step_size[None, :] * total, 0.0)
    dose_field = jnp.stack(dose, axis=1).reshape(vox_rows, plans)
    return (new_weights, dose_field)


def solution(mesh):
    in_specs = (
        P("phase", "vox", None),
        P(("phase", "vox"), None),
        P(),
        P("phase", "vox", None),
        P("phase", "vox"),
        P("phase", "vox"),
        P("vox"),
        P(),
        P(),
        P(),
    )
    out_specs = (P(("phase", "vox"), None), P("vox", None))
    return jax.shard_map(
        per_device, mesh=mesh, in_specs=in_specs, out_specs=out_specs, check_vma=False
    )
```

time: 324 us -> 271 us (0.84)
  waiting for transfers between devices: 151 us -> 88.6 us
  Pallas kernels: 0 us -> 38.6 us
  matrix products: 39.9 us -> 1.67 us
  starting transfers between devices: 85.7 us -> 119 us
  local copies, waits for them, and re-layouts: 33.7 us -> 16.3 us
  other arithmetic: 11.3 us -> 5.51 us
    ppermute x62 -> x96, waiting for transfers between devices: 151 us -> 88.6 us  [swap(): return lax.ppermute(x, axis, [(i, i ^ mask) for i in range(count)])]
    pallas_call x0 -> x12, Pallas kernels: none -> 38.6 us  [the longest x2 18.8 us: forward(): pl.pallas_call(functools.partial(forward_body, (vox, phases, rows, len(pi...]
    dot_general x9 -> x1, matrix products: 39.2 us -> 0.96 us  [per_device(): jnp.dot(member, prescribed, precision=highest, preferred_element_type=F32)]
    ppermute x62 -> x96, starting transfers between devices: 85.7 us -> 119 us  [swap(): return lax.ppermute(x, axis, [(i, i ^ mask) for i in range(count)])]
    gather x15 -> x0, local copies, waits for them, and re-layouts: 20.8 us -> none  [the longest x4 5.59 us: per_device(): parts = parts[place_phase][:, place_vox].transpose(1, 0, 2, 3)]
    unnamed x54 -> x22, local copies, waits for them, and re-layouts: 5.42 us -> 14.3 us
    scatter-add x2 -> x0, other arithmetic: 4.43 us -> none  [per_device(): jnp.zeros((local_blocks + 1, block_rows, plans), jnp.float32).at[received]]
  transfers between devices with their start and end apart: 62 -> 96, of which waited for: 41 -> 48; matrix products, arithmetic and copies ran while one was open for 3% -> 3% of each run, Pallas kernels for 0% -> 2%
where the time goes in v2:
time: 271 us
  starting transfers between devices  119 us (44%)
  waiting for transfers between devices  88.6 us (33%)
  Pallas kernels  38.6 us (14%)
  local copies, waits for them, and re-layouts  16.3 us (6%)
  other arithmetic  5.51 us (2%)
    ppermute x96, starting transfers between devices, swap(): return lax.ppermute(x, axis, [(i, i ^ mask) for i in range(count)])  119 us
    ppermute x96, waiting for transfers between devices, swap(): return lax.ppermute(x, axis, [(i, i ^ mask) for i in range(count)])  88.6 us
    pallas_call x2, Pallas kernels, forward(): pl.pallas_call(functools.partial(forward_body, (vox, phases, rows, len(pi...  18.8 us
    unnamed x22, local copies, waits for them, and re-layouts  14.3 us
    pallas_call x2, Pallas kernels, gradient_parts(): pl.pallas_call(functools.partial(gradient_body, (vox, phases, rows, cores...  13.9 us
  transfers between devices with their start and end apart: 96, of which 48 were waited for; matrix products, arithmetic and copies ran while one was open for 3% of the time, Pallas kernels for 2%

profile of v2, /device:TPU:0, one launch (start us, length us, event | category | flops | bytes accessed | tf_op | source)
XLA Modules:
  0.0 270.8 jit_solution(17412520709015178263)
XLA Ops:
  0.6 5.1 %collective-permute-start.2 = (f32[48,128]{1,0:T(8,128)}, f32[48,128]{1,0:T(8,128)S(1)}, u32[]{:S(2)}, u32[]{:S(2)}) collective-permute-start(f32[48,128]{1,0:T(8,128)} %param.15), channel_id=1, source_target_pairs={{0,24},{8,16},{16,8},{24,0},{1,25},{9,17},{17,9},{25,1},{2,26},{10... | collective-permute-start | bytes 73736 | tf_op jit(solution)/shard_map/ppermute | solution.py:25
  10.7 2.5 collective-permute-start.5
  15.2 2.3 collective-permute-done.5
  20.5 4.6 %copy-done.1 = f32[1,2048,1536]{2,1,0:T(8,128)S(1)} copy-done((f32[1,2048,1536]{2,1,0:T(8,128)S(1)}, f32[1,2048,1536]{2,1,0:T(8,128)}, u32[]{:S(2)}) %copy-start.1) | copy-done | bytes 12582936
  25.1 2.2 copy-done.3
  27.3 9.4 %dose_and_warp.2 = (f32[2,64,128]{2,1,0:T(8,128)S(1)}, f32[2,64,128]{2,1,0:T(8,128)S(1)}, f32[2,64,128]{2,1,0:T(8,128)S(1)}, f32[2,64,128]{2,1,0:T(8,128)S(1)}, ...) custom-call(s32[16]{0:T(128)S(1)} %get-tuple-element.184.source_ref,, ...), custom_call_target="tpu_custom_call" | custom-call | flops 3221225472 | bytes 12582912 | tf_op jit(solution)/shard_map/dose_and_warp/pallas_call | solution.py:118
  41.8 2.1 collective-permute-start.29
  43.9 1.9 collective-permute-start.30
  47.4 2.3 collective-permute-start.12
  53.2 1.6 collective-permute-done.13.refs_7_
  56.7 4.1 %collective-permute-done.31 = f32[8,64,128]{2,1,0:T(8,128)S(1)} collective-permute-done((f32[8,64,128]{2,1,0:T(8,128)S(1)}, f32[8,64,128]{2,1,0:T(8,128)S(1)}, u32[]{:S(2)}, u32[]{:S(2)}) %collective-permute-start.31) | collective-permute-done | bytes 262176 | tf_op jit(solution)/shard_map/ppermute | solution.py:25
  60.9 1.8 collective-permute-start.32
  62.7 2.6 collective-permute-done.14
  65.3 2.6 collective-permute-start.15
  68.0 10.1 %collective-permute-done.15 = f32[8,64,128]{2,1,0:T(8,128)S(1)} collective-permute-done((f32[8,64,128]{2,1,0:T(8,128)S(1)}, f32[8,64,128]{2,1,0:T(8,128)S(1)}, u32[]{:S(2)}, u32[]{:S(2)}) %collective-permute-start.15) | collective-permute-done | bytes 262176 | tf_op jit(solution)/shard_map/ppermute | solution.py:25
  78.1 6.7 %collective-permute-start.16 = (f32[8,64,128]{2,1,0:T(8,128)S(1)}, f32[8,64,128]{2,1,0:T(8,128)S(1)}, u32[]{:S(2)}, u32[]{:S(2)}) collective-permute-start(f32[8,64,128]{2,1,0:T(8,128)S(1)} %add.111.mine), channel_id=1, source_target_pairs={{0,8},{8,0},{16,24},{24,16},{1,9},{9,1},{17,25},{25,17},{2,10},{10... | collective-permute-start | bytes 786440 | tf_op jit(solution)/shard_map/ppermute | solution.py:25
  85.8 6.3 %collective-permute-done.16.other = f32[8,64,128]{2,1,0:T(8,128)S(1)} collective-permute-done((f32[8,64,128]{2,1,0:T(8,128)S(1)}, f32[8,64,128]{2,1,0:T(8,128)S(1)}, u32[]{:S(2)}, u32[]{:S(2)}) %collective-permute-start.16) | collective-permute-done | bytes 262176 | tf_op jit(solution)/shard_map/ppermute | solution.py:25
  93.0 2.9 %collective-permute-start.18 = (f32[2,64,128]{2,1,0:T(8,128)S(1)}, f32[2,64,128]{2,1,0:T(8,128)S(1)}, u32[]{:S(2)}, u32[]{:S(2)}) collective-permute-start(f32[2,64,128]{2,1,0:T(8,128)S(1)} %get-tuple-element.116), channel_id=1, source_target_pairs={{0,2},{1,3},{2,0},{3,1},{4,6},{5,7},{6,4},{7,5},{8,10},{9,11},{10,... | collective-permute-start | bytes 196616 | tf_op jit(solution)/shard_map/ppermute | solution.py:25
  98.4 3.3 %collective-permute-start.22 = (f32[2,64,128]{2,1,0:T(8,128)S(1)}, f32[2,64,128]{2,1,0:T(8,128)S(1)}, u32[]{:S(2)}, u32[]{:S(2)}) collective-permute-start(f32[2,64,128]{2,1,0:T(8,128)S(1)} %get-tuple-element.120), channel_id=1, source_target_pairs={{0,6},{1,7},{2,4},{3,5},{4,2},{5,3},{6,0},{7,1},{8,14},{9,15},{10,... | collective-permute-start | bytes 196616 | tf_op jit(solution)/shard_map/ppermute | solution.py:25
  102.4 1.7 collective-permute-start.35
  107.0 1.9 collective-permute-start.39
  110.0 2.7 %collective-permute-done.39.refs_18_ = f32[2,64,128]{2,1,0:T(8,128)S(1)} collective-permute-done((f32[2,64,128]{2,1,0:T(8,128)S(1)}, f32[2,64,128]{2,1,0:T(8,128)S(1)}, u32[]{:S(2)}, u32[]{:S(2)}) %collective-permute-start.39) | collective-permute-done | bytes 65568 | tf_op jit(solution)/shard_map/ppermute | solution.py:25
  113.6 4.6 %copy-done.2 = f32[1,2048,1536]{2,1,0:T(8,128)S(1)} copy-done((f32[1,2048,1536]{2,1,0:T(8,128)S(1)}, f32[1,2048,1536]{2,1,0:T(8,128)}, u32[]{:S(2)}) %copy-start.2) | copy-done | bytes 12582936
  118.1 2.2 copy-done.4
  120.3 6.9 %warp_back_and_gradient.2 = (f32[4,4,48,128]{3,2,1,0:T(8,128)S(1)}, f32[4,4,48,128]{3,2,1,0:T(8,128)S(1)}) custom-call(s32[16]{0:T(128)S(1)} %get-tuple-element.184.source_ref, s32[16]{0:T(128)S(1)} %get-tuple-element.183.valid_ref, s32[16]{0:T(128)S(1)} %get-tuple-element.182.tile_ref, s32[2]{0:T(128)S(1)} %pad_add_fusion.me_ref, ...), custom_call_target="tpu_custom_call" | custom-call | flops 3221225472 | bytes 12582912 | tf_op jit(solution)/shard_map/warp_back_and_gradient/pallas_call | solution.py:198
  129.3 2.2 collective-permute-start.42
  133.0 2.0 collective-permute-done.42
  135.1 2.6 collective-permute-done.44
  139.1 1.6 collective-permute-start.45
  140.7 2.6 collective-permute-start.47
  143.3 3.0 %collective-permute-done.47 = f32[48,128]{1,0:T(8,128)S(1)} collective-permute-done((f32[48,128]{1,0:T(8,128)S(1)}, f32[48,128]{1,0:T(8,128)S(1)}, u32[]{:S(2)}, u32[]{:S(2)}) %collective-permute-start.47) | collective-permute-done | bytes 24608 | tf_op jit(solution)/shard_map/ppermute | solution.py:25
  146.4 1.7 collective-permute-done.46
  148.1 1.5 collective-permute-start.50
  149.6 3.0 %collective-permute-start.48 = (f32[48,128]{1,0:T(8,128)S(1)}, f32[48,128]{1,0:T(8,128)S(1)}, u32[]{:S(2)}, u32[]{:S(2)}) collective-permute-start(f32[48,128]{1,0:T(8,128)S(1)} %fusion.21), channel_id=1, source_target_pairs={{0,8},{8,0},{16,24},{24,16},{1,9},{9,1},{17,25},{25,17},{2,10},{10... | collective-permute-start | bytes 73736 | tf_op jit(solution)/shard_map/ppermute | solution.py:25
  155.3 1.5 collective-permute-start.51
  160.0 2.4 collective-permute-done.53
  162.4 1.7 collective-permute-done.54.refs_5_
  164.2 9.4 %dose_and_warp.3 = (f32[2,64,128]{2,1,0:T(8,128)S(1)}, f32[2,64,128]{2,1,0:T(8,128)S(1)}, f32[2,64,128]{2,1,0:T(8,128)S(1)}, f32[2,64,128]{2,1,0:T(8,128)S(1)}, ...) custom-call(s32[16]{0:T(128)S(1)} %get-tuple-element.184.source_ref,, ...), custom_call_target="tpu_custom_call" | custom-call | flops 3221225472 | bytes 12582912 | tf_op jit(solution)/shard_map/dose_and_warp/pallas_call | solution.py:118
  174.4 1.5 collective-permute-start.73
  184.3 1.8 collective-permute-start.60
  187.4 1.9 collective-permute-start.79
  189.2 1.8 collective-permute-done.59.refs_5_
  192.0 1.9 collective-permute-start.62
  193.8 2.8 %collective-permute-done.79 = f32[8,64,128]{2,1,0:T(8,128)S(1)} collective-permute-done((f32[8,64,128]{2,1,0:T(8,128)S(1)}, f32[8,64,128]{2,1,0:T(8,128)S(1)}, u32[]{:S(2)}, u32[]{:S(2)}) %collective-permute-start.79) | collective-permute-done | bytes 262176 | tf_op jit(solution)/shard_map/ppermute | solution.py:25
  196.7 2.2 collective-permute-start.80
  198.9 3.2 %collective-permute-done.62 = f32[8,64,128]{2,1,0:T(8,128)S(1)} collective-permute-done((f32[8,64,128]{2,1,0:T(8,128)S(1)}, f32[8,64,128]{2,1,0:T(8,128)S(1)}, u32[]{:S(2)}, u32[]{:S(2)}) %collective-permute-start.62) | collective-permute-done | bytes 262176 | tf_op jit(solution)/shard_map/ppermute | solution.py:25
  202.1 2.1 collective-permute-start.63
  204.2 4.5 %collective-permute-done.80 = f32[8,64,128]{2,1,0:T(8,128)S(1)} collective-permute-done((f32[8,64,128]{2,1,0:T(8,128)S(1)}, f32[8,64,128]{2,1,0:T(8,128)S(1)}, u32[]{:S(2)}, u32[]{:S(2)}) %collective-permute-start.80) | collective-permute-done | bytes 262176 | tf_op jit(solution)/shard_map/ppermute | solution.py:25
  208.7 10.3 %collective-permute-start.81 = (f32[8,64,128]{2,1,0:T(8,128)S(1)}, f32[8,64,128]{2,1,0:T(8,128)S(1)}, u32[]{:S(2)}, u32[]{:S(2)}) collective-permute-start(f32[8,64,128]{2,1,0:T(8,128)S(1)} %add.124.mine), channel_id=1, source_target_pairs={{0,8},{8,0},{16,24},{24,16},{1,9},{9,1},{17,25},{25,17},{2,10},{10... | collective-permute-start | bytes 786440 | tf_op jit(solution)/shard_map/ppermute | solution.py:25
  219.1 4.2 %collective-permute-start.64 = (f32[8,64,128]{2,1,0:T(8,128)S(1)}, f32[8,64,128]{2,1,0:T(8,128)S(1)}, u32[]{:S(2)}, u32[]{:S(2)}) collective-permute-start(f32[8,64,128]{2,1,0:T(8,128)S(1)} %add.122.mine), channel_id=1, source_target_pairs={{0,8},{8,0},{16,24},{24,16},{1,9},{9,1},{17,25},{25,17},{2,10},{10... | collective-permute-start | bytes 786440 | tf_op jit(solution)/shard_map/ppermute | solution.py:25
  224.6 2.0 collective-permute-start.83
  227.2 1.9 collective-permute-done.64.other
  229.7 2.3 collective-permute-start.87
  232.9 2.2 collective-permute-start.66
  237.2 1.6 collective-permute-start.69
  239.7 2.5 collective-permute-done.69.refs_9_
  242.2 2.3 collective-permute-done.70.refs_10_
  244.8 6.9 %warp_back_and_gradient.3 = (f32[4,4,48,128]{3,2,1,0:T(8,128)S(1)}, f32[4,4,48,128]{3,2,1,0:T(8,128)S(1)}) custom-call(s32[16]{0:T(128)S(1)} %get-tuple-element.184.source_ref, s32[16]{0:T(128)S(1)} %get-tuple-element.183.valid_ref, s32[16]{0:T(128)S(1)} %get-tuple-element.182.tile_ref, s32[2]{0:T(128)S(1)} %pad_add_fusion.me_ref, ...), custom_call_target="tpu_custom_call" | custom-call | flops 3221225472 | bytes 12582912 | tf_op jit(solution)/shard_map/warp_back_and_gradient/pallas_call | solution.py:198
  254.1 1.7 collective-permute-start.92
  257.2 2.1 collective-permute-done.90
  259.3 1.6 collective-permute-done.92
  262.3 1.7 collective-permute-start.93
  264.0 1.5 collective-permute-start.95
  267.0 2.6 collective-permute-done.95
  (211 shorter events, 69.0 us)
Async XLA Ops:
  0.6 10.1 %collective-permute-start.2 = (f32[48,128]{1,0:T(8,128)}, f32[48,128]{1,0:T(8,128)S(1)}, u32[]{:S(2)}, u32[]{:S(2)}) collective-permute-start(f32[48,128]{1,0:T(8,128)} %param.15), channel_id=1, source_target_pairs={{0,24},{8,16},{16,8},{24,0},{1,25},{9,17},{17,9},{25,1},{2,26},{10... | collective-permute-start | bytes 73736 | tf_op jit(solution)/shard_map/ppermute | solution.py:25
  10.7 6.8 %collective-permute-start.5 = (f32[208,128]{1,0:T(8,128)S(1)}, f32[208,128]{1,0:T(8,128)S(1)}, u32[]{:S(2)}, u32[]{:S(2)}) collective-permute-start(f32[208,128]{1,0:T(8,128)S(1)} %constant_dynamic-update-slice_fusion), channel_id=1, source_target_pairs={{0,6},{1,7},{2,4},{3,5},{4,2},{5,3},{6,0},{7,1},{8,14},{9,15},{10,... | collective-permute-start | bytes 319496 | tf_op jit(solution)/shard_map/ppermute | solution.py:25
  37.7 6.2 %collective-permute-start.25 = (f32[2,64,128]{2,1,0:T(8,128)S(1)}, f32[2,64,128]{2,1,0:T(8,128)S(1)}, u32[]{:S(2)}, u32[]{:S(2)}) collective-permute-start(f32[2,64,128]{2,1,0:T(8,128)S(1)} %get-tuple-element.124), channel_id=1, source_target_pairs={{0,2},{1,3},{2,0},{3,1},{4,6},{5,7},{6,4},{7,5},{8,10},{9,11},{10,... | collective-permute-start | bytes 196616 | tf_op jit(solution)/shard_map/ppermute | solution.py:25
  39.3 6.6 %collective-permute-start.26 = (f32[2,64,128]{2,1,0:T(8,128)S(1)}, f32[2,64,128]{2,1,0:T(8,128)S(1)}, u32[]{:S(2)}, u32[]{:S(2)}) collective-permute-start(f32[2,64,128]{2,1,0:T(8,128)S(1)} %get-tuple-element.125), channel_id=1, source_target_pairs={{0,3},{1,2},{2,1},{3,0},{4,7},{5,6},{6,5},{7,4},{8,11},{9,10},{10,... | collective-permute-start | bytes 196616 | tf_op jit(solution)/shard_map/ppermute | solution.py:25
  39.9 6.1 %collective-permute-start.27 = (f32[2,64,128]{2,1,0:T(8,128)S(1)}, f32[2,64,128]{2,1,0:T(8,128)S(1)}, u32[]{:S(2)}, u32[]{:S(2)}) collective-permute-start(f32[2,64,128]{2,1,0:T(8,128)S(1)} %get-tuple-element.126), channel_id=1, source_target_pairs={{0,4},{1,5},{2,6},{3,7},{4,0},{5,1},{6,2},{7,3},{8,12},{9,13},{10,... | collective-permute-start | bytes 196616 | tf_op jit(solution)/shard_map/ppermute | solution.py:25
  41.8 5.5 %collective-permute-start.28 = (f32[2,64,128]{2,1,0:T(8,128)S(1)}, f32[2,64,128]{2,1,0:T(8,128)S(1)}, u32[]{:S(2)}, u32[]{:S(2)}) collective-permute-start(f32[2,64,128]{2,1,0:T(8,128)S(1)} %get-tuple-element.127), channel_id=1, source_target_pairs={{0,5},{1,4},{2,7},{3,6},{4,1},{5,0},{6,3},{7,2},{8,13},{9,12},{10,... | collective-permute-start | bytes 196616 | tf_op jit(solution)/shard_map/ppermute | solution.py:25
  41.8 5.6 %collective-permute-start.29 = (f32[2,64,128]{2,1,0:T(8,128)S(1)}, f32[2,64,128]{2,1,0:T(8,128)S(1)}, u32[]{:S(2)}, u32[]{:S(2)}) collective-permute-start(f32[2,64,128]{2,1,0:T(8,128)S(1)} %get-tuple-element.128), channel_id=1, source_target_pairs={{0,6},{1,7},{2,4},{3,5},{4,2},{5,3},{6,0},{7,1},{8,14},{9,15},{10,... | collective-permute-start | bytes 196616 | tf_op jit(solution)/shard_map/ppermute | solution.py:25
  43.9 5.8 %collective-permute-start.30 = (f32[2,64,128]{2,1,0:T(8,128)S(1)}, f32[2,64,128]{2,1,0:T(8,128)S(1)}, u32[]{:S(2)}, u32[]{:S(2)}) collective-permute-start(f32[2,64,128]{2,1,0:T(8,128)S(1)} %get-tuple-element.129), channel_id=1, source_target_pairs={{0,7},{1,6},{2,5},{3,4},{4,3},{5,2},{6,1},{7,0},{8,15},{9,14},{10,... | collective-permute-start | bytes 196616 | tf_op jit(solution)/shard_map/ppermute | solution.py:25
  45.9 5.8 %collective-permute-start.9 = (f32[2,64,128]{2,1,0:T(8,128)S(1)}, f32[2,64,128]{2,1,0:T(8,128)S(1)}, u32[]{:S(2)}, u32[]{:S(2)}) collective-permute-start(f32[2,64,128]{2,1,0:T(8,128)S(1)} %get-tuple-element.107), channel_id=1, source_target_pairs={{0,3},{1,2},{2,1},{3,0},{4,7},{5,6},{6,5},{7,4},{8,11},{9,10},{10,... | collective-permute-start | bytes 196616 | tf_op jit(solution)/shard_map/ppermute | solution.py:25
  46.0 5.8 %collective-permute-start.10 = (f32[2,64,128]{2,1,0:T(8,128)S(1)}, f32[2,64,128]{2,1,0:T(8,128)S(1)}, u32[]{:S(2)}, u32[]{:S(2)}) collective-permute-start(f32[2,64,128]{2,1,0:T(8,128)S(1)} %get-tuple-element.108), channel_id=1, source_target_pairs={{0,4},{1,5},{2,6},{3,7},{4,0},{5,1},{6,2},{7,3},{8,12},{9,13},{10,... | collective-permute-start | bytes 196616 | tf_op jit(solution)/shard_map/ppermute | solution.py:25
  47.4 5.8 %collective-permute-start.12 = (f32[2,64,128]{2,1,0:T(8,128)S(1)}, f32[2,64,128]{2,1,0:T(8,128)S(1)}, u32[]{:S(2)}, u32[]{:S(2)}) collective-permute-start(f32[2,64,128]{2,1,0:T(8,128)S(1)} %get-tuple-element.110), channel_id=1, source_target_pairs={{0,6},{1,7},{2,4},{3,5},{4,2},{5,3},{6,0},{7,1},{8,14},{9,15},{10,... | collective-permute-start | bytes 196616 | tf_op jit(solution)/shard_map/ppermute | solution.py:25
  49.7 5.2 %collective-permute-start.13 = (f32[2,64,128]{2,1,0:T(8,128)S(1)}, f32[2,64,128]{2,1,0:T(8,128)S(1)}, u32[]{:S(2)}, u32[]{:S(2)}) collective-permute-start(f32[2,64,128]{2,1,0:T(8,128)S(1)} %get-tuple-element.111), channel_id=1, source_target_pairs={{0,7},{1,6},{2,5},{3,4},{4,3},{5,2},{6,1},{7,0},{8,15},{9,14},{10,... | collective-permute-start | bytes 196616 | tf_op jit(solution)/shard_map/ppermute | solution.py:25
  51.8 9.0 %collective-permute-start.31 = (f32[8,64,128]{2,1,0:T(8,128)S(1)}, f32[8,64,128]{2,1,0:T(8,128)S(1)}, u32[]{:S(2)}, u32[]{:S(2)}) collective-permute-start(f32[8,64,128]{2,1,0:T(8,128)S(1)} %get-tuple-element.131), channel_id=1, source_target_pairs={{0,8},{8,0},{16,24},{24,16},{1,9},{9,1},{17,25},{25,17},{2,10},{10... | collective-permute-start | bytes 786440 | tf_op jit(solution)/shard_map/ppermute | solution.py:25
  55.7 9.6 %collective-permute-start.14 = (f32[8,64,128]{2,1,0:T(8,128)S(1)}, f32[8,64,128]{2,1,0:T(8,128)S(1)}, u32[]{:S(2)}, u32[]{:S(2)}) collective-permute-start(f32[8,64,128]{2,1,0:T(8,128)S(1)} %get-tuple-element.113), channel_id=1, source_target_pairs={{0,8},{8,0},{16,24},{24,16},{1,9},{9,1},{17,25},{25,17},{2,10},{10... | collective-permute-start | bytes 786440 | tf_op jit(solution)/shard_map/ppermute | solution.py:25
  60.9 24.8 %collective-permute-start.32 = (f32[8,64,128]{2,1,0:T(8,128)S(1)}, f32[8,64,128]{2,1,0:T(8,128)S(1)}, u32[]{:S(2)}, u32[]{:S(2)}) collective-permute-start(f32[8,64,128]{2,1,0:T(8,128)S(1)} %add.112), channel_id=1, source_target_pairs={{0,24},{8,16},{16,8},{24,0},{1,25},{9,17},{17,9},{25,1},{2,26},{10... | collective-permute-start | bytes 786440 | tf_op jit(solution)/shard_map/ppermute | solution.py:25
  65.3 12.8 %collective-permute-start.15 = (f32[8,64,128]{2,1,0:T(8,128)S(1)}, f32[8,64,128]{2,1,0:T(8,128)S(1)}, u32[]{:S(2)}, u32[]{:S(2)}) collective-permute-start(f32[8,64,128]{2,1,0:T(8,128)S(1)} %add.110), channel_id=1, source_target_pairs={{0,24},{8,16},{16,8},{24,0},{1,25},{9,17},{17,9},{25,1},{2,26},{10... | collective-permute-start | bytes 786440 | tf_op jit(solution)/shard_map/ppermute | solution.py:25
  78.1 13.9 %collective-permute-start.16 = (f32[8,64,128]{2,1,0:T(8,128)S(1)}, f32[8,64,128]{2,1,0:T(8,128)S(1)}, u32[]{:S(2)}, u32[]{:S(2)}) collective-permute-start(f32[8,64,128]{2,1,0:T(8,128)S(1)} %add.111.mine), channel_id=1, source_target_pairs={{0,8},{8,0},{16,24},{24,16},{1,9},{9,1},{17,25},{25,17},{2,10},{10... | collective-permute-start | bytes 786440 | tf_op jit(solution)/shard_map/ppermute | solution.py:25
  85.7 11.8 %collective-permute-start.33 = (f32[8,64,128]{2,1,0:T(8,128)S(1)}, f32[8,64,128]{2,1,0:T(8,128)S(1)}, u32[]{:S(2)}, u32[]{:S(2)}) collective-permute-start(f32[8,64,128]{2,1,0:T(8,128)S(1)} %add.113.mine), channel_id=1, source_target_pairs={{0,8},{8,0},{16,24},{24,16},{1,9},{9,1},{17,25},{25,17},{2,10},{10... | collective-permute-start | bytes 786440 | tf_op jit(solution)/shard_map/ppermute | solution.py:25
  92.9 5.4 %collective-permute-start.17 = (f32[2,64,128]{2,1,0:T(8,128)S(1)}, f32[2,64,128]{2,1,0:T(8,128)S(1)}, u32[]{:S(2)}, u32[]{:S(2)}) collective-permute-start(f32[2,64,128]{2,1,0:T(8,128)S(1)} %get-tuple-element.115), channel_id=1, source_target_pairs={{0,1},{1,0},{2,3},{3,2},{4,5},{5,4},{6,7},{7,6},{8,9},{9,8},{10,11... | collective-permute-start | bytes 196616 | tf_op jit(solution)/shard_map/ppermute | solution.py:25
  93.0 8.6 %collective-permute-start.18 = (f32[2,64,128]{2,1,0:T(8,128)S(1)}, f32[2,64,128]{2,1,0:T(8,128)S(1)}, u32[]{:S(2)}, u32[]{:S(2)}) collective-permute-start(f32[2,64,128]{2,1,0:T(8,128)S(1)} %get-tuple-element.116), channel_id=1, source_target_pairs={{0,2},{1,3},{2,0},{3,1},{4,6},{5,7},{6,4},{7,5},{8,10},{9,11},{10,... | collective-permute-start | bytes 196616 | tf_op jit(solution)/shard_map/ppermute | solution.py:25
  95.9 6.3 %collective-permute-start.19 = (f32[2,64,128]{2,1,0:T(8,128)S(1)}, f32[2,64,128]{2,1,0:T(8,128)S(1)}, u32[]{:S(2)}, u32[]{:S(2)}) collective-permute-start(f32[2,64,128]{2,1,0:T(8,128)S(1)} %get-tuple-element.117), channel_id=1, source_target_pairs={{0,3},{1,2},{2,1},{3,0},{4,7},{5,6},{6,5},{7,4},{8,11},{9,10},{10,... | collective-permute-start | bytes 196616 | tf_op jit(solution)/shard_map/ppermute | solution.py:25
  96.0 6.3 %collective-permute-start.20 = (f32[2,64,128]{2,1,0:T(8,128)S(1)}, f32[2,64,128]{2,1,0:T(8,128)S(1)}, u32[]{:S(2)}, u32[]{:S(2)}) collective-permute-start(f32[2,64,128]{2,1,0:T(8,128)S(1)} %get-tuple-element.118), channel_id=1, source_target_pairs={{0,4},{1,5},{2,6},{3,7},{4,0},{5,1},{6,2},{7,3},{8,12},{9,13},{10,... | collective-permute-start | bytes 196616 | tf_op jit(solution)/shard_map/ppermute | solution.py:25
  97.5 6.6 %collective-permute-start.21 = (f32[2,64,128]{2,1,0:T(8,128)S(1)}, f32[2,64,128]{2,1,0:T(8,128)S(1)}, u32[]{:S(2)}, u32[]{:S(2)}) collective-permute-start(f32[2,64,128]{2,1,0:T(8,128)S(1)} %get-tuple-element.119), channel_id=1, source_target_pairs={{0,5},{1,4},{2,7},{3,6},{4,1},{5,0},{6,3},{7,2},{8,13},{9,12},{10,... | collective-permute-start | bytes 196616 | tf_op jit(solution)/shard_map/ppermute | solution.py:25
  98.4 6.0 %collective-permute-start.22 = (f32[2,64,128]{2,1,0:T(8,128)S(1)}, f32[2,64,128]{2,1,0:T(8,128)S(1)}, u32[]{:S(2)}, u32[]{:S(2)}) collective-permute-start(f32[2,64,128]{2,1,0:T(8,128)S(1)} %get-tuple-element.120), channel_id=1, source_target_pairs={{0,6},{1,7},{2,4},{3,5},{4,2},{5,3},{6,0},{7,1},{8,14},{9,15},{10,... | collective-permute-start | bytes 196616 | tf_op jit(solution)/shard_map/ppermute | solution.py:25
  102.4 6.5 %collective-permute-start.35 = (f32[2,64,128]{2,1,0:T(8,128)S(1)}, f32[2,64,128]{2,1,0:T(8,128)S(1)}, u32[]{:S(2)}, u32[]{:S(2)}) collective-permute-start(f32[2,64,128]{2,1,0:T(8,128)S(1)} %get-tuple-element.134), channel_id=1, source_target_pairs={{0,2},{1,3},{2,0},{3,1},{4,6},{5,7},{6,4},{7,5},{8,10},{9,11},{10,... | collective-permute-start | bytes 196616 | tf_op jit(solution)/shard_map/ppermute | solution.py:25
  104.0 5.9 %collective-permute-start.36 = (f32[2,64,128]{2,1,0:T(8,128)S(1)}, f32[2,64,128]{2,1,0:T(8,128)S(1)}, u32[]{:S(2)}, u32[]{:S(2)}) collective-permute-start(f32[2,64,128]{2,1,0:T(8,128)S(1)} %get-tuple-element.135), channel_id=1, source_target_pairs={{0,3},{1,2},{2,1},{3,0},{4,7},{5,6},{6,5},{7,4},{8,11},{9,10},{10,... | collective-permute-start | bytes 196616 | tf_op jit(solution)/shard_map/ppermute | solution.py:25
  104.4 5.6 %collective-permute-start.37 = (f32[2,64,128]{2,1,0:T(8,128)S(1)}, f32[2,64,128]{2,1,0:T(8,128)S(1)}, u32[]{:S(2)}, u32[]{:S(2)}) collective-permute-start(f32[2,64,128]{2,1,0:T(8,128)S(1)} %get-tuple-element.136), channel_id=1, source_target_pairs={{0,4},{1,5},{2,6},{3,7},{4,0},{5,1},{6,2},{7,3},{8,12},{9,13},{10,... | collective-permute-start | bytes 196616 | tf_op jit(solution)/shard_map/ppermute | solution.py:25
  107.0 5.8 %collective-permute-start.39 = (f32[2,64,128]{2,1,0:T(8,128)S(1)}, f32[2,64,128]{2,1,0:T(8,128)S(1)}, u32[]{:S(2)}, u32[]{:S(2)}) collective-permute-start(f32[2,64,128]{2,1,0:T(8,128)S(1)} %get-tuple-element.138), channel_id=1, source_target_pairs={{0,6},{1,7},{2,4},{3,5},{4,2},{5,3},{6,0},{7,1},{8,14},{9,15},{10,... | collective-permute-start | bytes 196616 | tf_op jit(solution)/shard_map/ppermute | solution.py:25
  129.3 5.8 %collective-permute-start.42 = (f32[4,48,128]{2,1,0:T(8,128)S(1)}, f32[4,48,128]{2,1,0:T(8,128)S(1)}, u32[]{:S(2)}, u32[]{:S(2)}) collective-permute-start(f32[4,48,128]{2,1,0:T(8,128)S(1)} %get-tuple-element.194), channel_id=1, source_target_pairs={{0,2},{1,3},{2,0},{3,1},{4,6},{5,7},{6,4},{7,5},{8,10},{9,11},{10,... | collective-permute-start | bytes 294920 | tf_op jit(solution)/shard_map/ppermute | solution.py:25
  131.5 6.1 %collective-permute-start.44 = (f32[4,48,128]{2,1,0:T(8,128)S(1)}, f32[4,48,128]{2,1,0:T(8,128)S(1)}, u32[]{:S(2)}, u32[]{:S(2)}) collective-permute-start(f32[4,48,128]{2,1,0:T(8,128)S(1)} %get-tuple-element.195), channel_id=1, source_target_pairs={{0,6},{1,7},{2,4},{3,5},{4,2},{5,3},{6,0},{7,1},{8,14},{9,15},{10,... | collective-permute-start | bytes 294920 | tf_op jit(solution)/shard_map/ppermute | solution.py:25
  132.6 6.4 %collective-permute-start.43 = (f32[4,48,128]{2,1,0:T(8,128)S(1)}, f32[4,48,128]{2,1,0:T(8,128)S(1)}, u32[]{:S(2)}, u32[]{:S(2)}) collective-permute-start(f32[4,48,128]{2,1,0:T(8,128)S(1)} %get-tuple-element.196), channel_id=1, source_target_pairs={{0,4},{1,5},{2,6},{3,7},{4,0},{5,1},{6,2},{7,3},{8,12},{9,13},{10,... | collective-permute-start | bytes 294920 | tf_op jit(solution)/shard_map/ppermute | solution.py:25
  140.7 5.6 %collective-permute-start.47 = (f32[48,128]{1,0:T(8,128)S(1)}, f32[48,128]{1,0:T(8,128)S(1)}, u32[]{:S(2)}, u32[]{:S(2)}) collective-permute-start(f32[48,128]{1,0:T(8,128)S(1)} %get-tuple-element.203), channel_id=1, source_target_pairs={{0,24},{8,16},{16,8},{24,0},{1,25},{9,17},{17,9},{25,1},{2,26},{10... | collective-permute-start | bytes 73736 | tf_op jit(solution)/shard_map/ppermute | solution.py:25
  148.1 5.7 %collective-permute-start.50 = (f32[48,128]{1,0:T(8,128)S(1)}, f32[48,128]{1,0:T(8,128)S(1)}, u32[]{:S(2)}, u32[]{:S(2)}) collective-permute-start(f32[48,128]{1,0:T(8,128)S(1)} %fusion.21), channel_id=1, source_target_pairs={{0,24},{8,16},{16,8},{24,0},{1,25},{9,17},{17,9},{25,1},{2,26},{10... | collective-permute-start | bytes 73736 | tf_op jit(solution)/shard_map/ppermute | solution.py:25
  156.8 5.5 %collective-permute-start.53 = (f32[192,128]{1,0:T(8,128)S(1)}, f32[192,128]{1,0:T(8,128)S(1)}, u32[]{:S(2)}, u32[]{:S(2)}) collective-permute-start(f32[192,128]{1,0:T(8,128)S(1)} %get-tuple-element.201), channel_id=1, source_target_pairs={{0,6},{1,7},{2,4},{3,5},{4,2},{5,3},{6,0},{7,1},{8,14},{9,15},{10,... | collective-permute-start | bytes 294920 | tf_op jit(solution)/shard_map/ppermute | solution.py:25
  174.4 5.7 %collective-permute-start.73 = (f32[2,64,128]{2,1,0:T(8,128)S(1)}, f32[2,64,128]{2,1,0:T(8,128)S(1)}, u32[]{:S(2)}, u32[]{:S(2)}) collective-permute-start(f32[2,64,128]{2,1,0:T(8,128)S(1)} %get-tuple-element.162), channel_id=1, source_target_pairs={{0,2},{1,3},{2,0},{3,1},{4,6},{5,7},{6,4},{7,5},{8,10},{9,11},{10,... | collective-permute-start | bytes 196616 | tf_op jit(solution)/shard_map/ppermute | solution.py:25
  175.9 5.5 %collective-permute-start.74 = (f32[2,64,128]{2,1,0:T(8,128)S(1)}, f32[2,64,128]{2,1,0:T(8,128)S(1)}, u32[]{:S(2)}, u32[]{:S(2)}) collective-permute-start(f32[2,64,128]{2,1,0:T(8,128)S(1)} %get-tuple-element.163), channel_id=1, source_target_pairs={{0,3},{1,2},{2,1},{3,0},{4,7},{5,6},{6,5},{7,4},{8,11},{9,10},{10,... | collective-permute-start | bytes 196616 | tf_op jit(solution)/shard_map/ppermute | solution.py:25
  176.2 5.8 %collective-permute-start.75 = (f32[2,64,128]{2,1,0:T(8,128)S(1)}, f32[2,64,128]{2,1,0:T(8,128)S(1)}, u32[]{:S(2)}, u32[]{:S(2)}) collective-permute-start(f32[2,64,128]{2,1,0:T(8,128)S(1)} %get-tuple-element.164), channel_id=1, source_target_pairs={{0,4},{1,5},{2,6},{3,7},{4,0},{5,1},{6,2},{7,3},{8,12},{9,13},{10,... | collective-permute-start | bytes 196616 | tf_op jit(solution)/shard_map/ppermute | solution.py:25
  178.7 5.6 %collective-permute-start.77 = (f32[2,64,128]{2,1,0:T(8,128)S(1)}, f32[2,64,128]{2,1,0:T(8,128)S(1)}, u32[]{:S(2)}, u32[]{:S(2)}) collective-permute-start(f32[2,64,128]{2,1,0:T(8,128)S(1)} %get-tuple-element.166), channel_id=1, source_target_pairs={{0,6},{1,7},{2,4},{3,5},{4,2},{5,3},{6,0},{7,1},{8,14},{9,15},{10,... | collective-permute-start | bytes 196616 | tf_op jit(solution)/shard_map/ppermute | solution.py:25
  180.1 5.9 %collective-permute-start.78 = (f32[2,64,128]{2,1,0:T(8,128)S(1)}, f32[2,64,128]{2,1,0:T(8,128)S(1)}, u32[]{:S(2)}, u32[]{:S(2)}) collective-permute-start(f32[2,64,128]{2,1,0:T(8,128)S(1)} %get-tuple-element.167), channel_id=1, source_target_pairs={{0,7},{1,6},{2,5},{3,4},{4,3},{5,2},{6,1},{7,0},{8,15},{9,14},{10,... | collective-permute-start | bytes 196616 | tf_op jit(solution)/shard_map/ppermute | solution.py:25
  181.4 6.0 %collective-permute-start.57 = (f32[2,64,128]{2,1,0:T(8,128)S(1)}, f32[2,64,128]{2,1,0:T(8,128)S(1)}, u32[]{:S(2)}, u32[]{:S(2)}) collective-permute-start(f32[2,64,128]{2,1,0:T(8,128)S(1)} %get-tuple-element.145), channel_id=1, source_target_pairs={{0,3},{1,2},{2,1},{3,0},{4,7},{5,6},{6,5},{7,4},{8,11},{9,10},{10,... | collective-permute-start | bytes 196616 | tf_op jit(solution)/shard_map/ppermute | solution.py:25
  182.0 7.2 %collective-permute-start.58 = (f32[2,64,128]{2,1,0:T(8,128)S(1)}, f32[2,64,128]{2,1,0:T(8,128)S(1)}, u32[]{:S(2)}, u32[]{:S(2)}) collective-permute-start(f32[2,64,128]{2,1,0:T(8,128)S(1)} %get-tuple-element.146), channel_id=1, source_target_pairs={{0,4},{1,5},{2,6},{3,7},{4,0},{5,1},{6,2},{7,3},{8,12},{9,13},{10,... | collective-permute-start | bytes 196616 | tf_op jit(solution)/shard_map/ppermute | solution.py:25
  183.3 7.7 %collective-permute-start.59 = (f32[2,64,128]{2,1,0:T(8,128)S(1)}, f32[2,64,128]{2,1,0:T(8,128)S(1)}, u32[]{:S(2)}, u32[]{:S(2)}) collective-permute-start(f32[2,64,128]{2,1,0:T(8,128)S(1)} %get-tuple-element.147), channel_id=1, source_target_pairs={{0,5},{1,4},{2,7},{3,6},{4,1},{5,0},{6,3},{7,2},{8,13},{9,12},{10,... | collective-permute-start | bytes 196616 | tf_op jit(solution)/shard_map/ppermute | solution.py:25
  184.3 6.8 %collective-permute-start.60 = (f32[2,64,128]{2,1,0:T(8,128)S(1)}, f32[2,64,128]{2,1,0:T(8,128)S(1)}, u32[]{:S(2)}, u32[]{:S(2)}) collective-permute-start(f32[2,64,128]{2,1,0:T(8,128)S(1)} %get-tuple-element.148), channel_id=1, source_target_pairs={{0,6},{1,7},{2,4},{3,5},{4,2},{5,3},{6,0},{7,1},{8,14},{9,15},{10,... | collective-permute-start | bytes 196616 | tf_op jit(solution)/shard_map/ppermute | solution.py:25
  187.4 9.2 %collective-permute-start.79 = (f32[8,64,128]{2,1,0:T(8,128)S(1)}, f32[8,64,128]{2,1,0:T(8,128)S(1)}, u32[]{:S(2)}, u32[]{:S(2)}) collective-permute-start(f32[8,64,128]{2,1,0:T(8,128)S(1)} %get-tuple-element.169), channel_id=1, source_target_pairs={{0,8},{8,0},{16,24},{24,16},{1,9},{9,1},{17,25},{25,17},{2,10},{10... | collective-permute-start | bytes 786440 | tf_op jit(solution)/shard_map/ppermute | solution.py:25
  192.0 10.1 %collective-permute-start.62 = (f32[8,64,128]{2,1,0:T(8,128)S(1)}, f32[8,64,128]{2,1,0:T(8,128)S(1)}, u32[]{:S(2)}, u32[]{:S(2)}) collective-permute-start(f32[8,64,128]{2,1,0:T(8,128)S(1)} %get-tuple-element.151), channel_id=1, source_target_pairs={{0,8},{8,0},{16,24},{24,16},{1,9},{9,1},{17,25},{25,17},{2,10},{10... | collective-permute-start | bytes 786440 | tf_op jit(solution)/shard_map/ppermute | solution.py:25
  196.7 12.1 %collective-permute-start.80 = (f32[8,64,128]{2,1,0:T(8,128)S(1)}, f32[8,64,128]{2,1,0:T(8,128)S(1)}, u32[]{:S(2)}, u32[]{:S(2)}) collective-permute-start(f32[8,64,128]{2,1,0:T(8,128)S(1)} %add.123), channel_id=1, source_target_pairs={{0,24},{8,16},{16,8},{24,0},{1,25},{9,17},{17,9},{25,1},{2,26},{10... | collective-permute-start | bytes 786440 | tf_op jit(solution)/shard_map/ppermute | solution.py:25
  202.1 17.0 %collective-permute-start.63 = (f32[8,64,128]{2,1,0:T(8,128)S(1)}, f32[8,64,128]{2,1,0:T(8,128)S(1)}, u32[]{:S(2)}, u32[]{:S(2)}) collective-permute-start(f32[8,64,128]{2,1,0:T(8,128)S(1)} %add.121), channel_id=1, source_target_pairs={{0,24},{8,16},{16,8},{24,0},{1,25},{9,17},{17,9},{25,1},{2,26},{10... | collective-permute-start | bytes 786440 | tf_op jit(solution)/shard_map/ppermute | solution.py:25
  208.7 15.1 %collective-permute-start.81 = (f32[8,64,128]{2,1,0:T(8,128)S(1)}, f32[8,64,128]{2,1,0:T(8,128)S(1)}, u32[]{:S(2)}, u32[]{:S(2)}) collective-permute-start(f32[8,64,128]{2,1,0:T(8,128)S(1)} %add.124.mine), channel_id=1, source_target_pairs={{0,8},{8,0},{16,24},{24,16},{1,9},{9,1},{17,25},{25,17},{2,10},{10... | collective-permute-start | bytes 786440 | tf_op jit(solution)/shard_map/ppermute | solution.py:25
  219.1 9.9 %collective-permute-start.64 = (f32[8,64,128]{2,1,0:T(8,128)S(1)}, f32[8,64,128]{2,1,0:T(8,128)S(1)}, u32[]{:S(2)}, u32[]{:S(2)}) collective-permute-start(f32[8,64,128]{2,1,0:T(8,128)S(1)} %add.122.mine), channel_id=1, source_target_pairs={{0,8},{8,0},{16,24},{24,16},{1,9},{9,1},{17,25},{25,17},{2,10},{10... | collective-permute-start | bytes 786440 | tf_op jit(solution)/shard_map/ppermute | solution.py:25
  224.6 5.2 %collective-permute-start.82 = (f32[2,64,128]{2,1,0:T(8,128)S(1)}, f32[2,64,128]{2,1,0:T(8,128)S(1)}, u32[]{:S(2)}, u32[]{:S(2)}) collective-permute-start(f32[2,64,128]{2,1,0:T(8,128)S(1)} %get-tuple-element.171), channel_id=1, source_target_pairs={{0,1},{1,0},{2,3},{3,2},{4,5},{5,4},{6,7},{7,6},{8,9},{9,8},{10,11... | collective-permute-start | bytes 196616 | tf_op jit(solution)/shard_map/ppermute | solution.py:25
  224.6 7.4 %collective-permute-start.83 = (f32[2,64,128]{2,1,0:T(8,128)S(1)}, f32[2,64,128]{2,1,0:T(8,128)S(1)}, u32[]{:S(2)}, u32[]{:S(2)}) collective-permute-start(f32[2,64,128]{2,1,0:T(8,128)S(1)} %get-tuple-element.172), channel_id=1, source_target_pairs={{0,2},{1,3},{2,0},{3,1},{4,6},{5,7},{6,4},{7,5},{8,10},{9,11},{10,... | collective-permute-start | bytes 196616 | tf_op jit(solution)/shard_map/ppermute | solution.py:25
  226.6 5.6 %collective-permute-start.84 = (f32[2,64,128]{2,1,0:T(8,128)S(1)}, f32[2,64,128]{2,1,0:T(8,128)S(1)}, u32[]{:S(2)}, u32[]{:S(2)}) collective-permute-start(f32[2,64,128]{2,1,0:T(8,128)S(1)} %get-tuple-element.173), channel_id=1, source_target_pairs={{0,3},{1,2},{2,1},{3,0},{4,7},{5,6},{6,5},{7,4},{8,11},{9,10},{10,... | collective-permute-start | bytes 196616 | tf_op jit(solution)/shard_map/ppermute | solution.py:25
  226.7 6.2 %collective-permute-start.85 = (f32[2,64,128]{2,1,0:T(8,128)S(1)}, f32[2,64,128]{2,1,0:T(8,128)S(1)}, u32[]{:S(2)}, u32[]{:S(2)}) collective-permute-start(f32[2,64,128]{2,1,0:T(8,128)S(1)} %get-tuple-element.174), channel_id=1, source_target_pairs={{0,4},{1,5},{2,6},{3,7},{4,0},{5,1},{6,2},{7,3},{8,12},{9,13},{10,... | collective-permute-start | bytes 196616 | tf_op jit(solution)/shard_map/ppermute | solution.py:25
  229.0 6.1 %collective-permute-start.86 = (f32[2,64,128]{2,1,0:T(8,128)S(1)}, f32[2,64,128]{2,1,0:T(8,128)S(1)}, u32[]{:S(2)}, u32[]{:S(2)}) collective-permute-start(f32[2,64,128]{2,1,0:T(8,128)S(1)} %get-tuple-element.175), channel_id=1, source_target_pairs={{0,5},{1,4},{2,7},{3,6},{4,1},{5,0},{6,3},{7,2},{8,13},{9,12},{10,... | collective-permute-start | bytes 196616 | tf_op jit(solution)/shard_map/ppermute | solution.py:25
  229.7 5.5 %collective-permute-start.87 = (f32[2,64,128]{2,1,0:T(8,128)S(1)}, f32[2,64,128]{2,1,0:T(8,128)S(1)}, u32[]{:S(2)}, u32[]{:S(2)}) collective-permute-start(f32[2,64,128]{2,1,0:T(8,128)S(1)} %get-tuple-element.176), channel_id=1, source_target_pairs={{0,6},{1,7},{2,4},{3,5},{4,2},{5,3},{6,0},{7,1},{8,14},{9,15},{10,... | collective-permute-start | bytes 196616 | tf_op jit(solution)/shard_map/ppermute | solution.py:25
  232.1 5.1 %collective-permute-start.88 = (f32[2,64,128]{2,1,0:T(8,128)S(1)}, f32[2,64,128]{2,1,0:T(8,128)S(1)}, u32[]{:S(2)}, u32[]{:S(2)}) collective-permute-start(f32[2,64,128]{2,1,0:T(8,128)S(1)} %get-tuple-element.177), channel_id=1, source_target_pairs={{0,7},{1,6},{2,5},{3,4},{4,3},{5,2},{6,1},{7,0},{8,15},{9,14},{10,... | collective-permute-start | bytes 196616 | tf_op jit(solution)/shard_map/ppermute | solution.py:25
  232.2 6.6 %collective-permute-start.65 = (f32[2,64,128]{2,1,0:T(8,128)S(1)}, f32[2,64,128]{2,1,0:T(8,128)S(1)}, u32[]{:S(2)}, u32[]{:S(2)}) collective-permute-start(f32[2,64,128]{2,1,0:T(8,128)S(1)} %get-tuple-element.153), channel_id=1, source_target_pairs={{0,1},{1,0},{2,3},{3,2},{4,5},{5,4},{6,7},{7,6},{8,9},{9,8},{10,11... | collective-permute-start | bytes 196616 | tf_op jit(solution)/shard_map/ppermute | solution.py:25
  232.9 6.6 %collective-permute-start.66 = (f32[2,64,128]{2,1,0:T(8,128)S(1)}, f32[2,64,128]{2,1,0:T(8,128)S(1)}, u32[]{:S(2)}, u32[]{:S(2)}) collective-permute-start(f32[2,64,128]{2,1,0:T(8,128)S(1)} %get-tuple-element.154), channel_id=1, source_target_pairs={{0,2},{1,3},{2,0},{3,1},{4,6},{5,7},{6,4},{7,5},{8,10},{9,11},{10,... | collective-permute-start | bytes 196616 | tf_op jit(solution)/shard_map/ppermute | solution.py:25
  238.8 5.7 %collective-permute-start.70 = (f32[2,64,128]{2,1,0:T(8,128)S(1)}, f32[2,64,128]{2,1,0:T(8,128)S(1)}, u32[]{:S(2)}, u32[]{:S(2)}) collective-permute-start(f32[2,64,128]{2,1,0:T(8,128)S(1)} %get-tuple-element.158), channel_id=1, source_target_pairs={{0,6},{1,7},{2,4},{3,5},{4,2},{5,3},{6,0},{7,1},{8,14},{9,15},{10,... | collective-permute-start | bytes 196616 | tf_op jit(solution)/shard_map/ppermute | solution.py:25
  239.5 5.3 %collective-permute-start.71 = (f32[2,64,128]{2,1,0:T(8,128)S(1)}, f32[2,64,128]{2,1,0:T(8,128)S(1)}, u32[]{:S(2)}, u32[]{:S(2)}) collective-permute-start(f32[2,64,128]{2,1,0:T(8,128)S(1)} %get-tuple-element.159), channel_id=1, source_target_pairs={{0,7},{1,6},{2,5},{3,4},{4,3},{5,2},{6,1},{7,0},{8,15},{9,14},{10,... | collective-permute-start | bytes 196616 | tf_op jit(solution)/shard_map/ppermute | solution.py:25
  253.6 5.7 %collective-permute-start.90 = (f32[4,48,128]{2,1,0:T(8,128)S(1)}, f32[4,48,128]{2,1,0:T(8,128)S(1)}, u32[]{:S(2)}, u32[]{:S(2)}) collective-permute-start(f32[4,48,128]{2,1,0:T(8,128)S(1)} %get-tuple-element.191), channel_id=1, source_target_pairs={{0,2},{1,3},{2,0},{3,1},{4,6},{5,7},{6,4},{7,5},{8,10},{9,11},{10,... | collective-permute-start | bytes 294920 | tf_op jit(solution)/shard_map/ppermute | solution.py:25
  254.1 6.8 %collective-permute-start.92 = (f32[4,48,128]{2,1,0:T(8,128)S(1)}, f32[4,48,128]{2,1,0:T(8,128)S(1)}, u32[]{:S(2)}, u32[]{:S(2)}) collective-permute-start(f32[4,48,128]{2,1,0:T(8,128)S(1)} %get-tuple-element.192), channel_id=1, source_target_pairs={{0,6},{1,7},{2,4},{3,5},{4,2},{5,3},{6,0},{7,1},{8,14},{9,15},{10,... | collective-permute-start | bytes 294920 | tf_op jit(solution)/shard_map/ppermute | solution.py:25
  255.8 6.4 %collective-permute-start.91 = (f32[4,48,128]{2,1,0:T(8,128)S(1)}, f32[4,48,128]{2,1,0:T(8,128)S(1)}, u32[]{:S(2)}, u32[]{:S(2)}) collective-permute-start(f32[4,48,128]{2,1,0:T(8,128)S(1)} %get-tuple-element.193), channel_id=1, source_target_pairs={{0,4},{1,5},{2,6},{3,7},{4,0},{5,1},{6,2},{7,3},{8,12},{9,13},{10,... | collective-permute-start | bytes 294920 | tf_op jit(solution)/shard_map/ppermute | solution.py:25
  264.0 5.6 %collective-permute-start.95 = (f32[48,128]{1,0:T(8,128)S(1)}, f32[48,128]{1,0:T(8,128)S(1)}, u32[]{:S(2)}, u32[]{:S(2)}) collective-permute-start(f32[48,128]{1,0:T(8,128)S(1)} %get-tuple-element.198), channel_id=1, source_target_pairs={{0,24},{8,16},{16,8},{24,0},{1,25},{9,17},{17,9},{25,1},{2,26},{10... | collective-permute-start | bytes 73736 | tf_op jit(solution)/shard_map/ppermute | solution.py:25
  (41 other events, 343.7 us)

commit v3 on v2

v3 whole, which is shorter than its diff:
```python
import functools

import jax
import jax.numpy as jnp
from jax import lax
from jax.experimental import pallas as pl
from jax.experimental.pallas import tpu as pltpu
from jax.sharding import PartitionSpec as P

CAP = 2
NSTRUCT = 8
ITERS = 2
CHUNKS = 2
VOX = "vox"
PHASE = "phase"
LABEL_ROWS = 16
F32 = jnp.float32
BF16 = jnp.bfloat16
LARGE = 28 << 20
SMALL = 8 << 20
ROWS_AT_ONCE = 1024
COLUMNS_AT_ONCE = 512


def swap(x, axis, mask):
    count = lax.axis_size(axis)
    return lax.ppermute(x, axis, [(i, i ^ mask) for i in range(count)])


def spread(x, axis, masks):
    return [x] + [swap(x, axis, m) for m in masks]


def core_count():
    return min(2, lax.axis_size(VOX))


def halves(x, axis):
    big = x.astype(BF16)
    small = (x - big.astype(F32)).astype(BF16)
    return jnp.concatenate([big, small], axis=axis)


def term_sum(full, rows, cols):
    return full[:rows, :cols] + (full[:rows, cols:] + full[rows:, :cols])


def split_body(tile_ref, matrix, tiles, big, small, own, buffer, tile_buffer, sems, tile_sems):
    count, height, width = own.shape[0], buffer.shape[1], matrix.shape[1]
    steps = matrix.shape[0] // height

    def fetch(i):
        return pltpu.make_async_copy(
            matrix.at[pl.ds(i * height, height)], buffer.at[i % 2], sems.at[i % 2]
        )

    def fetch_tile(b):
        return pltpu.make_async_copy(tiles.at[tile_ref[b]], tile_buffer.at[b], tile_sems.at[b])

    fetch(0).start()
    for b in range(count):
        fetch_tile(b).start()
    for i in range(steps):
        fetch(i).wait()
        if i + 1 < steps:
            fetch(i + 1).start()
        x = buffer[i % 2]
        top = x.astype(BF16)
        big[i * height : (i + 1) * height, :] = top
        small[i * height : (i + 1) * height, :] = (x - top.astype(F32)).astype(BF16)
    for b in range(count):
        fetch_tile(b).wait()
        own[b] = halves(tile_buffer[b], 1)


def specs(count, space):
    return [pl.BlockSpec(memory_space=space)] * count


def split_terms(tile_index, matrix, warp_tiles, blocks):
    height, width = warp_tiles.shape[1:]
    step = 2 * height
    terms = jax.ShapeDtypeStruct(matrix.shape, BF16)
    return pl.pallas_call(
        split_body,
        in_specs=specs(1, pltpu.SMEM) + specs(2, pltpu.HBM),
        out_specs=specs(3, pltpu.VMEM),
        out_shape=[terms, terms, jax.ShapeDtypeStruct((blocks, height, 2 * width), BF16)],
        scratch_shapes=[
            pltpu.VMEM((2, step, matrix.shape[1]), F32),
            pltpu.VMEM((blocks, height, width), F32),
            pltpu.SemaphoreType.DMA((2,)),
            pltpu.SemaphoreType.DMA((blocks,)),
        ],
        compiler_params=pltpu.CompilerParams(vmem_limit_bytes=LARGE),
        cost_estimate=pl.CostEstimate(
            flops=matrix.size, bytes_accessed=matrix.size * 4, transcendentals=0
        ),
        name="split_terms",
    )(tile_index, matrix, warp_tiles)


def fill_weights(me_ref, out, pieces, rows, vox, masks):
    cores = len(pieces)
    for c, ref in enumerate(pieces):
        for k in range(vox // cores):
            for i, p in enumerate(masks):
                v = me_ref[0] ^ (k * cores + c)
                at = ((me_ref[1] ^ p) * vox + v) * rows
                out[pl.ds(pl.multiple_of(at, rows), rows), :] = halves(
                    ref[k, i * rows : (i + 1) * rows, :], 1
                )


def forward_body(dims, source_ref, valid_ref, me_ref, big, small, tiles, *refs):
    vox, masks, rows, pieces_n, chunks = dims
    pieces, outs = refs[:pieces_n], refs[pieces_n:-2]
    weights, dose = refs[-2:]
    plans = dose.shape[1]
    height = tiles.shape[1]
    if len(pieces[0].shape) == 2:
        weights[...] = halves(pieces[0][...], 1)
    else:
        fill_weights(me_ref, weights, pieces, rows, vox, masks)
    step = min(ROWS_AT_ONCE, dose.shape[0])

    def multiply(i, carry):
        at = pl.ds(pl.multiple_of(i * step, step), step)
        top = jnp.dot(big[at, :], weights[...], preferred_element_type=F32)
        rest = jnp.dot(small[at, :], weights[:, :plans], preferred_element_type=F32)
        dose[at, :] = top[:, :plans] + (top[:, plans:] + rest)
        return carry

    lax.fori_loop(0, dose.shape[0] // step, multiply, 0)
    part = height // chunks
    for m in range(vox):
        for j in range(CAP):
            s = m * CAP + j
            b = source_ref[s]
            block = dose[pl.ds(pl.multiple_of(b * height, height), height), :]
            tile = tiles[b]
            left = jnp.concatenate([tile[:, :height], tile[:, height:]], axis=0)
            full = jnp.dot(left, halves(block, 1), preferred_element_type=F32)
            warped = jnp.where(valid_ref[s] > 0, term_sum(full, height, plans), 0.0)
            for h in range(chunks):
                outs[h * vox + m][j] = warped[h * part : (h + 1) * part]


def forward(scalars, terms, pieces, rows, vox, masks):
    big, small, tiles = terms
    height = tiles.shape[1]
    vox_rows, spots = big.shape
    plans = pieces[0].shape[-1]
    out = jax.ShapeDtypeStruct((CAP, height // CHUNKS, plans), F32)
    return pl.pallas_call(
        functools.partial(forward_body, (vox, masks, rows, len(pieces), CHUNKS)),
        in_specs=specs(3, pltpu.SMEM) + specs(3 + len(pieces), pltpu.VMEM),
        out_specs=specs(vox * CHUNKS, pltpu.VMEM),
        out_shape=[out] * (vox * CHUNKS),
        scratch_shapes=[pltpu.VMEM((spots, 2 * plans), BF16), pltpu.VMEM((vox_rows, plans), F32)],
        compiler_params=pltpu.CompilerParams(vmem_limit_bytes=LARGE),
        cost_estimate=pl.CostEstimate(
            flops=8 * big.size * plans, bytes_accessed=big.size * 4, transcendentals=0
        ),
        name="dose_and_warp",
    )(*scalars, *terms, *pieces)


def gradient_body(dims, source_ref, valid_ref, me_ref, big, small, tiles, *refs):
    vox, masks, rows, cores, chunks = dims
    returned = refs[: vox * chunks]
    outs = refs[vox * chunks : -2]
    columns, turned = refs[-2:]
    height = tiles.shape[1]
    plans = turned.shape[1]
    spots = big.shape[1]
    for m in range(vox):
        for j in range(CAP):
            s = m * CAP + j

            @pl.when(valid_ref[s] > 0)
            def _():
                b = source_ref[s]
                adjoint = jnp.concatenate([returned[h * vox + m][j] for h in range(chunks)], axis=0)
                full = jnp.dot(halves(adjoint.T, 0), tiles[b], preferred_element_type=F32)
                at = pl.ds(pl.multiple_of(b * height, height), height)
                columns[:, at] = halves(term_sum(full, plans, height), 0)

    for first in range(0, spots, COLUMNS_AT_ONCE):
        last = min(first + COLUMNS_AT_ONCE, spots)
        top = jnp.dot(columns[...], big[:, first:last], preferred_element_type=F32)
        rest = jnp.dot(columns[:plans, :], small[:, first:last], preferred_element_type=F32)
        total = top[:plans] + (top[plans:] + rest)
        for i in range(0, last - first, plans):
            turned[first + i : first + i + plans, :] = total[:, i : i + plans].T
    if len(outs[0].shape) == 2:
        outs[0][...] = turned[...]
    else:
        for c in range(cores):
            for k in range(vox // cores):
                for i, p in enumerate(masks):
                    v = me_ref[0] ^ (k * cores + c)
                    at = ((me_ref[1] ^ p) * vox + v) * rows
                    outs[c][k, i * rows : (i + 1) * rows] = turned[
                        pl.ds(pl.multiple_of(at, rows), rows), :
                    ]


def gradient_parts(scalars, terms, returned, rows, vox, masks):
    big, small, tiles = terms
    vox_rows, spots = big.shape
    plans = returned[0].shape[-1]
    cores = core_count()
    if rows % 8 == 0:
        outs = [jax.ShapeDtypeStruct((vox // cores, len(masks) * rows, plans), F32)] * cores
    else:
        outs = [jax.ShapeDtypeStruct((spots, plans), F32)]
    return pl.pallas_call(
        functools.partial(gradient_body, (vox, masks, rows, cores, CHUNKS)),
        in_specs=specs(3, pltpu.SMEM) + specs(3 + len(returned), pltpu.VMEM),
        out_specs=specs(len(outs), pltpu.VMEM),
        out_shape=outs,
        scratch_shapes=[pltpu.VMEM((2 * plans, vox_rows), BF16), pltpu.VMEM((spots, plans), F32)],
        compiler_params=pltpu.CompilerParams(vmem_limit_bytes=LARGE),
        cost_estimate=pl.CostEstimate(
            flops=8 * big.size * plans, bytes_accessed=big.size * 4, transcendentals=0
        ),
        name="warp_back_and_gradient",
    )(*scalars, *terms, *returned)


def place_body(vox, which_ref, slot_ref, *refs):
    incoming, (give, keep, total) = refs[:vox], refs[vox:]
    total[...] = jnp.zeros_like(total)
    for m in range(vox):
        for j in range(CAP):
            slot = slot_ref[m * CAP + j]

            @pl.when(slot >= 0)
            def _():
                total[slot] += incoming[m][j]

    half = keep.shape[0]
    which = which_ref[0]
    keep[...] = total[pl.ds(which * half, half)]
    give[...] = total[pl.ds((1 - which) * half, half)]


def place(which, slots, incoming, blocks):
    vox = len(incoming)
    _, height, plans = incoming[0].shape
    half = jax.ShapeDtypeStruct((blocks // 2, height, plans), F32)
    smem = pl.BlockSpec(memory_space=pltpu.SMEM)
    vmem = pl.BlockSpec(memory_space=pltpu.VMEM)
    return pl.pallas_call(
        functools.partial(place_body, vox),
        in_specs=[smem, smem] + [vmem] * vox,
        out_specs=[vmem, vmem],
        out_shape=[half, half],
        scratch_shapes=[pltpu.VMEM((blocks, height, plans), F32)],
        compiler_params=pltpu.CompilerParams(vmem_limit_bytes=SMALL),
        name="place_blocks",
    )(which, slots, *incoming)


def pull_body(vox, with_dose, which_ref, slot_ref, mine, other, goal, scale, *refs):
    half = mine.shape[0]
    which = which_ref[0]
    field = refs[-1]
    field[pl.ds(which * half, half)] = mine[...]
    field[pl.ds((1 - which) * half, half)] = other[...]
    for m in range(vox):
        for j in range(CAP):
            slot = jnp.maximum(slot_ref[m * CAP + j], 0)
            refs[m][j] = scale[slot] * (field[slot] - goal[slot])
    if with_dose:
        refs[vox][...] = field[...]


def pull(which, slots, mine, other, goal, scale, vox, with_dose):
    half, height, plans = mine.shape
    smem = pl.BlockSpec(memory_space=pltpu.SMEM)
    vmem = pl.BlockSpec(memory_space=pltpu.VMEM)
    outs = [jax.ShapeDtypeStruct((CAP, height, plans), F32)] * vox
    if with_dose:
        outs = outs + [jax.ShapeDtypeStruct((2 * half, height, plans), F32)]
    return pl.pallas_call(
        functools.partial(pull_body, vox, with_dose),
        in_specs=[smem, smem] + [vmem] * 4,
        out_specs=[vmem] * len(outs),
        out_shape=outs,
        scratch_shapes=[pltpu.VMEM((2 * half, height, plans), F32)],
        compiler_params=pltpu.CompilerParams(vmem_limit_bytes=SMALL),
        name="adjoint_blocks",
    )(which, slots, mine, other, goal, scale)


def phase_steps():
    count, steps = lax.axis_size(PHASE), []
    while 2 ** len(steps) < count:
        steps.append(2 ** (len(steps) + 1) - 1)
    return steps


def chip_steps():
    count, steps, mask = lax.axis_size(VOX), [], core_count()
    while mask < count:
        steps.append(mask)
        mask *= 2
    return steps


def combined(steps):
    masks = [0]
    for s in steps:
        masks += [m ^ s for m in masks]
    return masks


def gather_along(x, axis, steps, backwards=False):
    out = x[None]
    for s in reversed(steps) if backwards else steps:
        other = swap(out, axis, s)
        out = jnp.stack([out, other], axis=1 if backwards else 0).reshape(-1, *x.shape)
    return out


def sum_along(x, axis, steps, backwards=False):
    for s in reversed(steps) if backwards else steps:
        pairs = x.reshape(2, -1, *x.shape[1:]) if backwards else x.reshape(-1, 2, *x.shape[1:])
        keep, give = (pairs[0], pairs[1]) if backwards else (pairs[:, 0], pairs[:, 1])
        x = keep + swap(give, axis, s)
    return x


def sum_everywhere(x, axis, steps):
    for i, s in enumerate(steps):
        other = swap(x, axis, s).reshape(-1, 2, 2**i, *x.shape[1:])
        x = x + jnp.concatenate([other[:, 1:], other[:, :1]], axis=1).reshape(x.shape)
    return x


def gather_chips(by_phase):
    half = by_phase.shape[0] // 2
    by_chip = jnp.concatenate(
        [
            gather_along(by_phase[:half], VOX, chip_steps()),
            gather_along(by_phase[half:], VOX, chip_steps(), True),
        ],
        axis=1,
    )
    return spread(by_chip, VOX, range(1, core_count()))


def sum_chips(parts):
    chips = parts[0]
    for m in range(1, len(parts)):
        chips = chips + swap(parts[m], VOX, m)
    half = chips.shape[1] // 2
    first = sum_along(chips[:, :half], VOX, chip_steps())
    second = sum_along(chips[:, half:], VOX, chip_steps(), True)
    return jnp.concatenate([first[0], second[0]], axis=0)


def exchange(pieces):
    return [pieces[0]] + [swap(pieces[m], VOX, m) for m in range(1, len(pieces))]


def phase_halves(give, keep):
    phases = lax.axis_size(PHASE)
    if phases == 1:
        return keep, give
    keep = keep + swap(give, PHASE, 1)
    span = 4
    while span <= phases:
        keep = keep + swap(keep, PHASE, span - 1)
        span *= 2
    return keep, swap(keep, PHASE, 1)


def per_device(
    influence,
    weights,
    warp_tiles,
    owners,
    owner_slot,
    tile_index,
    structure,
    prescribed,
    importance,
    step_size,
):
    highest = lax.Precision.HIGHEST
    matrix = influence[0]
    vox_rows, spots = matrix.shape
    block_rows = warp_tiles.shape[1]
    rows, plans = weights.shape
    local_blocks = vox_rows // block_rows
    vox = lax.axis_size(VOX)
    phases = lax.axis_size(PHASE)
    cores = core_count()
    me_vox = lax.axis_index(VOX)
    me_phase = lax.axis_index(PHASE)
    slots_all = vox * CAP
    part = block_rows // CHUNKS
    targets = owners[0, :, 0]
    which = ((me_phase ^ (me_phase >> 1)) & 1).astype(jnp.int32).reshape(1)

    def orders(names):
        before = jnp.tril(jnp.ones((local_blocks, local_blocks), jnp.int32), -1)
        same = (names[..., :, None] == names[..., None, :]).astype(jnp.int32)
        return jnp.sum(same * before, axis=-1)

    position = (targets ^ me_vox) * CAP + orders(targets)
    chosen_mask = jnp.arange(slots_all, dtype=jnp.int32)[:, None] == position[None, :]
    positions_i = jnp.arange(local_blocks, dtype=jnp.int32)
    source = jnp.sum(jnp.where(chosen_mask, positions_i[None, :], 0), axis=1)
    valid = jnp.sum(chosen_mask.astype(jnp.int32), axis=1)
    me = jnp.stack([me_vox, me_phase]).astype(jnp.int32)
    scalars = (source, valid, me)
    labels = jnp.zeros((LABEL_ROWS, plans), F32)
    labels = labels.at[0, :local_blocks].set(targets.astype(F32))
    labels = labels.at[1, :local_blocks].set(owner_slot[0].astype(F32))

    member = (structure[:, None] == jnp.arange(NSTRUCT, dtype=jnp.int32)[None, :]).astype(F32)
    target_dose = jnp.dot(member, prescribed, precision=highest, preferred_element_type=F32)
    voxel_weight = jnp.dot(
        member, importance[:, None], precision=highest, preferred_element_type=F32
    )
    voxel_weight = jnp.broadcast_to(voxel_weight, target_dose.shape)
    goals = target_dose.reshape(local_blocks, CHUNKS, part, plans)
    scales = voxel_weight.reshape(local_blocks, CHUNKS, part, plans)
    goals = [goals[:, h] for h in range(CHUNKS)]
    scales = [scales[:, h] for h in range(CHUNKS)]

    masks = combined(phase_steps())
    terms = split_terms(tile_index[0], matrix, warp_tiles, local_blocks)
    held = gather_along(weights, PHASE, phase_steps()).reshape(-1, plans)
    for iteration in range(ITERS):
        last = iteration == ITERS - 1
        if iteration == 0:
            pieces = gather_chips(jnp.concatenate([held, labels], axis=0))
            infos = jnp.stack(pieces, axis=1).reshape(vox, -1, plans)[:, phases * rows :]
            names = infos[:, 0, :local_blocks].astype(jnp.int32)
            slots = infos[:, 1, :local_blocks].astype(jnp.int32)
            order = jnp.where(names == me_vox, orders(names), -1)
            hit = order[:, None, :] == jnp.arange(CAP, dtype=jnp.int32)[None, :, None]
            received = jnp.sum(jnp.where(hit, slots[:, None, :] + 1, 0), axis=-1)
            received = received.reshape(slots_all) - 1
        else:
            pieces = gather_chips(held)
        if rows % 16:
            every = jnp.stack(pieces, axis=1).reshape(vox, -1, plans)[:, : phases * rows]
            every = every.reshape(vox, phases, rows, plans)
            back_to = jnp.asarray([masks.index(p) for p in range(phases)], jnp.int32)
            every = every[jnp.arange(vox) ^ me_vox][:, back_to[jnp.arange(phases) ^ me_phase]]
            pieces = [every.transpose(1, 0, 2, 3).reshape(spots, plans)]
        outgoing = forward(scalars, terms, pieces, rows, vox, masks)
        returned, dose = [], []
        incoming = [exchange(outgoing[h * vox : (h + 1) * vox]) for h in range(CHUNKS)]
        for h in range(CHUNKS):
            give, keep = place(which, received, incoming[h], local_blocks)
            mine, other = phase_halves(give, keep)
            back = pull(which, received, mine, other, goals[h], scales[h], vox, last)
            returned += exchange(back[:vox])
            dose += back[vox:]
        parts = gradient_parts(scalars, terms, returned, rows, vox, masks)
        if rows % 8:
            parts = parts[0].reshape(phases, vox, rows, plans)
            wanted = jnp.asarray(masks, jnp.int32) ^ me_phase
            parts = parts[wanted][:, jnp.arange(vox) ^ me_vox]
            parts = parts.transpose(1, 0, 2, 3).reshape(vox // cores, cores, phases * rows, plans)
            parts = [parts[:, c] for c in range(cores)]
        total = sum_chips(parts)
        if last:
            total = sum_along(total.reshape(phases, rows, plans), PHASE, phase_steps())[0]
            new_weights = jnp.maximum(held[:rows] - step_size[None, :] * total, 0.0)
        else:
            total = sum_everywhere(total.reshape(phases, rows, plans), PHASE, phase_steps())
            held = jnp.maximum(held - step_size[None, :] * total.reshape(held.shape), 0.0)
    dose_field = jnp.stack(dose, axis=1).reshape(vox_rows, plans)
    return (new_weights, dose_field)


def solution(mesh):
    in_specs = (
        P("phase", "vox", None),
        P(("phase", "vox"), None),
        P(),
        P("phase", "vox", None),
        P("phase", "vox"),
        P("phase", "vox"),
        P("vox"),
        P(),
        P(),
        P(),
    )
    out_specs = (P(("phase", "vox"), None), P("vox", None))
    return jax.shard_map(
        per_device, mesh=mesh, in_specs=in_specs, out_specs=out_specs, check_vma=False
    )
```

time: 271 us -> 274 us (1.011)
  starting transfers between devices: 119 us -> 125 us
  local copies, waits for them, and re-layouts: 16.3 us -> 10.6 us
  Pallas kernels: 38.6 us -> 42.5 us
    ppermute x96 -> x94, starting transfers between devices: 119 us -> 125 us  [swap(): return lax.ppermute(x, axis, [(i, i ^ mask) for i in range(count)])]
    unnamed x22, local copies, waits for them, and re-layouts: 14.3 us -> 8.44 us
    pallas_call x4 -> x5, Pallas kernels: 32.7 us -> 36.8 us  [the longest x2 14.6 us: gradient_parts(): pl.pallas_call(functools.partial(gradient_body, (vox, masks, rows, cores,...]
    ppermute x96 -> x94, waiting for transfers between devices: 88.6 us -> 86.9 us  [swap(): return lax.ppermute(x, axis, [(i, i ^ mask) for i in range(count)])]
  transfers between devices with their start and end apart: 96 -> 94, of which waited for: 48 -> 48; matrix products, arithmetic and copies ran while one was open for 3% -> 3% of each run, Pallas kernels for 2% -> 7%
where the time goes in v3:
time: 274 us; the launch traced here: 273 us
  starting transfers between devices  125 us (46%)
  waiting for transfers between devices  86.9 us (32%)
  Pallas kernels  42.5 us (16%)
  local copies, waits for them, and re-layouts  10.6 us (4%)
  other arithmetic  5.17 us (2%)
    ppermute x94, starting transfers between devices, swap(): return lax.ppermute(x, axis, [(i, i ^ mask) for i in range(count)])  125 us
    ppermute x94, waiting for transfers between devices, swap(): return lax.ppermute(x, axis, [(i, i ^ mask) for i in range(count)])  86.9 us
    pallas_call x2, Pallas kernels, gradient_parts(): pl.pallas_call(functools.partial(gradient_body, (vox, masks, rows, cores,...  14.6 us
    pallas_call x1, Pallas kernels, split_terms(): pl.pallas_call(split_body, in_specs=specs(1, pltpu.SMEM) + specs(2, pltpu...  12.4 us
    pallas_call x2, Pallas kernels, forward(): pl.pallas_call(functools.partial(forward_body, (vox, masks, rows, len(pie...  9.89 us
    unnamed x22, local copies, waits for them, and re-layouts  8.44 us
  transfers between devices with their start and end apart: 94, of which 48 were waited for; matrix products, arithmetic and copies ran while one was open for 3% of the time, Pallas kernels for 7%

profile of v3, /device:TPU:0, one launch (start us, length us, event | category | flops | bytes accessed | tf_op | source)
XLA Modules:
  0.0 273.1 jit_solution(1122123191155171584)
XLA Ops:
  0.6 3.1 %collective-permute-start = (f32[1,48,128]{2,1,0:T(8,128)}, f32[1,48,128]{2,1,0:T(8,128)S(1)}, u32[]{:S(2)}, u32[]{:S(2)}) collective-permute-start(f32[1,48,128]{2,1,0:T(8,128)} %bitcast.236), channel_id=1, source_target_pairs={{0,8},{8,0},{16,24},{24,16},{1,9},{9,1},{17,25},{25,17},{2,10},{10... | collective-permute-start | bytes 73736 | tf_op jit(solution)/shard_map/ppermute | solution.py:27
  6.5 4.0 %collective-permute-start.1 = (f32[2,48,128]{2,1,0:T(8,128)S(1)}, f32[2,48,128]{2,1,0:T(8,128)S(1)}, u32[]{:S(2)}, u32[]{:S(2)}) collective-permute-start(f32[2,48,128]{2,1,0:T(8,128)S(1)} %get-tuple-element.219), channel_id=1, source_target_pairs={{0,24},{8,16},{16,8},{24,0},{1,25},{9,17},{17,9},{25,1},{2,26},{10... | collective-permute-start | bytes 147464 | tf_op jit(solution)/shard_map/ppermute | solution.py:27
  12.6 1.8 collective-permute-start.4
  15.4 2.2 copy-done.5
  18.2 12.4 %split_terms.1 = (bf16[2048,1536]{1,0:T(8,128)(2,1)S(1)}, bf16[2048,1536]{1,0:T(8,128)(2,1)S(1)}, bf16[16,128,256]{2,1,0:T(8,128)(2,1)S(1)}) custom-call(s32[16]{0:T(128)S(1)} %bitcast.203, f32[2048,1536]{1,0:T(8,128)} %bitcast.204, f32[64,128,128]{2,1,0:T(8,128)S(1)} %copy-done.5), custom_call_target="tpu_custom_call" | custom-call | flops 3145728 | bytes 12582912 | tf_op jit(solution)/shard_map/split_terms/pallas_call | solution.py:84
  30.6 1.6 collective-permute-start.2
  32.8 2.0 collective-permute-done.2
  35.2 1.8 collective-permute-done.5
  37.0 2.6 collective-permute-done.3
  40.0 1.6 collective-permute-done.6.refs_1_
  41.7 5.0 %dose_and_warp.2 = (f32[2,64,128]{2,1,0:T(8,128)S(1)}, f32[2,64,128]{2,1,0:T(8,128)S(1)}, f32[2,64,128]{2,1,0:T(8,128)S(1)}, f32[2,64,128]{2,1,0:T(8,128)S(1)}, ...) custom-call(s32[16]{0:T(128)S(1)} %get-tuple-element.189.source_ref,, ...), custom_call_target="tpu_custom_call" | custom-call | flops 3221225472 | bytes 12582912 | tf_op jit(solution)/shard_map/dose_and_warp/pallas_call | solution.py:155
  46.9 1.5 collective-permute-start.8
  53.4 1.7 collective-permute-start.30
  58.8 2.1 collective-permute-start.13
  61.9 2.2 collective-permute-done.12.refs_6_
  66.5 4.4 %collective-permute-done.31 = f32[8,64,128]{2,1,0:T(8,128)S(1)} collective-permute-done((f32[8,64,128]{2,1,0:T(8,128)S(1)}, f32[8,64,128]{2,1,0:T(8,128)S(1)}, u32[]{:S(2)}, u32[]{:S(2)}) %collective-permute-start.31) | collective-permute-done | bytes 262176 | tf_op jit(solution)/shard_map/ppermute | solution.py:27
  71.0 3.4 %collective-permute-start.32 = (f32[8,64,128]{2,1,0:T(8,128)S(1)}, f32[8,64,128]{2,1,0:T(8,128)S(1)}, u32[]{:S(2)}, u32[]{:S(2)}) collective-permute-start(f32[8,64,128]{2,1,0:T(8,128)S(1)} %add.116), channel_id=1, source_target_pairs={{0,24},{8,16},{16,8},{24,0},{1,25},{9,17},{17,9},{25,1},{2,26},{10... | collective-permute-start | bytes 786440 | tf_op jit(solution)/shard_map/ppermute | solution.py:27
  74.4 1.7 collective-permute-done.14
  76.2 9.2 %collective-permute-start.15 = (f32[8,64,128]{2,1,0:T(8,128)S(1)}, f32[8,64,128]{2,1,0:T(8,128)S(1)}, u32[]{:S(2)}, u32[]{:S(2)}) collective-permute-start(f32[8,64,128]{2,1,0:T(8,128)S(1)} %add.114), channel_id=1, source_target_pairs={{0,24},{8,16},{16,8},{24,0},{1,25},{9,17},{17,9},{25,1},{2,26},{10... | collective-permute-start | bytes 786440 | tf_op jit(solution)/shard_map/ppermute | solution.py:27
  87.1 5.5 %collective-permute-done.15 = f32[8,64,128]{2,1,0:T(8,128)S(1)} collective-permute-done((f32[8,64,128]{2,1,0:T(8,128)S(1)}, f32[8,64,128]{2,1,0:T(8,128)S(1)}, u32[]{:S(2)}, u32[]{:S(2)}) %collective-permute-start.15) | collective-permute-done | bytes 262176 | tf_op jit(solution)/shard_map/ppermute | solution.py:27
  92.7 4.4 %collective-permute-start.16 = (f32[8,64,128]{2,1,0:T(8,128)S(1)}, f32[8,64,128]{2,1,0:T(8,128)S(1)}, u32[]{:S(2)}, u32[]{:S(2)}) collective-permute-start(f32[8,64,128]{2,1,0:T(8,128)S(1)} %add.115.mine), channel_id=1, source_target_pairs={{0,8},{8,0},{16,24},{24,16},{1,9},{9,1},{17,25},{25,17},{2,10},{10... | collective-permute-start | bytes 786440 | tf_op jit(solution)/shard_map/ppermute | solution.py:27
  101.2 2.0 collective-permute-done.16.other
  104.8 2.9 %collective-permute-start.40 = (f32[2,64,128]{2,1,0:T(8,128)S(1)}, f32[2,64,128]{2,1,0:T(8,128)S(1)}, u32[]{:S(2)}, u32[]{:S(2)}) collective-permute-start(f32[2,64,128]{2,1,0:T(8,128)S(1)} %get-tuple-element.145), channel_id=1, source_target_pairs={{0,7},{1,6},{2,5},{3,4},{4,3},{5,2},{6,1},{7,0},{8,15},{9,14},{10,... | collective-permute-start | bytes 196616 | tf_op jit(solution)/shard_map/ppermute | solution.py:27
  107.8 1.8 collective-permute-start.19
  112.2 1.5 collective-permute-start.22
  115.9 2.0 collective-permute-done.22.refs_6_
  119.0 2.8 %copy-done.2 = bf16[2048,1536]{1,0:T(8,128)(2,1)S(1)} copy-done((bf16[2048,1536]{1,0:T(8,128)(2,1)S(1)}, bf16[2048,1536]{1,0:T(8,128)(2,1)}, u32[]{:S(2)}) %copy-start.2) | copy-done | bytes 6291480
  121.8 2.8 %copy-done.4 = bf16[2048,1536]{1,0:T(8,128)(2,1)S(1)} copy-done((bf16[2048,1536]{1,0:T(8,128)(2,1)S(1)}, bf16[2048,1536]{1,0:T(8,128)(2,1)}, u32[]{:S(2)}) %copy-start.4) | copy-done | bytes 6291480
  124.6 7.3 %warp_back_and_gradient.2 = (f32[4,192,128]{2,1,0:T(8,128)S(1)}, f32[4,192,128]{2,1,0:T(8,128)S(1)}) custom-call(s32[16]{0:T(128)S(1)} %get-tuple-element.189.source_ref, s32[16]{0:T(128)S(1)} %get-tuple-element.188.valid_ref, s32[2]{0:T(128)S(1)} %pad_add_fusion.me_ref, bf16[2048,1536]{1,0:T(8,128)(2,1)S(1)} %copy-done.2, bf16[2048,1536]{1,0:T(8,128)(2,1)S(1)} %copy-done.4, ...), custom_call_target="tpu_custom_call" | custom-call | flops 3221225472 | bytes 12582912 | tf_op jit(solution)/shard_map/warp_back_and_gradient/pallas_call | solution.py:218
  132.0 1.6 collective-permute-done.41
  135.5 3.1 %collective-permute-done.44 = f32[2,96,128]{2,1,0:T(8,128)S(1)} collective-permute-done((f32[2,96,128]{2,1,0:T(8,128)S(1)}, f32[2,96,128]{2,1,0:T(8,128)S(1)}, u32[]{:S(2)}, u32[]{:S(2)}) %collective-permute-start.44) | collective-permute-done | bytes 98336 | tf_op jit(solution)/shard_map/ppermute | solution.py:27
  140.6 2.2 collective-permute-done.45
  145.7 3.2 %collective-permute-done.46 = f32[4,48,128]{2,1,0:T(8,128)S(1)} collective-permute-done((f32[4,48,128]{2,1,0:T(8,128)S(1)}, f32[4,48,128]{2,1,0:T(8,128)S(1)}, u32[]{:S(2)}, u32[]{:S(2)}) %collective-permute-start.46) | collective-permute-done | bytes 98336 | tf_op jit(solution)/shard_map/ppermute | solution.py:27
  148.9 2.9 %collective-permute-start.47 = (f32[4,48,128]{2,1,0:T(8,128)S(1)}, f32[4,48,128]{2,1,0:T(8,128)S(1)}, u32[]{:S(2)}, u32[]{:S(2)}) collective-permute-start(f32[4,48,128]{2,1,0:T(8,128)S(1)} %bitcast_add_fusion.1), channel_id=1, source_target_pairs={{0,24},{8,16},{16,8},{24,0},{1,25},{9,17},{17,9},{25,1},{2,26},{10... | collective-permute-start | bytes 294920 | tf_op jit(solution)/shard_map/ppermute | solution.py:27
  151.8 3.7 %collective-permute-done.47 = f32[4,48,128]{2,1,0:T(8,128)S(1)} collective-permute-done((f32[4,48,128]{2,1,0:T(8,128)S(1)}, f32[4,48,128]{2,1,0:T(8,128)S(1)}, u32[]{:S(2)}, u32[]{:S(2)}) %collective-permute-start.47) | collective-permute-done | bytes 98336 | tf_op jit(solution)/shard_map/ppermute | solution.py:27
  157.5 2.7 collective-permute-done.50
  162.2 2.8 %collective-permute-done.51 = f32[2,96,128]{2,1,0:T(8,128)S(1)} collective-permute-done((f32[2,96,128]{2,1,0:T(8,128)S(1)}, f32[2,96,128]{2,1,0:T(8,128)S(1)}, u32[]{:S(2)}, u32[]{:S(2)}) %collective-permute-start.51) | collective-permute-done | bytes 98336 | tf_op jit(solution)/shard_map/ppermute | solution.py:27
  166.0 1.7 collective-permute-done.52.refs_1_
  167.7 4.9 %dose_and_warp.3 = (f32[2,64,128]{2,1,0:T(8,128)S(1)}, f32[2,64,128]{2,1,0:T(8,128)S(1)}, f32[2,64,128]{2,1,0:T(8,128)S(1)}, f32[2,64,128]{2,1,0:T(8,128)S(1)}, ...) custom-call(s32[16]{0:T(128)S(1)} %get-tuple-element.189.source_ref,, ...), custom_call_target="tpu_custom_call" | custom-call | flops 3221225472 | bytes 12582912 | tf_op jit(solution)/shard_map/dose_and_warp/pallas_call | solution.py:155
  179.1 2.0 collective-permute-start.76
  184.6 1.8 collective-permute-start.59
  190.2 1.6 collective-permute-start.60
  191.7 4.7 %collective-permute-done.77 = f32[8,64,128]{2,1,0:T(8,128)S(1)} collective-permute-done((f32[8,64,128]{2,1,0:T(8,128)S(1)}, f32[8,64,128]{2,1,0:T(8,128)S(1)}, u32[]{:S(2)}, u32[]{:S(2)}) %collective-permute-start.77) | collective-permute-done | bytes 262176 | tf_op jit(solution)/shard_map/ppermute | solution.py:27
  196.5 2.1 collective-permute-start.78
  198.7 2.4 collective-permute-done.60
  201.0 4.2 %collective-permute-start.61 = (f32[8,64,128]{2,1,0:T(8,128)S(1)}, f32[8,64,128]{2,1,0:T(8,128)S(1)}, u32[]{:S(2)}, u32[]{:S(2)}) collective-permute-start(f32[8,64,128]{2,1,0:T(8,128)S(1)} %add.126), channel_id=1, source_target_pairs={{0,24},{8,16},{16,8},{24,0},{1,25},{9,17},{17,9},{25,1},{2,26},{10... | collective-permute-start | bytes 786440 | tf_op jit(solution)/shard_map/ppermute | solution.py:27
  205.3 4.2 %collective-permute-done.78 = f32[8,64,128]{2,1,0:T(8,128)S(1)} collective-permute-done((f32[8,64,128]{2,1,0:T(8,128)S(1)}, f32[8,64,128]{2,1,0:T(8,128)S(1)}, u32[]{:S(2)}, u32[]{:S(2)}) %collective-permute-start.78) | collective-permute-done | bytes 262176 | tf_op jit(solution)/shard_map/ppermute | solution.py:27
  209.5 7.6 %collective-permute-start.79 = (f32[8,64,128]{2,1,0:T(8,128)S(1)}, f32[8,64,128]{2,1,0:T(8,128)S(1)}, u32[]{:S(2)}, u32[]{:S(2)}) collective-permute-start(f32[8,64,128]{2,1,0:T(8,128)S(1)} %add.129.mine), channel_id=1, source_target_pairs={{0,8},{8,0},{16,24},{24,16},{1,9},{9,1},{17,25},{25,17},{2,10},{10... | collective-permute-start | bytes 786440 | tf_op jit(solution)/shard_map/ppermute | solution.py:27
  217.1 3.9 %collective-permute-start.62 = (f32[8,64,128]{2,1,0:T(8,128)S(1)}, f32[8,64,128]{2,1,0:T(8,128)S(1)}, u32[]{:S(2)}, u32[]{:S(2)}) collective-permute-start(f32[8,64,128]{2,1,0:T(8,128)S(1)} %add.127.mine), channel_id=1, source_target_pairs={{0,8},{8,0},{16,24},{24,16},{1,9},{9,1},{17,25},{25,17},{2,10},{10... | collective-permute-start | bytes 786440 | tf_op jit(solution)/shard_map/ppermute | solution.py:27
  222.3 1.5 collective-permute-start.81
  225.4 1.7 collective-permute-done.62.other
  227.8 1.8 collective-permute-start.85
  229.6 1.9 collective-permute-start.86
  233.4 1.6 collective-permute-start.66
  236.0 1.6 collective-permute-start.68
  238.7 2.5 collective-permute-done.68.refs_6_
  241.2 1.6 collective-permute-done.69.refs_7_
  242.7 7.3 %warp_back_and_gradient.3 = (f32[4,192,128]{2,1,0:T(8,128)S(1)}, f32[4,192,128]{2,1,0:T(8,128)S(1)}) custom-call(s32[16]{0:T(128)S(1)} %get-tuple-element.189.source_ref, s32[16]{0:T(128)S(1)} %get-tuple-element.188.valid_ref, s32[2]{0:T(128)S(1)} %pad_add_fusion.me_ref, bf16[2048,1536]{1,0:T(8,128)(2,1)S(1)} %copy-done.2, bf16[2048,1536]{1,0:T(8,128)(2,1)S(1)} %copy-done.4, ...), custom_call_target="tpu_custom_call" | custom-call | flops 3221225472 | bytes 12582912 | tf_op jit(solution)/shard_map/warp_back_and_gradient/pallas_call | solution.py:218
  250.2 1.6 collective-permute-done.87
  254.1 2.8 %collective-permute-done.90 = f32[2,96,128]{2,1,0:T(8,128)S(1)} collective-permute-done((f32[2,96,128]{2,1,0:T(8,128)S(1)}, f32[2,96,128]{2,1,0:T(8,128)S(1)}, u32[]{:S(2)}, u32[]{:S(2)}) %collective-permute-start.90) | collective-permute-done | bytes 98336 | tf_op jit(solution)/shard_map/ppermute | solution.py:27
  259.0 2.0 collective-permute-done.91
  262.2 2.0 collective-permute-start.92
  264.3 2.1 collective-permute-done.92
  266.4 4.3 %collective-permute-start.93 = (f32[1,48,128]{2,1,0:T(8,128)S(1)}, f32[1,48,128]{2,1,0:T(8,128)S(1)}, u32[]{:S(2)}, u32[]{:S(2)}) collective-permute-start(f32[1,48,128]{2,1,0:T(8,128)S(1)} %slice_bitcast_fusion.18), channel_id=1, source_target_pairs={{0,24},{8,16},{16,8},{24,0},{1,25},{9,17},{17,9},{25,1},{2,26},{10... | collective-permute-start | bytes 73736 | tf_op jit(solution)/shard_map/ppermute | solution.py:27
  (242 shorter events, 74.9 us)
Async XLA Ops:
  0.6 5.1 %collective-permute-start = (f32[1,48,128]{2,1,0:T(8,128)}, f32[1,48,128]{2,1,0:T(8,128)S(1)}, u32[]{:S(2)}, u32[]{:S(2)}) collective-permute-start(f32[1,48,128]{2,1,0:T(8,128)} %bitcast.236), channel_id=1, source_target_pairs={{0,8},{8,0},{16,24},{24,16},{1,9},{9,1},{17,25},{25,17},{2,10},{10... | collective-permute-start | bytes 73736 | tf_op jit(solution)/shard_map/ppermute | solution.py:27
  6.5 6.1 %collective-permute-start.1 = (f32[2,48,128]{2,1,0:T(8,128)S(1)}, f32[2,48,128]{2,1,0:T(8,128)S(1)}, u32[]{:S(2)}, u32[]{:S(2)}) collective-permute-start(f32[2,48,128]{2,1,0:T(8,128)S(1)} %get-tuple-element.219), channel_id=1, source_target_pairs={{0,24},{8,16},{16,8},{24,0},{1,25},{9,17},{17,9},{25,1},{2,26},{10... | collective-permute-start | bytes 147464 | tf_op jit(solution)/shard_map/ppermute | solution.py:27
  12.6 19.5 %collective-permute-start.4 = (f32[1,104,128]{2,1,0:T(8,128)S(1)}, f32[1,104,128]{2,1,0:T(8,128)S(1)}, u32[]{:S(2)}, u32[]{:S(2)}) collective-permute-start(f32[1,104,128]{2,1,0:T(8,128)S(1)} %get-tuple-element.216), channel_id=1, source_target_pairs={{0,4},{1,5},{2,6},{3,7},{4,0},{5,1},{6,2},{7,3},{8,12},{9,13},{10,... | collective-permute-start | bytes 159752 | tf_op jit(solution)/shard_map/ppermute | solution.py:27
  48.4 4.9 %collective-permute-start.25 = (f32[2,64,128]{2,1,0:T(8,128)S(1)}, f32[2,64,128]{2,1,0:T(8,128)S(1)}, u32[]{:S(2)}, u32[]{:S(2)}) collective-permute-start(f32[2,64,128]{2,1,0:T(8,128)S(1)} %get-tuple-element.130), channel_id=1, source_target_pairs={{0,2},{1,3},{2,0},{3,1},{4,6},{5,7},{6,4},{7,5},{8,10},{9,11},{10,... | collective-permute-start | bytes 196616 | tf_op jit(solution)/shard_map/ppermute | solution.py:27
  49.3 5.9 %collective-permute-start.26 = (f32[2,64,128]{2,1,0:T(8,128)S(1)}, f32[2,64,128]{2,1,0:T(8,128)S(1)}, u32[]{:S(2)}, u32[]{:S(2)}) collective-permute-start(f32[2,64,128]{2,1,0:T(8,128)S(1)} %get-tuple-element.131), channel_id=1, source_target_pairs={{0,3},{1,2},{2,1},{3,0},{4,7},{5,6},{6,5},{7,4},{8,11},{9,10},{10,... | collective-permute-start | bytes 196616 | tf_op jit(solution)/shard_map/ppermute | solution.py:27
  50.6 5.5 %collective-permute-start.27 = (f32[2,64,128]{2,1,0:T(8,128)S(1)}, f32[2,64,128]{2,1,0:T(8,128)S(1)}, u32[]{:S(2)}, u32[]{:S(2)}) collective-permute-start(f32[2,64,128]{2,1,0:T(8,128)S(1)} %get-tuple-element.132), channel_id=1, source_target_pairs={{0,4},{1,5},{2,6},{3,7},{4,0},{5,1},{6,2},{7,3},{8,12},{9,13},{10,... | collective-permute-start | bytes 196616 | tf_op jit(solution)/shard_map/ppermute | solution.py:27
  51.2 5.6 %collective-permute-start.28 = (f32[2,64,128]{2,1,0:T(8,128)S(1)}, f32[2,64,128]{2,1,0:T(8,128)S(1)}, u32[]{:S(2)}, u32[]{:S(2)}) collective-permute-start(f32[2,64,128]{2,1,0:T(8,128)S(1)} %get-tuple-element.133), channel_id=1, source_target_pairs={{0,5},{1,4},{2,7},{3,6},{4,1},{5,0},{6,3},{7,2},{8,13},{9,12},{10,... | collective-permute-start | bytes 196616 | tf_op jit(solution)/shard_map/ppermute | solution.py:27
  52.3 5.9 %collective-permute-start.29 = (f32[2,64,128]{2,1,0:T(8,128)S(1)}, f32[2,64,128]{2,1,0:T(8,128)S(1)}, u32[]{:S(2)}, u32[]{:S(2)}) collective-permute-start(f32[2,64,128]{2,1,0:T(8,128)S(1)} %get-tuple-element.134), channel_id=1, source_target_pairs={{0,6},{1,7},{2,4},{3,5},{4,2},{5,3},{6,0},{7,1},{8,14},{9,15},{10,... | collective-permute-start | bytes 196616 | tf_op jit(solution)/shard_map/ppermute | solution.py:27
  53.4 5.4 %collective-permute-start.30 = (f32[2,64,128]{2,1,0:T(8,128)S(1)}, f32[2,64,128]{2,1,0:T(8,128)S(1)}, u32[]{:S(2)}, u32[]{:S(2)}) collective-permute-start(f32[2,64,128]{2,1,0:T(8,128)S(1)} %get-tuple-element.135), channel_id=1, source_target_pairs={{0,7},{1,6},{2,5},{3,4},{4,3},{5,2},{6,1},{7,0},{8,15},{9,14},{10,... | collective-permute-start | bytes 196616 | tf_op jit(solution)/shard_map/ppermute | solution.py:27
  55.2 6.6 %collective-permute-start.9 = (f32[2,64,128]{2,1,0:T(8,128)S(1)}, f32[2,64,128]{2,1,0:T(8,128)S(1)}, u32[]{:S(2)}, u32[]{:S(2)}) collective-permute-start(f32[2,64,128]{2,1,0:T(8,128)S(1)} %get-tuple-element.113), channel_id=1, source_target_pairs={{0,3},{1,2},{2,1},{3,0},{4,7},{5,6},{6,5},{7,4},{8,11},{9,10},{10,... | collective-permute-start | bytes 196616 | tf_op jit(solution)/shard_map/ppermute | solution.py:27
  56.1 5.7 %collective-permute-start.10 = (f32[2,64,128]{2,1,0:T(8,128)S(1)}, f32[2,64,128]{2,1,0:T(8,128)S(1)}, u32[]{:S(2)}, u32[]{:S(2)}) collective-permute-start(f32[2,64,128]{2,1,0:T(8,128)S(1)} %get-tuple-element.114), channel_id=1, source_target_pairs={{0,4},{1,5},{2,6},{3,7},{4,0},{5,1},{6,2},{7,3},{8,12},{9,13},{10,... | collective-permute-start | bytes 196616 | tf_op jit(solution)/shard_map/ppermute | solution.py:27
  56.8 5.1 %collective-permute-start.11 = (f32[2,64,128]{2,1,0:T(8,128)S(1)}, f32[2,64,128]{2,1,0:T(8,128)S(1)}, u32[]{:S(2)}, u32[]{:S(2)}) collective-permute-start(f32[2,64,128]{2,1,0:T(8,128)S(1)} %get-tuple-element.115), channel_id=1, source_target_pairs={{0,5},{1,4},{2,7},{3,6},{4,1},{5,0},{6,3},{7,2},{8,13},{9,12},{10,... | collective-permute-start | bytes 196616 | tf_op jit(solution)/shard_map/ppermute | solution.py:27
  58.2 5.9 %collective-permute-start.12 = (f32[2,64,128]{2,1,0:T(8,128)S(1)}, f32[2,64,128]{2,1,0:T(8,128)S(1)}, u32[]{:S(2)}, u32[]{:S(2)}) collective-permute-start(f32[2,64,128]{2,1,0:T(8,128)S(1)} %get-tuple-element.116), channel_id=1, source_target_pairs={{0,6},{1,7},{2,4},{3,5},{4,2},{5,3},{6,0},{7,1},{8,14},{9,15},{10,... | collective-permute-start | bytes 196616 | tf_op jit(solution)/shard_map/ppermute | solution.py:27
  58.8 5.7 %collective-permute-start.13 = (f32[2,64,128]{2,1,0:T(8,128)S(1)}, f32[2,64,128]{2,1,0:T(8,128)S(1)}, u32[]{:S(2)}, u32[]{:S(2)}) collective-permute-start(f32[2,64,128]{2,1,0:T(8,128)S(1)} %get-tuple-element.117), channel_id=1, source_target_pairs={{0,7},{1,6},{2,5},{3,4},{4,3},{5,2},{6,1},{7,0},{8,15},{9,14},{10,... | collective-permute-start | bytes 196616 | tf_op jit(solution)/shard_map/ppermute | solution.py:27
  61.8 9.2 %collective-permute-start.31 = (f32[8,64,128]{2,1,0:T(8,128)S(1)}, f32[8,64,128]{2,1,0:T(8,128)S(1)}, u32[]{:S(2)}, u32[]{:S(2)}) collective-permute-start(f32[8,64,128]{2,1,0:T(8,128)S(1)} %get-tuple-element.137), channel_id=1, source_target_pairs={{0,8},{8,0},{16,24},{24,16},{1,9},{9,1},{17,25},{25,17},{2,10},{10... | collective-permute-start | bytes 786440 | tf_op jit(solution)/shard_map/ppermute | solution.py:27
  65.2 10.9 %collective-permute-start.14 = (f32[8,64,128]{2,1,0:T(8,128)S(1)}, f32[8,64,128]{2,1,0:T(8,128)S(1)}, u32[]{:S(2)}, u32[]{:S(2)}) collective-permute-start(f32[8,64,128]{2,1,0:T(8,128)S(1)} %get-tuple-element.119), channel_id=1, source_target_pairs={{0,8},{8,0},{16,24},{24,16},{1,9},{9,1},{17,25},{25,17},{2,10},{10... | collective-permute-start | bytes 786440 | tf_op jit(solution)/shard_map/ppermute | solution.py:27
  71.0 14.5 %collective-permute-start.32 = (f32[8,64,128]{2,1,0:T(8,128)S(1)}, f32[8,64,128]{2,1,0:T(8,128)S(1)}, u32[]{:S(2)}, u32[]{:S(2)}) collective-permute-start(f32[8,64,128]{2,1,0:T(8,128)S(1)} %add.116), channel_id=1, source_target_pairs={{0,24},{8,16},{16,8},{24,0},{1,25},{9,17},{17,9},{25,1},{2,26},{10... | collective-permute-start | bytes 786440 | tf_op jit(solution)/shard_map/ppermute | solution.py:27
  76.2 16.5 %collective-permute-start.15 = (f32[8,64,128]{2,1,0:T(8,128)S(1)}, f32[8,64,128]{2,1,0:T(8,128)S(1)}, u32[]{:S(2)}, u32[]{:S(2)}) collective-permute-start(f32[8,64,128]{2,1,0:T(8,128)S(1)} %add.114), channel_id=1, source_target_pairs={{0,24},{8,16},{16,8},{24,0},{1,25},{9,17},{17,9},{25,1},{2,26},{10... | collective-permute-start | bytes 786440 | tf_op jit(solution)/shard_map/ppermute | solution.py:27
  85.5 11.9 %collective-permute-start.33 = (f32[8,64,128]{2,1,0:T(8,128)S(1)}, f32[8,64,128]{2,1,0:T(8,128)S(1)}, u32[]{:S(2)}, u32[]{:S(2)}) collective-permute-start(f32[8,64,128]{2,1,0:T(8,128)S(1)} %add.117.mine), channel_id=1, source_target_pairs={{0,8},{8,0},{16,24},{24,16},{1,9},{9,1},{17,25},{25,17},{2,10},{10... | collective-permute-start | bytes 786440 | tf_op jit(solution)/shard_map/ppermute | solution.py:27
  92.7 10.5 %collective-permute-start.16 = (f32[8,64,128]{2,1,0:T(8,128)S(1)}, f32[8,64,128]{2,1,0:T(8,128)S(1)}, u32[]{:S(2)}, u32[]{:S(2)}) collective-permute-start(f32[8,64,128]{2,1,0:T(8,128)S(1)} %add.115.mine), channel_id=1, source_target_pairs={{0,8},{8,0},{16,24},{24,16},{1,9},{9,1},{17,25},{25,17},{2,10},{10... | collective-permute-start | bytes 786440 | tf_op jit(solution)/shard_map/ppermute | solution.py:27
  98.3 6.4 %collective-permute-start.34 = (f32[2,64,128]{2,1,0:T(8,128)S(1)}, f32[2,64,128]{2,1,0:T(8,128)S(1)}, u32[]{:S(2)}, u32[]{:S(2)}) collective-permute-start(f32[2,64,128]{2,1,0:T(8,128)S(1)} %get-tuple-element.139), channel_id=1, source_target_pairs={{0,1},{1,0},{2,3},{3,2},{4,5},{5,4},{6,7},{7,6},{8,9},{9,8},{10,11... | collective-permute-start | bytes 196616 | tf_op jit(solution)/shard_map/ppermute | solution.py:27
  98.4 6.4 %collective-permute-start.35 = (f32[2,64,128]{2,1,0:T(8,128)S(1)}, f32[2,64,128]{2,1,0:T(8,128)S(1)}, u32[]{:S(2)}, u32[]{:S(2)}) collective-permute-start(f32[2,64,128]{2,1,0:T(8,128)S(1)} %get-tuple-element.140), channel_id=1, source_target_pairs={{0,2},{1,3},{2,0},{3,1},{4,6},{5,7},{6,4},{7,5},{8,10},{9,11},{10,... | collective-permute-start | bytes 196616 | tf_op jit(solution)/shard_map/ppermute | solution.py:27
  99.2 8.5 %collective-permute-start.36 = (f32[2,64,128]{2,1,0:T(8,128)S(1)}, f32[2,64,128]{2,1,0:T(8,128)S(1)}, u32[]{:S(2)}, u32[]{:S(2)}) collective-permute-start(f32[2,64,128]{2,1,0:T(8,128)S(1)} %get-tuple-element.141), channel_id=1, source_target_pairs={{0,3},{1,2},{2,1},{3,0},{4,7},{5,6},{6,5},{7,4},{8,11},{9,10},{10,... | collective-permute-start | bytes 196616 | tf_op jit(solution)/shard_map/ppermute | solution.py:27
  100.2 7.6 %collective-permute-start.37 = (f32[2,64,128]{2,1,0:T(8,128)S(1)}, f32[2,64,128]{2,1,0:T(8,128)S(1)}, u32[]{:S(2)}, u32[]{:S(2)}) collective-permute-start(f32[2,64,128]{2,1,0:T(8,128)S(1)} %get-tuple-element.142), channel_id=1, source_target_pairs={{0,4},{1,5},{2,6},{3,7},{4,0},{5,1},{6,2},{7,3},{8,12},{9,13},{10,... | collective-permute-start | bytes 196616 | tf_op jit(solution)/shard_map/ppermute | solution.py:27
  104.7 5.9 %collective-permute-start.39 = (f32[2,64,128]{2,1,0:T(8,128)S(1)}, f32[2,64,128]{2,1,0:T(8,128)S(1)}, u32[]{:S(2)}, u32[]{:S(2)}) collective-permute-start(f32[2,64,128]{2,1,0:T(8,128)S(1)} %get-tuple-element.144), channel_id=1, source_target_pairs={{0,6},{1,7},{2,4},{3,5},{4,2},{5,3},{6,0},{7,1},{8,14},{9,15},{10,... | collective-permute-start | bytes 196616 | tf_op jit(solution)/shard_map/ppermute | solution.py:27
  104.8 6.7 %collective-permute-start.40 = (f32[2,64,128]{2,1,0:T(8,128)S(1)}, f32[2,64,128]{2,1,0:T(8,128)S(1)}, u32[]{:S(2)}, u32[]{:S(2)}) collective-permute-start(f32[2,64,128]{2,1,0:T(8,128)S(1)} %get-tuple-element.145), channel_id=1, source_target_pairs={{0,7},{1,6},{2,5},{3,4},{4,3},{5,2},{6,1},{7,0},{8,15},{9,14},{10,... | collective-permute-start | bytes 196616 | tf_op jit(solution)/shard_map/ppermute | solution.py:27
  107.8 5.9 %collective-permute-start.18 = (f32[2,64,128]{2,1,0:T(8,128)S(1)}, f32[2,64,128]{2,1,0:T(8,128)S(1)}, u32[]{:S(2)}, u32[]{:S(2)}) collective-permute-start(f32[2,64,128]{2,1,0:T(8,128)S(1)} %get-tuple-element.122), channel_id=1, source_target_pairs={{0,2},{1,3},{2,0},{3,1},{4,6},{5,7},{6,4},{7,5},{8,10},{9,11},{10,... | collective-permute-start | bytes 196616 | tf_op jit(solution)/shard_map/ppermute | solution.py:27
  107.8 7.2 %collective-permute-start.19 = (f32[2,64,128]{2,1,0:T(8,128)S(1)}, f32[2,64,128]{2,1,0:T(8,128)S(1)}, u32[]{:S(2)}, u32[]{:S(2)}) collective-permute-start(f32[2,64,128]{2,1,0:T(8,128)S(1)} %get-tuple-element.123), channel_id=1, source_target_pairs={{0,3},{1,2},{2,1},{3,0},{4,7},{5,6},{6,5},{7,4},{8,11},{9,10},{10,... | collective-permute-start | bytes 196616 | tf_op jit(solution)/shard_map/ppermute | solution.py:27
  112.2 5.6 %collective-permute-start.22 = (f32[2,64,128]{2,1,0:T(8,128)S(1)}, f32[2,64,128]{2,1,0:T(8,128)S(1)}, u32[]{:S(2)}, u32[]{:S(2)}) collective-permute-start(f32[2,64,128]{2,1,0:T(8,128)S(1)} %get-tuple-element.126), channel_id=1, source_target_pairs={{0,6},{1,7},{2,4},{3,5},{4,2},{5,3},{6,0},{7,1},{8,14},{9,15},{10,... | collective-permute-start | bytes 196616 | tf_op jit(solution)/shard_map/ppermute | solution.py:27
  113.7 5.3 %collective-permute-start.23 = (f32[2,64,128]{2,1,0:T(8,128)S(1)}, f32[2,64,128]{2,1,0:T(8,128)S(1)}, u32[]{:S(2)}, u32[]{:S(2)}) collective-permute-start(f32[2,64,128]{2,1,0:T(8,128)S(1)} %get-tuple-element.127), channel_id=1, source_target_pairs={{0,7},{1,6},{2,5},{3,4},{4,3},{5,2},{6,1},{7,0},{8,15},{9,14},{10,... | collective-permute-start | bytes 196616 | tf_op jit(solution)/shard_map/ppermute | solution.py:27
  133.7 4.9 %collective-permute-start.44 = (f32[2,96,128]{2,1,0:T(8,128)S(1)}, f32[2,96,128]{2,1,0:T(8,128)S(1)}, u32[]{:S(2)}, u32[]{:S(2)}) collective-permute-start(f32[2,96,128]{2,1,0:T(8,128)S(1)} %slice.221), channel_id=1, source_target_pairs={{0,4},{1,5},{2,6},{3,7},{4,0},{5,1},{6,2},{7,3},{8,12},{9,13},{10,... | collective-permute-start | bytes 294920 | tf_op jit(solution)/shard_map/ppermute | solution.py:27
  134.9 5.1 %collective-permute-start.42 = (f32[2,96,128]{2,1,0:T(8,128)S(1)}, f32[2,96,128]{2,1,0:T(8,128)S(1)}, u32[]{:S(2)}, u32[]{:S(2)}) collective-permute-start(f32[2,96,128]{2,1,0:T(8,128)S(1)} %slice_bitcast_fusion.4), channel_id=1, source_target_pairs={{0,2},{1,3},{2,0},{3,1},{4,6},{5,7},{6,4},{7,5},{8,10},{9,11},{10,... | collective-permute-start | bytes 294920 | tf_op jit(solution)/shard_map/ppermute | solution.py:27
  148.9 6.6 %collective-permute-start.47 = (f32[4,48,128]{2,1,0:T(8,128)S(1)}, f32[4,48,128]{2,1,0:T(8,128)S(1)}, u32[]{:S(2)}, u32[]{:S(2)}) collective-permute-start(f32[4,48,128]{2,1,0:T(8,128)S(1)} %bitcast_add_fusion.1), channel_id=1, source_target_pairs={{0,24},{8,16},{16,8},{24,0},{1,25},{9,17},{17,9},{25,1},{2,26},{10... | collective-permute-start | bytes 294920 | tf_op jit(solution)/shard_map/ppermute | solution.py:27
  156.2 4.9 %collective-permute-start.48 = (f32[1,96,128]{2,1,0:T(8,128)S(1)}, f32[1,96,128]{2,1,0:T(8,128)S(1)}, u32[]{:S(2)}, u32[]{:S(2)}) collective-permute-start(f32[1,96,128]{2,1,0:T(8,128)S(1)} %get-tuple-element.205), channel_id=1, source_target_pairs={{0,2},{1,3},{2,0},{3,1},{4,6},{5,7},{6,4},{7,5},{8,10},{9,11},{10,... | collective-permute-start | bytes 147464 | tf_op jit(solution)/shard_map/ppermute | solution.py:27
  174.1 4.9 %collective-permute-start.71 = (f32[2,64,128]{2,1,0:T(8,128)S(1)}, f32[2,64,128]{2,1,0:T(8,128)S(1)}, u32[]{:S(2)}, u32[]{:S(2)}) collective-permute-start(f32[2,64,128]{2,1,0:T(8,128)S(1)} %get-tuple-element.168), channel_id=1, source_target_pairs={{0,2},{1,3},{2,0},{3,1},{4,6},{5,7},{6,4},{7,5},{8,10},{9,11},{10,... | collective-permute-start | bytes 196616 | tf_op jit(solution)/shard_map/ppermute | solution.py:27
  175.0 6.1 %collective-permute-start.72 = (f32[2,64,128]{2,1,0:T(8,128)S(1)}, f32[2,64,128]{2,1,0:T(8,128)S(1)}, u32[]{:S(2)}, u32[]{:S(2)}) collective-permute-start(f32[2,64,128]{2,1,0:T(8,128)S(1)} %get-tuple-element.169), channel_id=1, source_target_pairs={{0,3},{1,2},{2,1},{3,0},{4,7},{5,6},{6,5},{7,4},{8,11},{9,10},{10,... | collective-permute-start | bytes 196616 | tf_op jit(solution)/shard_map/ppermute | solution.py:27
  175.9 5.6 %collective-permute-start.73 = (f32[2,64,128]{2,1,0:T(8,128)S(1)}, f32[2,64,128]{2,1,0:T(8,128)S(1)}, u32[]{:S(2)}, u32[]{:S(2)}) collective-permute-start(f32[2,64,128]{2,1,0:T(8,128)S(1)} %get-tuple-element.170), channel_id=1, source_target_pairs={{0,4},{1,5},{2,6},{3,7},{4,0},{5,1},{6,2},{7,3},{8,12},{9,13},{10,... | collective-permute-start | bytes 196616 | tf_op jit(solution)/shard_map/ppermute | solution.py:27
  177.3 5.0 %collective-permute-start.74 = (f32[2,64,128]{2,1,0:T(8,128)S(1)}, f32[2,64,128]{2,1,0:T(8,128)S(1)}, u32[]{:S(2)}, u32[]{:S(2)}) collective-permute-start(f32[2,64,128]{2,1,0:T(8,128)S(1)} %get-tuple-element.171), channel_id=1, source_target_pairs={{0,5},{1,4},{2,7},{3,6},{4,1},{5,0},{6,3},{7,2},{8,13},{9,12},{10,... | collective-permute-start | bytes 196616 | tf_op jit(solution)/shard_map/ppermute | solution.py:27
  177.6 5.6 %collective-permute-start.75 = (f32[2,64,128]{2,1,0:T(8,128)S(1)}, f32[2,64,128]{2,1,0:T(8,128)S(1)}, u32[]{:S(2)}, u32[]{:S(2)}) collective-permute-start(f32[2,64,128]{2,1,0:T(8,128)S(1)} %get-tuple-element.172), channel_id=1, source_target_pairs={{0,6},{1,7},{2,4},{3,5},{4,2},{5,3},{6,0},{7,1},{8,14},{9,15},{10,... | collective-permute-start | bytes 196616 | tf_op jit(solution)/shard_map/ppermute | solution.py:27
  179.1 5.6 %collective-permute-start.76 = (f32[2,64,128]{2,1,0:T(8,128)S(1)}, f32[2,64,128]{2,1,0:T(8,128)S(1)}, u32[]{:S(2)}, u32[]{:S(2)}) collective-permute-start(f32[2,64,128]{2,1,0:T(8,128)S(1)} %get-tuple-element.173), channel_id=1, source_target_pairs={{0,7},{1,6},{2,5},{3,4},{4,3},{5,2},{6,1},{7,0},{8,15},{9,14},{10,... | collective-permute-start | bytes 196616 | tf_op jit(solution)/shard_map/ppermute | solution.py:27
  181.1 6.1 %collective-permute-start.55 = (f32[2,64,128]{2,1,0:T(8,128)S(1)}, f32[2,64,128]{2,1,0:T(8,128)S(1)}, u32[]{:S(2)}, u32[]{:S(2)}) collective-permute-start(f32[2,64,128]{2,1,0:T(8,128)S(1)} %get-tuple-element.151), channel_id=1, source_target_pairs={{0,3},{1,2},{2,1},{3,0},{4,7},{5,6},{6,5},{7,4},{8,11},{9,10},{10,... | collective-permute-start | bytes 196616 | tf_op jit(solution)/shard_map/ppermute | solution.py:27
  181.5 6.7 %collective-permute-start.56 = (f32[2,64,128]{2,1,0:T(8,128)S(1)}, f32[2,64,128]{2,1,0:T(8,128)S(1)}, u32[]{:S(2)}, u32[]{:S(2)}) collective-permute-start(f32[2,64,128]{2,1,0:T(8,128)S(1)} %get-tuple-element.152), channel_id=1, source_target_pairs={{0,4},{1,5},{2,6},{3,7},{4,0},{5,1},{6,2},{7,3},{8,12},{9,13},{10,... | collective-permute-start | bytes 196616 | tf_op jit(solution)/shard_map/ppermute | solution.py:27
  182.3 7.1 %collective-permute-start.57 = (f32[2,64,128]{2,1,0:T(8,128)S(1)}, f32[2,64,128]{2,1,0:T(8,128)S(1)}, u32[]{:S(2)}, u32[]{:S(2)}) collective-permute-start(f32[2,64,128]{2,1,0:T(8,128)S(1)} %get-tuple-element.153), channel_id=1, source_target_pairs={{0,5},{1,4},{2,7},{3,6},{4,1},{5,0},{6,3},{7,2},{8,13},{9,12},{10,... | collective-permute-start | bytes 196616 | tf_op jit(solution)/shard_map/ppermute | solution.py:27
  183.3 6.1 %collective-permute-start.58 = (f32[2,64,128]{2,1,0:T(8,128)S(1)}, f32[2,64,128]{2,1,0:T(8,128)S(1)}, u32[]{:S(2)}, u32[]{:S(2)}) collective-permute-start(f32[2,64,128]{2,1,0:T(8,128)S(1)} %get-tuple-element.154), channel_id=1, source_target_pairs={{0,6},{1,7},{2,4},{3,5},{4,2},{5,3},{6,0},{7,1},{8,14},{9,15},{10,... | collective-permute-start | bytes 196616 | tf_op jit(solution)/shard_map/ppermute | solution.py:27
  187.2 9.2 %collective-permute-start.77 = (f32[8,64,128]{2,1,0:T(8,128)S(1)}, f32[8,64,128]{2,1,0:T(8,128)S(1)}, u32[]{:S(2)}, u32[]{:S(2)}) collective-permute-start(f32[8,64,128]{2,1,0:T(8,128)S(1)} %get-tuple-element.175), channel_id=1, source_target_pairs={{0,8},{8,0},{16,24},{24,16},{1,9},{9,1},{17,25},{25,17},{2,10},{10... | collective-permute-start | bytes 786440 | tf_op jit(solution)/shard_map/ppermute | solution.py:27
  190.2 10.8 %collective-permute-start.60 = (f32[8,64,128]{2,1,0:T(8,128)S(1)}, f32[8,64,128]{2,1,0:T(8,128)S(1)}, u32[]{:S(2)}, u32[]{:S(2)}) collective-permute-start(f32[8,64,128]{2,1,0:T(8,128)S(1)} %get-tuple-element.157), channel_id=1, source_target_pairs={{0,8},{8,0},{16,24},{24,16},{1,9},{9,1},{17,25},{25,17},{2,10},{10... | collective-permute-start | bytes 786440 | tf_op jit(solution)/shard_map/ppermute | solution.py:27
  196.5 13.0 %collective-permute-start.78 = (f32[8,64,128]{2,1,0:T(8,128)S(1)}, f32[8,64,128]{2,1,0:T(8,128)S(1)}, u32[]{:S(2)}, u32[]{:S(2)}) collective-permute-start(f32[8,64,128]{2,1,0:T(8,128)S(1)} %add.128), channel_id=1, source_target_pairs={{0,24},{8,16},{16,8},{24,0},{1,25},{9,17},{17,9},{25,1},{2,26},{10... | collective-permute-start | bytes 786440 | tf_op jit(solution)/shard_map/ppermute | solution.py:27
  201.0 16.0 %collective-permute-start.61 = (f32[8,64,128]{2,1,0:T(8,128)S(1)}, f32[8,64,128]{2,1,0:T(8,128)S(1)}, u32[]{:S(2)}, u32[]{:S(2)}) collective-permute-start(f32[8,64,128]{2,1,0:T(8,128)S(1)} %add.126), channel_id=1, source_target_pairs={{0,24},{8,16},{16,8},{24,0},{1,25},{9,17},{17,9},{25,1},{2,26},{10... | collective-permute-start | bytes 786440 | tf_op jit(solution)/shard_map/ppermute | solution.py:27
  209.5 12.0 %collective-permute-start.79 = (f32[8,64,128]{2,1,0:T(8,128)S(1)}, f32[8,64,128]{2,1,0:T(8,128)S(1)}, u32[]{:S(2)}, u32[]{:S(2)}) collective-permute-start(f32[8,64,128]{2,1,0:T(8,128)S(1)} %add.129.mine), channel_id=1, source_target_pairs={{0,8},{8,0},{16,24},{24,16},{1,9},{9,1},{17,25},{25,17},{2,10},{10... | collective-permute-start | bytes 786440 | tf_op jit(solution)/shard_map/ppermute | solution.py:27
  217.1 9.9 %collective-permute-start.62 = (f32[8,64,128]{2,1,0:T(8,128)S(1)}, f32[8,64,128]{2,1,0:T(8,128)S(1)}, u32[]{:S(2)}, u32[]{:S(2)}) collective-permute-start(f32[8,64,128]{2,1,0:T(8,128)S(1)} %add.127.mine), channel_id=1, source_target_pairs={{0,8},{8,0},{16,24},{24,16},{1,9},{9,1},{17,25},{25,17},{2,10},{10... | collective-permute-start | bytes 786440 | tf_op jit(solution)/shard_map/ppermute | solution.py:27
  222.2 5.5 %collective-permute-start.80 = (f32[2,64,128]{2,1,0:T(8,128)S(1)}, f32[2,64,128]{2,1,0:T(8,128)S(1)}, u32[]{:S(2)}, u32[]{:S(2)}) collective-permute-start(f32[2,64,128]{2,1,0:T(8,128)S(1)} %get-tuple-element.177), channel_id=1, source_target_pairs={{0,1},{1,0},{2,3},{3,2},{4,5},{5,4},{6,7},{7,6},{8,9},{9,8},{10,11... | collective-permute-start | bytes 196616 | tf_op jit(solution)/shard_map/ppermute | solution.py:27
  222.3 7.3 %collective-permute-start.81 = (f32[2,64,128]{2,1,0:T(8,128)S(1)}, f32[2,64,128]{2,1,0:T(8,128)S(1)}, u32[]{:S(2)}, u32[]{:S(2)}) collective-permute-start(f32[2,64,128]{2,1,0:T(8,128)S(1)} %get-tuple-element.178), channel_id=1, source_target_pairs={{0,2},{1,3},{2,0},{3,1},{4,6},{5,7},{6,4},{7,5},{8,10},{9,11},{10,... | collective-permute-start | bytes 196616 | tf_op jit(solution)/shard_map/ppermute | solution.py:27
  223.8 7.7 %collective-permute-start.82 = (f32[2,64,128]{2,1,0:T(8,128)S(1)}, f32[2,64,128]{2,1,0:T(8,128)S(1)}, u32[]{:S(2)}, u32[]{:S(2)}) collective-permute-start(f32[2,64,128]{2,1,0:T(8,128)S(1)} %get-tuple-element.179), channel_id=1, source_target_pairs={{0,3},{1,2},{2,1},{3,0},{4,7},{5,6},{6,5},{7,4},{8,11},{9,10},{10,... | collective-permute-start | bytes 196616 | tf_op jit(solution)/shard_map/ppermute | solution.py:27
  224.2 7.3 %collective-permute-start.83 = (f32[2,64,128]{2,1,0:T(8,128)S(1)}, f32[2,64,128]{2,1,0:T(8,128)S(1)}, u32[]{:S(2)}, u32[]{:S(2)}) collective-permute-start(f32[2,64,128]{2,1,0:T(8,128)S(1)} %get-tuple-element.180), channel_id=1, source_target_pairs={{0,4},{1,5},{2,6},{3,7},{4,0},{5,1},{6,2},{7,3},{8,12},{9,13},{10,... | collective-permute-start | bytes 196616 | tf_op jit(solution)/shard_map/ppermute | solution.py:27
  227.1 5.6 %collective-permute-start.84 = (f32[2,64,128]{2,1,0:T(8,128)S(1)}, f32[2,64,128]{2,1,0:T(8,128)S(1)}, u32[]{:S(2)}, u32[]{:S(2)}) collective-permute-start(f32[2,64,128]{2,1,0:T(8,128)S(1)} %get-tuple-element.181), channel_id=1, source_target_pairs={{0,5},{1,4},{2,7},{3,6},{4,1},{5,0},{6,3},{7,2},{8,13},{9,12},{10,... | collective-permute-start | bytes 196616 | tf_op jit(solution)/shard_map/ppermute | solution.py:27
  227.8 5.6 %collective-permute-start.85 = (f32[2,64,128]{2,1,0:T(8,128)S(1)}, f32[2,64,128]{2,1,0:T(8,128)S(1)}, u32[]{:S(2)}, u32[]{:S(2)}) collective-permute-start(f32[2,64,128]{2,1,0:T(8,128)S(1)} %get-tuple-element.182), channel_id=1, source_target_pairs={{0,6},{1,7},{2,4},{3,5},{4,2},{5,3},{6,0},{7,1},{8,14},{9,15},{10,... | collective-permute-start | bytes 196616 | tf_op jit(solution)/shard_map/ppermute | solution.py:27
  229.6 5.4 %collective-permute-start.86 = (f32[2,64,128]{2,1,0:T(8,128)S(1)}, f32[2,64,128]{2,1,0:T(8,128)S(1)}, u32[]{:S(2)}, u32[]{:S(2)}) collective-permute-start(f32[2,64,128]{2,1,0:T(8,128)S(1)} %get-tuple-element.183), channel_id=1, source_target_pairs={{0,7},{1,6},{2,5},{3,4},{4,3},{5,2},{6,1},{7,0},{8,15},{9,14},{10,... | collective-permute-start | bytes 196616 | tf_op jit(solution)/shard_map/ppermute | solution.py:27
  231.5 6.1 %collective-permute-start.64 = (f32[2,64,128]{2,1,0:T(8,128)S(1)}, f32[2,64,128]{2,1,0:T(8,128)S(1)}, u32[]{:S(2)}, u32[]{:S(2)}) collective-permute-start(f32[2,64,128]{2,1,0:T(8,128)S(1)} %get-tuple-element.160), channel_id=1, source_target_pairs={{0,2},{1,3},{2,0},{3,1},{4,6},{5,7},{6,4},{7,5},{8,10},{9,11},{10,... | collective-permute-start | bytes 196616 | tf_op jit(solution)/shard_map/ppermute | solution.py:27
  232.6 5.3 %collective-permute-start.65 = (f32[2,64,128]{2,1,0:T(8,128)S(1)}, f32[2,64,128]{2,1,0:T(8,128)S(1)}, u32[]{:S(2)}, u32[]{:S(2)}) collective-permute-start(f32[2,64,128]{2,1,0:T(8,128)S(1)} %get-tuple-element.161), channel_id=1, source_target_pairs={{0,3},{1,2},{2,1},{3,0},{4,7},{5,6},{6,5},{7,4},{8,11},{9,10},{10,... | collective-permute-start | bytes 196616 | tf_op jit(solution)/shard_map/ppermute | solution.py:27
  236.0 5.2 %collective-permute-start.68 = (f32[2,64,128]{2,1,0:T(8,128)S(1)}, f32[2,64,128]{2,1,0:T(8,128)S(1)}, u32[]{:S(2)}, u32[]{:S(2)}) collective-permute-start(f32[2,64,128]{2,1,0:T(8,128)S(1)} %get-tuple-element.164), channel_id=1, source_target_pairs={{0,6},{1,7},{2,4},{3,5},{4,2},{5,3},{6,0},{7,1},{8,14},{9,15},{10,... | collective-permute-start | bytes 196616 | tf_op jit(solution)/shard_map/ppermute | solution.py:27
  237.6 5.2 %collective-permute-start.69 = (f32[2,64,128]{2,1,0:T(8,128)S(1)}, f32[2,64,128]{2,1,0:T(8,128)S(1)}, u32[]{:S(2)}, u32[]{:S(2)}) collective-permute-start(f32[2,64,128]{2,1,0:T(8,128)S(1)} %get-tuple-element.165), channel_id=1, source_target_pairs={{0,7},{1,6},{2,5},{3,4},{4,3},{5,2},{6,1},{7,0},{8,15},{9,14},{10,... | collective-permute-start | bytes 196616 | tf_op jit(solution)/shard_map/ppermute | solution.py:27
  251.9 4.9 %collective-permute-start.90 = (f32[2,96,128]{2,1,0:T(8,128)S(1)}, f32[2,96,128]{2,1,0:T(8,128)S(1)}, u32[]{:S(2)}, u32[]{:S(2)}) collective-permute-start(f32[2,96,128]{2,1,0:T(8,128)S(1)} %slice.237), channel_id=1, source_target_pairs={{0,4},{1,5},{2,6},{3,7},{4,0},{5,1},{6,2},{7,3},{8,12},{9,13},{10,... | collective-permute-start | bytes 294920 | tf_op jit(solution)/shard_map/ppermute | solution.py:27
  253.0 5.0 %collective-permute-start.88 = (f32[2,96,128]{2,1,0:T(8,128)S(1)}, f32[2,96,128]{2,1,0:T(8,128)S(1)}, u32[]{:S(2)}, u32[]{:S(2)}) collective-permute-start(f32[2,96,128]{2,1,0:T(8,128)S(1)} %slice_bitcast_fusion.2), channel_id=1, source_target_pairs={{0,2},{1,3},{2,0},{3,1},{4,6},{5,7},{6,4},{7,5},{8,10},{9,11},{10,... | collective-permute-start | bytes 294920 | tf_op jit(solution)/shard_map/ppermute | solution.py:27
  266.4 6.1 %collective-permute-start.93 = (f32[1,48,128]{2,1,0:T(8,128)S(1)}, f32[1,48,128]{2,1,0:T(8,128)S(1)}, u32[]{:S(2)}, u32[]{:S(2)}) collective-permute-start(f32[1,48,128]{2,1,0:T(8,128)S(1)} %slice_bitcast_fusion.18), channel_id=1, source_target_pairs={{0,24},{8,16},{16,8},{24,0},{1,25},{9,17},{17,9},{25,1},{2,26},{10... | collective-permute-start | bytes 73736 | tf_op jit(solution)/shard_map/ppermute | solution.py:27
  (41 other events, 341.5 us)

commit v4 on v3

--- a/solution.py
+++ b/solution.py
@@ -16,10 +16,11 @@
 LABEL_ROWS = 16
 F32 = jnp.float32
 BF16 = jnp.bfloat16
-LARGE = 28 << 20
-SMALL = 8 << 20
+LARGE = 14 << 20
+SMALL = 4 << 20
 ROWS_AT_ONCE = 1024
 COLUMNS_AT_ONCE = 512
+FETCHES = 4
 
 
 def swap(x, axis, mask):
@@ -49,22 +50,25 @@
     count, height, width = own.shape[0], buffer.shape[1], matrix.shape[1]
     steps = matrix.shape[0] // height
 
+    depth = buffer.shape[0]
+
     def fetch(i):
         return pltpu.make_async_copy(
-            matrix.at[pl.ds(i * height, height)], buffer.at[i % 2], sems.at[i % 2]
+            matrix.at[pl.ds(i * height, height)], buffer.at[i % depth], sems.at[i % depth]
         )
 
     def fetch_tile(b):
         return pltpu.make_async_copy(tiles.at[tile_ref[b]], tile_buffer.at[b], tile_sems.at[b])
 
-    fetch(0).start()
+    for i in range(min(depth - 1, steps)):
+        fetch(i).start()
     for b in range(count):
         fetch_tile(b).start()
     for i in range(steps):
         fetch(i).wait()
-        if i + 1 < steps:
-            fetch(i + 1).start()
-        x = buffer[i % 2]
+        if i + depth - 1 < steps:
+            fetch(i + depth - 1).start()
+        x = buffer[i % depth]
         top = x.astype(BF16)
         big[i * height : (i + 1) * height, :] = top
         small[i * height : (i + 1) * height, :] = (x - top.astype(F32)).astype(BF16)
@@ -87,9 +91,9 @@
         out_specs=specs(3, pltpu.VMEM),
         out_shape=[terms, terms, jax.ShapeDtypeStruct((blocks, height, 2 * width), BF16)],
         scratch_shapes=[
-            pltpu.VMEM((2, step, matrix.shape[1]), F32),
+            pltpu.VMEM((FETCHES, step, matrix.shape[1]), F32),
             pltpu.VMEM((blocks, height, width), F32),
-            pltpu.SemaphoreType.DMA((2,)),
+            pltpu.SemaphoreType.DMA((FETCHES,)),
             pltpu.SemaphoreType.DMA((blocks,)),
         ],
         compiler_params=pltpu.CompilerParams(vmem_limit_bytes=LARGE),
@@ -112,38 +116,38 @@
                 )
 
 
+def warp_chunk(h, chunks, cores, source_ref, valid_ref, tiles, dose, outs):
+    height = tiles.shape[1]
+    part = height // chunks
+    for k, out in enumerate(outs):
+        for c in range(cores):
+            for j in range(CAP):
+                s = (k * cores + c) * CAP + j
+                b = source_ref[s]
+                block = dose[pl.ds(pl.multiple_of(b * height, height), height), :]
+                tile = tiles[b, h * part : (h + 1) * part, :]
+                left = jnp.concatenate([tile[:, :height], tile[:, height:]], axis=0)
+                full = jnp.dot(left, halves(block, 1), preferred_element_type=F32)
+                warped = term_sum(full, part, dose.shape[1])
+                out[c, j] = jnp.where(valid_ref[s] > 0, warped, 0.0)
+
+
 def forward_body(dims, source_ref, valid_ref, me_ref, big, small, tiles, *refs):
-    vox, masks, rows, pieces_n, chunks = dims
+    vox, masks, rows, pieces_n, chunks, cores = dims
     pieces, outs = refs[:pieces_n], refs[pieces_n:-2]
-    weights, dose = refs[-2:]
+    dose, weights = refs[-2:]
     plans = dose.shape[1]
-    height = tiles.shape[1]
     if len(pieces[0].shape) == 2:
         weights[...] = halves(pieces[0][...], 1)
     else:
         fill_weights(me_ref, weights, pieces, rows, vox, masks)
     step = min(ROWS_AT_ONCE, dose.shape[0])
-
-    def multiply(i, carry):
-        at = pl.ds(pl.multiple_of(i * step, step), step)
+    for first in range(0, dose.shape[0], step):
+        at = slice(first, first + step)
         top = jnp.dot(big[at, :], weights[...], preferred_element_type=F32)
         rest = jnp.dot(small[at, :], weights[:, :plans], preferred_element_type=F32)
         dose[at, :] = top[:, :plans] + (top[:, plans:] + rest)
-        return carry
-
-    lax.fori_loop(0, dose.shape[0] // step, multiply, 0)
-    part = height // chunks
-    for m in range(vox):
-        for j in range(CAP):
-            s = m * CAP + j
-            b = source_ref[s]
-            block = dose[pl.ds(pl.multiple_of(b * height, height), height), :]
-            tile = tiles[b]
-            left = jnp.concatenate([tile[:, :height], tile[:, height:]], axis=0)
-            full = jnp.dot(left, halves(block, 1), preferred_element_type=F32)
-            warped = jnp.where(valid_ref[s] > 0, term_sum(full, height, plans), 0.0)
-            for h in range(chunks):
-                outs[h * vox + m][j] = warped[h * part : (h + 1) * part]
+    warp_chunk(0, chunks, cores, source_ref, valid_ref, tiles, dose, outs)
 
 
 def forward(scalars, terms, pieces, rows, vox, masks):
@@ -151,13 +155,15 @@
     height = tiles.shape[1]
     vox_rows, spots = big.shape
     plans = pieces[0].shape[-1]
-    out = jax.ShapeDtypeStruct((CAP, height // CHUNKS, plans), F32)
+    cores = core_count()
+    out = jax.ShapeDtypeStruct((cores, CAP, height // CHUNKS, plans), F32)
+    outs = [out] * (vox // cores) + [jax.ShapeDtypeStruct((vox_rows, plans), F32)]
     return pl.pallas_call(
-        functools.partial(forward_body, (vox, masks, rows, len(pieces), CHUNKS)),
+        functools.partial(forward_body, (vox, masks, rows, len(pieces), CHUNKS, cores)),
         in_specs=specs(3, pltpu.SMEM) + specs(3 + len(pieces), pltpu.VMEM),
-        out_specs=specs(vox * CHUNKS, pltpu.VMEM),
-        out_shape=[out] * (vox * CHUNKS),
-        scratch_shapes=[pltpu.VMEM((spots, 2 * plans), BF16), pltpu.VMEM((vox_rows, plans), F32)],
+        out_specs=specs(len(outs), pltpu.VMEM),
+        out_shape=outs,
+        scratch_shapes=[pltpu.VMEM((spots, 2 * plans), BF16)],
         compiler_params=pltpu.CompilerParams(vmem_limit_bytes=LARGE),
         cost_estimate=pl.CostEstimate(
             flops=8 * big.size * plans, bytes_accessed=big.size * 4, transcendentals=0
@@ -166,30 +172,66 @@
     )(*scalars, *terms, *pieces)
 
 
+def later_body(h, chunks, cores, source_ref, valid_ref, tiles, dose, after, *outs):
+    warp_chunk(h, chunks, cores, source_ref, valid_ref, tiles, dose, outs)
+
+
+def forward_later(h, scalars, tiles, dose, after, vox):
+    height = tiles.shape[1]
+    cores = core_count()
+    out = jax.ShapeDtypeStruct((cores, CAP, height // CHUNKS, dose.shape[1]), F32)
+    return pl.pallas_call(
+        functools.partial(later_body, h, CHUNKS, cores),
+        in_specs=specs(2, pltpu.SMEM) + specs(2, pltpu.VMEM) + specs(1, pl.ANY),
+        out_specs=specs(vox // cores, pltpu.VMEM),
+        out_shape=[out] * (vox // cores),
+        compiler_params=pltpu.CompilerParams(vmem_limit_bytes=SMALL),
+        name="warp_later",
+    )(*scalars[:2], tiles, dose, after)
+
+
+def piece(arrived, across, cores, m):
+    k, c = m // cores, m % cores
+    return arrived[k].at[0] if c == 0 else across[(c - 1) * len(arrived) + k]
+
+
 def gradient_body(dims, source_ref, valid_ref, me_ref, big, small, tiles, *refs):
     vox, masks, rows, cores, chunks = dims
-    returned = refs[: vox * chunks]
-    outs = refs[vox * chunks : -2]
+    chips = vox // cores
+    each = chips * cores
+    returned = refs[: each * chunks]
+    outs = refs[each * chunks : -2]
     columns, turned = refs[-2:]
     height = tiles.shape[1]
     plans = turned.shape[1]
-    spots = big.shape[1]
+    vox_rows, spots = big.shape
+    spare = vox_rows // height
     for m in range(vox):
+        found = [
+            piece(
+                returned[h * each : h * each + chips],
+                returned[h * each + chips : (h + 1) * each],
+                cores,
+                m,
+            )
+            for h in range(chunks)
+        ]
         for j in range(CAP):
             s = m * CAP + j
-
-            @pl.when(valid_ref[s] > 0)
-            def _():
-                b = source_ref[s]
-                adjoint = jnp.concatenate([returned[h * vox + m][j] for h in range(chunks)], axis=0)
-                full = jnp.dot(halves(adjoint.T, 0), tiles[b], preferred_element_type=F32)
-                at = pl.ds(pl.multiple_of(b * height, height), height)
-                columns[:, at] = halves(term_sum(full, plans, height), 0)
+            b = source_ref[s]
+            adjoint = jnp.concatenate([f[j] for f in found], axis=0)
+            full = jnp.dot(halves(adjoint.T, 0), tiles[b], preferred_element_type=F32)
+            to = jnp.where(valid_ref[s] > 0, b, spare) * height
+            columns[:, pl.ds(pl.multiple_of(to, height), height)] = halves(
+                term_sum(full, plans, height), 0
+            )
 
     for first in range(0, spots, COLUMNS_AT_ONCE):
         last = min(first + COLUMNS_AT_ONCE, spots)
-        top = jnp.dot(columns[...], big[:, first:last], preferred_element_type=F32)
-        rest = jnp.dot(columns[:plans, :], small[:, first:last], preferred_element_type=F32)
+        top = jnp.dot(columns[:, :vox_rows], big[:, first:last], preferred_element_type=F32)
+        rest = jnp.dot(
+            columns[:plans, :vox_rows], small[:, first:last], preferred_element_type=F32
+        )
         total = top[:plans] + (top[plans:] + rest)
         for i in range(0, last - first, plans):
             turned[first + i : first + i + plans, :] = total[:, i : i + plans].T
@@ -220,7 +262,9 @@
         in_specs=specs(3, pltpu.SMEM) + specs(3 + len(returned), pltpu.VMEM),
         out_specs=specs(len(outs), pltpu.VMEM),
         out_shape=outs,
-        scratch_shapes=[pltpu.VMEM((2 * plans, vox_rows), BF16), pltpu.VMEM((spots, plans), F32)],
+        scratch_shapes=[pltpu.VMEM((2 * plans, vox_rows + tiles.shape[1]), BF16),
+            pltpu.VMEM((spots, plans), F32),
+        ],
         compiler_params=pltpu.CompilerParams(vmem_limit_bytes=LARGE),
         cost_estimate=pl.CostEstimate(
             flops=8 * big.size * plans, bytes_accessed=big.size * 4, transcendentals=0
@@ -229,16 +273,19 @@
     )(*scalars, *terms, *returned)
 
 
-def place_body(vox, which_ref, slot_ref, *refs):
-    incoming, (give, keep, total) = refs[:vox], refs[vox:]
+def place_body(vox, cores, which_ref, slot_ref, *refs):
+    chips = vox // cores
+    arrived, across = refs[:chips], refs[chips:vox]
+    give, keep, total = refs[vox:]
     total[...] = jnp.zeros_like(total)
     for m in range(vox):
+        blocks = piece(arrived, across, cores, m)
         for j in range(CAP):
             slot = slot_ref[m * CAP + j]
 
             @pl.when(slot >= 0)
             def _():
-                total[slot] += incoming[m][j]
+                total[slot] += blocks[j]
 
     half = keep.shape[0]
     which = which_ref[0]
@@ -248,14 +295,12 @@
 
 def place(which, slots, incoming, blocks):
     vox = len(incoming)
-    _, height, plans = incoming[0].shape
+    height, plans = incoming[0].shape[-2:]
     half = jax.ShapeDtypeStruct((blocks // 2, height, plans), F32)
-    smem = pl.BlockSpec(memory_space=pltpu.SMEM)
-    vmem = pl.BlockSpec(memory_space=pltpu.VMEM)
     return pl.pallas_call(
-        functools.partial(place_body, vox),
-        in_specs=[smem, smem] + [vmem] * vox,
-        out_specs=[vmem, vmem],
+        functools.partial(place_body, vox, core_count()),
+        in_specs=specs(2, pltpu.SMEM) + specs(vox, pltpu.VMEM),
+        out_specs=specs(2, pltpu.VMEM),
         out_shape=[half, half],
         scratch_shapes=[pltpu.VMEM((blocks, height, plans), F32)],
         compiler_params=pltpu.CompilerParams(vmem_limit_bytes=SMALL),
@@ -263,7 +308,7 @@
     )(which, slots, *incoming)
 
 
-def pull_body(vox, with_dose, which_ref, slot_ref, mine, other, goal, scale, *refs):
+def pull_body(vox, cores, with_dose, which_ref, slot_ref, mine, other, goal, scale, *refs):
     half = mine.shape[0]
     which = which_ref[0]
     field = refs[-1]
@@ -272,22 +317,21 @@
     for m in range(vox):
         for j in range(CAP):
             slot = jnp.maximum(slot_ref[m * CAP + j], 0)
-            refs[m][j] = scale[slot] * (field[slot] - goal[slot])
+            refs[m // cores][m % cores, j] = scale[slot] * (field[slot] - goal[slot])
     if with_dose:
-        refs[vox][...] = field[...]
+        refs[vox // cores][...] = field[...]
 
 
 def pull(which, slots, mine, other, goal, scale, vox, with_dose):
     half, height, plans = mine.shape
-    smem = pl.BlockSpec(memory_space=pltpu.SMEM)
-    vmem = pl.BlockSpec(memory_space=pltpu.VMEM)
-    outs = [jax.ShapeDtypeStruct((CAP, height, plans), F32)] * vox
+    cores = core_count()
+    outs = [jax.ShapeDtypeStruct((cores, CAP, height, plans), F32)] * (vox // cores)
     if with_dose:
         outs = outs + [jax.ShapeDtypeStruct((2 * half, height, plans), F32)]
     return pl.pallas_call(
-        functools.partial(pull_body, vox, with_dose),
-        in_specs=[smem, smem] + [vmem] * 4,
-        out_specs=[vmem] * len(outs),
+        functools.partial(pull_body, vox, cores, with_dose),
+        in_specs=specs(2, pltpu.SMEM) + specs(4, pltpu.VMEM),
+        out_specs=specs(len(outs), pltpu.VMEM),
         out_shape=outs,
         scratch_shapes=[pltpu.VMEM((2 * half, height, plans), F32)],
         compiler_params=pltpu.CompilerParams(vmem_limit_bytes=SMALL),
@@ -302,14 +346,6 @@
     return steps
 
 
-def chip_steps():
-    count, steps, mask = lax.axis_size(VOX), [], core_count()
-    while mask < count:
-        steps.append(mask)
-        mask *= 2
-    return steps
-
-
 def combined(steps):
     masks = [0]
     for s in steps:
@@ -317,22 +353,6 @@
     return masks
 
 
-def gather_along(x, axis, steps, backwards=False):
-    out = x[None]
-    for s in reversed(steps) if backwards else steps:
-        other = swap(out, axis, s)
-        out = jnp.stack([out, other], axis=1 if backwards else 0).reshape(-1, *x.shape)
-    return out
-
-
-def sum_along(x, axis, steps, backwards=False):
-    for s in reversed(steps) if backwards else steps:
-        pairs = x.reshape(2, -1, *x.shape[1:]) if backwards else x.reshape(-1, 2, *x.shape[1:])
-        keep, give = (pairs[0], pairs[1]) if backwards else (pairs[:, 0], pairs[:, 1])
-        x = keep + swap(give, axis, s)
-    return x
-
-
 def sum_everywhere(x, axis, steps):
     for i, s in enumerate(steps):
         other = swap(x, axis, s).reshape(-1, 2, 2**i, *x.shape[1:])
@@ -341,29 +361,26 @@
 
 
 def gather_chips(by_phase):
-    half = by_phase.shape[0] // 2
-    by_chip = jnp.concatenate(
-        [
-            gather_along(by_phase[:half], VOX, chip_steps()),
-            gather_along(by_phase[half:], VOX, chip_steps(), True),
-        ],
-        axis=1,
-    )
-    return spread(by_chip, VOX, range(1, core_count()))
+    cores = core_count()
+    by_chip = jnp.stack(spread(by_phase, VOX, range(cores, lax.axis_size(VOX), cores)))
+    return spread(by_chip, VOX, range(1, cores))
 
 
 def sum_chips(parts):
+    cores = len(parts)
     chips = parts[0]
-    for m in range(1, len(parts)):
+    for m in range(1, cores):
         chips = chips + swap(parts[m], VOX, m)
-    half = chips.shape[1] // 2
-    first = sum_along(chips[:, :half], VOX, chip_steps())
-    second = sum_along(chips[:, half:], VOX, chip_steps(), True)
-    return jnp.concatenate([first[0], second[0]], axis=0)
+    mine = chips[0]
+    for k in range(1, chips.shape[0]):
+        mine = mine + swap(chips[k], VOX, k * cores)
+    return mine
 
 
 def exchange(pieces):
-    return [pieces[0]] + [swap(pieces[m], VOX, m) for m in range(1, len(pieces))]
+    cores = core_count()
+    arrived = [pieces[0]] + [swap(pieces[k], VOX, k * cores) for k in range(1, len(pieces))]
+    return arrived + [swap(a[c], VOX, c) for c in range(1, cores) for a in arrived]
 
 
 def phase_halves(give, keep):
@@ -435,7 +452,7 @@
 
     masks = combined(phase_steps())
     terms = split_terms(tile_index[0], matrix, warp_tiles, local_blocks)
-    held = gather_along(weights, PHASE, phase_steps()).reshape(-1, plans)
+    held = jnp.concatenate(spread(weights, PHASE, masks[1:]), axis=0)
     for iteration in range(ITERS):
         last = iteration == ITERS - 1
         if iteration == 0:
@@ -455,15 +472,16 @@
             back_to = jnp.asarray([masks.index(p) for p in range(phases)], jnp.int32)
             every = every[jnp.arange(vox) ^ me_vox][:, back_to[jnp.arange(phases) ^ me_phase]]
             pieces = [every.transpose(1, 0, 2, 3).reshape(spots, plans)]
-        outgoing = forward(scalars, terms, pieces, rows, vox, masks)
+        *outgoing, block_dose = forward(scalars, terms, pieces, rows, vox, masks)
         returned, dose = [], []
-        incoming = [exchange(outgoing[h * vox : (h + 1) * vox]) for h in range(CHUNKS)]
         for h in range(CHUNKS):
-            give, keep = place(which, received, incoming[h], local_blocks)
+            if h > 0:
+                outgoing = forward_later(h, scalars, terms[2], block_dose, give, vox)
+            give, keep = place(which, received, exchange(outgoing), local_blocks)
             mine, other = phase_halves(give, keep)
             back = pull(which, received, mine, other, goals[h], scales[h], vox, last)
-            returned += exchange(back[:vox])
-            dose += back[vox:]
+            returned += exchange(back[: vox // cores])
+            dose += back[vox // cores :]
         parts = gradient_parts(scalars, terms, returned, rows, vox, masks)
         if rows % 8:
             parts = parts[0].reshape(phases, vox, rows, plans)
@@ -473,7 +491,10 @@
             parts = [parts[:, c] for c in range(cores)]
         total = sum_chips(parts)
         if last:
-            total = sum_along(total.reshape(phases, rows, plans), PHASE, phase_steps())[0]
+            split = total.reshape(phases, rows, plans)
+            total = split[0]
+            for i, m in enumerate(masks[1:], 1):
+                total = total + swap(split[i], PHASE, m)
             new_weights = jnp.maximum(held[:rows] - step_size[None, :] * total, 0.0)
         else:
             total = sum_everywhere(total.reshape(phases, rows, plans), PHASE, phase_steps())

time: 274 us -> 274 us (level)
  starting transfers between devices: 125 us -> 93.7 us
  waiting for transfers between devices: 86.9 us -> 118 us
  Pallas kernels: 42.5 us -> 31.1 us
  local copies, waits for them, and re-layouts: 10.6 us -> 19.6 us
    ppermute x94 -> x92, waiting for transfers between devices: 86.9 us -> 118 us  [swap(): return lax.ppermute(x, axis, [(i, i ^ mask) for i in range(count)])]
    ppermute x94 -> x92, starting transfers between devices: 125 us -> 93.7 us  [swap(): return lax.ppermute(x, axis, [(i, i ^ mask) for i in range(count)])]
    pallas_call x1, Pallas kernels: 12.4 us -> 4.88 us  [split_terms(): pl.pallas_call(split_body, in_specs=specs(1, pltpu.SMEM) + specs(2, pltpu...]
    pallas_call x2, Pallas kernels: 14.6 us -> 8.13 us  [gradient_parts(): pl.pallas_call(functools.partial(gradient_body, (vox, masks, rows, cores,...]
    unnamed x22 -> x60, local copies, waits for them, and re-layouts: 8.44 us -> 12.6 us
    pallas_call x8 -> x10, Pallas kernels: 5.74 us -> 9.15 us  [the longest x4 4.51 us: place(): pl.pallas_call(functools.partial(place_body, vox, core_count()), in_specs...]
  transfers between devices with their start and end apart: 94 -> 92, of which waited for: 48 -> 58; matrix products, arithmetic and copies ran while one was open for 3% -> 6% of each run, Pallas kernels for 7% -> 4%
where the time goes in v4:
time: 274 us; the launch traced here: 273 us
  waiting for transfers between devices  118 us (43%)
  starting transfers between devices  93.7 us (34%)
  Pallas kernels  31.1 us (11%)
  local copies, waits for them, and re-layouts  19.6 us (7%)
  other arithmetic  5.21 us (2%)
  matrix products  3.67 us (1%)
    ppermute x92, waiting for transfers between devices, swap(): return lax.ppermute(x, axis, [(i, i ^ mask) for i in range(count)])  118 us
    ppermute x92, starting transfers between devices, swap(): return lax.ppermute(x, axis, [(i, i ^ mask) for i in range(count)])  93.7 us
    unnamed x60, local copies, waits for them, and re-layouts  12.6 us
    pallas_call x2, Pallas kernels, forward(): pl.pallas_call(functools.partial(forward_body, (vox, masks, rows, len(pie...  8.97 us
    pallas_call x2, Pallas kernels, gradient_parts(): pl.pallas_call(functools.partial(gradient_body, (vox, masks, rows, cores,...  8.13 us
  transfers between devices with their start and end apart: 92, of which 58 were waited for; matrix products, arithmetic and copies ran while one was open for 6% of the time, Pallas kernels for 4%

profile of v4, /device:TPU:0, one launch (start us, length us, event | category | flops | bytes accessed | tf_op | source)
XLA Modules:
  0.0 273.1 jit_solution(5478618535761292357)
XLA Ops:
  0.6 3.1 %collective-permute-start = (f32[48,128]{1,0:T(8,128)}, f32[48,128]{1,0:T(8,128)S(1)}, u32[]{:S(2)}, u32[]{:S(2)}) collective-permute-start(f32[48,128]{1,0:T(8,128)} %param.15), channel_id=1, source_target_pairs={{0,8},{8,0},{16,24},{24,16},{1,9},{9,1},{17,25},{25,17},{2,10},{10... | collective-permute-start | bytes 73736 | tf_op jit(solution)/shard_map/ppermute | solution.py:28
  3.7 2.5 collective-permute-start.1
  11.4 2.5 collective-permute-start.5
  15.9 4.6 %copy-done.6 = f32[1,2048,1536]{2,1,0:T(8,128)S(1)} copy-done((f32[1,2048,1536]{2,1,0:T(8,128)S(1)}, f32[1,2048,1536]{2,1,0:T(8,128)}, u32[]{:S(2)}) %copy-start.6) | copy-done | bytes 12582936
  20.5 2.2 copy-done.7
  23.3 4.9 %split_terms.1 = (bf16[2048,1536]{1,0:T(8,128)(2,1)S(1)}, bf16[2048,1536]{1,0:T(8,128)(2,1)S(1)}, bf16[16,128,256]{2,1,0:T(8,128)(2,1)S(1)}) custom-call(s32[16]{0:T(128)S(1)} %bitcast.161, f32[2048,1536]{1,0:T(8,128)S(1)} %bitcast.157, f32[64,128,128]{2,1,0:T(8,128)S(1)} %copy-done.7), custom_call_target="tpu_custom_call" | custom-call | flops 3145728 | bytes 12582912 | tf_op jit(solution)/shard_map/split_terms/pallas_call | solution.py:88
  28.6 1.6 collective-permute-done.6.refs_1_
  30.6 4.5 %dose_and_warp.2 = (f32[2,2,64,128]{3,2,1,0:T(8,128)S(1)}, f32[2,2,64,128]{3,2,1,0:T(8,128)S(1)}, f32[2,2,64,128]{3,2,1,0:T(8,128)S(1)}, f32[2,2,64,128]{3,2,1,0:T(8,128)S(1)}, f32[2048,128]{1,0:T(8,128)S(1)}) custom-call(s32[16]{0:T(128)S(1)} %get-tuple-element.129.source_ref, s32[16]{0:T(128)S(1)} %get-tuple-element.128.valid_ref, ...), custom_call_target="tpu_custom_call" | custom-call | flops 3221225472 | bytes 12582912 | tf_op jit(solution)/shard_map/dose_and_warp/pallas_call | solution.py:161
  35.2 1.6 collective-permute-start.7
  38.9 2.2 collective-permute-done.7.refs_1_
  41.1 3.7 %collective-permute-done.8.refs_2_ = f32[2,2,64,128]{3,2,1,0:T(8,128)S(1)} collective-permute-done((f32[2,2,64,128]{3,2,1,0:T(8,128)S(1)}, f32[2,2,64,128]{3,2,1,0:T(8,128)S(1)}, u32[]{:S(2)}, u32[]{:S(2)}) %collective-permute-start.8) | collective-permute-done | bytes 131104 | tf_op jit(solution)/shard_map/ppermute | solution.py:28
  53.4 2.2 collective-permute-done.24.refs_1_
  59.2 2.0 fusion
  61.2 1.5 broadcast_in_dim.59
  65.0 1.6 collective-permute-start.31
  69.7 1.6 fusion.1
  71.4 2.4 collective-permute-done.31
  74.9 5.6 %collective-permute-done.15 = f32[8,64,128]{2,1,0:T(8,128)S(1)} collective-permute-done((f32[8,64,128]{2,1,0:T(8,128)S(1)}, f32[8,64,128]{2,1,0:T(8,128)S(1)}, u32[]{:S(2)}, u32[]{:S(2)}) %collective-permute-start.15) | collective-permute-done | bytes 262176 | tf_op jit(solution)/shard_map/ppermute | solution.py:28
  80.6 8.1 %collective-permute-start.16 = (f32[8,64,128]{2,1,0:T(8,128)S(1)}, f32[8,64,128]{2,1,0:T(8,128)S(1)}, u32[]{:S(2)}, u32[]{:S(2)}) collective-permute-start(f32[8,64,128]{2,1,0:T(8,128)S(1)} %add.112.mine), channel_id=1, source_target_pairs={{0,8},{8,0},{16,24},{24,16},{1,9},{9,1},{17,25},{25,17},{2,10},{10... | collective-permute-start | bytes 786440 | tf_op jit(solution)/shard_map/ppermute | solution.py:28
  88.9 4.7 %collective-permute-start.33 = (f32[8,64,128]{2,1,0:T(8,128)S(1)}, f32[8,64,128]{2,1,0:T(8,128)S(1)}, u32[]{:S(2)}, u32[]{:S(2)}) collective-permute-start(f32[8,64,128]{2,1,0:T(8,128)S(1)} %add.114.mine), channel_id=1, source_target_pairs={{0,8},{8,0},{16,24},{24,16},{1,9},{9,1},{17,25},{25,17},{2,10},{10... | collective-permute-start | bytes 786440 | tf_op jit(solution)/shard_map/ppermute | solution.py:28
  96.2 1.5 collective-permute-start.18
  98.3 2.6 collective-permute-done.17.refs_1_
  105.1 5.4 %collective-permute-done.34.refs_9_ = f32[2,2,64,128]{3,2,1,0:T(8,128)S(1)} collective-permute-done((f32[2,2,64,128]{3,2,1,0:T(8,128)S(1)}, f32[2,2,64,128]{3,2,1,0:T(8,128)S(1)}, u32[]{:S(2)}, u32[]{:S(2)}) %collective-permute-start.34) | collective-permute-done | bytes 131104 | tf_op jit(solution)/shard_map/ppermute | solution.py:28
  111.4 4.2 %collective-permute-done.35.refs_10_ = f32[2,2,64,128]{3,2,1,0:T(8,128)S(1)} collective-permute-done((f32[2,2,64,128]{3,2,1,0:T(8,128)S(1)}, f32[2,2,64,128]{3,2,1,0:T(8,128)S(1)}, u32[]{:S(2)}, u32[]{:S(2)}) %collective-permute-start.35) | collective-permute-done | bytes 131104 | tf_op jit(solution)/shard_map/ppermute | solution.py:28
  116.6 4.9 %collective-permute-done.36.refs_11_ = f32[2,2,64,128]{3,2,1,0:T(8,128)S(1)} collective-permute-done((f32[2,2,64,128]{3,2,1,0:T(8,128)S(1)}, f32[2,2,64,128]{3,2,1,0:T(8,128)S(1)}, u32[]{:S(2)}, u32[]{:S(2)}) %collective-permute-start.36) | collective-permute-done | bytes 131104 | tf_op jit(solution)/shard_map/ppermute | solution.py:28
  123.5 2.8 %copy-done.4 = bf16[2048,1536]{1,0:T(8,128)(2,1)S(1)} copy-done((bf16[2048,1536]{1,0:T(8,128)(2,1)S(1)}, bf16[2048,1536]{1,0:T(8,128)(2,1)}, u32[]{:S(2)}) %copy-start.4) | copy-done | bytes 6291480
  127.0 4.1 %warp_back_and_gradient.2 = (f32[4,192,128]{2,1,0:T(8,128)S(1)}, f32[4,192,128]{2,1,0:T(8,128)S(1)}) custom-call(s32[16]{0:T(128)S(1)} %get-tuple-element.129.source_ref, s32[16]{0:T(128)S(1)} %get-tuple-element.128.valid_ref, s32[2]{0:T(128)S(1)} %copy-done.12, bf16[2048,1536]{1,0:T(8,128)(2,1)S(1)} %bitcast.154, bf16[2048,1536]{1,0:T(8,128)(2,1)S(1)} %copy-done.4, ...), custom_call_target="tpu_custom_call" | custom-call | flops 3221225472 | bytes 12582912 | tf_op jit(solution)/shard_map/warp_back_and_gradient/pallas_call | solution.py:260
  134.5 2.0 collective-permute-start.44
  136.4 2.1 collective-permute-done.42
  138.8 1.6 collective-permute-done.44
  140.4 2.4 collective-permute-start.45
  142.8 2.6 collective-permute-done.45
  145.4 1.6 collective-permute-start.46
  147.0 5.0 %collective-permute-done.46 = f32[4,48,128]{2,1,0:T(8,128)S(1)} collective-permute-done((f32[4,48,128]{2,1,0:T(8,128)S(1)}, f32[4,48,128]{2,1,0:T(8,128)S(1)}, u32[]{:S(2)}, u32[]{:S(2)}) %collective-permute-start.46) | collective-permute-done | bytes 98336 | tf_op jit(solution)/shard_map/ppermute | solution.py:28
  152.1 1.9 collective-permute-start.47
  156.8 1.8 collective-permute-done.48
  160.0 1.7 collective-permute-done.50.refs_1_
  161.7 4.5 %dose_and_warp.3 = (f32[2,2,64,128]{3,2,1,0:T(8,128)S(1)}, f32[2,2,64,128]{3,2,1,0:T(8,128)S(1)}, f32[2,2,64,128]{3,2,1,0:T(8,128)S(1)}, f32[2,2,64,128]{3,2,1,0:T(8,128)S(1)}, f32[2048,128]{1,0:T(8,128)S(1)}) custom-call(s32[16]{0:T(128)S(1)} %get-tuple-element.129.source_ref, s32[16]{0:T(128)S(1)} %get-tuple-element.128.valid_ref, s32[2]{0:T(128)S(1)} %copy-done.12, ...), custom_call_target="tpu_custom_call" | custom-call | flops 3221225472 | bytes 12582912 | tf_op jit(solution)/shard_map/dose_and_warp/pallas_call | solution.py:161
  168.2 1.6 collective-permute-start.53
  169.8 2.8 %collective-permute-done.51.refs_1_ = f32[2,2,64,128]{3,2,1,0:T(8,128)S(1)} collective-permute-done((f32[2,2,64,128]{3,2,1,0:T(8,128)S(1)}, f32[2,2,64,128]{3,2,1,0:T(8,128)S(1)}, u32[]{:S(2)}, u32[]{:S(2)}) %collective-permute-start.51) | collective-permute-done | bytes 131104 | tf_op jit(solution)/shard_map/ppermute | solution.py:28
  173.9 1.8 collective-permute-done.53.refs_3_
  177.8 1.6 collective-permute-start.58
  181.2 1.7 collective-permute-start.69
  183.9 2.7 collective-permute-done.68.refs_1_
  186.6 2.6 collective-permute-done.69.refs_2_
  192.3 1.7 collective-permute-start.59
  194.0 6.7 %collective-permute-done.75 = f32[8,64,128]{2,1,0:T(8,128)S(1)} collective-permute-done((f32[8,64,128]{2,1,0:T(8,128)S(1)}, f32[8,64,128]{2,1,0:T(8,128)S(1)}, u32[]{:S(2)}, u32[]{:S(2)}) %collective-permute-start.75) | collective-permute-done | bytes 262176 | tf_op jit(solution)/shard_map/ppermute | solution.py:28
  201.3 5.4 %collective-permute-done.59 = f32[8,64,128]{2,1,0:T(8,128)S(1)} collective-permute-done((f32[8,64,128]{2,1,0:T(8,128)S(1)}, f32[8,64,128]{2,1,0:T(8,128)S(1)}, u32[]{:S(2)}, u32[]{:S(2)}) %collective-permute-start.59) | collective-permute-done | bytes 262176 | tf_op jit(solution)/shard_map/ppermute | solution.py:28
  206.7 7.6 %collective-permute-start.60 = (f32[8,64,128]{2,1,0:T(8,128)S(1)}, f32[8,64,128]{2,1,0:T(8,128)S(1)}, u32[]{:S(2)}, u32[]{:S(2)}) collective-permute-start(f32[8,64,128]{2,1,0:T(8,128)S(1)} %add.123.mine), channel_id=1, source_target_pairs={{0,8},{8,0},{16,24},{24,16},{1,9},{9,1},{17,25},{25,17},{2,10},{10... | collective-permute-start | bytes 786440 | tf_op jit(solution)/shard_map/ppermute | solution.py:28
  214.4 4.7 %collective-permute-start.77 = (f32[8,64,128]{2,1,0:T(8,128)S(1)}, f32[8,64,128]{2,1,0:T(8,128)S(1)}, u32[]{:S(2)}, u32[]{:S(2)}) collective-permute-start(f32[8,64,128]{2,1,0:T(8,128)S(1)} %add.125.mine), channel_id=1, source_target_pairs={{0,8},{8,0},{16,24},{24,16},{1,9},{9,1},{17,25},{25,17},{2,10},{10... | collective-permute-start | bytes 786440 | tf_op jit(solution)/shard_map/ppermute | solution.py:28
  220.9 3.1 %collective-permute-start.62 = (f32[2,2,64,128]{3,2,1,0:T(8,128)S(1)}, f32[2,2,64,128]{3,2,1,0:T(8,128)S(1)}, u32[]{:S(2)}, u32[]{:S(2)}) collective-permute-start(f32[2,2,64,128]{3,2,1,0:T(8,128)S(1)} %get-tuple-element.111), channel_id=1, source_target_pairs={{0,4},{1,5},{2,6},{3,7},{4,0},{5,1},{6,2},{7,3},{8,12},{9,13},{10,... | collective-permute-start | bytes 393224 | tf_op jit(solution)/shard_map/ppermute | solution.py:28
  224.4 1.6 collective-permute-done.61.refs_1_
  225.9 2.0 collective-permute-done.62.refs_2_
  227.9 1.9 collective-permute-done.63.refs_3_
  231.6 5.0 %collective-permute-done.78.refs_9_ = f32[2,2,64,128]{3,2,1,0:T(8,128)S(1)} collective-permute-done((f32[2,2,64,128]{3,2,1,0:T(8,128)S(1)}, f32[2,2,64,128]{3,2,1,0:T(8,128)S(1)}, u32[]{:S(2)}, u32[]{:S(2)}) %collective-permute-start.78) | collective-permute-done | bytes 131104 | tf_op jit(solution)/shard_map/ppermute | solution.py:28
  237.2 4.5 %collective-permute-done.79.refs_10_ = f32[2,2,64,128]{3,2,1,0:T(8,128)S(1)} collective-permute-done((f32[2,2,64,128]{3,2,1,0:T(8,128)S(1)}, f32[2,2,64,128]{3,2,1,0:T(8,128)S(1)}, u32[]{:S(2)}, u32[]{:S(2)}) %collective-permute-start.79) | collective-permute-done | bytes 131104 | tf_op jit(solution)/shard_map/ppermute | solution.py:28
  242.5 5.1 %collective-permute-done.80.refs_11_ = f32[2,2,64,128]{3,2,1,0:T(8,128)S(1)} collective-permute-done((f32[2,2,64,128]{3,2,1,0:T(8,128)S(1)}, f32[2,2,64,128]{3,2,1,0:T(8,128)S(1)}, u32[]{:S(2)}, u32[]{:S(2)}) %collective-permute-start.80) | collective-permute-done | bytes 131104 | tf_op jit(solution)/shard_map/ppermute | solution.py:28
  249.6 4.1 %warp_back_and_gradient.3 = (f32[4,192,128]{2,1,0:T(8,128)S(1)}, f32[4,192,128]{2,1,0:T(8,128)S(1)}) custom-call(s32[16]{0:T(128)S(1)} %get-tuple-element.129.source_ref, s32[16]{0:T(128)S(1)} %get-tuple-element.128.valid_ref, s32[2]{0:T(128)S(1)} %copy-done.13, bf16[2048,1536]{1,0:T(8,128)(2,1)S(1)} %bitcast.156, bf16[2048,1536]{1,0:T(8,128)(2,1)S(1)} %copy-done.5, ...), custom_call_target="tpu_custom_call" | custom-call | flops 3221225472 | bytes 12582912 | tf_op jit(solution)/shard_map/warp_back_and_gradient/pallas_call | solution.py:260
  257.0 2.1 collective-permute-start.88
  259.1 1.8 collective-permute-done.86
  260.9 2.4 collective-permute-done.87
  263.4 2.0 collective-permute-start.89
  265.4 2.3 collective-permute-start.90
  268.9 2.2 collective-permute-done.90
  (281 shorter events, 74.9 us)
Async XLA Ops:
  0.6 7.9 %collective-permute-start = (f32[48,128]{1,0:T(8,128)}, f32[48,128]{1,0:T(8,128)S(1)}, u32[]{:S(2)}, u32[]{:S(2)}) collective-permute-start(f32[48,128]{1,0:T(8,128)} %param.15), channel_id=1, source_target_pairs={{0,8},{8,0},{16,24},{24,16},{1,9},{9,1},{17,25},{25,17},{2,10},{10... | collective-permute-start | bytes 73736 | tf_op jit(solution)/shard_map/ppermute | solution.py:28
  3.7 6.2 %collective-permute-start.1 = (f32[48,128]{1,0:T(8,128)}, f32[48,128]{1,0:T(8,128)S(1)}, u32[]{:S(2)}, u32[]{:S(2)}) collective-permute-start(f32[48,128]{1,0:T(8,128)} %param.15), channel_id=1, source_target_pairs={{0,24},{8,16},{16,8},{24,0},{1,25},{9,17},{17,9},{25,1},{2,26},{10... | collective-permute-start | bytes 73736 | tf_op jit(solution)/shard_map/ppermute | solution.py:28
  6.2 5.2 %collective-permute-start.2 = (f32[48,128]{1,0:T(8,128)}, f32[48,128]{1,0:T(8,128)S(1)}, u32[]{:S(2)}, u32[]{:S(2)}) collective-permute-start(f32[48,128]{1,0:T(8,128)} %param.15), channel_id=1, source_target_pairs={{0,16},{8,24},{16,0},{24,8},{1,17},{9,25},{17,1},{25,9},{2,18},{10... | collective-permute-start | bytes 73736 | tf_op jit(solution)/shard_map/ppermute | solution.py:28
  11.4 16.8 %collective-permute-start.5 = (f32[208,128]{1,0:T(8,128)S(1)}, f32[208,128]{1,0:T(8,128)S(1)}, u32[]{:S(2)}, u32[]{:S(2)}) collective-permute-start(f32[208,128]{1,0:T(8,128)S(1)} %constant_dynamic-update-slice_fusion), channel_id=1, source_target_pairs={{0,6},{1,7},{2,4},{3,5},{4,2},{5,3},{6,0},{7,1},{8,14},{9,15},{10,... | collective-permute-start | bytes 319496 | tf_op jit(solution)/shard_map/ppermute | solution.py:28
  13.9 14.3 %collective-permute-start.3 = (f32[208,128]{1,0:T(8,128)S(1)}, f32[208,128]{1,0:T(8,128)S(1)}, u32[]{:S(2)}, u32[]{:S(2)}) collective-permute-start(f32[208,128]{1,0:T(8,128)S(1)} %constant_dynamic-update-slice_fusion), channel_id=1, source_target_pairs={{0,2},{1,3},{2,0},{3,1},{4,6},{5,7},{6,4},{7,5},{8,10},{9,11},{10,... | collective-permute-start | bytes 319496 | tf_op jit(solution)/shard_map/ppermute | solution.py:28
  14.5 13.8 %collective-permute-start.4 = (f32[208,128]{1,0:T(8,128)S(1)}, f32[208,128]{1,0:T(8,128)S(1)}, u32[]{:S(2)}, u32[]{:S(2)}) collective-permute-start(f32[208,128]{1,0:T(8,128)S(1)} %constant_dynamic-update-slice_fusion), channel_id=1, source_target_pairs={{0,4},{1,5},{2,6},{3,7},{4,0},{5,1},{6,2},{7,3},{8,12},{9,13},{10,... | collective-permute-start | bytes 319496 | tf_op jit(solution)/shard_map/ppermute | solution.py:28
  35.2 5.9 %collective-permute-start.7 = (f32[2,2,64,128]{3,2,1,0:T(8,128)S(1)}, f32[2,2,64,128]{3,2,1,0:T(8,128)S(1)}, u32[]{:S(2)}, u32[]{:S(2)}) collective-permute-start(f32[2,2,64,128]{3,2,1,0:T(8,128)S(1)} %get-tuple-element.81), channel_id=1, source_target_pairs={{0,2},{1,3},{2,0},{3,1},{4,6},{5,7},{6,4},{7,5},{8,10},{9,11},{10,... | collective-permute-start | bytes 393224 | tf_op jit(solution)/shard_map/ppermute | solution.py:28
  36.7 8.1 %collective-permute-start.8 = (f32[2,2,64,128]{3,2,1,0:T(8,128)S(1)}, f32[2,2,64,128]{3,2,1,0:T(8,128)S(1)}, u32[]{:S(2)}, u32[]{:S(2)}) collective-permute-start(f32[2,2,64,128]{3,2,1,0:T(8,128)S(1)} %get-tuple-element.82), channel_id=1, source_target_pairs={{0,4},{1,5},{2,6},{3,7},{4,0},{5,1},{6,2},{7,3},{8,12},{9,13},{10,... | collective-permute-start | bytes 393224 | tf_op jit(solution)/shard_map/ppermute | solution.py:28
  38.2 6.6 %collective-permute-start.9 = (f32[2,2,64,128]{3,2,1,0:T(8,128)S(1)}, f32[2,2,64,128]{3,2,1,0:T(8,128)S(1)}, u32[]{:S(2)}, u32[]{:S(2)}) collective-permute-start(f32[2,2,64,128]{3,2,1,0:T(8,128)S(1)} %get-tuple-element.83), channel_id=1, source_target_pairs={{0,6},{1,7},{2,4},{3,5},{4,2},{5,3},{6,0},{7,1},{8,14},{9,15},{10,... | collective-permute-start | bytes 393224 | tf_op jit(solution)/shard_map/ppermute | solution.py:28
  38.7 6.8 %collective-permute-start.10 = (f32[2,64,128]{2,1,0:T(8,128)S(1)}, f32[2,64,128]{2,1,0:T(8,128)S(1)}, u32[]{:S(2)}, u32[]{:S(2)}) collective-permute-start(f32[2,64,128]{2,1,0:T(8,128)S(1)} %slice_bitcast_fusion.41), channel_id=1, source_target_pairs={{0,1},{1,0},{2,3},{3,2},{4,5},{5,4},{6,7},{7,6},{8,9},{9,8},{10,11... | collective-permute-start | bytes 196616 | tf_op jit(solution)/shard_map/ppermute | solution.py:28
  47.7 18.9 %collective-permute-start.14 = (f32[8,64,128]{2,1,0:T(8,128)}, f32[8,64,128]{2,1,0:T(8,128)}, u32[]{:S(2)}, u32[]{:S(2)}) collective-permute-start(f32[8,64,128]{2,1,0:T(8,128)} %get-tuple-element.85.after), channel_id=1, source_target_pairs={{0,8},{8,0},{16,24},{24,16},{1,9},{9,1},{17,25},{25,17},{2,10},{10... | collective-permute-start | bytes 786440 | tf_op jit(solution)/shard_map/ppermute | solution.py:28
  49.2 6.4 %collective-permute-start.24 = (f32[2,2,64,128]{3,2,1,0:T(8,128)S(1)}, f32[2,2,64,128]{3,2,1,0:T(8,128)S(1)}, u32[]{:S(2)}, u32[]{:S(2)}) collective-permute-start(f32[2,2,64,128]{3,2,1,0:T(8,128)S(1)} %get-tuple-element.92), channel_id=1, source_target_pairs={{0,2},{1,3},{2,0},{3,1},{4,6},{5,7},{6,4},{7,5},{8,10},{9,11},{10,... | collective-permute-start | bytes 393224 | tf_op jit(solution)/shard_map/ppermute | solution.py:28
  50.3 6.6 %collective-permute-start.25 = (f32[2,2,64,128]{3,2,1,0:T(8,128)S(1)}, f32[2,2,64,128]{3,2,1,0:T(8,128)S(1)}, u32[]{:S(2)}, u32[]{:S(2)}) collective-permute-start(f32[2,2,64,128]{3,2,1,0:T(8,128)S(1)} %get-tuple-element.93), channel_id=1, source_target_pairs={{0,4},{1,5},{2,6},{3,7},{4,0},{5,1},{6,2},{7,3},{8,12},{9,13},{10,... | collective-permute-start | bytes 393224 | tf_op jit(solution)/shard_map/ppermute | solution.py:28
  51.4 7.2 %collective-permute-start.26 = (f32[2,2,64,128]{3,2,1,0:T(8,128)S(1)}, f32[2,2,64,128]{3,2,1,0:T(8,128)S(1)}, u32[]{:S(2)}, u32[]{:S(2)}) collective-permute-start(f32[2,2,64,128]{3,2,1,0:T(8,128)S(1)} %get-tuple-element.94), channel_id=1, source_target_pairs={{0,6},{1,7},{2,4},{3,5},{4,2},{5,3},{6,0},{7,1},{8,14},{9,15},{10,... | collective-permute-start | bytes 393224 | tf_op jit(solution)/shard_map/ppermute | solution.py:28
  53.4 9.4 %collective-permute-start.27 = (f32[2,64,128]{2,1,0:T(8,128)}, f32[2,64,128]{2,1,0:T(8,128)}, u32[]{:S(2)}, u32[]{:S(2)}) collective-permute-start(f32[2,64,128]{2,1,0:T(8,128)} %slice_bitcast_fusion.39), channel_id=1, source_target_pairs={{0,1},{1,0},{2,3},{3,2},{4,5},{5,4},{6,7},{7,6},{8,9},{9,8},{10,11... | collective-permute-start | bytes 196616 | tf_op jit(solution)/shard_map/ppermute | solution.py:28
  56.3 6.5 %collective-permute-start.28 = (f32[2,64,128]{2,1,0:T(8,128)}, f32[2,64,128]{2,1,0:T(8,128)}, u32[]{:S(2)}, u32[]{:S(2)}) collective-permute-start(f32[2,64,128]{2,1,0:T(8,128)} %slice_bitcast_fusion.27), channel_id=1, source_target_pairs={{0,1},{1,0},{2,3},{3,2},{4,5},{5,4},{6,7},{7,6},{8,9},{9,8},{10,11... | collective-permute-start | bytes 196616 | tf_op jit(solution)/shard_map/ppermute | solution.py:28
  57.5 5.2 %collective-permute-start.29 = (f32[2,64,128]{2,1,0:T(8,128)}, f32[2,64,128]{2,1,0:T(8,128)}, u32[]{:S(2)}, u32[]{:S(2)}) collective-permute-start(f32[2,64,128]{2,1,0:T(8,128)} %slice_bitcast_fusion.26), channel_id=1, source_target_pairs={{0,1},{1,0},{2,3},{3,2},{4,5},{5,4},{6,7},{7,6},{8,9},{9,8},{10,11... | collective-permute-start | bytes 196616 | tf_op jit(solution)/shard_map/ppermute | solution.py:28
  65.0 8.8 %collective-permute-start.31 = (f32[8,64,128]{2,1,0:T(8,128)S(1)}, f32[8,64,128]{2,1,0:T(8,128)S(1)}, u32[]{:S(2)}, u32[]{:S(2)}) collective-permute-start(f32[8,64,128]{2,1,0:T(8,128)S(1)} %get-tuple-element.96), channel_id=1, source_target_pairs={{0,8},{8,0},{16,24},{24,16},{1,9},{9,1},{17,25},{25,17},{2,10},{10... | collective-permute-start | bytes 786440 | tf_op jit(solution)/shard_map/ppermute | solution.py:28
  67.7 12.9 %collective-permute-start.15 = (f32[8,64,128]{2,1,0:T(8,128)S(1)}, f32[8,64,128]{2,1,0:T(8,128)S(1)}, u32[]{:S(2)}, u32[]{:S(2)}) collective-permute-start(f32[8,64,128]{2,1,0:T(8,128)S(1)} %add.111), channel_id=1, source_target_pairs={{0,24},{8,16},{16,8},{24,0},{1,25},{9,17},{17,9},{25,1},{2,26},{10... | collective-permute-start | bytes 786440 | tf_op jit(solution)/shard_map/ppermute | solution.py:28
  73.8 15.0 %collective-permute-start.32 = (f32[8,64,128]{2,1,0:T(8,128)S(1)}, f32[8,64,128]{2,1,0:T(8,128)S(1)}, u32[]{:S(2)}, u32[]{:S(2)}) collective-permute-start(f32[8,64,128]{2,1,0:T(8,128)S(1)} %add.113), channel_id=1, source_target_pairs={{0,24},{8,16},{16,8},{24,0},{1,25},{9,17},{17,9},{25,1},{2,26},{10... | collective-permute-start | bytes 786440 | tf_op jit(solution)/shard_map/ppermute | solution.py:28
  80.6 13.3 %collective-permute-start.16 = (f32[8,64,128]{2,1,0:T(8,128)S(1)}, f32[8,64,128]{2,1,0:T(8,128)S(1)}, u32[]{:S(2)}, u32[]{:S(2)}) collective-permute-start(f32[8,64,128]{2,1,0:T(8,128)S(1)} %add.112.mine), channel_id=1, source_target_pairs={{0,8},{8,0},{16,24},{24,16},{1,9},{9,1},{17,25},{25,17},{2,10},{10... | collective-permute-start | bytes 786440 | tf_op jit(solution)/shard_map/ppermute | solution.py:28
  88.9 14.8 %collective-permute-start.33 = (f32[8,64,128]{2,1,0:T(8,128)S(1)}, f32[8,64,128]{2,1,0:T(8,128)S(1)}, u32[]{:S(2)}, u32[]{:S(2)}) collective-permute-start(f32[8,64,128]{2,1,0:T(8,128)S(1)} %add.114.mine), channel_id=1, source_target_pairs={{0,8},{8,0},{16,24},{24,16},{1,9},{9,1},{17,25},{25,17},{2,10},{10... | collective-permute-start | bytes 786440 | tf_op jit(solution)/shard_map/ppermute | solution.py:28
  94.8 6.1 %collective-permute-start.17 = (f32[2,2,64,128]{3,2,1,0:T(8,128)S(1)}, f32[2,2,64,128]{3,2,1,0:T(8,128)S(1)}, u32[]{:S(2)}, u32[]{:S(2)}) collective-permute-start(f32[2,2,64,128]{3,2,1,0:T(8,128)S(1)} %get-tuple-element.87), channel_id=1, source_target_pairs={{0,2},{1,3},{2,0},{3,1},{4,6},{5,7},{6,4},{7,5},{8,10},{9,11},{10,... | collective-permute-start | bytes 393224 | tf_op jit(solution)/shard_map/ppermute | solution.py:28
  96.2 5.9 %collective-permute-start.18 = (f32[2,2,64,128]{3,2,1,0:T(8,128)S(1)}, f32[2,2,64,128]{3,2,1,0:T(8,128)S(1)}, u32[]{:S(2)}, u32[]{:S(2)}) collective-permute-start(f32[2,2,64,128]{3,2,1,0:T(8,128)S(1)} %get-tuple-element.88), channel_id=1, source_target_pairs={{0,4},{1,5},{2,6},{3,7},{4,0},{5,1},{6,2},{7,3},{8,12},{9,13},{10,... | collective-permute-start | bytes 393224 | tf_op jit(solution)/shard_map/ppermute | solution.py:28
  97.8 5.9 %collective-permute-start.19 = (f32[2,2,64,128]{3,2,1,0:T(8,128)S(1)}, f32[2,2,64,128]{3,2,1,0:T(8,128)S(1)}, u32[]{:S(2)}, u32[]{:S(2)}) collective-permute-start(f32[2,2,64,128]{3,2,1,0:T(8,128)S(1)} %get-tuple-element.89), channel_id=1, source_target_pairs={{0,6},{1,7},{2,4},{3,5},{4,2},{5,3},{6,0},{7,1},{8,14},{9,15},{10,... | collective-permute-start | bytes 393224 | tf_op jit(solution)/shard_map/ppermute | solution.py:28
  98.3 23.2 %collective-permute-start.20 = (f32[2,64,128]{2,1,0:T(8,128)S(1)}, f32[2,64,128]{2,1,0:T(8,128)S(1)}, u32[]{:S(2)}, u32[]{:S(2)}) collective-permute-start(f32[2,64,128]{2,1,0:T(8,128)S(1)} %slice_bitcast_fusion.40), channel_id=1, source_target_pairs={{0,1},{1,0},{2,3},{3,2},{4,5},{5,4},{6,7},{7,6},{8,9},{9,8},{10,11... | collective-permute-start | bytes 196616 | tf_op jit(solution)/shard_map/ppermute | solution.py:28
  100.9 21.2 %collective-permute-start.21 = (f32[2,64,128]{2,1,0:T(8,128)S(1)}, f32[2,64,128]{2,1,0:T(8,128)S(1)}, u32[]{:S(2)}, u32[]{:S(2)}) collective-permute-start(f32[2,64,128]{2,1,0:T(8,128)S(1)} %slice_bitcast_fusion.30), channel_id=1, source_target_pairs={{0,1},{1,0},{2,3},{3,2},{4,5},{5,4},{6,7},{7,6},{8,9},{9,8},{10,11... | collective-permute-start | bytes 196616 | tf_op jit(solution)/shard_map/ppermute | solution.py:28
  102.1 20.1 %collective-permute-start.22 = (f32[2,64,128]{2,1,0:T(8,128)S(1)}, f32[2,64,128]{2,1,0:T(8,128)S(1)}, u32[]{:S(2)}, u32[]{:S(2)}) collective-permute-start(f32[2,64,128]{2,1,0:T(8,128)S(1)} %slice_bitcast_fusion.29), channel_id=1, source_target_pairs={{0,1},{1,0},{2,3},{3,2},{4,5},{5,4},{6,7},{7,6},{8,9},{9,8},{10,11... | collective-permute-start | bytes 196616 | tf_op jit(solution)/shard_map/ppermute | solution.py:28
  103.6 19.0 %collective-permute-start.23 = (f32[2,64,128]{2,1,0:T(8,128)S(1)}, f32[2,64,128]{2,1,0:T(8,128)S(1)}, u32[]{:S(2)}, u32[]{:S(2)}) collective-permute-start(f32[2,64,128]{2,1,0:T(8,128)S(1)} %slice_bitcast_fusion.28), channel_id=1, source_target_pairs={{0,1},{1,0},{2,3},{3,2},{4,5},{5,4},{6,7},{7,6},{8,9},{9,8},{10,11... | collective-permute-start | bytes 196616 | tf_op jit(solution)/shard_map/ppermute | solution.py:28
  104.5 6.0 %collective-permute-start.34 = (f32[2,2,64,128]{3,2,1,0:T(8,128)S(1)}, f32[2,2,64,128]{3,2,1,0:T(8,128)S(1)}, u32[]{:S(2)}, u32[]{:S(2)}) collective-permute-start(f32[2,2,64,128]{3,2,1,0:T(8,128)S(1)} %get-tuple-element.98), channel_id=1, source_target_pairs={{0,2},{1,3},{2,0},{3,1},{4,6},{5,7},{6,4},{7,5},{8,10},{9,11},{10,... | collective-permute-start | bytes 393224 | tf_op jit(solution)/shard_map/ppermute | solution.py:28
  115.6 5.9 %collective-permute-start.36 = (f32[2,2,64,128]{3,2,1,0:T(8,128)S(1)}, f32[2,2,64,128]{3,2,1,0:T(8,128)S(1)}, u32[]{:S(2)}, u32[]{:S(2)}) collective-permute-start(f32[2,2,64,128]{3,2,1,0:T(8,128)S(1)} %get-tuple-element.100), channel_id=1, source_target_pairs={{0,6},{1,7},{2,4},{3,5},{4,2},{5,3},{6,0},{7,1},{8,14},{9,15},{10,... | collective-permute-start | bytes 393224 | tf_op jit(solution)/shard_map/ppermute | solution.py:28
  132.9 5.7 %collective-permute-start.42 = (f32[192,128]{1,0:T(8,128)S(1)}, f32[192,128]{1,0:T(8,128)S(1)}, u32[]{:S(2)}, u32[]{:S(2)}) collective-permute-start(f32[192,128]{1,0:T(8,128)S(1)} %get-tuple-element.139), channel_id=1, source_target_pairs={{0,2},{1,3},{2,0},{3,1},{4,6},{5,7},{6,4},{7,5},{8,10},{9,11},{10,... | collective-permute-start | bytes 294920 | tf_op jit(solution)/shard_map/ppermute | solution.py:28
  133.5 5.3 %collective-permute-start.43 = (f32[192,128]{1,0:T(8,128)S(1)}, f32[192,128]{1,0:T(8,128)S(1)}, u32[]{:S(2)}, u32[]{:S(2)}) collective-permute-start(f32[192,128]{1,0:T(8,128)S(1)} %get-tuple-element.141), channel_id=1, source_target_pairs={{0,4},{1,5},{2,6},{3,7},{4,0},{5,1},{6,2},{7,3},{8,12},{9,13},{10,... | collective-permute-start | bytes 294920 | tf_op jit(solution)/shard_map/ppermute | solution.py:28
  134.5 5.9 %collective-permute-start.44 = (f32[192,128]{1,0:T(8,128)S(1)}, f32[192,128]{1,0:T(8,128)S(1)}, u32[]{:S(2)}, u32[]{:S(2)}) collective-permute-start(f32[192,128]{1,0:T(8,128)S(1)} %get-tuple-element.140), channel_id=1, source_target_pairs={{0,6},{1,7},{2,4},{3,5},{4,2},{5,3},{6,0},{7,1},{8,14},{9,15},{10,... | collective-permute-start | bytes 294920 | tf_op jit(solution)/shard_map/ppermute | solution.py:28
  145.4 6.6 %collective-permute-start.46 = (f32[4,48,128]{2,1,0:T(8,128)S(1)}, f32[4,48,128]{2,1,0:T(8,128)S(1)}, u32[]{:S(2)}, u32[]{:S(2)}) collective-permute-start(f32[4,48,128]{2,1,0:T(8,128)S(1)} %bitcast_add_fusion.1), channel_id=1, source_target_pairs={{0,24},{8,16},{16,8},{24,0},{1,25},{9,17},{17,9},{25,1},{2,26},{10... | collective-permute-start | bytes 294920 | tf_op jit(solution)/shard_map/ppermute | solution.py:28
  154.3 5.5 %collective-permute-start.49 = (f32[192,128]{1,0:T(8,128)S(1)}, f32[192,128]{1,0:T(8,128)S(1)}, u32[]{:S(2)}, u32[]{:S(2)}) collective-permute-start(f32[192,128]{1,0:T(8,128)S(1)} %fusion.10), channel_id=1, source_target_pairs={{0,6},{1,7},{2,4},{3,5},{4,2},{5,3},{6,0},{7,1},{8,14},{9,15},{10,... | collective-permute-start | bytes 294920 | tf_op jit(solution)/shard_map/ppermute | solution.py:28
  166.2 6.4 %collective-permute-start.51 = (f32[2,2,64,128]{3,2,1,0:T(8,128)S(1)}, f32[2,2,64,128]{3,2,1,0:T(8,128)S(1)}, u32[]{:S(2)}, u32[]{:S(2)}) collective-permute-start(f32[2,2,64,128]{3,2,1,0:T(8,128)S(1)} %get-tuple-element.104), channel_id=1, source_target_pairs={{0,2},{1,3},{2,0},{3,1},{4,6},{5,7},{6,4},{7,5},{8,10},{9,11},{10,... | collective-permute-start | bytes 393224 | tf_op jit(solution)/shard_map/ppermute | solution.py:28
  167.3 6.6 %collective-permute-start.52 = (f32[2,2,64,128]{3,2,1,0:T(8,128)S(1)}, f32[2,2,64,128]{3,2,1,0:T(8,128)S(1)}, u32[]{:S(2)}, u32[]{:S(2)}) collective-permute-start(f32[2,2,64,128]{3,2,1,0:T(8,128)S(1)} %get-tuple-element.105), channel_id=1, source_target_pairs={{0,4},{1,5},{2,6},{3,7},{4,0},{5,1},{6,2},{7,3},{8,12},{9,13},{10,... | collective-permute-start | bytes 393224 | tf_op jit(solution)/shard_map/ppermute | solution.py:28
  168.2 7.6 %collective-permute-start.53 = (f32[2,2,64,128]{3,2,1,0:T(8,128)S(1)}, f32[2,2,64,128]{3,2,1,0:T(8,128)S(1)}, u32[]{:S(2)}, u32[]{:S(2)}) collective-permute-start(f32[2,2,64,128]{3,2,1,0:T(8,128)S(1)} %get-tuple-element.106), channel_id=1, source_target_pairs={{0,6},{1,7},{2,4},{3,5},{4,2},{5,3},{6,0},{7,1},{8,14},{9,15},{10,... | collective-permute-start | bytes 393224 | tf_op jit(solution)/shard_map/ppermute | solution.py:28
  169.7 6.0 %collective-permute-start.54 = (f32[2,64,128]{2,1,0:T(8,128)S(1)}, f32[2,64,128]{2,1,0:T(8,128)S(1)}, u32[]{:S(2)}, u32[]{:S(2)}) collective-permute-start(f32[2,64,128]{2,1,0:T(8,128)S(1)} %slice_bitcast_fusion.37), channel_id=1, source_target_pairs={{0,1},{1,0},{2,3},{3,2},{4,5},{5,4},{6,7},{7,6},{8,9},{9,8},{10,11... | collective-permute-start | bytes 196616 | tf_op jit(solution)/shard_map/ppermute | solution.py:28
  177.8 14.5 %collective-permute-start.58 = (f32[8,64,128]{2,1,0:T(8,128)S(1)}, f32[8,64,128]{2,1,0:T(8,128)S(1)}, u32[]{:S(2)}, u32[]{:S(2)}) collective-permute-start(f32[8,64,128]{2,1,0:T(8,128)S(1)} %get-tuple-element.108.after), channel_id=1, source_target_pairs={{0,8},{8,0},{16,24},{24,16},{1,9},{9,1},{17,25},{25,17},{2,10},{10... | collective-permute-start | bytes 786440 | tf_op jit(solution)/shard_map/ppermute | solution.py:28
  180.3 6.3 %collective-permute-start.68 = (f32[2,2,64,128]{3,2,1,0:T(8,128)S(1)}, f32[2,2,64,128]{3,2,1,0:T(8,128)S(1)}, u32[]{:S(2)}, u32[]{:S(2)}) collective-permute-start(f32[2,2,64,128]{3,2,1,0:T(8,128)S(1)} %get-tuple-element.115), channel_id=1, source_target_pairs={{0,2},{1,3},{2,0},{3,1},{4,6},{5,7},{6,4},{7,5},{8,10},{9,11},{10,... | collective-permute-start | bytes 393224 | tf_op jit(solution)/shard_map/ppermute | solution.py:28
  181.2 8.0 %collective-permute-start.69 = (f32[2,2,64,128]{3,2,1,0:T(8,128)S(1)}, f32[2,2,64,128]{3,2,1,0:T(8,128)S(1)}, u32[]{:S(2)}, u32[]{:S(2)}) collective-permute-start(f32[2,2,64,128]{3,2,1,0:T(8,128)S(1)} %get-tuple-element.116), channel_id=1, source_target_pairs={{0,4},{1,5},{2,6},{3,7},{4,0},{5,1},{6,2},{7,3},{8,12},{9,13},{10,... | collective-permute-start | bytes 393224 | tf_op jit(solution)/shard_map/ppermute | solution.py:28
  182.9 6.3 %collective-permute-start.70 = (f32[2,2,64,128]{3,2,1,0:T(8,128)S(1)}, f32[2,2,64,128]{3,2,1,0:T(8,128)S(1)}, u32[]{:S(2)}, u32[]{:S(2)}) collective-permute-start(f32[2,2,64,128]{3,2,1,0:T(8,128)S(1)} %get-tuple-element.117), channel_id=1, source_target_pairs={{0,6},{1,7},{2,4},{3,5},{4,2},{5,3},{6,0},{7,1},{8,14},{9,15},{10,... | collective-permute-start | bytes 393224 | tf_op jit(solution)/shard_map/ppermute | solution.py:28
  183.9 5.9 %collective-permute-start.71 = (f32[2,64,128]{2,1,0:T(8,128)S(1)}, f32[2,64,128]{2,1,0:T(8,128)S(1)}, u32[]{:S(2)}, u32[]{:S(2)}) collective-permute-start(f32[2,64,128]{2,1,0:T(8,128)S(1)} %slice_bitcast_fusion.35), channel_id=1, source_target_pairs={{0,1},{1,0},{2,3},{3,2},{4,5},{5,4},{6,7},{7,6},{8,9},{9,8},{10,11... | collective-permute-start | bytes 196616 | tf_op jit(solution)/shard_map/ppermute | solution.py:28
  191.7 9.0 %collective-permute-start.75 = (f32[8,64,128]{2,1,0:T(8,128)S(1)}, f32[8,64,128]{2,1,0:T(8,128)S(1)}, u32[]{:S(2)}, u32[]{:S(2)}) collective-permute-start(f32[8,64,128]{2,1,0:T(8,128)S(1)} %get-tuple-element.119), channel_id=1, source_target_pairs={{0,8},{8,0},{16,24},{24,16},{1,9},{9,1},{17,25},{25,17},{2,10},{10... | collective-permute-start | bytes 786440 | tf_op jit(solution)/shard_map/ppermute | solution.py:28
  192.3 14.4 %collective-permute-start.59 = (f32[8,64,128]{2,1,0:T(8,128)S(1)}, f32[8,64,128]{2,1,0:T(8,128)S(1)}, u32[]{:S(2)}, u32[]{:S(2)}) collective-permute-start(f32[8,64,128]{2,1,0:T(8,128)S(1)} %add.122), channel_id=1, source_target_pairs={{0,24},{8,16},{16,8},{24,0},{1,25},{9,17},{17,9},{25,1},{2,26},{10... | collective-permute-start | bytes 786440 | tf_op jit(solution)/shard_map/ppermute | solution.py:28
  200.7 13.6 %collective-permute-start.76 = (f32[8,64,128]{2,1,0:T(8,128)S(1)}, f32[8,64,128]{2,1,0:T(8,128)S(1)}, u32[]{:S(2)}, u32[]{:S(2)}) collective-permute-start(f32[8,64,128]{2,1,0:T(8,128)S(1)} %add.124), channel_id=1, source_target_pairs={{0,24},{8,16},{16,8},{24,0},{1,25},{9,17},{17,9},{25,1},{2,26},{10... | collective-permute-start | bytes 786440 | tf_op jit(solution)/shard_map/ppermute | solution.py:28
  206.7 12.4 %collective-permute-start.60 = (f32[8,64,128]{2,1,0:T(8,128)S(1)}, f32[8,64,128]{2,1,0:T(8,128)S(1)}, u32[]{:S(2)}, u32[]{:S(2)}) collective-permute-start(f32[8,64,128]{2,1,0:T(8,128)S(1)} %add.123.mine), channel_id=1, source_target_pairs={{0,8},{8,0},{16,24},{24,16},{1,9},{9,1},{17,25},{25,17},{2,10},{10... | collective-permute-start | bytes 786440 | tf_op jit(solution)/shard_map/ppermute | solution.py:28
  214.4 15.5 %collective-permute-start.77 = (f32[8,64,128]{2,1,0:T(8,128)S(1)}, f32[8,64,128]{2,1,0:T(8,128)S(1)}, u32[]{:S(2)}, u32[]{:S(2)}) collective-permute-start(f32[8,64,128]{2,1,0:T(8,128)S(1)} %add.125.mine), channel_id=1, source_target_pairs={{0,8},{8,0},{16,24},{24,16},{1,9},{9,1},{17,25},{25,17},{2,10},{10... | collective-permute-start | bytes 786440 | tf_op jit(solution)/shard_map/ppermute | solution.py:28
  219.8 6.1 %collective-permute-start.61 = (f32[2,2,64,128]{3,2,1,0:T(8,128)S(1)}, f32[2,2,64,128]{3,2,1,0:T(8,128)S(1)}, u32[]{:S(2)}, u32[]{:S(2)}) collective-permute-start(f32[2,2,64,128]{3,2,1,0:T(8,128)S(1)} %get-tuple-element.110), channel_id=1, source_target_pairs={{0,2},{1,3},{2,0},{3,1},{4,6},{5,7},{6,4},{7,5},{8,10},{9,11},{10,... | collective-permute-start | bytes 393224 | tf_op jit(solution)/shard_map/ppermute | solution.py:28
  220.9 7.0 %collective-permute-start.62 = (f32[2,2,64,128]{3,2,1,0:T(8,128)S(1)}, f32[2,2,64,128]{3,2,1,0:T(8,128)S(1)}, u32[]{:S(2)}, u32[]{:S(2)}) collective-permute-start(f32[2,2,64,128]{3,2,1,0:T(8,128)S(1)} %get-tuple-element.111), channel_id=1, source_target_pairs={{0,4},{1,5},{2,6},{3,7},{4,0},{5,1},{6,2},{7,3},{8,12},{9,13},{10,... | collective-permute-start | bytes 393224 | tf_op jit(solution)/shard_map/ppermute | solution.py:28
  224.0 5.9 %collective-permute-start.63 = (f32[2,2,64,128]{3,2,1,0:T(8,128)S(1)}, f32[2,2,64,128]{3,2,1,0:T(8,128)S(1)}, u32[]{:S(2)}, u32[]{:S(2)}) collective-permute-start(f32[2,2,64,128]{3,2,1,0:T(8,128)S(1)} %get-tuple-element.112), channel_id=1, source_target_pairs={{0,6},{1,7},{2,4},{3,5},{4,2},{5,3},{6,0},{7,1},{8,14},{9,15},{10,... | collective-permute-start | bytes 393224 | tf_op jit(solution)/shard_map/ppermute | solution.py:28
  224.4 23.2 %collective-permute-start.64 = (f32[2,64,128]{2,1,0:T(8,128)S(1)}, f32[2,64,128]{2,1,0:T(8,128)S(1)}, u32[]{:S(2)}, u32[]{:S(2)}) collective-permute-start(f32[2,64,128]{2,1,0:T(8,128)S(1)} %slice_bitcast_fusion.36), channel_id=1, source_target_pairs={{0,1},{1,0},{2,3},{3,2},{4,5},{5,4},{6,7},{7,6},{8,9},{9,8},{10,11... | collective-permute-start | bytes 196616 | tf_op jit(solution)/shard_map/ppermute | solution.py:28
  225.9 22.2 %collective-permute-start.65 = (f32[2,64,128]{2,1,0:T(8,128)S(1)}, f32[2,64,128]{2,1,0:T(8,128)S(1)}, u32[]{:S(2)}, u32[]{:S(2)}) collective-permute-start(f32[2,64,128]{2,1,0:T(8,128)S(1)} %slice_bitcast_fusion.18), channel_id=1, source_target_pairs={{0,1},{1,0},{2,3},{3,2},{4,5},{5,4},{6,7},{7,6},{8,9},{9,8},{10,11... | collective-permute-start | bytes 196616 | tf_op jit(solution)/shard_map/ppermute | solution.py:28
  227.9 20.3 %collective-permute-start.66 = (f32[2,64,128]{2,1,0:T(8,128)S(1)}, f32[2,64,128]{2,1,0:T(8,128)S(1)}, u32[]{:S(2)}, u32[]{:S(2)}) collective-permute-start(f32[2,64,128]{2,1,0:T(8,128)S(1)} %slice_bitcast_fusion.17), channel_id=1, source_target_pairs={{0,1},{1,0},{2,3},{3,2},{4,5},{5,4},{6,7},{7,6},{8,9},{9,8},{10,11... | collective-permute-start | bytes 196616 | tf_op jit(solution)/shard_map/ppermute | solution.py:28
  229.9 18.8 %collective-permute-start.67 = (f32[2,64,128]{2,1,0:T(8,128)S(1)}, f32[2,64,128]{2,1,0:T(8,128)S(1)}, u32[]{:S(2)}, u32[]{:S(2)}) collective-permute-start(f32[2,64,128]{2,1,0:T(8,128)S(1)} %slice_bitcast_fusion.16), channel_id=1, source_target_pairs={{0,1},{1,0},{2,3},{3,2},{4,5},{5,4},{6,7},{7,6},{8,9},{9,8},{10,11... | collective-permute-start | bytes 196616 | tf_op jit(solution)/shard_map/ppermute | solution.py:28
  230.6 6.0 %collective-permute-start.78 = (f32[2,2,64,128]{3,2,1,0:T(8,128)S(1)}, f32[2,2,64,128]{3,2,1,0:T(8,128)S(1)}, u32[]{:S(2)}, u32[]{:S(2)}) collective-permute-start(f32[2,2,64,128]{3,2,1,0:T(8,128)S(1)} %get-tuple-element.121), channel_id=1, source_target_pairs={{0,2},{1,3},{2,0},{3,1},{4,6},{5,7},{6,4},{7,5},{8,10},{9,11},{10,... | collective-permute-start | bytes 393224 | tf_op jit(solution)/shard_map/ppermute | solution.py:28
  241.7 5.9 %collective-permute-start.80 = (f32[2,2,64,128]{3,2,1,0:T(8,128)S(1)}, f32[2,2,64,128]{3,2,1,0:T(8,128)S(1)}, u32[]{:S(2)}, u32[]{:S(2)}) collective-permute-start(f32[2,2,64,128]{3,2,1,0:T(8,128)S(1)} %get-tuple-element.123), channel_id=1, source_target_pairs={{0,6},{1,7},{2,4},{3,5},{4,2},{5,3},{6,0},{7,1},{8,14},{9,15},{10,... | collective-permute-start | bytes 393224 | tf_op jit(solution)/shard_map/ppermute | solution.py:28
  255.5 5.4 %collective-permute-start.86 = (f32[192,128]{1,0:T(8,128)S(1)}, f32[192,128]{1,0:T(8,128)S(1)}, u32[]{:S(2)}, u32[]{:S(2)}) collective-permute-start(f32[192,128]{1,0:T(8,128)S(1)} %get-tuple-element.136), channel_id=1, source_target_pairs={{0,2},{1,3},{2,0},{3,1},{4,6},{5,7},{6,4},{7,5},{8,10},{9,11},{10,... | collective-permute-start | bytes 294920 | tf_op jit(solution)/shard_map/ppermute | solution.py:28
  256.5 6.9 %collective-permute-start.87 = (f32[192,128]{1,0:T(8,128)S(1)}, f32[192,128]{1,0:T(8,128)S(1)}, u32[]{:S(2)}, u32[]{:S(2)}) collective-permute-start(f32[192,128]{1,0:T(8,128)S(1)} %get-tuple-element.138), channel_id=1, source_target_pairs={{0,4},{1,5},{2,6},{3,7},{4,0},{5,1},{6,2},{7,3},{8,12},{9,13},{10,... | collective-permute-start | bytes 294920 | tf_op jit(solution)/shard_map/ppermute | solution.py:28
  257.0 6.4 %collective-permute-start.88 = (f32[192,128]{1,0:T(8,128)S(1)}, f32[192,128]{1,0:T(8,128)S(1)}, u32[]{:S(2)}, u32[]{:S(2)}) collective-permute-start(f32[192,128]{1,0:T(8,128)S(1)} %get-tuple-element.137), channel_id=1, source_target_pairs={{0,6},{1,7},{2,4},{3,5},{4,2},{5,3},{6,0},{7,1},{8,14},{9,15},{10,... | collective-permute-start | bytes 294920 | tf_op jit(solution)/shard_map/ppermute | solution.py:28
  263.4 5.4 %collective-permute-start.89 = (f32[48,128]{1,0:T(8,128)S(1)}, f32[48,128]{1,0:T(8,128)S(1)}, u32[]{:S(2)}, u32[]{:S(2)}) collective-permute-start(f32[48,128]{1,0:T(8,128)S(1)} %get-tuple-element.142), channel_id=1, source_target_pairs={{0,8},{8,0},{16,24},{24,16},{1,9},{9,1},{17,25},{25,17},{2,10},{10... | collective-permute-start | bytes 73736 | tf_op jit(solution)/shard_map/ppermute | solution.py:28
  265.4 5.6 %collective-permute-start.90 = (f32[48,128]{1,0:T(8,128)S(1)}, f32[48,128]{1,0:T(8,128)S(1)}, u32[]{:S(2)}, u32[]{:S(2)}) collective-permute-start(f32[48,128]{1,0:T(8,128)S(1)} %get-tuple-element.144), channel_id=1, source_target_pairs={{0,24},{8,16},{16,8},{24,0},{1,25},{9,17},{17,9},{25,1},{2,26},{10... | collective-permute-start | bytes 73736 | tf_op jit(solution)/shard_map/ppermute | solution.py:28
  (56 other events, 769.5 us)

commit v5 on v4

--- a/solution.py
+++ b/solution.py
@@ -20,7 +20,8 @@
 SMALL = 4 << 20
 ROWS_AT_ONCE = 1024
 COLUMNS_AT_ONCE = 512
-FETCHES = 4
+HUGE = 36 << 20
+BRIEF = pl.CostEstimate(flops=1, bytes_accessed=1, transcendentals=0)
 
 
 def swap(x, axis, mask):
@@ -46,62 +47,8 @@
     return full[:rows, :cols] + (full[:rows, cols:] + full[rows:, :cols])
 
 
-def split_body(tile_ref, matrix, tiles, big, small, own, buffer, tile_buffer, sems, tile_sems):
-    count, height, width = own.shape[0], buffer.shape[1], matrix.shape[1]
-    steps = matrix.shape[0] // height
-
-    depth = buffer.shape[0]
-
-    def fetch(i):
-        return pltpu.make_async_copy(
-            matrix.at[pl.ds(i * height, height)], buffer.at[i % depth], sems.at[i % depth]
-        )
-
-    def fetch_tile(b):
-        return pltpu.make_async_copy(tiles.at[tile_ref[b]], tile_buffer.at[b], tile_sems.at[b])
-
-    for i in range(min(depth - 1, steps)):
-        fetch(i).start()
-    for b in range(count):
-        fetch_tile(b).start()
-    for i in range(steps):
-        fetch(i).wait()
-        if i + depth - 1 < steps:
-            fetch(i + depth - 1).start()
-        x = buffer[i % depth]
-        top = x.astype(BF16)
-        big[i * height : (i + 1) * height, :] = top
-        small[i * height : (i + 1) * height, :] = (x - top.astype(F32)).astype(BF16)
-    for b in range(count):
-        fetch_tile(b).wait()
-        own[b] = halves(tile_buffer[b], 1)
-
-
 def specs(count, space):
     return [pl.BlockSpec(memory_space=space)] * count
-
-
-def split_terms(tile_index, matrix, warp_tiles, blocks):
-    height, width = warp_tiles.shape[1:]
-    step = 2 * height
-    terms = jax.ShapeDtypeStruct(matrix.shape, BF16)
-    return pl.pallas_call(
-        split_body,
-        in_specs=specs(1, pltpu.SMEM) + specs(2, pltpu.HBM),
-        out_specs=specs(3, pltpu.VMEM),
-        out_shape=[terms, terms, jax.ShapeDtypeStruct((blocks, height, 2 * width), BF16)],
-        scratch_shapes=[
-            pltpu.VMEM((FETCHES, step, matrix.shape[1]), F32),
-            pltpu.VMEM((blocks, height, width), F32),
-            pltpu.SemaphoreType.DMA((FETCHES,)),
-            pltpu.SemaphoreType.DMA((blocks,)),
-        ],
-        compiler_params=pltpu.CompilerParams(vmem_limit_bytes=LARGE),
-        cost_estimate=pl.CostEstimate(
-            flops=matrix.size, bytes_accessed=matrix.size * 4, transcendentals=0
-        ),
-        name="split_terms",
-    )(tile_index, matrix, warp_tiles)
 
 
 def fill_weights(me_ref, out, pieces, rows, vox, masks):
@@ -119,8 +66,8 @@
 def warp_chunk(h, chunks, cores, source_ref, valid_ref, tiles, dose, outs):
     height = tiles.shape[1]
     part = height // chunks
-    for k, out in enumerate(outs):
-        for c in range(cores):
+    for c, out in enumerate(outs):
+        for k in range(out.shape[0]):
             for j in range(CAP):
                 s = (k * cores + c) * CAP + j
                 b = source_ref[s]
@@ -129,7 +76,7 @@
                 left = jnp.concatenate([tile[:, :height], tile[:, height:]], axis=0)
                 full = jnp.dot(left, halves(block, 1), preferred_element_type=F32)
                 warped = term_sum(full, part, dose.shape[1])
-                out[c, j] = jnp.where(valid_ref[s] > 0, warped, 0.0)
+                out[k, j] = jnp.where(valid_ref[s] > 0, warped, 0.0)
 
 
 def forward_body(dims, source_ref, valid_ref, me_ref, big, small, tiles, *refs):
@@ -150,14 +97,94 @@
     warp_chunk(0, chunks, cores, source_ref, valid_ref, tiles, dose, outs)
 
 
+def first_body(
+    dims, source_ref, valid_ref, me_ref, tile_ref, matrix, warp_tiles, *refs
+):
+    vox, masks, rows, pieces_n, chunks, cores = dims
+    pieces, outs = refs[:pieces_n], refs[pieces_n:-9]
+    dose, big, small, tiles, weights, buffer, tile_buffer, sems, tile_sems = refs[-9:]
+    plans = dose.shape[1]
+    steps, height = buffer.shape[:2]
+    count = tiles.shape[0]
+
+    def fetch(i):
+        return pltpu.make_async_copy(
+            matrix.at[pl.ds(i * height, height)], buffer.at[i], sems.at[i]
+        )
+
+    def fetch_tile(b):
+        return pltpu.make_async_copy(warp_tiles.at[tile_ref[b]], tile_buffer.at[b], tile_sems.at[b])
+
+    def multiply(i):
+        at = slice(i * height, (i + 1) * height)
+        top = jnp.dot(big[at, :], weights[...], preferred_element_type=F32)
+        rest = jnp.dot(small[at, :], weights[:, :plans], preferred_element_type=F32)
+        dose[at, :] = top[:, :plans] + (top[:, plans:] + rest)
+
+    for i in range(steps):
+        fetch(i).start()
+    for b in range(count):
+        fetch_tile(b).start()
+    if len(pieces[0].shape) == 2:
+        weights[...] = halves(pieces[0][...], 1)
+    else:
+        fill_weights(me_ref, weights, pieces, rows, vox, masks)
+    for i in range(steps):
+        fetch(i).wait()
+        x = buffer[i]
+        top = x.astype(BF16)
+        big[i * height : (i + 1) * height, :] = top
+        small[i * height : (i + 1) * height, :] = (x - top.astype(F32)).astype(BF16)
+        if i > 0:
+            multiply(i - 1)
+    for b in range(count):
+        fetch_tile(b).wait()
+        tiles[b] = halves(tile_buffer[b], 1)
+    multiply(steps - 1)
+    warp_chunk(0, chunks, cores, source_ref, valid_ref, tiles, dose, outs)
+
+
+def first_forward(scalars, tile_index, matrix, warp_tiles, pieces, rows, vox, masks):
+    height, width = warp_tiles.shape[1:]
+    vox_rows, spots = matrix.shape
+    plans = pieces[0].shape[-1]
+    cores = core_count()
+    count = vox_rows // height
+    step = 2 * height
+    out = jax.ShapeDtypeStruct((vox // cores, CAP, height // CHUNKS, plans), F32)
+    terms = jax.ShapeDtypeStruct(matrix.shape, BF16)
+    outs = [out] * cores + [
+        jax.ShapeDtypeStruct((vox_rows, plans), F32),
+        terms,
+        terms,
+        jax.ShapeDtypeStruct((count, height, 2 * width), BF16),
+    ]
+    return pl.pallas_call(
+        functools.partial(first_body, (vox, masks, rows, len(pieces), CHUNKS, cores)),
+        in_specs=specs(4, pltpu.SMEM) + specs(2, pltpu.HBM) + specs(len(pieces), pltpu.VMEM),
+        out_specs=specs(len(outs), pltpu.VMEM),
+        out_shape=outs,
+        scratch_shapes=[
+            pltpu.VMEM((spots, 2 * plans), BF16),
+            pltpu.VMEM((vox_rows // step, step, spots), F32),
+            pltpu.VMEM((count, height, width), F32),
+            pltpu.SemaphoreType.DMA((vox_rows // step,)),
+            pltpu.SemaphoreType.DMA((count,)),
+        ],
+        compiler_params=pltpu.CompilerParams(vmem_limit_bytes=HUGE),
+        cost_estimate=BRIEF,
+        name="first_dose_and_warp",
+    )(*scalars, tile_index, matrix, warp_tiles, *pieces)
+
+
 def forward(scalars, terms, pieces, rows, vox, masks):
     big, small, tiles = terms
     height = tiles.shape[1]
     vox_rows, spots = big.shape
     plans = pieces[0].shape[-1]
     cores = core_count()
-    out = jax.ShapeDtypeStruct((cores, CAP, height // CHUNKS, plans), F32)
-    outs = [out] * (vox // cores) + [jax.ShapeDtypeStruct((vox_rows, plans), F32)]
+    out = jax.ShapeDtypeStruct((vox // cores, CAP, height // CHUNKS, plans), F32)
+    outs = [out] * cores + [jax.ShapeDtypeStruct((vox_rows, plans), F32)]
     return pl.pallas_call(
         functools.partial(forward_body, (vox, masks, rows, len(pieces), CHUNKS, cores)),
         in_specs=specs(3, pltpu.SMEM) + specs(3 + len(pieces), pltpu.VMEM),
@@ -165,9 +192,7 @@
         out_shape=outs,
         scratch_shapes=[pltpu.VMEM((spots, 2 * plans), BF16)],
         compiler_params=pltpu.CompilerParams(vmem_limit_bytes=LARGE),
-        cost_estimate=pl.CostEstimate(
-            flops=8 * big.size * plans, bytes_accessed=big.size * 4, transcendentals=0
-        ),
+        cost_estimate=BRIEF,
         name="dose_and_warp",
     )(*scalars, *terms, *pieces)
 
@@ -179,43 +204,34 @@
 def forward_later(h, scalars, tiles, dose, after, vox):
     height = tiles.shape[1]
     cores = core_count()
-    out = jax.ShapeDtypeStruct((cores, CAP, height // CHUNKS, dose.shape[1]), F32)
+    out = jax.ShapeDtypeStruct((vox // cores, CAP, height // CHUNKS, dose.shape[1]), F32)
     return pl.pallas_call(
         functools.partial(later_body, h, CHUNKS, cores),
         in_specs=specs(2, pltpu.SMEM) + specs(2, pltpu.VMEM) + specs(1, pl.ANY),
-        out_specs=specs(vox // cores, pltpu.VMEM),
-        out_shape=[out] * (vox // cores),
+        out_specs=specs(cores, pltpu.VMEM),
+        out_shape=[out] * cores,
         compiler_params=pltpu.CompilerParams(vmem_limit_bytes=SMALL),
+        cost_estimate=BRIEF,
         name="warp_later",
     )(*scalars[:2], tiles, dose, after)
 
 
-def piece(arrived, across, cores, m):
-    k, c = m // cores, m % cores
-    return arrived[k].at[0] if c == 0 else across[(c - 1) * len(arrived) + k]
+def piece(arrived, cores, m):
+    return arrived[m // cores].at[m % cores]
 
 
 def gradient_body(dims, source_ref, valid_ref, me_ref, big, small, tiles, *refs):
     vox, masks, rows, cores, chunks = dims
     chips = vox // cores
-    each = chips * cores
-    returned = refs[: each * chunks]
-    outs = refs[each * chunks : -2]
+    returned = refs[: chips * chunks]
+    outs = refs[chips * chunks : -2]
     columns, turned = refs[-2:]
     height = tiles.shape[1]
     plans = turned.shape[1]
     vox_rows, spots = big.shape
     spare = vox_rows // height
     for m in range(vox):
-        found = [
-            piece(
-                returned[h * each : h * each + chips],
-                returned[h * each + chips : (h + 1) * each],
-                cores,
-                m,
-            )
-            for h in range(chunks)
-        ]
+        found = [piece(returned[h * chips : (h + 1) * chips], cores, m) for h in range(chunks)]
         for j in range(CAP):
             s = m * CAP + j
             b = source_ref[s]
@@ -266,20 +282,17 @@
             pltpu.VMEM((spots, plans), F32),
         ],
         compiler_params=pltpu.CompilerParams(vmem_limit_bytes=LARGE),
-        cost_estimate=pl.CostEstimate(
-            flops=8 * big.size * plans, bytes_accessed=big.size * 4, transcendentals=0
-        ),
+        cost_estimate=BRIEF,
         name="warp_back_and_gradient",
     )(*scalars, *terms, *returned)
 
 
 def place_body(vox, cores, which_ref, slot_ref, *refs):
     chips = vox // cores
-    arrived, across = refs[:chips], refs[chips:vox]
-    give, keep, total = refs[vox:]
+    arrived, (give, keep, total) = refs[:chips], refs[chips:]
     total[...] = jnp.zeros_like(total)
     for m in range(vox):
-        blocks = piece(arrived, across, cores, m)
+        blocks = piece(arrived, cores, m)
         for j in range(CAP):
             slot = slot_ref[m * CAP + j]
 
@@ -294,16 +307,18 @@
 
 
 def place(which, slots, incoming, blocks):
-    vox = len(incoming)
+    cores = core_count()
+    vox = len(incoming) * cores
     height, plans = incoming[0].shape[-2:]
     half = jax.ShapeDtypeStruct((blocks // 2, height, plans), F32)
     return pl.pallas_call(
-        functools.partial(place_body, vox, core_count()),
-        in_specs=specs(2, pltpu.SMEM) + specs(vox, pltpu.VMEM),
+        functools.partial(place_body, vox, cores),
+        in_specs=specs(2, pltpu.SMEM) + specs(len(incoming), pltpu.VMEM),
         out_specs=specs(2, pltpu.VMEM),
         out_shape=[half, half],
         scratch_shapes=[pltpu.VMEM((blocks, height, plans), F32)],
         compiler_params=pltpu.CompilerParams(vmem_limit_bytes=SMALL),
+        cost_estimate=BRIEF,
         name="place_blocks",
     )(which, slots, *incoming)
 
@@ -317,15 +332,15 @@
     for m in range(vox):
         for j in range(CAP):
             slot = jnp.maximum(slot_ref[m * CAP + j], 0)
-            refs[m // cores][m % cores, j] = scale[slot] * (field[slot] - goal[slot])
+            refs[m % cores][m // cores, j] = scale[slot] * (field[slot] - goal[slot])
     if with_dose:
-        refs[vox // cores][...] = field[...]
+        refs[cores][...] = field[...]
 
 
 def pull(which, slots, mine, other, goal, scale, vox, with_dose):
     half, height, plans = mine.shape
     cores = core_count()
-    outs = [jax.ShapeDtypeStruct((cores, CAP, height, plans), F32)] * (vox // cores)
+    outs = [jax.ShapeDtypeStruct((vox // cores, CAP, height, plans), F32)] * cores
     if with_dose:
         outs = outs + [jax.ShapeDtypeStruct((2 * half, height, plans), F32)]
     return pl.pallas_call(
@@ -335,6 +350,7 @@
         out_shape=outs,
         scratch_shapes=[pltpu.VMEM((2 * half, height, plans), F32)],
         compiler_params=pltpu.CompilerParams(vmem_limit_bytes=SMALL),
+        cost_estimate=BRIEF,
         name="adjoint_blocks",
     )(which, slots, mine, other, goal, scale)
 
@@ -378,9 +394,10 @@
 
 
 def exchange(pieces):
-    cores = core_count()
-    arrived = [pieces[0]] + [swap(pieces[k], VOX, k * cores) for k in range(1, len(pieces))]
-    return arrived + [swap(a[c], VOX, c) for c in range(1, cores) for a in arrived]
+    cores = len(pieces)
+    crossed = [pieces[0]] + [swap(pieces[c], VOX, c) for c in range(1, cores)]
+    chips = [jnp.stack([p[k] for p in crossed]) for k in range(pieces[0].shape[0])]
+    return [chips[0]] + [swap(chips[k], VOX, k * cores) for k in range(1, len(chips))]
 
 
 def phase_halves(give, keep):
@@ -451,7 +468,6 @@
     scales = [scales[:, h] for h in range(CHUNKS)]
 
     masks = combined(phase_steps())
-    terms = split_terms(tile_index[0], matrix, warp_tiles, local_blocks)
     held = jnp.concatenate(spread(weights, PHASE, masks[1:]), axis=0)
     for iteration in range(ITERS):
         last = iteration == ITERS - 1
@@ -472,7 +488,13 @@
             back_to = jnp.asarray([masks.index(p) for p in range(phases)], jnp.int32)
             every = every[jnp.arange(vox) ^ me_vox][:, back_to[jnp.arange(phases) ^ me_phase]]
             pieces = [every.transpose(1, 0, 2, 3).reshape(spots, plans)]
-        *outgoing, block_dose = forward(scalars, terms, pieces, rows, vox, masks)
+        if iteration == 0:
+            *outgoing, block_dose, big, small, own_tiles = first_forward(
+                scalars, tile_index[0], matrix, warp_tiles, pieces, rows, vox, masks
+            )
+            terms = (big, small, own_tiles)
+        else:
+            *outgoing, block_dose = forward(scalars, terms, pieces, rows, vox, masks)
         returned, dose = [], []
         for h in range(CHUNKS):
             if h > 0:
@@ -480,8 +502,8 @@
             give, keep = place(which, received, exchange(outgoing), local_blocks)
             mine, other = phase_halves(give, keep)
             back = pull(which, received, mine, other, goals[h], scales[h], vox, last)
-            returned += exchange(back[: vox // cores])
-            dose += back[vox // cores :]
+            returned += exchange(back[:cores])
+            dose += back[cores:]
         parts = gradient_parts(scalars, terms, returned, rows, vox, masks)
         if rows % 8:
             parts = parts[0].reshape(phases, vox, rows, plans)

time: 274 us -> 243 us (0.89)
  starting transfers between devices: 93.7 us -> 80.3 us
  waiting for transfers between devices: 118 us -> 106 us
  local copies, waits for them, and re-layouts: 19.6 us -> 12.6 us
    ppermute x92 -> x68, starting transfers between devices: 93.7 us -> 80.3 us  [swap(): return lax.ppermute(x, axis, [(i, i ^ mask) for i in range(count)])]
    ppermute x92 -> x68, waiting for transfers between devices: 118 us -> 106 us  [swap(): return lax.ppermute(x, axis, [(i, i ^ mask) for i in range(count)])]
    pallas_call x5, Pallas kernels: 9.4 us -> 15.3 us  [the longest x1 11.9 us: first_forward(): pl.pallas_call(functools.partial(first_body, (vox, masks, rows, len(piece...]
    unnamed x60 -> x42, local copies, waits for them, and re-layouts: 12.6 us -> 7.14 us
    pallas_call x2 -> x1, Pallas kernels: 8.97 us -> 4.48 us  [forward(): pl.pallas_call(functools.partial(forward_body, (vox, masks, rows, len(pie...]
  transfers between devices with their start and end apart: 92 -> 68, of which waited for: 58 -> 50; matrix products, arithmetic and copies ran while one was open for 6% -> 5% of each run, Pallas kernels for 4% -> 2%
where the time goes in v5:
time: 243 us; the launch traced here: 242 us
  waiting for transfers between devices  106 us (44%)
  starting transfers between devices  80.3 us (33%)
  Pallas kernels  33.4 us (14%)
  local copies, waits for them, and re-layouts  12.6 us (5%)
  other arithmetic  5.19 us (2%)
  matrix products  3.11 us (1%)
    ppermute x68, waiting for transfers between devices, swap(): return lax.ppermute(x, axis, [(i, i ^ mask) for i in range(count)])  106 us
    ppermute x68, starting transfers between devices, swap(): return lax.ppermute(x, axis, [(i, i ^ mask) for i in range(count)])  80.3 us
    pallas_call x1, Pallas kernels, first_forward(): pl.pallas_call(functools.partial(first_body, (vox, masks, rows, len(piece...  11.9 us
    pallas_call x2, Pallas kernels, gradient_parts(): pl.pallas_call(functools.partial(gradient_body, (vox, masks, rows, cores,...  8.21 us
    unnamed x42, local copies, waits for them, and re-layouts  7.14 us
  transfers between devices with their start and end apart: 68, of which 50 were waited for; matrix products, arithmetic and copies ran while one was open for 5% of the time, Pallas kernels for 2%

profile of v5, /device:TPU:0, one launch (start us, length us, event | category | flops | bytes accessed | tf_op | source)
XLA Modules:
  0.0 242.4 jit_solution(3884751262936634850)
XLA Ops:
  0.6 3.1 %collective-permute-start = (f32[48,128]{1,0:T(8,128)}, f32[48,128]{1,0:T(8,128)S(1)}, u32[]{:S(2)}, u32[]{:S(2)}) collective-permute-start(f32[48,128]{1,0:T(8,128)} %param.15), channel_id=1, source_target_pairs={{0,8},{8,0},{16,24},{24,16},{1,9},{9,1},{17,25},{25,17},{2,10},{10... | collective-permute-start | bytes 73736 | tf_op jit(solution)/shard_map/ppermute | solution.py:29
  3.7 2.5 %collective-permute-start.1 = (f32[48,128]{1,0:T(8,128)}, f32[48,128]{1,0:T(8,128)S(1)}, u32[]{:S(2)}, u32[]{:S(2)}) collective-permute-start(f32[48,128]{1,0:T(8,128)} %param.15), channel_id=1, source_target_pairs={{0,24},{8,16},{16,8},{24,0},{1,25},{9,17},{17,9},{25,1},{2,26},{10... | collective-permute-start | bytes 73736 | tf_op jit(solution)/shard_map/ppermute | solution.py:29
  9.9 1.5 collective-permute-done.2
  11.4 1.5 collective-permute-start.3
  12.9 1.5 collective-permute-start.4
  15.6 1.7 collective-permute-done.3
  18.4 1.6 collective-permute-done.5
  20.4 2.4 fusion.1
  23.9 11.9 %first_dose_and_warp.1 = (f32[4,2,64,128]{3,2,1,0:T(8,128)S(1)}, f32[4,2,64,128]{3,2,1,0:T(8,128)S(1)}, f32[2048,128]{1,0:T(8,128)S(1)}, bf16[2048,1536]{1,0:T(8...) custom-call(s32[16]{0:T(128)S(1)} %get-tuple-element.97.source_ref, ...), custom_call_target="tpu_custom_call" | custom-call | flops 1 | bytes 1 | tf_op jit(solution)/shard_map/first_dose_and_warp/pallas_call | solution.py:162
  35.8 2.7 %copy-done.2 = bf16[2048,1536]{1,0:T(8,128)(2,1)} copy-done((bf16[2048,1536]{1,0:T(8,128)(2,1)}, bf16[2048,1536]{1,0:T(8,128)(2,1)S(1)}, u32[]{:S(2)}) %copy-start.2) | copy-done | bytes 6291480
  41.7 1.6 collective-permute-start.9
  43.3 1.6 collective-permute-start.8
  45.1 3.4 %collective-permute-done.10.refs_3_ = f32[2,2,64,128]{3,2,1,0:T(8,128)S(1)} collective-permute-done((f32[2,2,64,128]{3,2,1,0:T(8,128)S(1)}, f32[2,2,64,128]{3,2,1,0:T(8,128)S(1)}, u32[]{:S(2)}, u32[]{:S(2)}) %collective-permute-start.10) | collective-permute-done | bytes 131104 | tf_op jit(solution)/shard_map/ppermute | solution.py:29
  48.5 1.6 collective-permute-done.9.refs_2_
  52.2 1.7 warp_later.2
  59.1 1.5 collective-permute-start.20
  61.5 2.8 %collective-permute-done.11 = f32[8,64,128]{2,1,0:T(8,128)S(1)} collective-permute-done((f32[8,64,128]{2,1,0:T(8,128)}, f32[8,64,128]{2,1,0:T(8,128)S(1)}, u32[]{:S(2)}, u32[]{:S(2)}) %collective-permute-start.11) | collective-permute-done | bytes 262176 | tf_op jit(solution)/shard_map/ppermute | solution.py:29
  65.6 1.6 collective-permute-done.20.refs_2_
  68.2 1.6 collective-permute-start.22
  69.8 5.7 %collective-permute-done.12 = f32[8,64,128]{2,1,0:T(8,128)S(1)} collective-permute-done((f32[8,64,128]{2,1,0:T(8,128)S(1)}, f32[8,64,128]{2,1,0:T(8,128)S(1)}, u32[]{:S(2)}, u32[]{:S(2)}) %collective-permute-start.12) | collective-permute-done | bytes 262176 | tf_op jit(solution)/shard_map/ppermute | solution.py:29
  75.5 3.1 %collective-permute-start.13 = (f32[8,64,128]{2,1,0:T(8,128)S(1)}, f32[8,64,128]{2,1,0:T(8,128)S(1)}, u32[]{:S(2)}, u32[]{:S(2)}) collective-permute-start(f32[8,64,128]{2,1,0:T(8,128)S(1)} %add.112.mine), channel_id=1, source_target_pairs={{0,8},{8,0},{16,24},{24,16},{1,9},{9,1},{17,25},{25,17},{2,10},{10... | collective-permute-start | bytes 786440 | tf_op jit(solution)/shard_map/ppermute | solution.py:29
  80.0 2.0 collective-permute-start.23
  82.0 4.5 %collective-permute-done.13.other = f32[8,64,128]{2,1,0:T(8,128)S(1)} collective-permute-done((f32[8,64,128]{2,1,0:T(8,128)S(1)}, f32[8,64,128]{2,1,0:T(8,128)S(1)}, u32[]{:S(2)}, u32[]{:S(2)}) %collective-permute-start.13) | collective-permute-done | bytes 262176 | tf_op jit(solution)/shard_map/ppermute | solution.py:29
  87.5 4.0 %collective-permute-done.23 = f32[8,64,128]{2,1,0:T(8,128)S(1)} collective-permute-done((f32[8,64,128]{2,1,0:T(8,128)S(1)}, f32[8,64,128]{2,1,0:T(8,128)S(1)}, u32[]{:S(2)}, u32[]{:S(2)}) %collective-permute-start.23) | collective-permute-done | bytes 262176 | tf_op jit(solution)/shard_map/ppermute | solution.py:29
  91.5 2.0 collective-permute-start.24
  94.8 1.5 collective-permute-start.16
  96.3 2.3 collective-permute-done.24.other
  102.4 1.4 collective-permute-start.27
  105.9 3.5 %collective-permute-done.28.refs_7_ = f32[2,2,64,128]{3,2,1,0:T(8,128)S(1)} collective-permute-done((f32[2,2,64,128]{3,2,1,0:T(8,128)S(1)}, f32[2,2,64,128]{3,2,1,0:T(8,128)S(1)}, u32[]{:S(2)}, u32[]{:S(2)}) %collective-permute-start.28) | collective-permute-done | bytes 131104 | tf_op jit(solution)/shard_map/ppermute | solution.py:29
  111.2 4.1 %warp_back_and_gradient.2 = (f32[4,192,128]{2,1,0:T(8,128)S(1)}, f32[4,192,128]{2,1,0:T(8,128)S(1)}) custom-call(s32[16]{0:T(128)S(1)} %get-tuple-element.97.source_ref, s32[16]{0:T(128)S(1)} %get-tuple-element.96.valid_ref, s32[2]{0:T(128)S(1)} %pad_add_fusion.me_ref, bf16[2048,1536]{1,0:T(8,128)(2,1)S(1)} %bitcast.90, bf16[2048,1536]{1,0:T(8,128)(2,1)S(1)} %bitcast.92, ...), custom_call_target="tpu_custom_call" | custom-call | flops 1 | bytes 1 | tf_op jit(solution)/shard_map/warp_back_and_gradient/pallas_call | solution.py:276
  115.4 1.7 collective-permute-done.29
  119.0 1.7 collective-permute-start.32
  122.1 3.1 %collective-permute-done.31 = f32[192,128]{1,0:T(8,128)S(1)} collective-permute-done((f32[192,128]{1,0:T(8,128)S(1)}, f32[192,128]{1,0:T(8,128)S(1)}, u32[]{:S(2)}, u32[]{:S(2)}) %collective-permute-start.31) | collective-permute-done | bytes 98336 | tf_op jit(solution)/shard_map/ppermute | solution.py:29
  125.2 1.8 collective-permute-start.33
  127.0 2.9 %collective-permute-done.33 = f32[4,48,128]{2,1,0:T(8,128)S(1)} collective-permute-done((f32[4,48,128]{2,1,0:T(8,128)S(1)}, f32[4,48,128]{2,1,0:T(8,128)S(1)}, u32[]{:S(2)}, u32[]{:S(2)}) %collective-permute-start.33) | collective-permute-done | bytes 98336 | tf_op jit(solution)/shard_map/ppermute | solution.py:29
  131.1 5.4 %collective-permute-done.34 = f32[4,48,128]{2,1,0:T(8,128)S(1)} collective-permute-done((f32[4,48,128]{2,1,0:T(8,128)S(1)}, f32[4,48,128]{2,1,0:T(8,128)S(1)}, u32[]{:S(2)}, u32[]{:S(2)}) %collective-permute-start.34) | collective-permute-done | bytes 98336 | tf_op jit(solution)/shard_map/ppermute | solution.py:29
  138.7 1.4 collective-permute-start.37
  142.0 2.2 collective-permute-done.37
  144.3 1.7 collective-permute-done.38.refs_1_
  146.1 4.5 %dose_and_warp.1 = (f32[4,2,64,128]{3,2,1,0:T(8,128)S(1)}, f32[4,2,64,128]{3,2,1,0:T(8,128)S(1)}, f32[2048,128]{1,0:T(8,128)S(1)}) custom-call(s32[16]{0:T(128)S(1)} %get-tuple-element.97.source_ref, s32[16]{0:T(128)S(1)} %get-tuple-element.96.valid_ref, s32[2]{0:T(128)S(1)} %pad_add_fusion.me_ref, bf16[2048,1536]{1,0:T(8,128)(2,1)S(1)} %bitcast.90, ...), custom_call_target="tpu_custom_call" | custom-call | flops 1 | bytes 1 | tf_op jit(solution)/shard_map/dose_and_warp/pallas_call | solution.py:188
  152.2 1.5 collective-permute-start.42
  155.9 3.6 %collective-permute-done.42.refs_3_ = f32[2,2,64,128]{3,2,1,0:T(8,128)S(1)} collective-permute-done((f32[2,2,64,128]{3,2,1,0:T(8,128)S(1)}, f32[2,2,64,128]{3,2,1,0:T(8,128)S(1)}, u32[]{:S(2)}, u32[]{:S(2)}) %collective-permute-start.42) | collective-permute-done | bytes 131104 | tf_op jit(solution)/shard_map/ppermute | solution.py:29
  159.5 2.0 collective-permute-done.41.refs_2_
  164.9 1.5 collective-permute-start.53
  166.4 5.7 %collective-permute-done.43 = f32[8,64,128]{2,1,0:T(8,128)S(1)} collective-permute-done((f32[8,64,128]{2,1,0:T(8,128)S(1)}, f32[8,64,128]{2,1,0:T(8,128)S(1)}, u32[]{:S(2)}, u32[]{:S(2)}) %collective-permute-start.43) | collective-permute-done | bytes 262176 | tf_op jit(solution)/shard_map/ppermute | solution.py:29
  175.4 3.0 %collective-permute-done.52.refs_2_ = f32[2,2,64,128]{3,2,1,0:T(8,128)S(1)} collective-permute-done((f32[2,2,64,128]{3,2,1,0:T(8,128)S(1)}, f32[2,2,64,128]{3,2,1,0:T(8,128)S(1)}, u32[]{:S(2)}, u32[]{:S(2)}) %collective-permute-start.52) | collective-permute-done | bytes 131104 | tf_op jit(solution)/shard_map/ppermute | solution.py:29
  180.4 1.6 collective-permute-done.44
  182.0 4.5 %collective-permute-start.45 = (f32[8,64,128]{2,1,0:T(8,128)S(1)}, f32[8,64,128]{2,1,0:T(8,128)S(1)}, u32[]{:S(2)}, u32[]{:S(2)}) collective-permute-start(f32[8,64,128]{2,1,0:T(8,128)S(1)} %add.123.mine), channel_id=1, source_target_pairs={{0,8},{8,0},{16,24},{24,16},{1,9},{9,1},{17,25},{25,17},{2,10},{10... | collective-permute-start | bytes 786440 | tf_op jit(solution)/shard_map/ppermute | solution.py:29
  186.5 2.4 collective-permute-done.54
  188.9 2.5 %collective-permute-start.55 = (f32[8,64,128]{2,1,0:T(8,128)S(1)}, f32[8,64,128]{2,1,0:T(8,128)S(1)}, u32[]{:S(2)}, u32[]{:S(2)}) collective-permute-start(f32[8,64,128]{2,1,0:T(8,128)S(1)} %add.124), channel_id=1, source_target_pairs={{0,24},{8,16},{16,8},{24,0},{1,25},{9,17},{17,9},{25,1},{2,26},{10... | collective-permute-start | bytes 786440 | tf_op jit(solution)/shard_map/ppermute | solution.py:29
  191.4 3.5 %collective-permute-done.45.other = f32[8,64,128]{2,1,0:T(8,128)S(1)} collective-permute-done((f32[8,64,128]{2,1,0:T(8,128)S(1)}, f32[8,64,128]{2,1,0:T(8,128)S(1)}, u32[]{:S(2)}, u32[]{:S(2)}) %collective-permute-start.45) | collective-permute-done | bytes 262176 | tf_op jit(solution)/shard_map/ppermute | solution.py:29
  195.7 3.2 %collective-permute-done.55 = f32[8,64,128]{2,1,0:T(8,128)S(1)} collective-permute-done((f32[8,64,128]{2,1,0:T(8,128)S(1)}, f32[8,64,128]{2,1,0:T(8,128)S(1)}, u32[]{:S(2)}, u32[]{:S(2)}) %collective-permute-start.55) | collective-permute-done | bytes 262176 | tf_op jit(solution)/shard_map/ppermute | solution.py:29
  199.0 1.6 collective-permute-start.56
  203.2 2.4 collective-permute-done.56.other
  206.3 1.5 collective-permute-start.47
  207.9 2.0 collective-permute-start.60
  212.6 4.3 %collective-permute-done.60.refs_7_ = f32[2,2,64,128]{3,2,1,0:T(8,128)S(1)} collective-permute-done((f32[2,2,64,128]{3,2,1,0:T(8,128)S(1)}, f32[2,2,64,128]{3,2,1,0:T(8,128)S(1)}, u32[]{:S(2)}, u32[]{:S(2)}) %collective-permute-start.60) | collective-permute-done | bytes 131104 | tf_op jit(solution)/shard_map/ppermute | solution.py:29
  218.1 4.1 %warp_back_and_gradient.3 = (f32[4,192,128]{2,1,0:T(8,128)S(1)}, f32[4,192,128]{2,1,0:T(8,128)S(1)}) custom-call(s32[16]{0:T(128)S(1)} %get-tuple-element.97.source_ref, s32[16]{0:T(128)S(1)} %get-tuple-element.96.valid_ref, s32[2]{0:T(128)S(1)} %pad_add_fusion.me_ref, bf16[2048,1536]{1,0:T(8,128)(2,1)S(1)} %bitcast.90, bf16[2048,1536]{1,0:T(8,128)(2,1)S(1)} %bitcast.94, ...), custom_call_target="tpu_custom_call" | custom-call | flops 1 | bytes 1 | tf_op jit(solution)/shard_map/warp_back_and_gradient/pallas_call | solution.py:276
  222.3 1.7 collective-permute-done.61
  226.2 1.5 collective-permute-start.64
  229.0 1.8 collective-permute-done.63
  230.8 1.5 collective-permute-done.64
  233.3 3.7 %collective-permute-start.66 = (f32[48,128]{1,0:T(8,128)S(1)}, f32[48,128]{1,0:T(8,128)S(1)}, u32[]{:S(2)}, u32[]{:S(2)}) collective-permute-start(f32[48,128]{1,0:T(8,128)S(1)} %get-tuple-element.176), channel_id=1, source_target_pairs={{0,24},{8,16},{16,8},{24,0},{1,25},{9,17},{17,9},{25,1},{2,26},{10... | collective-permute-start | bytes 73736 | tf_op jit(solution)/shard_map/ppermute | solution.py:29
  239.1 2.6 %collective-permute-done.67 = f32[48,128]{1,0:T(8,128)S(1)} collective-permute-done((f32[48,128]{1,0:T(8,128)S(1)}, f32[48,128]{1,0:T(8,128)S(1)}, u32[]{:S(2)}, u32[]{:S(2)}) %collective-permute-start.67) | collective-permute-done | bytes 24608 | tf_op jit(solution)/shard_map/ppermute | solution.py:29
  (230 shorter events, 69.4 us)
Async XLA Ops:
  0.6 8.8 %collective-permute-start = (f32[48,128]{1,0:T(8,128)}, f32[48,128]{1,0:T(8,128)S(1)}, u32[]{:S(2)}, u32[]{:S(2)}) collective-permute-start(f32[48,128]{1,0:T(8,128)} %param.15), channel_id=1, source_target_pairs={{0,8},{8,0},{16,24},{24,16},{1,9},{9,1},{17,25},{25,17},{2,10},{10... | collective-permute-start | bytes 73736 | tf_op jit(solution)/shard_map/ppermute | solution.py:29
  3.7 6.2 %collective-permute-start.1 = (f32[48,128]{1,0:T(8,128)}, f32[48,128]{1,0:T(8,128)S(1)}, u32[]{:S(2)}, u32[]{:S(2)}) collective-permute-start(f32[48,128]{1,0:T(8,128)} %param.15), channel_id=1, source_target_pairs={{0,24},{8,16},{16,8},{24,0},{1,25},{9,17},{17,9},{25,1},{2,26},{10... | collective-permute-start | bytes 73736 | tf_op jit(solution)/shard_map/ppermute | solution.py:29
  6.2 5.2 %collective-permute-start.2 = (f32[48,128]{1,0:T(8,128)}, f32[48,128]{1,0:T(8,128)S(1)}, u32[]{:S(2)}, u32[]{:S(2)}) collective-permute-start(f32[48,128]{1,0:T(8,128)} %param.15), channel_id=1, source_target_pairs={{0,16},{8,24},{16,0},{24,8},{1,17},{9,25},{17,1},{25,9},{2,18},{10... | collective-permute-start | bytes 73736 | tf_op jit(solution)/shard_map/ppermute | solution.py:29
  11.4 5.8 %collective-permute-start.3 = (f32[208,128]{1,0:T(8,128)S(1)}, f32[208,128]{1,0:T(8,128)S(1)}, u32[]{:S(2)}, u32[]{:S(2)}) collective-permute-start(f32[208,128]{1,0:T(8,128)S(1)} %constant_dynamic-update-slice_fusion), channel_id=1, source_target_pairs={{0,2},{1,3},{2,0},{3,1},{4,6},{5,7},{6,4},{7,5},{8,10},{9,11},{10,... | collective-permute-start | bytes 319496 | tf_op jit(solution)/shard_map/ppermute | solution.py:29
  12.9 5.5 %collective-permute-start.4 = (f32[208,128]{1,0:T(8,128)S(1)}, f32[208,128]{1,0:T(8,128)S(1)}, u32[]{:S(2)}, u32[]{:S(2)}) collective-permute-start(f32[208,128]{1,0:T(8,128)S(1)} %constant_dynamic-update-slice_fusion), channel_id=1, source_target_pairs={{0,4},{1,5},{2,6},{3,7},{4,0},{5,1},{6,2},{7,3},{8,12},{9,13},{10,... | collective-permute-start | bytes 319496 | tf_op jit(solution)/shard_map/ppermute | solution.py:29
  14.4 5.6 %collective-permute-start.5 = (f32[208,128]{1,0:T(8,128)S(1)}, f32[208,128]{1,0:T(8,128)S(1)}, u32[]{:S(2)}, u32[]{:S(2)}) collective-permute-start(f32[208,128]{1,0:T(8,128)S(1)} %constant_dynamic-update-slice_fusion), channel_id=1, source_target_pairs={{0,6},{1,7},{2,4},{3,5},{4,2},{5,3},{6,0},{7,1},{8,14},{9,15},{10,... | collective-permute-start | bytes 319496 | tf_op jit(solution)/shard_map/ppermute | solution.py:29
  20.1 2.7 %collective-permute-start.6 = (f32[4,208,128]{2,1,0:T(8,128)S(1)}, f32[4,208,128]{2,1,0:T(8,128)S(1)}, u32[]{:S(2)}, u32[]{:S(2)}) collective-permute-start(f32[4,208,128]{2,1,0:T(8,128)S(1)} %get-tuple-element.103.refs_0_), channel_id=1, source_target_pairs={{0,1},{1,0},{2,3},{3,2},{4,5},{5,4},{6,7},{7,6},{8,9},{9,8},{10,11... | collective-permute-start | bytes 1277960 | tf_op jit(solution)/shard_map/ppermute | solution.py:29
  39.4 1.7 collective-permute-start.7
  41.1 7.3 %collective-permute-start.10 = (f32[2,2,64,128]{3,2,1,0:T(8,128)S(1)}, f32[2,2,64,128]{3,2,1,0:T(8,128)S(1)}, u32[]{:S(2)}, u32[]{:S(2)}) collective-permute-start(f32[2,2,64,128]{3,2,1,0:T(8,128)S(1)} %pad_maximum_fusion.7), channel_id=1, source_target_pairs={{0,6},{1,7},{2,4},{3,5},{4,2},{5,3},{6,0},{7,1},{8,14},{9,15},{10,... | collective-permute-start | bytes 393224 | tf_op jit(solution)/shard_map/ppermute | solution.py:29
  41.7 8.4 %collective-permute-start.9 = (f32[2,2,64,128]{3,2,1,0:T(8,128)S(1)}, f32[2,2,64,128]{3,2,1,0:T(8,128)S(1)}, u32[]{:S(2)}, u32[]{:S(2)}) collective-permute-start(f32[2,2,64,128]{3,2,1,0:T(8,128)S(1)} %pad_maximum_fusion.6), channel_id=1, source_target_pairs={{0,4},{1,5},{2,6},{3,7},{4,0},{5,1},{6,2},{7,3},{8,12},{9,13},{10,... | collective-permute-start | bytes 393224 | tf_op jit(solution)/shard_map/ppermute | solution.py:29
  43.3 6.8 %collective-permute-start.8 = (f32[2,2,64,128]{3,2,1,0:T(8,128)S(1)}, f32[2,2,64,128]{3,2,1,0:T(8,128)S(1)}, u32[]{:S(2)}, u32[]{:S(2)}) collective-permute-start(f32[2,2,64,128]{3,2,1,0:T(8,128)S(1)} %pad_maximum_fusion.5), channel_id=1, source_target_pairs={{0,2},{1,3},{2,0},{3,1},{4,6},{5,7},{6,4},{7,5},{8,10},{9,11},{10,... | collective-permute-start | bytes 393224 | tf_op jit(solution)/shard_map/ppermute | solution.py:29
  54.5 2.3 collective-permute-start.18
  55.4 9.0 %collective-permute-start.11 = (f32[8,64,128]{2,1,0:T(8,128)}, f32[8,64,128]{2,1,0:T(8,128)S(1)}, u32[]{:S(2)}, u32[]{:S(2)}) collective-permute-start(f32[8,64,128]{2,1,0:T(8,128)} %copy-done.6), channel_id=1, source_target_pairs={{0,8},{8,0},{16,24},{24,16},{1,9},{9,1},{17,25},{25,17},{2,10},{10... | collective-permute-start | bytes 786440 | tf_op jit(solution)/shard_map/ppermute | solution.py:29
  57.8 7.8 %collective-permute-start.21 = (f32[2,2,64,128]{3,2,1,0:T(8,128)S(1)}, f32[2,2,64,128]{3,2,1,0:T(8,128)S(1)}, u32[]{:S(2)}, u32[]{:S(2)}) collective-permute-start(f32[2,2,64,128]{3,2,1,0:T(8,128)S(1)} %pad_maximum_fusion.15), channel_id=1, source_target_pairs={{0,6},{1,7},{2,4},{3,5},{4,2},{5,3},{6,0},{7,1},{8,14},{9,15},{10,... | collective-permute-start | bytes 393224 | tf_op jit(solution)/shard_map/ppermute | solution.py:29
  59.1 8.1 %collective-permute-start.20 = (f32[2,2,64,128]{3,2,1,0:T(8,128)S(1)}, f32[2,2,64,128]{3,2,1,0:T(8,128)S(1)}, u32[]{:S(2)}, u32[]{:S(2)}) collective-permute-start(f32[2,2,64,128]{3,2,1,0:T(8,128)S(1)} %pad_maximum_fusion.14), channel_id=1, source_target_pairs={{0,4},{1,5},{2,6},{3,7},{4,0},{5,1},{6,2},{7,3},{8,12},{9,13},{10,... | collective-permute-start | bytes 393224 | tf_op jit(solution)/shard_map/ppermute | solution.py:29
  60.6 6.6 %collective-permute-start.19 = (f32[2,2,64,128]{3,2,1,0:T(8,128)S(1)}, f32[2,2,64,128]{3,2,1,0:T(8,128)S(1)}, u32[]{:S(2)}, u32[]{:S(2)}) collective-permute-start(f32[2,2,64,128]{3,2,1,0:T(8,128)S(1)} %pad_maximum_fusion.13), channel_id=1, source_target_pairs={{0,2},{1,3},{2,0},{3,1},{4,6},{5,7},{6,4},{7,5},{8,10},{9,11},{10,... | collective-permute-start | bytes 393224 | tf_op jit(solution)/shard_map/ppermute | solution.py:29
  64.4 11.1 %collective-permute-start.12 = (f32[8,64,128]{2,1,0:T(8,128)S(1)}, f32[8,64,128]{2,1,0:T(8,128)S(1)}, u32[]{:S(2)}, u32[]{:S(2)}) collective-permute-start(f32[8,64,128]{2,1,0:T(8,128)S(1)} %add.111), channel_id=1, source_target_pairs={{0,24},{8,16},{16,8},{24,0},{1,25},{9,17},{17,9},{25,1},{2,26},{10... | collective-permute-start | bytes 786440 | tf_op jit(solution)/shard_map/ppermute | solution.py:29
  68.2 11.8 %collective-permute-start.22 = (f32[8,64,128]{2,1,0:T(8,128)S(1)}, f32[8,64,128]{2,1,0:T(8,128)S(1)}, u32[]{:S(2)}, u32[]{:S(2)}) collective-permute-start(f32[8,64,128]{2,1,0:T(8,128)S(1)} %get-tuple-element.74), channel_id=1, source_target_pairs={{0,8},{8,0},{16,24},{24,16},{1,9},{9,1},{17,25},{25,17},{2,10},{10... | collective-permute-start | bytes 786440 | tf_op jit(solution)/shard_map/ppermute | solution.py:29
  75.5 11.0 %collective-permute-start.13 = (f32[8,64,128]{2,1,0:T(8,128)S(1)}, f32[8,64,128]{2,1,0:T(8,128)S(1)}, u32[]{:S(2)}, u32[]{:S(2)}) collective-permute-start(f32[8,64,128]{2,1,0:T(8,128)S(1)} %add.112.mine), channel_id=1, source_target_pairs={{0,8},{8,0},{16,24},{24,16},{1,9},{9,1},{17,25},{25,17},{2,10},{10... | collective-permute-start | bytes 786440 | tf_op jit(solution)/shard_map/ppermute | solution.py:29
  80.0 11.5 %collective-permute-start.23 = (f32[8,64,128]{2,1,0:T(8,128)S(1)}, f32[8,64,128]{2,1,0:T(8,128)S(1)}, u32[]{:S(2)}, u32[]{:S(2)}) collective-permute-start(f32[8,64,128]{2,1,0:T(8,128)S(1)} %add.113), channel_id=1, source_target_pairs={{0,24},{8,16},{16,8},{24,0},{1,25},{9,17},{17,9},{25,1},{2,26},{10... | collective-permute-start | bytes 786440 | tf_op jit(solution)/shard_map/ppermute | solution.py:29
  87.4 6.1 %collective-permute-start.14 = (f32[4,2,64,128]{3,2,1,0:T(8,128)S(1)}, f32[4,2,64,128]{3,2,1,0:T(8,128)S(1)}, u32[]{:S(2)}, u32[]{:S(2)}) collective-permute-start(f32[4,2,64,128]{3,2,1,0:T(8,128)S(1)} %get-tuple-element.69), channel_id=1, source_target_pairs={{0,1},{1,0},{2,3},{3,2},{4,5},{5,4},{6,7},{7,6},{8,9},{9,8},{10,11... | collective-permute-start | bytes 786440 | tf_op jit(solution)/shard_map/ppermute | solution.py:29
  91.5 7.0 %collective-permute-start.24 = (f32[8,64,128]{2,1,0:T(8,128)S(1)}, f32[8,64,128]{2,1,0:T(8,128)S(1)}, u32[]{:S(2)}, u32[]{:S(2)}) collective-permute-start(f32[8,64,128]{2,1,0:T(8,128)S(1)} %add.114.mine), channel_id=1, source_target_pairs={{0,8},{8,0},{16,24},{24,16},{1,9},{9,1},{17,25},{25,17},{2,10},{10... | collective-permute-start | bytes 786440 | tf_op jit(solution)/shard_map/ppermute | solution.py:29
  93.5 10.3 %collective-permute-start.17 = (f32[2,2,64,128]{3,2,1,0:T(8,128)S(1)}, f32[2,2,64,128]{3,2,1,0:T(8,128)S(1)}, u32[]{:S(2)}, u32[]{:S(2)}) collective-permute-start(f32[2,2,64,128]{3,2,1,0:T(8,128)S(1)} %pad_maximum_fusion.11), channel_id=1, source_target_pairs={{0,6},{1,7},{2,4},{3,5},{4,2},{5,3},{6,0},{7,1},{8,14},{9,15},{10,... | collective-permute-start | bytes 393224 | tf_op jit(solution)/shard_map/ppermute | solution.py:29
  94.8 10.0 %collective-permute-start.16 = (f32[2,2,64,128]{3,2,1,0:T(8,128)S(1)}, f32[2,2,64,128]{3,2,1,0:T(8,128)S(1)}, u32[]{:S(2)}, u32[]{:S(2)}) collective-permute-start(f32[2,2,64,128]{3,2,1,0:T(8,128)S(1)} %pad_maximum_fusion.10), channel_id=1, source_target_pairs={{0,4},{1,5},{2,6},{3,7},{4,0},{5,1},{6,2},{7,3},{8,12},{9,13},{10,... | collective-permute-start | bytes 393224 | tf_op jit(solution)/shard_map/ppermute | solution.py:29
  99.5 6.4 %collective-permute-start.15 = (f32[2,2,64,128]{3,2,1,0:T(8,128)S(1)}, f32[2,2,64,128]{3,2,1,0:T(8,128)S(1)}, u32[]{:S(2)}, u32[]{:S(2)}) collective-permute-start(f32[2,2,64,128]{3,2,1,0:T(8,128)S(1)} %pad_maximum_fusion.9), channel_id=1, source_target_pairs={{0,2},{1,3},{2,0},{3,1},{4,6},{5,7},{6,4},{7,5},{8,10},{9,11},{10,... | collective-permute-start | bytes 393224 | tf_op jit(solution)/shard_map/ppermute | solution.py:29
  101.1 8.3 %collective-permute-start.28 = (f32[2,2,64,128]{3,2,1,0:T(8,128)S(1)}, f32[2,2,64,128]{3,2,1,0:T(8,128)S(1)}, u32[]{:S(2)}, u32[]{:S(2)}) collective-permute-start(f32[2,2,64,128]{3,2,1,0:T(8,128)S(1)} %pad_maximum_fusion.19), channel_id=1, source_target_pairs={{0,6},{1,7},{2,4},{3,5},{4,2},{5,3},{6,0},{7,1},{8,14},{9,15},{10,... | collective-permute-start | bytes 393224 | tf_op jit(solution)/shard_map/ppermute | solution.py:29
  102.4 8.2 %collective-permute-start.27 = (f32[2,2,64,128]{3,2,1,0:T(8,128)S(1)}, f32[2,2,64,128]{3,2,1,0:T(8,128)S(1)}, u32[]{:S(2)}, u32[]{:S(2)}) collective-permute-start(f32[2,2,64,128]{3,2,1,0:T(8,128)S(1)} %pad_maximum_fusion.18), channel_id=1, source_target_pairs={{0,4},{1,5},{2,6},{3,7},{4,0},{5,1},{6,2},{7,3},{8,12},{9,13},{10,... | collective-permute-start | bytes 393224 | tf_op jit(solution)/shard_map/ppermute | solution.py:29
  103.9 7.3 %collective-permute-start.26 = (f32[2,2,64,128]{3,2,1,0:T(8,128)S(1)}, f32[2,2,64,128]{3,2,1,0:T(8,128)S(1)}, u32[]{:S(2)}, u32[]{:S(2)}) collective-permute-start(f32[2,2,64,128]{3,2,1,0:T(8,128)S(1)} %pad_maximum_fusion.17), channel_id=1, source_target_pairs={{0,2},{1,3},{2,0},{3,1},{4,6},{5,7},{6,4},{7,5},{8,10},{9,11},{10,... | collective-permute-start | bytes 393224 | tf_op jit(solution)/shard_map/ppermute | solution.py:29
  115.3 1.8 collective-permute-start.29
  117.2 4.9 %collective-permute-start.30 = (f32[192,128]{1,0:T(8,128)S(1)}, f32[192,128]{1,0:T(8,128)S(1)}, u32[]{:S(2)}, u32[]{:S(2)}) collective-permute-start(f32[192,128]{1,0:T(8,128)S(1)} %get-tuple-element.107), channel_id=1, source_target_pairs={{0,2},{1,3},{2,0},{3,1},{4,6},{5,7},{6,4},{7,5},{8,10},{9,11},{10,... | collective-permute-start | bytes 294920 | tf_op jit(solution)/shard_map/ppermute | solution.py:29
  118.4 6.7 %collective-permute-start.31 = (f32[192,128]{1,0:T(8,128)S(1)}, f32[192,128]{1,0:T(8,128)S(1)}, u32[]{:S(2)}, u32[]{:S(2)}) collective-permute-start(f32[192,128]{1,0:T(8,128)S(1)} %get-tuple-element.109), channel_id=1, source_target_pairs={{0,4},{1,5},{2,6},{3,7},{4,0},{5,1},{6,2},{7,3},{8,12},{9,13},{10,... | collective-permute-start | bytes 294920 | tf_op jit(solution)/shard_map/ppermute | solution.py:29
  119.0 6.1 %collective-permute-start.32 = (f32[192,128]{1,0:T(8,128)S(1)}, f32[192,128]{1,0:T(8,128)S(1)}, u32[]{:S(2)}, u32[]{:S(2)}) collective-permute-start(f32[192,128]{1,0:T(8,128)S(1)} %get-tuple-element.108), channel_id=1, source_target_pairs={{0,6},{1,7},{2,4},{3,5},{4,2},{5,3},{6,0},{7,1},{8,14},{9,15},{10,... | collective-permute-start | bytes 294920 | tf_op jit(solution)/shard_map/ppermute | solution.py:29
  125.2 4.7 %collective-permute-start.33 = (f32[4,48,128]{2,1,0:T(8,128)S(1)}, f32[4,48,128]{2,1,0:T(8,128)S(1)}, u32[]{:S(2)}, u32[]{:S(2)}) collective-permute-start(f32[4,48,128]{2,1,0:T(8,128)S(1)} %bitcast.102), channel_id=1, source_target_pairs={{0,8},{8,0},{16,24},{24,16},{1,9},{9,1},{17,25},{25,17},{2,10},{10... | collective-permute-start | bytes 294920 | tf_op jit(solution)/shard_map/ppermute | solution.py:29
  129.9 6.6 %collective-permute-start.34 = (f32[4,48,128]{2,1,0:T(8,128)S(1)}, f32[4,48,128]{2,1,0:T(8,128)S(1)}, u32[]{:S(2)}, u32[]{:S(2)}) collective-permute-start(f32[4,48,128]{2,1,0:T(8,128)S(1)} %bitcast_add_fusion.1), channel_id=1, source_target_pairs={{0,24},{8,16},{16,8},{24,0},{1,25},{9,17},{17,9},{25,1},{2,26},{10... | collective-permute-start | bytes 294920 | tf_op jit(solution)/shard_map/ppermute | solution.py:29
  136.6 4.7 %collective-permute-start.35 = (f32[192,128]{1,0:T(8,128)S(1)}, f32[192,128]{1,0:T(8,128)S(1)}, u32[]{:S(2)}, u32[]{:S(2)}) collective-permute-start(f32[192,128]{1,0:T(8,128)S(1)} %fusion.10), channel_id=1, source_target_pairs={{0,2},{1,3},{2,0},{3,1},{4,6},{5,7},{6,4},{7,5},{8,10},{9,11},{10,... | collective-permute-start | bytes 294920 | tf_op jit(solution)/shard_map/ppermute | solution.py:29
  137.4 4.6 %collective-permute-start.36 = (f32[192,128]{1,0:T(8,128)S(1)}, f32[192,128]{1,0:T(8,128)S(1)}, u32[]{:S(2)}, u32[]{:S(2)}) collective-permute-start(f32[192,128]{1,0:T(8,128)S(1)} %fusion.10), channel_id=1, source_target_pairs={{0,4},{1,5},{2,6},{3,7},{4,0},{5,1},{6,2},{7,3},{8,12},{9,13},{10,... | collective-permute-start | bytes 294920 | tf_op jit(solution)/shard_map/ppermute | solution.py:29
  138.7 5.5 %collective-permute-start.37 = (f32[192,128]{1,0:T(8,128)S(1)}, f32[192,128]{1,0:T(8,128)S(1)}, u32[]{:S(2)}, u32[]{:S(2)}) collective-permute-start(f32[192,128]{1,0:T(8,128)S(1)} %fusion.10), channel_id=1, source_target_pairs={{0,6},{1,7},{2,4},{3,5},{4,2},{5,3},{6,0},{7,1},{8,14},{9,15},{10,... | collective-permute-start | bytes 294920 | tf_op jit(solution)/shard_map/ppermute | solution.py:29
  144.3 1.8 collective-permute-start.38
  152.2 7.3 %collective-permute-start.42 = (f32[2,2,64,128]{3,2,1,0:T(8,128)S(1)}, f32[2,2,64,128]{3,2,1,0:T(8,128)S(1)}, u32[]{:S(2)}, u32[]{:S(2)}) collective-permute-start(f32[2,2,64,128]{3,2,1,0:T(8,128)S(1)} %pad_maximum_fusion.23), channel_id=1, source_target_pairs={{0,6},{1,7},{2,4},{3,5},{4,2},{5,3},{6,0},{7,1},{8,14},{9,15},{10,... | collective-permute-start | bytes 393224 | tf_op jit(solution)/shard_map/ppermute | solution.py:29
  153.7 7.8 %collective-permute-start.41 = (f32[2,2,64,128]{3,2,1,0:T(8,128)S(1)}, f32[2,2,64,128]{3,2,1,0:T(8,128)S(1)}, u32[]{:S(2)}, u32[]{:S(2)}) collective-permute-start(f32[2,2,64,128]{3,2,1,0:T(8,128)S(1)} %pad_maximum_fusion.22), channel_id=1, source_target_pairs={{0,4},{1,5},{2,6},{3,7},{4,0},{5,1},{6,2},{7,3},{8,12},{9,13},{10,... | collective-permute-start | bytes 393224 | tf_op jit(solution)/shard_map/ppermute | solution.py:29
  154.6 6.9 %collective-permute-start.40 = (f32[2,2,64,128]{3,2,1,0:T(8,128)S(1)}, f32[2,2,64,128]{3,2,1,0:T(8,128)S(1)}, u32[]{:S(2)}, u32[]{:S(2)}) collective-permute-start(f32[2,2,64,128]{3,2,1,0:T(8,128)S(1)} %pad_maximum_fusion.21), channel_id=1, source_target_pairs={{0,2},{1,3},{2,0},{3,1},{4,6},{5,7},{6,4},{7,5},{8,10},{9,11},{10,... | collective-permute-start | bytes 393224 | tf_op jit(solution)/shard_map/ppermute | solution.py:29
  163.3 8.7 %collective-permute-start.43 = (f32[8,64,128]{2,1,0:T(8,128)S(1)}, f32[8,64,128]{2,1,0:T(8,128)S(1)}, u32[]{:S(2)}, u32[]{:S(2)}) collective-permute-start(f32[8,64,128]{2,1,0:T(8,128)S(1)} %get-tuple-element.82.after), channel_id=1, source_target_pairs={{0,8},{8,0},{16,24},{24,16},{1,9},{9,1},{17,25},{25,17},{2,10},{10... | collective-permute-start | bytes 786440 | tf_op jit(solution)/shard_map/ppermute | solution.py:29
  164.9 10.5 %collective-permute-start.53 = (f32[2,2,64,128]{3,2,1,0:T(8,128)S(1)}, f32[2,2,64,128]{3,2,1,0:T(8,128)S(1)}, u32[]{:S(2)}, u32[]{:S(2)}) collective-permute-start(f32[2,2,64,128]{3,2,1,0:T(8,128)S(1)} %pad_maximum_fusion.31), channel_id=1, source_target_pairs={{0,6},{1,7},{2,4},{3,5},{4,2},{5,3},{6,0},{7,1},{8,14},{9,15},{10,... | collective-permute-start | bytes 393224 | tf_op jit(solution)/shard_map/ppermute | solution.py:29
  172.1 9.9 %collective-permute-start.44 = (f32[8,64,128]{2,1,0:T(8,128)S(1)}, f32[8,64,128]{2,1,0:T(8,128)S(1)}, u32[]{:S(2)}, u32[]{:S(2)}) collective-permute-start(f32[8,64,128]{2,1,0:T(8,128)S(1)} %add.122), channel_id=1, source_target_pairs={{0,24},{8,16},{16,8},{24,0},{1,25},{9,17},{17,9},{25,1},{2,26},{10... | collective-permute-start | bytes 786440 | tf_op jit(solution)/shard_map/ppermute | solution.py:29
  173.4 5.0 %collective-permute-start.52 = (f32[2,2,64,128]{3,2,1,0:T(8,128)S(1)}, f32[2,2,64,128]{3,2,1,0:T(8,128)S(1)}, u32[]{:S(2)}, u32[]{:S(2)}) collective-permute-start(f32[2,2,64,128]{3,2,1,0:T(8,128)S(1)} %pad_maximum_fusion.30), channel_id=1, source_target_pairs={{0,4},{1,5},{2,6},{3,7},{4,0},{5,1},{6,2},{7,3},{8,12},{9,13},{10,... | collective-permute-start | bytes 393224 | tf_op jit(solution)/shard_map/ppermute | solution.py:29
  174.3 5.0 %collective-permute-start.51 = (f32[2,2,64,128]{3,2,1,0:T(8,128)S(1)}, f32[2,2,64,128]{3,2,1,0:T(8,128)S(1)}, u32[]{:S(2)}, u32[]{:S(2)}) collective-permute-start(f32[2,2,64,128]{3,2,1,0:T(8,128)S(1)} %pad_maximum_fusion.29), channel_id=1, source_target_pairs={{0,2},{1,3},{2,0},{3,1},{4,6},{5,7},{6,4},{7,5},{8,10},{9,11},{10,... | collective-permute-start | bytes 393224 | tf_op jit(solution)/shard_map/ppermute | solution.py:29
  180.3 8.5 %collective-permute-start.54 = (f32[8,64,128]{2,1,0:T(8,128)S(1)}, f32[8,64,128]{2,1,0:T(8,128)S(1)}, u32[]{:S(2)}, u32[]{:S(2)}) collective-permute-start(f32[8,64,128]{2,1,0:T(8,128)S(1)} %get-tuple-element.89), channel_id=1, source_target_pairs={{0,8},{8,0},{16,24},{24,16},{1,9},{9,1},{17,25},{25,17},{2,10},{10... | collective-permute-start | bytes 786440 | tf_op jit(solution)/shard_map/ppermute | solution.py:29
  182.0 12.8 %collective-permute-start.45 = (f32[8,64,128]{2,1,0:T(8,128)S(1)}, f32[8,64,128]{2,1,0:T(8,128)S(1)}, u32[]{:S(2)}, u32[]{:S(2)}) collective-permute-start(f32[8,64,128]{2,1,0:T(8,128)S(1)} %add.123.mine), channel_id=1, source_target_pairs={{0,8},{8,0},{16,24},{24,16},{1,9},{9,1},{17,25},{25,17},{2,10},{10... | collective-permute-start | bytes 786440 | tf_op jit(solution)/shard_map/ppermute | solution.py:29
  188.9 10.0 %collective-permute-start.55 = (f32[8,64,128]{2,1,0:T(8,128)S(1)}, f32[8,64,128]{2,1,0:T(8,128)S(1)}, u32[]{:S(2)}, u32[]{:S(2)}) collective-permute-start(f32[8,64,128]{2,1,0:T(8,128)S(1)} %add.124), channel_id=1, source_target_pairs={{0,24},{8,16},{16,8},{24,0},{1,25},{9,17},{17,9},{25,1},{2,26},{10... | collective-permute-start | bytes 786440 | tf_op jit(solution)/shard_map/ppermute | solution.py:29
  195.6 5.0 %collective-permute-start.46 = (f32[4,2,64,128]{3,2,1,0:T(8,128)S(1)}, f32[4,2,64,128]{3,2,1,0:T(8,128)S(1)}, u32[]{:S(2)}, u32[]{:S(2)}) collective-permute-start(f32[4,2,64,128]{3,2,1,0:T(8,128)S(1)} %get-tuple-element.84), channel_id=1, source_target_pairs={{0,1},{1,0},{2,3},{3,2},{4,5},{5,4},{6,7},{7,6},{8,9},{9,8},{10,11... | collective-permute-start | bytes 786440 | tf_op jit(solution)/shard_map/ppermute | solution.py:29
  199.0 6.6 %collective-permute-start.56 = (f32[8,64,128]{2,1,0:T(8,128)S(1)}, f32[8,64,128]{2,1,0:T(8,128)S(1)}, u32[]{:S(2)}, u32[]{:S(2)}) collective-permute-start(f32[8,64,128]{2,1,0:T(8,128)S(1)} %add.125.mine), channel_id=1, source_target_pairs={{0,8},{8,0},{16,24},{24,16},{1,9},{9,1},{17,25},{25,17},{2,10},{10... | collective-permute-start | bytes 786440 | tf_op jit(solution)/shard_map/ppermute | solution.py:29
  200.6 10.3 %collective-permute-start.49 = (f32[2,2,64,128]{3,2,1,0:T(8,128)S(1)}, f32[2,2,64,128]{3,2,1,0:T(8,128)S(1)}, u32[]{:S(2)}, u32[]{:S(2)}) collective-permute-start(f32[2,2,64,128]{3,2,1,0:T(8,128)S(1)} %pad_maximum_fusion.27), channel_id=1, source_target_pairs={{0,6},{1,7},{2,4},{3,5},{4,2},{5,3},{6,0},{7,1},{8,14},{9,15},{10,... | collective-permute-start | bytes 393224 | tf_op jit(solution)/shard_map/ppermute | solution.py:29
  202.1 9.6 %collective-permute-start.48 = (f32[2,2,64,128]{3,2,1,0:T(8,128)S(1)}, f32[2,2,64,128]{3,2,1,0:T(8,128)S(1)}, u32[]{:S(2)}, u32[]{:S(2)}) collective-permute-start(f32[2,2,64,128]{3,2,1,0:T(8,128)S(1)} %pad_maximum_fusion.26), channel_id=1, source_target_pairs={{0,4},{1,5},{2,6},{3,7},{4,0},{5,1},{6,2},{7,3},{8,12},{9,13},{10,... | collective-permute-start | bytes 393224 | tf_op jit(solution)/shard_map/ppermute | solution.py:29
  206.3 6.2 %collective-permute-start.47 = (f32[2,2,64,128]{3,2,1,0:T(8,128)S(1)}, f32[2,2,64,128]{3,2,1,0:T(8,128)S(1)}, u32[]{:S(2)}, u32[]{:S(2)}) collective-permute-start(f32[2,2,64,128]{3,2,1,0:T(8,128)S(1)} %pad_maximum_fusion.25), channel_id=1, source_target_pairs={{0,2},{1,3},{2,0},{3,1},{4,6},{5,7},{6,4},{7,5},{8,10},{9,11},{10,... | collective-permute-start | bytes 393224 | tf_op jit(solution)/shard_map/ppermute | solution.py:29
  207.9 8.9 %collective-permute-start.60 = (f32[2,2,64,128]{3,2,1,0:T(8,128)S(1)}, f32[2,2,64,128]{3,2,1,0:T(8,128)S(1)}, u32[]{:S(2)}, u32[]{:S(2)}) collective-permute-start(f32[2,2,64,128]{3,2,1,0:T(8,128)S(1)} %pad_maximum_fusion.35), channel_id=1, source_target_pairs={{0,6},{1,7},{2,4},{3,5},{4,2},{5,3},{6,0},{7,1},{8,14},{9,15},{10,... | collective-permute-start | bytes 393224 | tf_op jit(solution)/shard_map/ppermute | solution.py:29
  209.9 8.2 %collective-permute-start.59 = (f32[2,2,64,128]{3,2,1,0:T(8,128)S(1)}, f32[2,2,64,128]{3,2,1,0:T(8,128)S(1)}, u32[]{:S(2)}, u32[]{:S(2)}) collective-permute-start(f32[2,2,64,128]{3,2,1,0:T(8,128)S(1)} %pad_maximum_fusion.34), channel_id=1, source_target_pairs={{0,4},{1,5},{2,6},{3,7},{4,0},{5,1},{6,2},{7,3},{8,12},{9,13},{10,... | collective-permute-start | bytes 393224 | tf_op jit(solution)/shard_map/ppermute | solution.py:29
  210.9 7.2 %collective-permute-start.58 = (f32[2,2,64,128]{3,2,1,0:T(8,128)S(1)}, f32[2,2,64,128]{3,2,1,0:T(8,128)S(1)}, u32[]{:S(2)}, u32[]{:S(2)}) collective-permute-start(f32[2,2,64,128]{3,2,1,0:T(8,128)S(1)} %pad_maximum_fusion.33), channel_id=1, source_target_pairs={{0,2},{1,3},{2,0},{3,1},{4,6},{5,7},{6,4},{7,5},{8,10},{9,11},{10,... | collective-permute-start | bytes 393224 | tf_op jit(solution)/shard_map/ppermute | solution.py:29
  222.3 1.8 collective-permute-start.61
  224.1 4.9 %collective-permute-start.62 = (f32[192,128]{1,0:T(8,128)S(1)}, f32[192,128]{1,0:T(8,128)S(1)}, u32[]{:S(2)}, u32[]{:S(2)}) collective-permute-start(f32[192,128]{1,0:T(8,128)S(1)} %get-tuple-element.104), channel_id=1, source_target_pairs={{0,2},{1,3},{2,0},{3,1},{4,6},{5,7},{6,4},{7,5},{8,10},{9,11},{10,... | collective-permute-start | bytes 294920 | tf_op jit(solution)/shard_map/ppermute | solution.py:29
  225.5 5.3 %collective-permute-start.63 = (f32[192,128]{1,0:T(8,128)S(1)}, f32[192,128]{1,0:T(8,128)S(1)}, u32[]{:S(2)}, u32[]{:S(2)}) collective-permute-start(f32[192,128]{1,0:T(8,128)S(1)} %get-tuple-element.106), channel_id=1, source_target_pairs={{0,4},{1,5},{2,6},{3,7},{4,0},{5,1},{6,2},{7,3},{8,12},{9,13},{10,... | collective-permute-start | bytes 294920 | tf_op jit(solution)/shard_map/ppermute | solution.py:29
  226.2 6.1 %collective-permute-start.64 = (f32[192,128]{1,0:T(8,128)S(1)}, f32[192,128]{1,0:T(8,128)S(1)}, u32[]{:S(2)}, u32[]{:S(2)}) collective-permute-start(f32[192,128]{1,0:T(8,128)S(1)} %get-tuple-element.105), channel_id=1, source_target_pairs={{0,6},{1,7},{2,4},{3,5},{4,2},{5,3},{6,0},{7,1},{8,14},{9,15},{10,... | collective-permute-start | bytes 294920 | tf_op jit(solution)/shard_map/ppermute | solution.py:29
  232.3 6.2 %collective-permute-start.65 = (f32[48,128]{1,0:T(8,128)S(1)}, f32[48,128]{1,0:T(8,128)S(1)}, u32[]{:S(2)}, u32[]{:S(2)}) collective-permute-start(f32[48,128]{1,0:T(8,128)S(1)} %get-tuple-element.174), channel_id=1, source_target_pairs={{0,8},{8,0},{16,24},{24,16},{1,9},{9,1},{17,25},{25,17},{2,10},{10... | collective-permute-start | bytes 73736 | tf_op jit(solution)/shard_map/ppermute | solution.py:29
  233.3 5.8 %collective-permute-start.66 = (f32[48,128]{1,0:T(8,128)S(1)}, f32[48,128]{1,0:T(8,128)S(1)}, u32[]{:S(2)}, u32[]{:S(2)}) collective-permute-start(f32[48,128]{1,0:T(8,128)S(1)} %get-tuple-element.176), channel_id=1, source_target_pairs={{0,24},{8,16},{16,8},{24,0},{1,25},{9,17},{17,9},{25,1},{2,26},{10... | collective-permute-start | bytes 73736 | tf_op jit(solution)/shard_map/ppermute | solution.py:29
  237.0 4.7 %collective-permute-start.67 = (f32[48,128]{1,0:T(8,128)S(1)}, f32[48,128]{1,0:T(8,128)S(1)}, u32[]{:S(2)}, u32[]{:S(2)}) collective-permute-start(f32[48,128]{1,0:T(8,128)S(1)} %get-tuple-element.175), channel_id=1, source_target_pairs={{0,16},{8,24},{16,0},{24,8},{1,17},{9,25},{17,1},{25,9},{2,18},{10... | collective-permute-start | bytes 73736 | tf_op jit(solution)/shard_map/ppermute | solution.py:29
  (23 other events, 425.9 us)

commit v6 on v5

v6 whole, which is shorter than its diff:
```python
import functools

import jax
import jax.numpy as jnp
from jax import lax
from jax.experimental import pallas as pl
from jax.experimental.pallas import tpu as pltpu
from jax.sharding import PartitionSpec as P

CAP = 2
NSTRUCT = 8
ITERS = 2
CHUNKS = 2
VOX = "vox"
PHASE = "phase"
LABEL_ROWS = 16
F32 = jnp.float32
BF16 = jnp.bfloat16
LARGE = 14 << 20
SMALL = 4 << 20
ROWS_AT_ONCE = 512
BLOCK_ROWS_AT_ONCE = 256
BRIEF = pl.CostEstimate(flops=1, bytes_accessed=1, transcendentals=0)


def swap(x, axis, mask):
    count = lax.axis_size(axis)
    return lax.ppermute(x, axis, [(i, i ^ mask) for i in range(count)])


def spread(x, axis, masks):
    return [x] + [swap(x, axis, m) for m in masks]


def core_count():
    return min(2, lax.axis_size(VOX))


def terms(x):
    big = x.astype(BF16)
    return big, (x - big.astype(F32)).astype(BF16)


def halves(x, axis):
    return jnp.concatenate(terms(x), axis=axis)


def term_sum(full, rows, cols):
    return full[:rows, :cols] + (full[:rows, cols:] + full[rows:, :cols])


def specs(count, space):
    return [pl.BlockSpec(memory_space=space)] * count


def fill_weights(me_ref, out, pieces, rows, vox, masks):
    cores = len(pieces)
    for c, ref in enumerate(pieces):
        for k in range(vox // cores):
            for i, p in enumerate(masks):
                v = me_ref[0] ^ (k * cores + c)
                at = ((me_ref[1] ^ p) * vox + v) * rows
                out[pl.ds(pl.multiple_of(at, rows), rows), :] = halves(
                    ref[k, i * rows : (i + 1) * rows, :], 1
                )


def warp(chunks, cores, source_ref, valid_ref, tiles, dose, outs):
    height = tiles.shape[1]
    plans = dose.shape[1]
    part = height // chunks
    for c in range(cores):
        for k in range(outs[0].shape[0]):
            for j in range(CAP):
                s = (k * cores + c) * CAP + j
                b = source_ref[s]
                block = dose[pl.ds(pl.multiple_of(b * height, height), height), :]
                full = jnp.dot(
                    halves(tiles[b], 0), halves(block, 1), preferred_element_type=F32
                )
                warped = jnp.where(valid_ref[s] > 0, term_sum(full, height, plans), 0.0)
                for h in range(chunks):
                    outs[h * cores + c][k, j] = warped[h * part : (h + 1) * part]


def forward_body(dims, source_ref, valid_ref, me_ref, matrix, tiles, *refs):
    vox, masks, rows, pieces_n, chunks, cores = dims
    pieces, outs = refs[:pieces_n], refs[pieces_n:-2]
    dose, weights = refs[-2:]
    plans = dose.shape[1]
    if len(pieces[0].shape) == 2:
        weights[...] = halves(pieces[0][...], 1)
    else:
        fill_weights(me_ref, weights, pieces, rows, vox, masks)
    step = min(ROWS_AT_ONCE, dose.shape[0])
    for first in range(0, dose.shape[0], step):
        at = slice(first, first + step)
        big, small = terms(matrix[at, :])
        top = jnp.dot(big, weights[...], preferred_element_type=F32)
        rest = jnp.dot(small, weights[:, :plans], preferred_element_type=F32)
        dose[at, :] = top[:, :plans] + (top[:, plans:] + rest)
    warp(chunks, cores, source_ref, valid_ref, tiles, dose, outs)


def forward(scalars, matrix, tiles, pieces, rows, vox, masks):
    height = tiles.shape[1]
    vox_rows, spots = matrix.shape
    plans = pieces[0].shape[-1]
    cores = core_count()
    out = jax.ShapeDtypeStruct((vox // cores, CAP, height // CHUNKS, plans), F32)
    outs = [out] * (cores * CHUNKS)
    return pl.pallas_call(
        functools.partial(forward_body, (vox, masks, rows, len(pieces), CHUNKS, cores)),
        in_specs=specs(3, pltpu.SMEM) + specs(2 + len(pieces), pltpu.VMEM),
        out_specs=specs(len(outs), pltpu.VMEM),
        out_shape=outs,
        scratch_shapes=[pltpu.VMEM((vox_rows, plans), F32), pltpu.VMEM((spots, 2 * plans), BF16)],
        compiler_params=pltpu.CompilerParams(vmem_limit_bytes=LARGE),
        cost_estimate=BRIEF,
        name="dose_and_warp",
    )(*scalars, matrix, tiles, *pieces)


def piece(arrived, cores, m):
    return arrived[m // cores].at[m % cores]


def gradient_body(dims, source_ref, valid_ref, me_ref, matrix, tiles, *refs):
    vox, masks, rows, cores, chunks = dims
    chips = vox // cores
    returned = refs[: chips * chunks]
    outs = refs[chips * chunks : -3]
    columns, total, turned = refs[-3:]
    height = tiles.shape[1]
    plans = turned.shape[1]
    vox_rows, spots = matrix.shape
    spare = vox_rows // height
    for m in range(vox):
        found = [piece(returned[h * chips : (h + 1) * chips], cores, m) for h in range(chunks)]
        for j in range(CAP):
            s = m * CAP + j
            b = source_ref[s]
            adjoint = jnp.concatenate([f[j] for f in found], axis=0)
            full = jnp.dot(
                halves(adjoint.T, 0), halves(tiles[b], 1), preferred_element_type=F32
            )
            to = jnp.where(valid_ref[s] > 0, b, spare) * height
            columns[:, pl.ds(pl.multiple_of(to, height), height)] = halves(
                term_sum(full, plans, height), 0
            )

    step = min(BLOCK_ROWS_AT_ONCE, vox_rows)
    for first in range(0, vox_rows, step):
        at = slice(first, first + step)
        big, small = terms(matrix[at, :])
        top = jnp.dot(columns[:, at], big, preferred_element_type=F32)
        rest = jnp.dot(columns[:plans, at], small, preferred_element_type=F32)
        part = top[:plans] + (top[plans:] + rest)
        total[...] = part if first == 0 else total[...] + part
    for i in range(0, spots, plans):
        turned[i : i + plans, :] = total[:, i : i + plans].T
    if len(outs[0].shape) == 2:
        outs[0][...] = turned[...]
    else:
        for c in range(cores):
            for k in range(vox // cores):
                for i, p in enumerate(masks):
                    v = me_ref[0] ^ (k * cores + c)
                    at = ((me_ref[1] ^ p) * vox + v) * rows
                    outs[c][k, i * rows : (i + 1) * rows] = turned[
                        pl.ds(pl.multiple_of(at, rows), rows), :
                    ]


def gradient_parts(scalars, matrix, tiles, returned, rows, vox, masks):
    vox_rows, spots = matrix.shape
    plans = returned[0].shape[-1]
    cores = core_count()
    if rows % 8 == 0:
        outs = [jax.ShapeDtypeStruct((vox // cores, len(masks) * rows, plans), F32)] * cores
    else:
        outs = [jax.ShapeDtypeStruct((spots, plans), F32)]
    return pl.pallas_call(
        functools.partial(gradient_body, (vox, masks, rows, cores, CHUNKS)),
        in_specs=specs(3, pltpu.SMEM) + specs(2 + len(returned), pltpu.VMEM),
        out_specs=specs(len(outs), pltpu.VMEM),
        out_shape=outs,
        scratch_shapes=[pltpu.VMEM((2 * plans, vox_rows + tiles.shape[1]), BF16),
            pltpu.VMEM((plans, spots), F32),
            pltpu.VMEM((spots, plans), F32),
        ],
        compiler_params=pltpu.CompilerParams(vmem_limit_bytes=LARGE),
        cost_estimate=BRIEF,
        name="warp_back_and_gradient",
    )(*scalars, matrix, tiles, *returned)


def place_body(vox, cores, which_ref, slot_ref, *refs):
    chips = vox // cores
    arrived, (give, keep, total) = refs[:chips], refs[chips:]
    total[...] = jnp.zeros_like(total)
    for m in range(vox):
        blocks = piece(arrived, cores, m)
        for j in range(CAP):
            slot = slot_ref[m * CAP + j]

            @pl.when(slot >= 0)
            def _():
                total[slot] += blocks[j]

    half = keep.shape[0]
    which = which_ref[0]
    keep[...] = total[pl.ds(which * half, half)]
    give[...] = total[pl.ds((1 - which) * half, half)]


def place(which, slots, incoming, blocks):
    cores = core_count()
    vox = len(incoming) * cores
    height, plans = incoming[0].shape[-2:]
    half = jax.ShapeDtypeStruct((blocks // 2, height, plans), F32)
    return pl.pallas_call(
        functools.partial(place_body, vox, cores),
        in_specs=specs(2, pltpu.SMEM) + specs(len(incoming), pltpu.VMEM),
        out_specs=specs(2, pltpu.VMEM),
        out_shape=[half, half],
        scratch_shapes=[pltpu.VMEM((blocks, height, plans), F32)],
        compiler_params=pltpu.CompilerParams(vmem_limit_bytes=SMALL),
        cost_estimate=BRIEF,
        name="place_blocks",
    )(which, slots, *incoming)


def pull_body(vox, cores, with_dose, which_ref, slot_ref, mine, other, goal, scale, *refs):
    half = mine.shape[0]
    which = which_ref[0]
    field = refs[-1]
    field[pl.ds(which * half, half)] = mine[...]
    field[pl.ds((1 - which) * half, half)] = other[...]
    for m in range(vox):
        for j in range(CAP):
            slot = jnp.maximum(slot_ref[m * CAP + j], 0)
            refs[m % cores][m // cores, j] = scale[slot] * (field[slot] - goal[slot])
    if with_dose:
        refs[cores][...] = field[...]


def pull(which, slots, mine, other, goal, scale, vox, with_dose):
    half, height, plans = mine.shape
    cores = core_count()
    outs = [jax.ShapeDtypeStruct((vox // cores, CAP, height, plans), F32)] * cores
    if with_dose:
        outs = outs + [jax.ShapeDtypeStruct((2 * half, height, plans), F32)]
    return pl.pallas_call(
        functools.partial(pull_body, vox, cores, with_dose),
        in_specs=specs(2, pltpu.SMEM) + specs(4, pltpu.VMEM),
        out_specs=specs(len(outs), pltpu.VMEM),
        out_shape=outs,
        scratch_shapes=[pltpu.VMEM((2 * half, height, plans), F32)],
        compiler_params=pltpu.CompilerParams(vmem_limit_bytes=SMALL),
        cost_estimate=BRIEF,
        name="adjoint_blocks",
    )(which, slots, mine, other, goal, scale)


def phase_steps():
    count, steps = lax.axis_size(PHASE), []
    while 2 ** len(steps) < count:
        steps.append(2 ** (len(steps) + 1) - 1)
    return steps


def combined(steps):
    masks = [0]
    for s in steps:
        masks += [m ^ s for m in masks]
    return masks


def sum_everywhere(x, axis, steps):
    for i, s in enumerate(steps):
        other = swap(x, axis, s).reshape(-1, 2, 2**i, *x.shape[1:])
        x = x + jnp.concatenate([other[:, 1:], other[:, :1]], axis=1).reshape(x.shape)
    return x


def gather_chips(by_phase):
    cores = core_count()
    by_chip = jnp.stack(spread(by_phase, VOX, range(cores, lax.axis_size(VOX), cores)))
    return spread(by_chip, VOX, range(1, cores))


def sum_chips(parts):
    cores = len(parts)
    chips = parts[0]
    for m in range(1, cores):
        chips = chips + swap(parts[m], VOX, m)
    mine = chips[0]
    for k in range(1, chips.shape[0]):
        mine = mine + swap(chips[k], VOX, k * cores)
    return mine


def cross(pieces):
    cores = len(pieces)
    crossed = [pieces[0]] + [swap(pieces[c], VOX, c) for c in range(1, cores)]
    return [jnp.stack([p[k] for p in crossed]) for k in range(pieces[0].shape[0])]


def send(chips):
    cores = core_count()
    return [chips[0]] + [swap(chips[k], VOX, k * cores) for k in range(1, len(chips))]


def exchange(pieces):
    return send(cross(pieces))


def phase_stages(half):
    for step in phase_steps()[1:-1]:
        half = half + swap(half, PHASE, step)
    return half, swap(half, PHASE, phase_steps()[-1])


def tie(x, other):
    return lax.optimization_barrier((x, other))[0]


def goals_and_scales(structure, prescribed, importance, blocks, height):
    highest = lax.Precision.HIGHEST
    member = (structure[:, None] == jnp.arange(NSTRUCT, dtype=jnp.int32)[None, :]).astype(F32)
    target_dose = jnp.dot(member, prescribed, precision=highest, preferred_element_type=F32)
    voxel_weight = jnp.dot(
        member, importance[:, None], precision=highest, preferred_element_type=F32
    )
    voxel_weight = jnp.broadcast_to(voxel_weight, target_dose.shape)
    shape = (blocks, CHUNKS, height // CHUNKS, prescribed.shape[1])
    cut = [x.reshape(shape) for x in (target_dose, voxel_weight)]
    return [[x[:, h] for h in range(CHUNKS)] for x in cut]


def per_device(
    influence,
    weights,
    warp_tiles,
    owners,
    owner_slot,
    tile_index,
    structure,
    prescribed,
    importance,
    step_size,
):
    matrix = influence[0]
    vox_rows, spots = matrix.shape
    block_rows = warp_tiles.shape[1]
    rows, plans = weights.shape
    local_blocks = vox_rows // block_rows
    vox = lax.axis_size(VOX)
    phases = lax.axis_size(PHASE)
    cores = core_count()
    me_vox = lax.axis_index(VOX)
    me_phase = lax.axis_index(PHASE)
    slots_all = vox * CAP
    targets = owners[0, :, 0]
    which = ((me_phase ^ (me_phase >> 1)) & 1).astype(jnp.int32).reshape(1)

    def orders(names):
        before = jnp.tril(jnp.ones((local_blocks, local_blocks), jnp.int32), -1)
        same = (names[..., :, None] == names[..., None, :]).astype(jnp.int32)
        return jnp.sum(same * before, axis=-1)

    position = (targets ^ me_vox) * CAP + orders(targets)
    chosen_mask = jnp.arange(slots_all, dtype=jnp.int32)[:, None] == position[None, :]
    positions_i = jnp.arange(local_blocks, dtype=jnp.int32)
    source = jnp.sum(jnp.where(chosen_mask, positions_i[None, :], 0), axis=1)
    valid = jnp.sum(chosen_mask.astype(jnp.int32), axis=1)
    me = jnp.stack([me_vox, me_phase]).astype(jnp.int32)
    scalars = (source, valid, me)
    labels = jnp.zeros((LABEL_ROWS, plans), F32)
    labels = labels.at[0, :local_blocks].set(targets.astype(F32))
    labels = labels.at[1, :local_blocks].set(owner_slot[0].astype(F32))

    masks = combined(phase_steps())
    tiles = warp_tiles[tile_index[0]]
    held = jnp.concatenate(spread(weights, PHASE, masks[1:]), axis=0)
    for iteration in range(ITERS):
        last = iteration == ITERS - 1
        if iteration == 0:
            pieces = gather_chips(jnp.concatenate([held, labels], axis=0))
            infos = jnp.stack(pieces, axis=1).reshape(vox, -1, plans)[:, phases * rows :]
            names = infos[:, 0, :local_blocks].astype(jnp.int32)
            slots = infos[:, 1, :local_blocks].astype(jnp.int32)
            order = jnp.where(names == me_vox, orders(names), -1)
            hit = order[:, None, :] == jnp.arange(CAP, dtype=jnp.int32)[None, :, None]
            received = jnp.sum(jnp.where(hit, slots[:, None, :] + 1, 0), axis=-1)
            received = received.reshape(slots_all) - 1
        else:
            pieces = gather_chips(held)
        if rows % 16:
            every = jnp.stack(pieces, axis=1).reshape(vox, -1, plans)[:, : phases * rows]
            every = every.reshape(vox, phases, rows, plans)
            back_to = jnp.asarray([masks.index(p) for p in range(phases)], jnp.int32)
            every = every[jnp.arange(vox) ^ me_vox][:, back_to[jnp.arange(phases) ^ me_phase]]
            pieces = [every.transpose(1, 0, 2, 3).reshape(spots, plans)]
        outgoing = forward(scalars, matrix, tiles, pieces, rows, vox, masks)
        returned, dose = [], []
        incoming, held_halves, seconds = exchange(outgoing[:cores]), [], []
        for h in range(CHUNKS):
            give, keep = place(which, received, incoming, local_blocks)
            got = swap(give, PHASE, 1)
            if iteration == 0 and h == 0:
                goals, scales = goals_and_scales(
                    tie(structure, give), prescribed, importance, local_blocks, block_rows
                )
            if h + 1 < CHUNKS:
                later = outgoing[(h + 1) * cores : (h + 2) * cores]
                incoming = exchange([tie(x, incoming[1]) for x in later])
            if h > 0:
                got = tie(got, seconds[-1])
            half, second = phase_stages(keep + got)
            held_halves.append(half)
            seconds.append(second)
        for h in range(CHUNKS):
            second = seconds[h] if h == 0 else tie(seconds[h], other)
            mine = held_halves[h] + second
            other = swap(mine, PHASE, 1)
            back = pull(which, received, mine, other, goals[h], scales[h], vox, last)
            returned += exchange(back[:cores])
            dose += back[cores:]
        parts = gradient_parts(scalars, matrix, tiles, returned, rows, vox, masks)
        if rows % 8:
            parts = parts[0].reshape(phases, vox, rows, plans)
            wanted = jnp.asarray(masks, jnp.int32) ^ me_phase
            parts = parts[wanted][:, jnp.arange(vox) ^ me_vox]
            parts = parts.transpose(1, 0, 2, 3).reshape(vox // cores, cores, phases * rows, plans)
            parts = [parts[:, c] for c in range(cores)]
        total = sum_chips(parts)
        if last:
            split = total.reshape(phases, rows, plans)
            total = split[0]
            for i, m in enumerate(masks[1:], 1):
                total = total + swap(split[i], PHASE, m)
            new_weights = jnp.maximum(held[:rows] - step_size[None, :] * total, 0.0)
        else:
            total = sum_everywhere(total.reshape(phases, rows, plans), PHASE, phase_steps())
            held = jnp.maximum(held - step_size[None, :] * total.reshape(held.shape), 0.0)
    dose_field = jnp.stack(dose, axis=1).reshape(vox_rows, plans)
    return (new_weights, dose_field)


def solution(mesh):
    in_specs = (
        P("phase", "vox", None),
        P(("phase", "vox"), None),
        P(),
        P("phase", "vox", None),
        P("phase", "vox"),
        P("phase", "vox"),
        P("vox"),
        P(),
        P(),
        P(),
    )
    out_specs = (P(("phase", "vox"), None), P("vox", None))
    return jax.shard_map(
        per_device, mesh=mesh, in_specs=in_specs, out_specs=out_specs, check_vma=False
    )
```

time: 243 us -> 231 us (0.951)
  Pallas kernels: 33.4 us -> 25.1 us
  starting transfers between devices: 80.3 us -> 75.6 us
  local copies, waits for them, and re-layouts: 12.6 us -> 15.1 us
    pallas_call x3 -> x0, Pallas kernels: 14.5 us -> none  [the longest x1 11.9 us: first_forward(): pl.pallas_call(functools.partial(first_body, (vox, masks, rows, len(piece...]
    pallas_call x1 -> x2, Pallas kernels: 4.48 us -> 9.6 us  [forward(): pl.pallas_call(functools.partial(forward_body, (vox, masks, rows, len(pie...]
    ppermute x68, starting transfers between devices: 80.3 us -> 75.6 us  [swap(): return lax.ppermute(x, axis, [(i, i ^ mask) for i in range(count)])]
    unnamed x42 -> x18, local copies, waits for them, and re-layouts: 7.14 us -> 9.95 us
    gather x0 -> x1, local copies, waits for them, and re-layouts: none -> 2.8 us  [per_device(): tiles = warp_tiles[tile_index[0]]]
  transfers between devices with their start and end apart: 68 -> 68, of which waited for: 50 -> 52; matrix products, arithmetic and copies ran while one was open for 5% -> 5% of each run, Pallas kernels for 2% -> 3%
where the time goes in v6:
time: 231 us
  waiting for transfers between devices  106 us (46%)
  starting transfers between devices  75.6 us (33%)
  Pallas kernels  25.1 us (11%)
  local copies, waits for them, and re-layouts  15.1 us (7%)
  other arithmetic  5.79 us (3%)
    ppermute x68, waiting for transfers between devices, swap(): return lax.ppermute(x, axis, [(i, i ^ mask) for i in range(count)])  106 us
    ppermute x68, starting transfers between devices, swap(): return lax.ppermute(x, axis, [(i, i ^ mask) for i in range(count)])  75.6 us
    unnamed x18, local copies, waits for them, and re-layouts  9.95 us
    pallas_call x2, Pallas kernels, forward(): pl.pallas_call(functools.partial(forward_body, (vox, masks, rows, len(pie...  9.6 us
    pallas_call x2, Pallas kernels, gradient_parts(): pl.pallas_call(functools.partial(gradient_body, (vox, masks, rows, cores,...  9.36 us
  transfers between devices with their start and end apart: 68, of which 52 were waited for; matrix products, arithmetic and copies ran while one was open for 5% of the time, Pallas kernels for 3%

profile of v6, /device:TPU:0, one launch (start us, length us, event | category | flops | bytes accessed | tf_op | source)
XLA Modules:
  0.0 231.0 jit_solution(12076788990640414541)
XLA Ops:
  0.6 3.1 %collective-permute-start = (f32[48,128]{1,0:T(8,128)}, f32[48,128]{1,0:T(8,128)S(1)}, u32[]{:S(2)}, u32[]{:S(2)}) collective-permute-start(f32[48,128]{1,0:T(8,128)} %param.15), channel_id=1, source_target_pairs={{0,8},{8,0},{16,24},{24,16},{1,9},{9,1},{17,25},{25,17},{2,10},{10... | collective-permute-start | bytes 73736 | tf_op jit(solution)/shard_map/ppermute | solution.py:28
  3.7 2.5 %collective-permute-start.1 = (f32[48,128]{1,0:T(8,128)}, f32[48,128]{1,0:T(8,128)S(1)}, u32[]{:S(2)}, u32[]{:S(2)}) collective-permute-start(f32[48,128]{1,0:T(8,128)} %param.15), channel_id=1, source_target_pairs={{0,24},{8,16},{16,8},{24,0},{1,25},{9,17},{17,9},{25,1},{2,26},{10... | collective-permute-start | bytes 73736 | tf_op jit(solution)/shard_map/ppermute | solution.py:28
  11.4 1.5 collective-permute-start.4
  12.9 1.4 collective-permute-start.5
  14.9 2.8 %gather_fusion = f32[16,128,128]{2,1,0:T(8,128)S(1)} fusion(f32[64,128,128]{2,1,0:T(8,128)} %param.16, s32[1024]{0:T(1024)S(1)} %pad_clamp_fusion), kind=kCustom, calls=%fused_computation | custom fusion | bytes 2097216 | tf_op jit(solution)/shard_map/gather | solution.py:385
  21.0 4.6 %copy-done.1 = f32[1,2048,1536]{2,1,0:T(8,128)S(1)} copy-done((f32[1,2048,1536]{2,1,0:T(8,128)S(1)}, f32[1,2048,1536]{2,1,0:T(8,128)}, u32[]{:S(2)}) %copy-start.1) | copy-done | bytes 12582936
  25.5 4.8 %dose_and_warp.2 = (f32[4,2,64,128]{3,2,1,0:T(8,128)S(1)}, f32[4,2,64,128]{3,2,1,0:T(8,128)S(1)}, f32[4,2,64,128]{3,2,1,0:T(8,128)S(1)}, f32[4,2,64,128]{3,2,1,0:T(8,128)S(1)}) custom-call(s32[16]{0:T(128)S(1)} %get-tuple-element.105.source_ref, s32[16]{0:T(128)S(1)} %get-tuple-element.104.valid_ref, s32[2]{0:T(128)S(1)} %pad_add_fusion.me_ref, ...), custom_call_target="tpu_custom_call" | custom-call | flops 1 | bytes 1 | tf_op jit(solution)/shard_map/dose_and_warp/pallas_call | solution.py:112
  33.2 1.9 collective-permute-start.10
  35.7 2.7 %collective-permute-done.8.refs_1_ = f32[2,2,64,128]{3,2,1,0:T(8,128)S(1)} collective-permute-done((f32[2,2,64,128]{3,2,1,0:T(8,128)S(1)}, f32[2,2,64,128]{3,2,1,0:T(8,128)S(1)}, u32[]{:S(2)}, u32[]{:S(2)}) %collective-permute-start.8) | collective-permute-done | bytes 131104 | tf_op jit(solution)/shard_map/ppermute | solution.py:28
  38.5 3.1 %collective-permute-done.10.refs_3_ = f32[2,2,64,128]{3,2,1,0:T(8,128)S(1)} collective-permute-done((f32[2,2,64,128]{3,2,1,0:T(8,128)S(1)}, f32[2,2,64,128]{3,2,1,0:T(8,128)S(1)}, u32[]{:S(2)}, u32[]{:S(2)}) %collective-permute-start.10) | collective-permute-done | bytes 131104 | tf_op jit(solution)/shard_map/ppermute | solution.py:28
  41.5 1.5 collective-permute-done.9.refs_2_
  47.5 1.6 collective-permute-start.20
  51.3 1.8 collective-permute-start.12
  55.3 1.4 collective-permute-start.22
  56.8 4.1 %collective-permute-done.12 = f32[8,64,128]{2,1,0:T(8,128)S(1)} collective-permute-done((f32[8,64,128]{2,1,0:T(8,128)S(1)}, f32[8,64,128]{2,1,0:T(8,128)S(1)}, u32[]{:S(2)}, u32[]{:S(2)}) %collective-permute-start.12) | collective-permute-done | bytes 262176 | tf_op jit(solution)/shard_map/ppermute | solution.py:28
  60.9 3.2 %collective-permute-start.13 = (f32[8,64,128]{2,1,0:T(8,128)S(1)}, f32[8,64,128]{2,1,0:T(8,128)S(1)}, u32[]{:S(2)}, u32[]{:S(2)}) collective-permute-start(f32[8,64,128]{2,1,0:T(8,128)S(1)} %add.123.mine), channel_id=1, source_target_pairs={{0,8},{8,0},{16,24},{24,16},{1,9},{9,1},{17,25},{25,17},{2,10},{10... | collective-permute-start | bytes 786440 | tf_op jit(solution)/shard_map/ppermute | solution.py:28
  65.6 2.1 collective-permute-start.23
  67.7 4.4 %collective-permute-done.13.other = f32[8,64,128]{2,1,0:T(8,128)S(1)} collective-permute-done((f32[8,64,128]{2,1,0:T(8,128)S(1)}, f32[8,64,128]{2,1,0:T(8,128)S(1)}, u32[]{:S(2)}, u32[]{:S(2)}) %collective-permute-start.13) | collective-permute-done | bytes 262176 | tf_op jit(solution)/shard_map/ppermute | solution.py:28
  73.1 4.4 %collective-permute-done.23 = f32[8,64,128]{2,1,0:T(8,128)S(1)} collective-permute-done((f32[8,64,128]{2,1,0:T(8,128)S(1)}, f32[8,64,128]{2,1,0:T(8,128)S(1)}, u32[]{:S(2)}, u32[]{:S(2)}) %collective-permute-start.23) | collective-permute-done | bytes 262176 | tf_op jit(solution)/shard_map/ppermute | solution.py:28
  79.4 1.7 collective-permute-start.16
  81.1 2.9 %collective-permute-done.24.other = f32[8,64,128]{2,1,0:T(8,128)S(1)} collective-permute-done((f32[8,64,128]{2,1,0:T(8,128)S(1)}, f32[8,64,128]{2,1,0:T(8,128)S(1)}, u32[]{:S(2)}, u32[]{:S(2)}) %collective-permute-start.24) | collective-permute-done | bytes 262176 | tf_op jit(solution)/shard_map/ppermute | solution.py:28
  87.6 1.6 collective-permute-start.27
  91.3 2.8 %collective-permute-done.28.refs_7_ = f32[2,2,64,128]{3,2,1,0:T(8,128)S(1)} collective-permute-done((f32[2,2,64,128]{3,2,1,0:T(8,128)S(1)}, f32[2,2,64,128]{3,2,1,0:T(8,128)S(1)}, u32[]{:S(2)}, u32[]{:S(2)}) %collective-permute-start.28) | collective-permute-done | bytes 131104 | tf_op jit(solution)/shard_map/ppermute | solution.py:28
  94.0 1.7 collective-permute-done.27.refs_6_
  96.5 4.6 %copy-done.2 = f32[1,2048,1536]{2,1,0:T(8,128)S(1)} copy-done((f32[1,2048,1536]{2,1,0:T(8,128)S(1)}, f32[1,2048,1536]{2,1,0:T(8,128)}, u32[]{:S(2)}) %copy-start.2) | copy-done | bytes 12582936
  101.1 4.7 %warp_back_and_gradient.2 = (f32[4,192,128]{2,1,0:T(8,128)S(1)}, f32[4,192,128]{2,1,0:T(8,128)S(1)}) custom-call(s32[16]{0:T(128)S(1)} %get-tuple-element.105.source_ref, s32[16]{0:T(128)S(1)} %get-tuple-element.104.valid_ref, s32[2]{0:T(128)S(1)} %pad_add_fusion.me_ref, f32[2048,1536]{1,0:T(8,128)S(1)} %bitcast.93, f32[16,128,128]{2,1,0:T(8,128)S(1)} %gather_fusion, ...), custom_call_target="tpu_custom_call" | custom-call | flops 1 | bytes 1 | tf_op jit(solution)/shard_map/warp_back_and_gradient/pallas_call | solution.py:183
  105.9 1.7 collective-permute-done.29
  109.4 1.9 collective-permute-start.32
  111.2 1.3 collective-permute-done.30
  112.6 3.0 %collective-permute-done.31 = f32[192,128]{1,0:T(8,128)S(1)} collective-permute-done((f32[192,128]{1,0:T(8,128)S(1)}, f32[192,128]{1,0:T(8,128)S(1)}, u32[]{:S(2)}, u32[]{:S(2)}) %collective-permute-start.31) | collective-permute-done | bytes 98336 | tf_op jit(solution)/shard_map/ppermute | solution.py:28
  116.4 3.9 %collective-permute-done.33 = f32[4,48,128]{2,1,0:T(8,128)S(1)} collective-permute-done((f32[4,48,128]{2,1,0:T(8,128)S(1)}, f32[4,48,128]{2,1,0:T(8,128)S(1)}, u32[]{:S(2)}, u32[]{:S(2)}) %collective-permute-start.33) | collective-permute-done | bytes 98336 | tf_op jit(solution)/shard_map/ppermute | solution.py:28
  121.5 5.4 %collective-permute-done.34 = f32[4,48,128]{2,1,0:T(8,128)S(1)} collective-permute-done((f32[4,48,128]{2,1,0:T(8,128)S(1)}, f32[4,48,128]{2,1,0:T(8,128)S(1)}, u32[]{:S(2)}, u32[]{:S(2)}) %collective-permute-start.34) | collective-permute-done | bytes 98336 | tf_op jit(solution)/shard_map/ppermute | solution.py:28
  128.7 1.8 collective-permute-start.37
  132.5 1.7 collective-permute-done.37
  134.3 1.7 collective-permute-done.38.refs_1_
  136.0 4.8 %dose_and_warp.3 = (f32[4,2,64,128]{3,2,1,0:T(8,128)S(1)}, f32[4,2,64,128]{3,2,1,0:T(8,128)S(1)}, f32[4,2,64,128]{3,2,1,0:T(8,128)S(1)}, f32[4,2,64,128]{3,2,1,0:T(8,128)S(1)}) custom-call(s32[16]{0:T(128)S(1)} %get-tuple-element.105.source_ref, s32[16]{0:T(128)S(1)} %get-tuple-element.104.valid_ref, s32[2]{0:T(128)S(1)} %pad_add_fusion.me_ref, ...), custom_call_target="tpu_custom_call" | custom-call | flops 1 | bytes 1 | tf_op jit(solution)/shard_map/dose_and_warp/pallas_call | solution.py:112
  141.1 1.4 collective-permute-done.39
  143.7 1.6 collective-permute-start.42
  146.2 2.7 %collective-permute-done.40.refs_1_ = f32[2,2,64,128]{3,2,1,0:T(8,128)S(1)} collective-permute-done((f32[2,2,64,128]{3,2,1,0:T(8,128)S(1)}, f32[2,2,64,128]{3,2,1,0:T(8,128)S(1)}, u32[]{:S(2)}, u32[]{:S(2)}) %collective-permute-start.40) | collective-permute-done | bytes 131104 | tf_op jit(solution)/shard_map/ppermute | solution.py:28
  148.9 2.7 %collective-permute-done.42.refs_3_ = f32[2,2,64,128]{3,2,1,0:T(8,128)S(1)} collective-permute-done((f32[2,2,64,128]{3,2,1,0:T(8,128)S(1)}, f32[2,2,64,128]{3,2,1,0:T(8,128)S(1)}, u32[]{:S(2)}, u32[]{:S(2)}) %collective-permute-start.42) | collective-permute-done | bytes 131104 | tf_op jit(solution)/shard_map/ppermute | solution.py:28
  151.6 1.5 collective-permute-done.41.refs_2_
  154.1 1.5 collective-permute-start.53
  155.6 5.8 %collective-permute-done.43 = f32[8,64,128]{2,1,0:T(8,128)S(1)} collective-permute-done((f32[8,64,128]{2,1,0:T(8,128)S(1)}, f32[8,64,128]{2,1,0:T(8,128)S(1)}, u32[]{:S(2)}, u32[]{:S(2)}) %collective-permute-start.43) | collective-permute-done | bytes 262176 | tf_op jit(solution)/shard_map/ppermute | solution.py:28
  161.4 1.4 collective-permute-start.44
  164.7 3.2 %collective-permute-done.52.refs_2_ = f32[2,2,64,128]{3,2,1,0:T(8,128)S(1)} collective-permute-done((f32[2,2,64,128]{3,2,1,0:T(8,128)S(1)}, f32[2,2,64,128]{3,2,1,0:T(8,128)S(1)}, u32[]{:S(2)}, u32[]{:S(2)}) %collective-permute-start.52) | collective-permute-done | bytes 131104 | tf_op jit(solution)/shard_map/ppermute | solution.py:28
  169.9 4.3 %collective-permute-start.45 = (f32[8,64,128]{2,1,0:T(8,128)S(1)}, f32[8,64,128]{2,1,0:T(8,128)S(1)}, u32[]{:S(2)}, u32[]{:S(2)}) collective-permute-start(f32[8,64,128]{2,1,0:T(8,128)S(1)} %add.134.mine), channel_id=1, source_target_pairs={{0,8},{8,0},{16,24},{24,16},{1,9},{9,1},{17,25},{25,17},{2,10},{10... | collective-permute-start | bytes 786440 | tf_op jit(solution)/shard_map/ppermute | solution.py:28
  174.2 4.6 %collective-permute-done.54 = f32[8,64,128]{2,1,0:T(8,128)S(1)} collective-permute-done((f32[8,64,128]{2,1,0:T(8,128)S(1)}, f32[8,64,128]{2,1,0:T(8,128)S(1)}, u32[]{:S(2)}, u32[]{:S(2)}) %collective-permute-start.54) | collective-permute-done | bytes 262176 | tf_op jit(solution)/shard_map/ppermute | solution.py:28
  178.9 1.4 collective-permute-start.55
  180.3 3.2 %collective-permute-done.45.other = f32[8,64,128]{2,1,0:T(8,128)S(1)} collective-permute-done((f32[8,64,128]{2,1,0:T(8,128)S(1)}, f32[8,64,128]{2,1,0:T(8,128)S(1)}, u32[]{:S(2)}, u32[]{:S(2)}) %collective-permute-start.45) | collective-permute-done | bytes 262176 | tf_op jit(solution)/shard_map/ppermute | solution.py:28
  184.3 3.7 %collective-permute-done.55 = f32[8,64,128]{2,1,0:T(8,128)S(1)} collective-permute-done((f32[8,64,128]{2,1,0:T(8,128)S(1)}, f32[8,64,128]{2,1,0:T(8,128)S(1)}, u32[]{:S(2)}, u32[]{:S(2)}) %collective-permute-start.55) | collective-permute-done | bytes 262176 | tf_op jit(solution)/shard_map/ppermute | solution.py:28
  188.0 1.7 collective-permute-start.56
  189.8 1.8 collective-permute-start.49
  192.5 2.0 collective-permute-done.56.other
  196.8 1.8 collective-permute-start.60
  201.6 3.5 %collective-permute-done.60.refs_7_ = f32[2,2,64,128]{3,2,1,0:T(8,128)S(1)} collective-permute-done((f32[2,2,64,128]{3,2,1,0:T(8,128)S(1)}, f32[2,2,64,128]{3,2,1,0:T(8,128)S(1)}, u32[]{:S(2)}, u32[]{:S(2)}) %collective-permute-start.60) | collective-permute-done | bytes 131104 | tf_op jit(solution)/shard_map/ppermute | solution.py:28
  205.1 1.7 collective-permute-done.59.refs_6_
  206.9 4.7 %warp_back_and_gradient.3 = (f32[4,192,128]{2,1,0:T(8,128)S(1)}, f32[4,192,128]{2,1,0:T(8,128)S(1)}) custom-call(s32[16]{0:T(128)S(1)} %get-tuple-element.105.source_ref, s32[16]{0:T(128)S(1)} %get-tuple-element.104.valid_ref, s32[2]{0:T(128)S(1)} %pad_add_fusion.me_ref, f32[2048,1536]{1,0:T(8,128)S(1)} %bitcast.95, f32[16,128,128]{2,1,0:T(8,128)S(1)} %gather_fusion, ...), custom_call_target="tpu_custom_call" | custom-call | flops 1 | bytes 1 | tf_op jit(solution)/shard_map/warp_back_and_gradient/pallas_call | solution.py:183
  211.6 1.7 collective-permute-done.61
  217.0 1.4 collective-permute-done.62
  218.3 2.1 collective-permute-done.63
  221.4 1.6 collective-permute-start.65
  223.0 2.6 %collective-permute-start.66 = (f32[48,128]{1,0:T(8,128)S(1)}, f32[48,128]{1,0:T(8,128)S(1)}, u32[]{:S(2)}, u32[]{:S(2)}) collective-permute-start(f32[48,128]{1,0:T(8,128)S(1)} %get-tuple-element.184), channel_id=1, source_target_pairs={{0,24},{8,16},{16,8},{24,0},{1,25},{9,17},{17,9},{25,1},{2,26},{10... | collective-permute-start | bytes 73736 | tf_op jit(solution)/shard_map/ppermute | solution.py:28
  226.7 1.9 collective-permute-done.66
  228.7 1.7 collective-permute-done.67
  (204 shorter events, 60.3 us)
Async XLA Ops:
  0.6 9.5 %collective-permute-start = (f32[48,128]{1,0:T(8,128)}, f32[48,128]{1,0:T(8,128)S(1)}, u32[]{:S(2)}, u32[]{:S(2)}) collective-permute-start(f32[48,128]{1,0:T(8,128)} %param.15), channel_id=1, source_target_pairs={{0,8},{8,0},{16,24},{24,16},{1,9},{9,1},{17,25},{25,17},{2,10},{10... | collective-permute-start | bytes 73736 | tf_op jit(solution)/shard_map/ppermute | solution.py:28
  3.7 6.4 %collective-permute-start.1 = (f32[48,128]{1,0:T(8,128)}, f32[48,128]{1,0:T(8,128)S(1)}, u32[]{:S(2)}, u32[]{:S(2)}) collective-permute-start(f32[48,128]{1,0:T(8,128)} %param.15), channel_id=1, source_target_pairs={{0,24},{8,16},{16,8},{24,0},{1,25},{9,17},{17,9},{25,1},{2,26},{10... | collective-permute-start | bytes 73736 | tf_op jit(solution)/shard_map/ppermute | solution.py:28
  6.2 5.2 %collective-permute-start.2 = (f32[48,128]{1,0:T(8,128)}, f32[48,128]{1,0:T(8,128)S(1)}, u32[]{:S(2)}, u32[]{:S(2)}) collective-permute-start(f32[48,128]{1,0:T(8,128)} %param.15), channel_id=1, source_target_pairs={{0,16},{8,24},{16,0},{24,8},{1,17},{9,25},{17,1},{25,9},{2,18},{10... | collective-permute-start | bytes 73736 | tf_op jit(solution)/shard_map/ppermute | solution.py:28
  11.4 6.3 %collective-permute-start.4 = (f32[208,128]{1,0:T(8,128)S(1)}, f32[208,128]{1,0:T(8,128)S(1)}, u32[]{:S(2)}, u32[]{:S(2)}) collective-permute-start(f32[208,128]{1,0:T(8,128)S(1)} %constant_dynamic-update-slice_fusion), channel_id=1, source_target_pairs={{0,4},{1,5},{2,6},{3,7},{4,0},{5,1},{6,2},{7,3},{8,12},{9,13},{10,... | collective-permute-start | bytes 319496 | tf_op jit(solution)/shard_map/ppermute | solution.py:28
  12.9 5.6 %collective-permute-start.5 = (f32[208,128]{1,0:T(8,128)S(1)}, f32[208,128]{1,0:T(8,128)S(1)}, u32[]{:S(2)}, u32[]{:S(2)}) collective-permute-start(f32[208,128]{1,0:T(8,128)S(1)} %constant_dynamic-update-slice_fusion), channel_id=1, source_target_pairs={{0,6},{1,7},{2,4},{3,5},{4,2},{5,3},{6,0},{7,1},{8,14},{9,15},{10,... | collective-permute-start | bytes 319496 | tf_op jit(solution)/shard_map/ppermute | solution.py:28
  14.4 4.7 %collective-permute-start.3 = (f32[208,128]{1,0:T(8,128)S(1)}, f32[208,128]{1,0:T(8,128)S(1)}, u32[]{:S(2)}, u32[]{:S(2)}) collective-permute-start(f32[208,128]{1,0:T(8,128)S(1)} %constant_dynamic-update-slice_fusion), channel_id=1, source_target_pairs={{0,2},{1,3},{2,0},{3,1},{4,6},{5,7},{6,4},{7,5},{8,10},{9,11},{10,... | collective-permute-start | bytes 319496 | tf_op jit(solution)/shard_map/ppermute | solution.py:28
  19.1 1.8 collective-permute-start.6
  32.0 6.4 %collective-permute-start.8 = (f32[2,2,64,128]{3,2,1,0:T(8,128)S(1)}, f32[2,2,64,128]{3,2,1,0:T(8,128)S(1)}, u32[]{:S(2)}, u32[]{:S(2)}) collective-permute-start(f32[2,2,64,128]{3,2,1,0:T(8,128)S(1)} %pad_maximum_fusion.5), channel_id=1, source_target_pairs={{0,2},{1,3},{2,0},{3,1},{4,6},{5,7},{6,4},{7,5},{8,10},{9,11},{10,... | collective-permute-start | bytes 393224 | tf_op jit(solution)/shard_map/ppermute | solution.py:28
  33.2 8.3 %collective-permute-start.10 = (f32[2,2,64,128]{3,2,1,0:T(8,128)S(1)}, f32[2,2,64,128]{3,2,1,0:T(8,128)S(1)}, u32[]{:S(2)}, u32[]{:S(2)}) collective-permute-start(f32[2,2,64,128]{3,2,1,0:T(8,128)S(1)} %pad_maximum_fusion.7), channel_id=1, source_target_pairs={{0,6},{1,7},{2,4},{3,5},{4,2},{5,3},{6,0},{7,1},{8,14},{9,15},{10,... | collective-permute-start | bytes 393224 | tf_op jit(solution)/shard_map/ppermute | solution.py:28
  35.2 7.9 %collective-permute-start.9 = (f32[2,2,64,128]{3,2,1,0:T(8,128)S(1)}, f32[2,2,64,128]{3,2,1,0:T(8,128)S(1)}, u32[]{:S(2)}, u32[]{:S(2)}) collective-permute-start(f32[2,2,64,128]{3,2,1,0:T(8,128)S(1)} %pad_maximum_fusion.6), channel_id=1, source_target_pairs={{0,4},{1,5},{2,6},{3,7},{4,0},{5,1},{6,2},{7,3},{8,12},{9,13},{10,... | collective-permute-start | bytes 393224 | tf_op jit(solution)/shard_map/ppermute | solution.py:28
  38.4 7.8 %collective-permute-start.18 = (f32[4,2,64,128]{3,2,1,0:T(8,128)S(1)}, f32[4,2,64,128]{3,2,1,0:T(8,128)S(1)}, u32[]{:S(2)}, u32[]{:S(2)}) collective-permute-start(f32[4,2,64,128]{3,2,1,0:T(8,128)S(1)} %get-tuple-element.75), channel_id=1, source_target_pairs={{0,1},{1,0},{2,3},{3,2},{4,5},{5,4},{6,7},{7,6},{8,9},{9,8},{10,11... | collective-permute-start | bytes 786440 | tf_op jit(solution)/shard_map/ppermute | solution.py:28
  43.8 7.5 %collective-permute-start.11 = (f32[8,64,128]{2,1,0:T(8,128)S(1)}, f32[8,64,128]{2,1,0:T(8,128)S(1)}, u32[]{:S(2)}, u32[]{:S(2)}) collective-permute-start(f32[8,64,128]{2,1,0:T(8,128)S(1)} %get-tuple-element.68), channel_id=1, source_target_pairs={{0,8},{8,0},{16,24},{24,16},{1,9},{9,1},{17,25},{25,17},{2,10},{10... | collective-permute-start | bytes 786440 | tf_op jit(solution)/shard_map/ppermute | solution.py:28
  46.3 6.8 %collective-permute-start.21 = (f32[2,2,64,128]{3,2,1,0:T(8,128)S(1)}, f32[2,2,64,128]{3,2,1,0:T(8,128)S(1)}, u32[]{:S(2)}, u32[]{:S(2)}) collective-permute-start(f32[2,2,64,128]{3,2,1,0:T(8,128)S(1)} %pad_maximum_fusion.15), channel_id=1, source_target_pairs={{0,6},{1,7},{2,4},{3,5},{4,2},{5,3},{6,0},{7,1},{8,14},{9,15},{10,... | collective-permute-start | bytes 393224 | tf_op jit(solution)/shard_map/ppermute | solution.py:28
  47.5 6.9 %collective-permute-start.20 = (f32[2,2,64,128]{3,2,1,0:T(8,128)S(1)}, f32[2,2,64,128]{3,2,1,0:T(8,128)S(1)}, u32[]{:S(2)}, u32[]{:S(2)}) collective-permute-start(f32[2,2,64,128]{3,2,1,0:T(8,128)S(1)} %pad_maximum_fusion.14), channel_id=1, source_target_pairs={{0,4},{1,5},{2,6},{3,7},{4,0},{5,1},{6,2},{7,3},{8,12},{9,13},{10,... | collective-permute-start | bytes 393224 | tf_op jit(solution)/shard_map/ppermute | solution.py:28
  49.2 5.2 %collective-permute-start.19 = (f32[2,2,64,128]{3,2,1,0:T(8,128)S(1)}, f32[2,2,64,128]{3,2,1,0:T(8,128)S(1)}, u32[]{:S(2)}, u32[]{:S(2)}) collective-permute-start(f32[2,2,64,128]{3,2,1,0:T(8,128)S(1)} %pad_maximum_fusion.13), channel_id=1, source_target_pairs={{0,2},{1,3},{2,0},{3,1},{4,6},{5,7},{6,4},{7,5},{8,10},{9,11},{10,... | collective-permute-start | bytes 393224 | tf_op jit(solution)/shard_map/ppermute | solution.py:28
  51.3 9.6 %collective-permute-start.12 = (f32[8,64,128]{2,1,0:T(8,128)S(1)}, f32[8,64,128]{2,1,0:T(8,128)S(1)}, u32[]{:S(2)}, u32[]{:S(2)}) collective-permute-start(f32[8,64,128]{2,1,0:T(8,128)S(1)} %add.122), channel_id=1, source_target_pairs={{0,24},{8,16},{16,8},{24,0},{1,25},{9,17},{17,9},{25,1},{2,26},{10... | collective-permute-start | bytes 786440 | tf_op jit(solution)/shard_map/ppermute | solution.py:28
  55.3 10.2 %collective-permute-start.22 = (f32[8,64,128]{2,1,0:T(8,128)S(1)}, f32[8,64,128]{2,1,0:T(8,128)S(1)}, u32[]{:S(2)}, u32[]{:S(2)}) collective-permute-start(f32[8,64,128]{2,1,0:T(8,128)S(1)} %get-tuple-element.77), channel_id=1, source_target_pairs={{0,8},{8,0},{16,24},{24,16},{1,9},{9,1},{17,25},{25,17},{2,10},{10... | collective-permute-start | bytes 786440 | tf_op jit(solution)/shard_map/ppermute | solution.py:28
  60.9 11.2 %collective-permute-start.13 = (f32[8,64,128]{2,1,0:T(8,128)S(1)}, f32[8,64,128]{2,1,0:T(8,128)S(1)}, u32[]{:S(2)}, u32[]{:S(2)}) collective-permute-start(f32[8,64,128]{2,1,0:T(8,128)S(1)} %add.123.mine), channel_id=1, source_target_pairs={{0,8},{8,0},{16,24},{24,16},{1,9},{9,1},{17,25},{25,17},{2,10},{10... | collective-permute-start | bytes 786440 | tf_op jit(solution)/shard_map/ppermute | solution.py:28
  65.6 11.9 %collective-permute-start.23 = (f32[8,64,128]{2,1,0:T(8,128)S(1)}, f32[8,64,128]{2,1,0:T(8,128)S(1)}, u32[]{:S(2)}, u32[]{:S(2)}) collective-permute-start(f32[8,64,128]{2,1,0:T(8,128)S(1)} %add.124), channel_id=1, source_target_pairs={{0,24},{8,16},{16,8},{24,0},{1,25},{9,17},{17,9},{25,1},{2,26},{10... | collective-permute-start | bytes 786440 | tf_op jit(solution)/shard_map/ppermute | solution.py:28
  73.0 5.8 %collective-permute-start.14 = (f32[4,2,64,128]{3,2,1,0:T(8,128)S(1)}, f32[4,2,64,128]{3,2,1,0:T(8,128)S(1)}, u32[]{:S(2)}, u32[]{:S(2)}) collective-permute-start(f32[4,2,64,128]{3,2,1,0:T(8,128)S(1)} %get-tuple-element.71), channel_id=1, source_target_pairs={{0,1},{1,0},{2,3},{3,2},{4,5},{5,4},{6,7},{7,6},{8,9},{9,8},{10,11... | collective-permute-start | bytes 786440 | tf_op jit(solution)/shard_map/ppermute | solution.py:28
  77.5 6.4 %collective-permute-start.24 = (f32[8,64,128]{2,1,0:T(8,128)S(1)}, f32[8,64,128]{2,1,0:T(8,128)S(1)}, u32[]{:S(2)}, u32[]{:S(2)}) collective-permute-start(f32[8,64,128]{2,1,0:T(8,128)S(1)} %add.125.mine), channel_id=1, source_target_pairs={{0,8},{8,0},{16,24},{24,16},{1,9},{9,1},{17,25},{25,17},{2,10},{10... | collective-permute-start | bytes 786440 | tf_op jit(solution)/shard_map/ppermute | solution.py:28
  78.8 10.4 %collective-permute-start.17 = (f32[2,2,64,128]{3,2,1,0:T(8,128)S(1)}, f32[2,2,64,128]{3,2,1,0:T(8,128)S(1)}, u32[]{:S(2)}, u32[]{:S(2)}) collective-permute-start(f32[2,2,64,128]{3,2,1,0:T(8,128)S(1)} %pad_maximum_fusion.11), channel_id=1, source_target_pairs={{0,6},{1,7},{2,4},{3,5},{4,2},{5,3},{6,0},{7,1},{8,14},{9,15},{10,... | collective-permute-start | bytes 393224 | tf_op jit(solution)/shard_map/ppermute | solution.py:28
  79.4 10.8 %collective-permute-start.16 = (f32[2,2,64,128]{3,2,1,0:T(8,128)S(1)}, f32[2,2,64,128]{3,2,1,0:T(8,128)S(1)}, u32[]{:S(2)}, u32[]{:S(2)}) collective-permute-start(f32[2,2,64,128]{3,2,1,0:T(8,128)S(1)} %pad_maximum_fusion.10), channel_id=1, source_target_pairs={{0,4},{1,5},{2,6},{3,7},{4,0},{5,1},{6,2},{7,3},{8,12},{9,13},{10,... | collective-permute-start | bytes 393224 | tf_op jit(solution)/shard_map/ppermute | solution.py:28
  84.9 6.4 %collective-permute-start.15 = (f32[2,2,64,128]{3,2,1,0:T(8,128)S(1)}, f32[2,2,64,128]{3,2,1,0:T(8,128)S(1)}, u32[]{:S(2)}, u32[]{:S(2)}) collective-permute-start(f32[2,2,64,128]{3,2,1,0:T(8,128)S(1)} %pad_maximum_fusion.9), channel_id=1, source_target_pairs={{0,2},{1,3},{2,0},{3,1},{4,6},{5,7},{6,4},{7,5},{8,10},{9,11},{10,... | collective-permute-start | bytes 393224 | tf_op jit(solution)/shard_map/ppermute | solution.py:28
  86.5 7.6 %collective-permute-start.28 = (f32[2,2,64,128]{3,2,1,0:T(8,128)S(1)}, f32[2,2,64,128]{3,2,1,0:T(8,128)S(1)}, u32[]{:S(2)}, u32[]{:S(2)}) collective-permute-start(f32[2,2,64,128]{3,2,1,0:T(8,128)S(1)} %pad_maximum_fusion.19), channel_id=1, source_target_pairs={{0,6},{1,7},{2,4},{3,5},{4,2},{5,3},{6,0},{7,1},{8,14},{9,15},{10,... | collective-permute-start | bytes 393224 | tf_op jit(solution)/shard_map/ppermute | solution.py:28
  87.6 8.1 %collective-permute-start.27 = (f32[2,2,64,128]{3,2,1,0:T(8,128)S(1)}, f32[2,2,64,128]{3,2,1,0:T(8,128)S(1)}, u32[]{:S(2)}, u32[]{:S(2)}) collective-permute-start(f32[2,2,64,128]{3,2,1,0:T(8,128)S(1)} %pad_maximum_fusion.18), channel_id=1, source_target_pairs={{0,4},{1,5},{2,6},{3,7},{4,0},{5,1},{6,2},{7,3},{8,12},{9,13},{10,... | collective-permute-start | bytes 393224 | tf_op jit(solution)/shard_map/ppermute | solution.py:28
  89.3 7.3 %collective-permute-start.26 = (f32[2,2,64,128]{3,2,1,0:T(8,128)S(1)}, f32[2,2,64,128]{3,2,1,0:T(8,128)S(1)}, u32[]{:S(2)}, u32[]{:S(2)}) collective-permute-start(f32[2,2,64,128]{3,2,1,0:T(8,128)S(1)} %pad_maximum_fusion.17), channel_id=1, source_target_pairs={{0,2},{1,3},{2,0},{3,1},{4,6},{5,7},{6,4},{7,5},{8,10},{9,11},{10,... | collective-permute-start | bytes 393224 | tf_op jit(solution)/shard_map/ppermute | solution.py:28
  105.8 1.8 collective-permute-start.29
  107.7 4.9 %collective-permute-start.30 = (f32[192,128]{1,0:T(8,128)S(1)}, f32[192,128]{1,0:T(8,128)S(1)}, u32[]{:S(2)}, u32[]{:S(2)}) collective-permute-start(f32[192,128]{1,0:T(8,128)S(1)} %get-tuple-element.115), channel_id=1, source_target_pairs={{0,2},{1,3},{2,0},{3,1},{4,6},{5,7},{6,4},{7,5},{8,10},{9,11},{10,... | collective-permute-start | bytes 294920 | tf_op jit(solution)/shard_map/ppermute | solution.py:28
  108.9 6.7 %collective-permute-start.31 = (f32[192,128]{1,0:T(8,128)S(1)}, f32[192,128]{1,0:T(8,128)S(1)}, u32[]{:S(2)}, u32[]{:S(2)}) collective-permute-start(f32[192,128]{1,0:T(8,128)S(1)} %get-tuple-element.117), channel_id=1, source_target_pairs={{0,4},{1,5},{2,6},{3,7},{4,0},{5,1},{6,2},{7,3},{8,12},{9,13},{10,... | collective-permute-start | bytes 294920 | tf_op jit(solution)/shard_map/ppermute | solution.py:28
  109.4 6.2 %collective-permute-start.32 = (f32[192,128]{1,0:T(8,128)S(1)}, f32[192,128]{1,0:T(8,128)S(1)}, u32[]{:S(2)}, u32[]{:S(2)}) collective-permute-start(f32[192,128]{1,0:T(8,128)S(1)} %get-tuple-element.116), channel_id=1, source_target_pairs={{0,6},{1,7},{2,4},{3,5},{4,2},{5,3},{6,0},{7,1},{8,14},{9,15},{10,... | collective-permute-start | bytes 294920 | tf_op jit(solution)/shard_map/ppermute | solution.py:28
  115.6 4.7 %collective-permute-start.33 = (f32[4,48,128]{2,1,0:T(8,128)S(1)}, f32[4,48,128]{2,1,0:T(8,128)S(1)}, u32[]{:S(2)}, u32[]{:S(2)}) collective-permute-start(f32[4,48,128]{2,1,0:T(8,128)S(1)} %bitcast.101), channel_id=1, source_target_pairs={{0,8},{8,0},{16,24},{24,16},{1,9},{9,1},{17,25},{25,17},{2,10},{10... | collective-permute-start | bytes 294920 | tf_op jit(solution)/shard_map/ppermute | solution.py:28
  120.4 6.5 %collective-permute-start.34 = (f32[4,48,128]{2,1,0:T(8,128)S(1)}, f32[4,48,128]{2,1,0:T(8,128)S(1)}, u32[]{:S(2)}, u32[]{:S(2)}) collective-permute-start(f32[4,48,128]{2,1,0:T(8,128)S(1)} %bitcast_add_fusion.1), channel_id=1, source_target_pairs={{0,24},{8,16},{16,8},{24,0},{1,25},{9,17},{17,9},{25,1},{2,26},{10... | collective-permute-start | bytes 294920 | tf_op jit(solution)/shard_map/ppermute | solution.py:28
  126.9 4.7 %collective-permute-start.35 = (f32[192,128]{1,0:T(8,128)S(1)}, f32[192,128]{1,0:T(8,128)S(1)}, u32[]{:S(2)}, u32[]{:S(2)}) collective-permute-start(f32[192,128]{1,0:T(8,128)S(1)} %fusion.10), channel_id=1, source_target_pairs={{0,2},{1,3},{2,0},{3,1},{4,6},{5,7},{6,4},{7,5},{8,10},{9,11},{10,... | collective-permute-start | bytes 294920 | tf_op jit(solution)/shard_map/ppermute | solution.py:28
  127.9 4.6 %collective-permute-start.36 = (f32[192,128]{1,0:T(8,128)S(1)}, f32[192,128]{1,0:T(8,128)S(1)}, u32[]{:S(2)}, u32[]{:S(2)}) collective-permute-start(f32[192,128]{1,0:T(8,128)S(1)} %fusion.10), channel_id=1, source_target_pairs={{0,4},{1,5},{2,6},{3,7},{4,0},{5,1},{6,2},{7,3},{8,12},{9,13},{10,... | collective-permute-start | bytes 294920 | tf_op jit(solution)/shard_map/ppermute | solution.py:28
  128.7 5.5 %collective-permute-start.37 = (f32[192,128]{1,0:T(8,128)S(1)}, f32[192,128]{1,0:T(8,128)S(1)}, u32[]{:S(2)}, u32[]{:S(2)}) collective-permute-start(f32[192,128]{1,0:T(8,128)S(1)} %fusion.10), channel_id=1, source_target_pairs={{0,6},{1,7},{2,4},{3,5},{4,2},{5,3},{6,0},{7,1},{8,14},{9,15},{10,... | collective-permute-start | bytes 294920 | tf_op jit(solution)/shard_map/ppermute | solution.py:28
  134.2 1.8 collective-permute-start.38
  142.5 6.4 %collective-permute-start.40 = (f32[2,2,64,128]{3,2,1,0:T(8,128)S(1)}, f32[2,2,64,128]{3,2,1,0:T(8,128)S(1)}, u32[]{:S(2)}, u32[]{:S(2)}) collective-permute-start(f32[2,2,64,128]{3,2,1,0:T(8,128)S(1)} %pad_maximum_fusion.21), channel_id=1, source_target_pairs={{0,2},{1,3},{2,0},{3,1},{4,6},{5,7},{6,4},{7,5},{8,10},{9,11},{10,... | collective-permute-start | bytes 393224 | tf_op jit(solution)/shard_map/ppermute | solution.py:28
  143.7 7.9 %collective-permute-start.42 = (f32[2,2,64,128]{3,2,1,0:T(8,128)S(1)}, f32[2,2,64,128]{3,2,1,0:T(8,128)S(1)}, u32[]{:S(2)}, u32[]{:S(2)}) collective-permute-start(f32[2,2,64,128]{3,2,1,0:T(8,128)S(1)} %pad_maximum_fusion.23), channel_id=1, source_target_pairs={{0,6},{1,7},{2,4},{3,5},{4,2},{5,3},{6,0},{7,1},{8,14},{9,15},{10,... | collective-permute-start | bytes 393224 | tf_op jit(solution)/shard_map/ppermute | solution.py:28
  145.3 7.9 %collective-permute-start.41 = (f32[2,2,64,128]{3,2,1,0:T(8,128)S(1)}, f32[2,2,64,128]{3,2,1,0:T(8,128)S(1)}, u32[]{:S(2)}, u32[]{:S(2)}) collective-permute-start(f32[2,2,64,128]{3,2,1,0:T(8,128)S(1)} %pad_maximum_fusion.22), channel_id=1, source_target_pairs={{0,4},{1,5},{2,6},{3,7},{4,0},{5,1},{6,2},{7,3},{8,12},{9,13},{10,... | collective-permute-start | bytes 393224 | tf_op jit(solution)/shard_map/ppermute | solution.py:28
  148.9 5.1 %collective-permute-start.50 = (f32[4,2,64,128]{3,2,1,0:T(8,128)S(1)}, f32[4,2,64,128]{3,2,1,0:T(8,128)S(1)}, u32[]{:S(2)}, u32[]{:S(2)}) collective-permute-start(f32[4,2,64,128]{3,2,1,0:T(8,128)S(1)} %get-tuple-element.93), channel_id=1, source_target_pairs={{0,1},{1,0},{2,3},{3,2},{4,5},{5,4},{6,7},{7,6},{8,9},{9,8},{10,11... | collective-permute-start | bytes 786440 | tf_op jit(solution)/shard_map/ppermute | solution.py:28
  153.9 7.4 %collective-permute-start.43 = (f32[8,64,128]{2,1,0:T(8,128)S(1)}, f32[8,64,128]{2,1,0:T(8,128)S(1)}, u32[]{:S(2)}, u32[]{:S(2)}) collective-permute-start(f32[8,64,128]{2,1,0:T(8,128)S(1)} %get-tuple-element.87), channel_id=1, source_target_pairs={{0,8},{8,0},{16,24},{24,16},{1,9},{9,1},{17,25},{25,17},{2,10},{10... | collective-permute-start | bytes 786440 | tf_op jit(solution)/shard_map/ppermute | solution.py:28
  154.1 10.6 %collective-permute-start.53 = (f32[2,2,64,128]{3,2,1,0:T(8,128)S(1)}, f32[2,2,64,128]{3,2,1,0:T(8,128)S(1)}, u32[]{:S(2)}, u32[]{:S(2)}) collective-permute-start(f32[2,2,64,128]{3,2,1,0:T(8,128)S(1)} %pad_maximum_fusion.31), channel_id=1, source_target_pairs={{0,6},{1,7},{2,4},{3,5},{4,2},{5,3},{6,0},{7,1},{8,14},{9,15},{10,... | collective-permute-start | bytes 393224 | tf_op jit(solution)/shard_map/ppermute | solution.py:28
  161.4 8.5 %collective-permute-start.44 = (f32[8,64,128]{2,1,0:T(8,128)S(1)}, f32[8,64,128]{2,1,0:T(8,128)S(1)}, u32[]{:S(2)}, u32[]{:S(2)}) collective-permute-start(f32[8,64,128]{2,1,0:T(8,128)S(1)} %add.133), channel_id=1, source_target_pairs={{0,24},{8,16},{16,8},{24,0},{1,25},{9,17},{17,9},{25,1},{2,26},{10... | collective-permute-start | bytes 786440 | tf_op jit(solution)/shard_map/ppermute | solution.py:28
  162.8 5.0 %collective-permute-start.52 = (f32[2,2,64,128]{3,2,1,0:T(8,128)S(1)}, f32[2,2,64,128]{3,2,1,0:T(8,128)S(1)}, u32[]{:S(2)}, u32[]{:S(2)}) collective-permute-start(f32[2,2,64,128]{3,2,1,0:T(8,128)S(1)} %pad_maximum_fusion.30), channel_id=1, source_target_pairs={{0,4},{1,5},{2,6},{3,7},{4,0},{5,1},{6,2},{7,3},{8,12},{9,13},{10,... | collective-permute-start | bytes 393224 | tf_op jit(solution)/shard_map/ppermute | solution.py:28
  163.7 5.0 %collective-permute-start.51 = (f32[2,2,64,128]{3,2,1,0:T(8,128)S(1)}, f32[2,2,64,128]{3,2,1,0:T(8,128)S(1)}, u32[]{:S(2)}, u32[]{:S(2)}) collective-permute-start(f32[2,2,64,128]{3,2,1,0:T(8,128)S(1)} %pad_maximum_fusion.29), channel_id=1, source_target_pairs={{0,2},{1,3},{2,0},{3,1},{4,6},{5,7},{6,4},{7,5},{8,10},{9,11},{10,... | collective-permute-start | bytes 393224 | tf_op jit(solution)/shard_map/ppermute | solution.py:28
  169.8 9.1 %collective-permute-start.54 = (f32[8,64,128]{2,1,0:T(8,128)S(1)}, f32[8,64,128]{2,1,0:T(8,128)S(1)}, u32[]{:S(2)}, u32[]{:S(2)}) collective-permute-start(f32[8,64,128]{2,1,0:T(8,128)S(1)} %get-tuple-element.95), channel_id=1, source_target_pairs={{0,8},{8,0},{16,24},{24,16},{1,9},{9,1},{17,25},{25,17},{2,10},{10... | collective-permute-start | bytes 786440 | tf_op jit(solution)/shard_map/ppermute | solution.py:28
  169.9 13.5 %collective-permute-start.45 = (f32[8,64,128]{2,1,0:T(8,128)S(1)}, f32[8,64,128]{2,1,0:T(8,128)S(1)}, u32[]{:S(2)}, u32[]{:S(2)}) collective-permute-start(f32[8,64,128]{2,1,0:T(8,128)S(1)} %add.134.mine), channel_id=1, source_target_pairs={{0,8},{8,0},{16,24},{24,16},{1,9},{9,1},{17,25},{25,17},{2,10},{10... | collective-permute-start | bytes 786440 | tf_op jit(solution)/shard_map/ppermute | solution.py:28
  178.9 9.1 %collective-permute-start.55 = (f32[8,64,128]{2,1,0:T(8,128)S(1)}, f32[8,64,128]{2,1,0:T(8,128)S(1)}, u32[]{:S(2)}, u32[]{:S(2)}) collective-permute-start(f32[8,64,128]{2,1,0:T(8,128)S(1)} %add.135), channel_id=1, source_target_pairs={{0,24},{8,16},{16,8},{24,0},{1,25},{9,17},{17,9},{25,1},{2,26},{10... | collective-permute-start | bytes 786440 | tf_op jit(solution)/shard_map/ppermute | solution.py:28
  184.1 5.6 %collective-permute-start.46 = (f32[4,2,64,128]{3,2,1,0:T(8,128)S(1)}, f32[4,2,64,128]{3,2,1,0:T(8,128)S(1)}, u32[]{:S(2)}, u32[]{:S(2)}) collective-permute-start(f32[4,2,64,128]{3,2,1,0:T(8,128)S(1)} %get-tuple-element.89), channel_id=1, source_target_pairs={{0,1},{1,0},{2,3},{3,2},{4,5},{5,4},{6,7},{7,6},{8,9},{9,8},{10,11... | collective-permute-start | bytes 786440 | tf_op jit(solution)/shard_map/ppermute | solution.py:28
  188.0 6.4 %collective-permute-start.56 = (f32[8,64,128]{2,1,0:T(8,128)S(1)}, f32[8,64,128]{2,1,0:T(8,128)S(1)}, u32[]{:S(2)}, u32[]{:S(2)}) collective-permute-start(f32[8,64,128]{2,1,0:T(8,128)S(1)} %add.136.mine), channel_id=1, source_target_pairs={{0,8},{8,0},{16,24},{24,16},{1,9},{9,1},{17,25},{25,17},{2,10},{10... | collective-permute-start | bytes 786440 | tf_op jit(solution)/shard_map/ppermute | solution.py:28
  189.8 9.8 %collective-permute-start.49 = (f32[2,2,64,128]{3,2,1,0:T(8,128)S(1)}, f32[2,2,64,128]{3,2,1,0:T(8,128)S(1)}, u32[]{:S(2)}, u32[]{:S(2)}) collective-permute-start(f32[2,2,64,128]{3,2,1,0:T(8,128)S(1)} %pad_maximum_fusion.27), channel_id=1, source_target_pairs={{0,6},{1,7},{2,4},{3,5},{4,2},{5,3},{6,0},{7,1},{8,14},{9,15},{10,... | collective-permute-start | bytes 393224 | tf_op jit(solution)/shard_map/ppermute | solution.py:28
  191.6 9.0 %collective-permute-start.48 = (f32[2,2,64,128]{3,2,1,0:T(8,128)S(1)}, f32[2,2,64,128]{3,2,1,0:T(8,128)S(1)}, u32[]{:S(2)}, u32[]{:S(2)}) collective-permute-start(f32[2,2,64,128]{3,2,1,0:T(8,128)S(1)} %pad_maximum_fusion.26), channel_id=1, source_target_pairs={{0,4},{1,5},{2,6},{3,7},{4,0},{5,1},{6,2},{7,3},{8,12},{9,13},{10,... | collective-permute-start | bytes 393224 | tf_op jit(solution)/shard_map/ppermute | solution.py:28
  195.2 6.4 %collective-permute-start.47 = (f32[2,2,64,128]{3,2,1,0:T(8,128)S(1)}, f32[2,2,64,128]{3,2,1,0:T(8,128)S(1)}, u32[]{:S(2)}, u32[]{:S(2)}) collective-permute-start(f32[2,2,64,128]{3,2,1,0:T(8,128)S(1)} %pad_maximum_fusion.25), channel_id=1, source_target_pairs={{0,2},{1,3},{2,0},{3,1},{4,6},{5,7},{6,4},{7,5},{8,10},{9,11},{10,... | collective-permute-start | bytes 393224 | tf_op jit(solution)/shard_map/ppermute | solution.py:28
  196.8 8.3 %collective-permute-start.60 = (f32[2,2,64,128]{3,2,1,0:T(8,128)S(1)}, f32[2,2,64,128]{3,2,1,0:T(8,128)S(1)}, u32[]{:S(2)}, u32[]{:S(2)}) collective-permute-start(f32[2,2,64,128]{3,2,1,0:T(8,128)S(1)} %pad_maximum_fusion.35), channel_id=1, source_target_pairs={{0,6},{1,7},{2,4},{3,5},{4,2},{5,3},{6,0},{7,1},{8,14},{9,15},{10,... | collective-permute-start | bytes 393224 | tf_op jit(solution)/shard_map/ppermute | solution.py:28
  198.7 8.1 %collective-permute-start.59 = (f32[2,2,64,128]{3,2,1,0:T(8,128)S(1)}, f32[2,2,64,128]{3,2,1,0:T(8,128)S(1)}, u32[]{:S(2)}, u32[]{:S(2)}) collective-permute-start(f32[2,2,64,128]{3,2,1,0:T(8,128)S(1)} %pad_maximum_fusion.34), channel_id=1, source_target_pairs={{0,4},{1,5},{2,6},{3,7},{4,0},{5,1},{6,2},{7,3},{8,12},{9,13},{10,... | collective-permute-start | bytes 393224 | tf_op jit(solution)/shard_map/ppermute | solution.py:28
  199.6 7.3 %collective-permute-start.58 = (f32[2,2,64,128]{3,2,1,0:T(8,128)S(1)}, f32[2,2,64,128]{3,2,1,0:T(8,128)S(1)}, u32[]{:S(2)}, u32[]{:S(2)}) collective-permute-start(f32[2,2,64,128]{3,2,1,0:T(8,128)S(1)} %pad_maximum_fusion.33), channel_id=1, source_target_pairs={{0,2},{1,3},{2,0},{3,1},{4,6},{5,7},{6,4},{7,5},{8,10},{9,11},{10,... | collective-permute-start | bytes 393224 | tf_op jit(solution)/shard_map/ppermute | solution.py:28
  211.6 1.8 collective-permute-start.61
  213.4 4.9 %collective-permute-start.62 = (f32[192,128]{1,0:T(8,128)S(1)}, f32[192,128]{1,0:T(8,128)S(1)}, u32[]{:S(2)}, u32[]{:S(2)}) collective-permute-start(f32[192,128]{1,0:T(8,128)S(1)} %get-tuple-element.112), channel_id=1, source_target_pairs={{0,2},{1,3},{2,0},{3,1},{4,6},{5,7},{6,4},{7,5},{8,10},{9,11},{10,... | collective-permute-start | bytes 294920 | tf_op jit(solution)/shard_map/ppermute | solution.py:28
  214.6 5.8 %collective-permute-start.63 = (f32[192,128]{1,0:T(8,128)S(1)}, f32[192,128]{1,0:T(8,128)S(1)}, u32[]{:S(2)}, u32[]{:S(2)}) collective-permute-start(f32[192,128]{1,0:T(8,128)S(1)} %get-tuple-element.114), channel_id=1, source_target_pairs={{0,4},{1,5},{2,6},{3,7},{4,0},{5,1},{6,2},{7,3},{8,12},{9,13},{10,... | collective-permute-start | bytes 294920 | tf_op jit(solution)/shard_map/ppermute | solution.py:28
  215.8 5.5 %collective-permute-start.64 = (f32[192,128]{1,0:T(8,128)S(1)}, f32[192,128]{1,0:T(8,128)S(1)}, u32[]{:S(2)}, u32[]{:S(2)}) collective-permute-start(f32[192,128]{1,0:T(8,128)S(1)} %get-tuple-element.113), channel_id=1, source_target_pairs={{0,6},{1,7},{2,4},{3,5},{4,2},{5,3},{6,0},{7,1},{8,14},{9,15},{10,... | collective-permute-start | bytes 294920 | tf_op jit(solution)/shard_map/ppermute | solution.py:28
  221.4 5.3 %collective-permute-start.65 = (f32[48,128]{1,0:T(8,128)S(1)}, f32[48,128]{1,0:T(8,128)S(1)}, u32[]{:S(2)}, u32[]{:S(2)}) collective-permute-start(f32[48,128]{1,0:T(8,128)S(1)} %get-tuple-element.182), channel_id=1, source_target_pairs={{0,8},{8,0},{16,24},{24,16},{1,9},{9,1},{17,25},{25,17},{2,10},{10... | collective-permute-start | bytes 73736 | tf_op jit(solution)/shard_map/ppermute | solution.py:28
  223.0 5.6 %collective-permute-start.66 = (f32[48,128]{1,0:T(8,128)S(1)}, f32[48,128]{1,0:T(8,128)S(1)}, u32[]{:S(2)}, u32[]{:S(2)}) collective-permute-start(f32[48,128]{1,0:T(8,128)S(1)} %get-tuple-element.184), channel_id=1, source_target_pairs={{0,24},{8,16},{16,8},{24,0},{1,25},{9,17},{17,9},{25,1},{2,26},{10... | collective-permute-start | bytes 73736 | tf_op jit(solution)/shard_map/ppermute | solution.py:28
  225.6 4.7 %collective-permute-start.67 = (f32[48,128]{1,0:T(8,128)S(1)}, f32[48,128]{1,0:T(8,128)S(1)}, u32[]{:S(2)}, u32[]{:S(2)}) collective-permute-start(f32[48,128]{1,0:T(8,128)S(1)} %get-tuple-element.183), channel_id=1, source_target_pairs={{0,16},{8,24},{16,0},{24,8},{1,17},{9,25},{17,1},{25,9},{2,18},{10... | collective-permute-start | bytes 73736 | tf_op jit(solution)/shard_map/ppermute | solution.py:28
  (11 other events, 140.0 us)

commit v7 on v6

--- a/solution.py
+++ b/solution.py
@@ -231,7 +231,8 @@
     )(which, slots, *incoming)
 
 
-def pull_body(vox, cores, with_dose, which_ref, slot_ref, mine, other, goal, scale, *refs):
+def pull_body(vox, cores, with_dose, ahead, which_ref, slot_ref, mine, other, goal, scale, *refs):
+    refs = refs[ahead:]
     half = mine.shape[0]
     which = which_ref[0]
     field = refs[-1]
@@ -245,22 +246,22 @@
         refs[cores][...] = field[...]
 
 
-def pull(which, slots, mine, other, goal, scale, vox, with_dose):
+def pull(which, slots, mine, other, goal, scale, vox, with_dose, ahead):
     half, height, plans = mine.shape
     cores = core_count()
     outs = [jax.ShapeDtypeStruct((vox // cores, CAP, height, plans), F32)] * cores
     if with_dose:
         outs = outs + [jax.ShapeDtypeStruct((2 * half, height, plans), F32)]
     return pl.pallas_call(
-        functools.partial(pull_body, vox, cores, with_dose),
-        in_specs=specs(2, pltpu.SMEM) + specs(4, pltpu.VMEM),
+        functools.partial(pull_body, vox, cores, with_dose, len(ahead)),
+        in_specs=specs(2, pltpu.SMEM) + specs(4 + len(ahead), pltpu.VMEM),
         out_specs=specs(len(outs), pltpu.VMEM),
         out_shape=outs,
         scratch_shapes=[pltpu.VMEM((2 * half, height, plans), F32)],
         compiler_params=pltpu.CompilerParams(vmem_limit_bytes=SMALL),
         cost_estimate=BRIEF,
         name="adjoint_blocks",
-    )(which, slots, mine, other, goal, scale)
+    )(which, slots, mine, other, goal, scale, *ahead)
 
 
 def phase_steps():
@@ -314,6 +315,22 @@
 
 def exchange(pieces):
     return send(cross(pieces))
+
+
+def hold_body(matrix, x, out):
+    out[...] = x[0, :8, :]
+
+
+def hold(matrix, x):
+    return pl.pallas_call(
+        hold_body,
+        in_specs=specs(2, pltpu.VMEM),
+        out_specs=pl.BlockSpec(memory_space=pltpu.VMEM),
+        out_shape=jax.ShapeDtypeStruct((8, x.shape[-1]), F32),
+        compiler_params=pltpu.CompilerParams(vmem_limit_bytes=SMALL),
+        cost_estimate=BRIEF,
+        name="hold",
+    )(matrix, x)
 
 
 def phase_stages(half):
@@ -415,7 +432,7 @@
                 )
             if h + 1 < CHUNKS:
                 later = outgoing[(h + 1) * cores : (h + 2) * cores]
-                incoming = exchange([tie(x, incoming[1]) for x in later])
+                incoming = exchange([tie(x, incoming[2]) for x in later])
             if h > 0:
                 got = tie(got, seconds[-1])
             half, second = phase_stages(keep + got)
@@ -425,7 +442,8 @@
             second = seconds[h] if h == 0 else tie(seconds[h], other)
             mine = held_halves[h] + second
             other = swap(mine, PHASE, 1)
-            back = pull(which, received, mine, other, goals[h], scales[h], vox, last)
+            ahead = [hold(matrix, held_halves[1])] if iteration == 0 and h == 0 else []
+            back = pull(which, received, mine, other, goals[h], scales[h], vox, last, ahead)
             returned += exchange(back[:cores])
             dose += back[cores:]
         parts = gradient_parts(scalars, matrix, tiles, returned, rows, vox, masks)

time: 231 us -> 225 us (0.974)
  waiting for transfers between devices: 106 us -> 101 us
    ppermute x68, waiting for transfers between devices: 106 us -> 101 us  [swap(): return lax.ppermute(x, axis, [(i, i ^ mask) for i in range(count)])]
    unnamed x18 -> x20, local copies, waits for them, and re-layouts: 9.95 us -> 9.95 us
  transfers between devices with their start and end apart: 68 -> 68, of which waited for: 52 -> 51; matrix products, arithmetic and copies ran while one was open for 5% -> 5% of each run, Pallas kernels for 3% -> 3%
where the time goes in v7:
time: 225 us
  waiting for transfers between devices  101 us (45%)
  starting transfers between devices  74.8 us (33%)
  Pallas kernels  25.1 us (11%)
  local copies, waits for them, and re-layouts  15.1 us (7%)
  other arithmetic  5.81 us (3%)
    ppermute x68, waiting for transfers between devices, swap(): return lax.ppermute(x, axis, [(i, i ^ mask) for i in range(count)])  101 us
    ppermute x68, starting transfers between devices, swap(): return lax.ppermute(x, axis, [(i, i ^ mask) for i in range(count)])  74.8 us
    unnamed x20, local copies, waits for them, and re-layouts  9.95 us
    pallas_call x2, Pallas kernels, forward(): pl.pallas_call(functools.partial(forward_body, (vox, masks, rows, len(pie...  9.61 us
    pallas_call x2, Pallas kernels, gradient_parts(): pl.pallas_call(functools.partial(gradient_body, (vox, masks, rows, cores,...  9.37 us
  transfers between devices with their start and end apart: 68, of which 51 were waited for; matrix products, arithmetic and copies ran while one was open for 5% of the time, Pallas kernels for 3%

profile of v7, /device:TPU:0, one launch (start us, length us, event | category | flops | bytes accessed | tf_op | source)
XLA Modules:
  0.0 225.1 jit_solution(1724935404710746507)
XLA Ops:
  0.6 3.1 %collective-permute-start = (f32[48,128]{1,0:T(8,128)}, f32[48,128]{1,0:T(8,128)S(1)}, u32[]{:S(2)}, u32[]{:S(2)}) collective-permute-start(f32[48,128]{1,0:T(8,128)} %param.15), channel_id=1, source_target_pairs={{0,8},{8,0},{16,24},{24,16},{1,9},{9,1},{17,25},{25,17},{2,10},{10... | collective-permute-start | bytes 73736 | tf_op jit(solution)/shard_map/ppermute | solution.py:28
  3.7 2.5 %collective-permute-start.1 = (f32[48,128]{1,0:T(8,128)}, f32[48,128]{1,0:T(8,128)S(1)}, u32[]{:S(2)}, u32[]{:S(2)}) collective-permute-start(f32[48,128]{1,0:T(8,128)} %param.15), channel_id=1, source_target_pairs={{0,24},{8,16},{16,8},{24,0},{1,25},{9,17},{17,9},{25,1},{2,26},{10... | collective-permute-start | bytes 73736 | tf_op jit(solution)/shard_map/ppermute | solution.py:28
  10.2 1.3 collective-permute-done.2
  11.4 1.5 collective-permute-start.4
  12.9 1.4 collective-permute-start.5
  14.9 2.8 %gather_fusion = f32[16,128,128]{2,1,0:T(8,128)S(1)} fusion(f32[64,128,128]{2,1,0:T(8,128)} %param.16, s32[1024]{0:T(1024)S(1)} %pad_clamp_fusion), kind=kCustom, calls=%fused_computation | custom fusion | bytes 2097216 | tf_op jit(solution)/shard_map/gather | solution.py:402
  21.0 4.6 %copy-done.1 = f32[1,2048,1536]{2,1,0:T(8,128)S(1)} copy-done((f32[1,2048,1536]{2,1,0:T(8,128)S(1)}, f32[1,2048,1536]{2,1,0:T(8,128)}, u32[]{:S(2)}) %copy-start.1) | copy-done | bytes 12582936
  25.5 4.8 %dose_and_warp.2 = (f32[4,2,64,128]{3,2,1,0:T(8,128)S(1)}, f32[4,2,64,128]{3,2,1,0:T(8,128)S(1)}, f32[4,2,64,128]{3,2,1,0:T(8,128)S(1)}, f32[4,2,64,128]{3,2,1,0:T(8,128)S(1)}) custom-call(s32[16]{0:T(128)S(1)} %get-tuple-element.105.source_ref, s32[16]{0:T(128)S(1)} %get-tuple-element.104.valid_ref, s32[2]{0:T(128)S(1)} %pad_add_fusion.me_ref, ...), custom_call_target="tpu_custom_call" | custom-call | flops 1 | bytes 1 | tf_op jit(solution)/shard_map/dose_and_warp/pallas_call | solution.py:112
  32.0 1.6 collective-permute-start.9
  35.7 4.2 %collective-permute-done.9.refs_2_ = f32[2,2,64,128]{3,2,1,0:T(8,128)S(1)} collective-permute-done((f32[2,2,64,128]{3,2,1,0:T(8,128)S(1)}, f32[2,2,64,128]{3,2,1,0:T(8,128)S(1)}, u32[]{:S(2)}, u32[]{:S(2)}) %collective-permute-start.9) | collective-permute-done | bytes 131104 | tf_op jit(solution)/shard_map/ppermute | solution.py:28
  45.1 2.2 collective-permute-start.17
  49.9 1.8 collective-permute-start.12
  54.2 1.5 collective-permute-start.18
  55.7 4.4 %collective-permute-done.12 = f32[8,64,128]{2,1,0:T(8,128)S(1)} collective-permute-done((f32[8,64,128]{2,1,0:T(8,128)S(1)}, f32[8,64,128]{2,1,0:T(8,128)S(1)}, u32[]{:S(2)}, u32[]{:S(2)}) %collective-permute-start.12) | collective-permute-done | bytes 262176 | tf_op jit(solution)/shard_map/ppermute | solution.py:28
  60.1 2.5 %collective-permute-start.13 = (f32[8,64,128]{2,1,0:T(8,128)S(1)}, f32[8,64,128]{2,1,0:T(8,128)S(1)}, u32[]{:S(2)}, u32[]{:S(2)}) collective-permute-start(f32[8,64,128]{2,1,0:T(8,128)S(1)} %add.123.mine), channel_id=1, source_target_pairs={{0,8},{8,0},{16,24},{24,16},{1,9},{9,1},{17,25},{25,17},{2,10},{10... | collective-permute-start | bytes 786440 | tf_op jit(solution)/shard_map/ppermute | solution.py:28
  62.7 1.9 collective-permute-done.18
  64.7 1.5 collective-permute-start.23
  66.2 4.6 %copy-done.2 = f32[1,2048,1536]{2,1,0:T(8,128)S(1)} copy-done((f32[1,2048,1536]{2,1,0:T(8,128)S(1)}, f32[1,2048,1536]{2,1,0:T(8,128)}, u32[]{:S(2)}) %copy-start.2) | copy-done | bytes 12582936
  71.8 4.1 %collective-permute-done.23 = f32[8,64,128]{2,1,0:T(8,128)S(1)} collective-permute-done((f32[8,64,128]{2,1,0:T(8,128)S(1)}, f32[8,64,128]{2,1,0:T(8,128)S(1)}, u32[]{:S(2)}, u32[]{:S(2)}) %collective-permute-start.23) | collective-permute-done | bytes 262176 | tf_op jit(solution)/shard_map/ppermute | solution.py:28
  76.1 3.4 %collective-permute-start.22 = (f32[2,2,64,128]{3,2,1,0:T(8,128)S(1)}, f32[2,2,64,128]{3,2,1,0:T(8,128)S(1)}, u32[]{:S(2)}, u32[]{:S(2)}) collective-permute-start(f32[2,2,64,128]{3,2,1,0:T(8,128)S(1)} %pad_maximum_fusion.15), channel_id=1, source_target_pairs={{0,6},{1,7},{2,4},{3,5},{4,2},{5,3},{6,0},{7,1},{8,14},{9,15},{10,... | collective-permute-start | bytes 393224 | tf_op jit(solution)/shard_map/ppermute | solution.py:28
  79.6 2.8 %collective-permute-done.24.other = f32[8,64,128]{2,1,0:T(8,128)S(1)} collective-permute-done((f32[8,64,128]{2,1,0:T(8,128)S(1)}, f32[8,64,128]{2,1,0:T(8,128)S(1)}, u32[]{:S(2)}, u32[]{:S(2)}) %collective-permute-start.24) | collective-permute-done | bytes 262176 | tf_op jit(solution)/shard_map/ppermute | solution.py:28
  84.9 2.7 %collective-permute-start.28 = (f32[2,2,64,128]{3,2,1,0:T(8,128)S(1)}, f32[2,2,64,128]{3,2,1,0:T(8,128)S(1)}, u32[]{:S(2)}, u32[]{:S(2)}) collective-permute-start(f32[2,2,64,128]{3,2,1,0:T(8,128)S(1)} %pad_maximum_fusion.19), channel_id=1, source_target_pairs={{0,6},{1,7},{2,4},{3,5},{4,2},{5,3},{6,0},{7,1},{8,14},{9,15},{10,... | collective-permute-start | bytes 393224 | tf_op jit(solution)/shard_map/ppermute | solution.py:28
  89.4 4.5 %collective-permute-done.28.refs_7_ = f32[2,2,64,128]{3,2,1,0:T(8,128)S(1)} collective-permute-done((f32[2,2,64,128]{3,2,1,0:T(8,128)S(1)}, f32[2,2,64,128]{3,2,1,0:T(8,128)S(1)}, u32[]{:S(2)}, u32[]{:S(2)}) %collective-permute-start.28) | collective-permute-done | bytes 131104 | tf_op jit(solution)/shard_map/ppermute | solution.py:28
  93.9 1.7 collective-permute-done.27.refs_6_
  95.7 4.7 %warp_back_and_gradient.2 = (f32[4,192,128]{2,1,0:T(8,128)S(1)}, f32[4,192,128]{2,1,0:T(8,128)S(1)}) custom-call(s32[16]{0:T(128)S(1)} %get-tuple-element.105.source_ref, s32[16]{0:T(128)S(1)} %get-tuple-element.104.valid_ref, s32[2]{0:T(128)S(1)} %pad_add_fusion.me_ref, f32[2048,1536]{1,0:T(8,128)S(1)} %bitcast.94, f32[16,128,128]{2,1,0:T(8,128)S(1)} %gather_fusion, ...), custom_call_target="tpu_custom_call" | custom-call | flops 1 | bytes 1 | tf_op jit(solution)/shard_map/warp_back_and_gradient/pallas_call | solution.py:183
  100.5 1.7 collective-permute-done.29
  103.2 1.6 collective-permute-start.31
  105.8 1.7 collective-permute-done.30
  107.6 1.4 collective-permute-done.31
  109.0 1.3 collective-permute-done.32
  111.2 3.8 %collective-permute-done.33 = f32[4,48,128]{2,1,0:T(8,128)S(1)} collective-permute-done((f32[4,48,128]{2,1,0:T(8,128)S(1)}, f32[4,48,128]{2,1,0:T(8,128)S(1)}, u32[]{:S(2)}, u32[]{:S(2)}) %collective-permute-start.33) | collective-permute-done | bytes 98336 | tf_op jit(solution)/shard_map/ppermute | solution.py:28
  116.2 5.3 %collective-permute-done.34 = f32[4,48,128]{2,1,0:T(8,128)S(1)} collective-permute-done((f32[4,48,128]{2,1,0:T(8,128)S(1)}, f32[4,48,128]{2,1,0:T(8,128)S(1)}, u32[]{:S(2)}, u32[]{:S(2)}) %collective-permute-start.34) | collective-permute-done | bytes 98336 | tf_op jit(solution)/shard_map/ppermute | solution.py:28
  122.5 1.3 collective-permute-start.36
  123.8 1.4 collective-permute-start.37
  127.1 2.2 collective-permute-done.37
  129.4 1.7 collective-permute-done.38.refs_1_
  131.1 4.8 %dose_and_warp.3 = (f32[4,2,64,128]{3,2,1,0:T(8,128)S(1)}, f32[4,2,64,128]{3,2,1,0:T(8,128)S(1)}, f32[4,2,64,128]{3,2,1,0:T(8,128)S(1)}, f32[4,2,64,128]{3,2,1,0:T(8,128)S(1)}) custom-call(s32[16]{0:T(128)S(1)} %get-tuple-element.105.source_ref, s32[16]{0:T(128)S(1)} %get-tuple-element.104.valid_ref, s32[2]{0:T(128)S(1)} %pad_add_fusion.me_ref, ...), custom_call_target="tpu_custom_call" | custom-call | flops 1 | bytes 1 | tf_op jit(solution)/shard_map/dose_and_warp/pallas_call | solution.py:112
  136.2 1.4 collective-permute-done.39
  138.4 1.8 collective-permute-start.42
  141.3 4.7 %collective-permute-done.41.refs_2_ = f32[2,2,64,128]{3,2,1,0:T(8,128)S(1)} collective-permute-done((f32[2,2,64,128]{3,2,1,0:T(8,128)S(1)}, f32[2,2,64,128]{3,2,1,0:T(8,128)S(1)}, u32[]{:S(2)}, u32[]{:S(2)}) %collective-permute-start.41) | collective-permute-done | bytes 131104 | tf_op jit(solution)/shard_map/ppermute | solution.py:28
  146.0 1.3 collective-permute-done.40.refs_1_
  149.6 5.9 %collective-permute-done.43 = f32[8,64,128]{2,1,0:T(8,128)S(1)} collective-permute-done((f32[8,64,128]{2,1,0:T(8,128)S(1)}, f32[8,64,128]{2,1,0:T(8,128)S(1)}, u32[]{:S(2)}, u32[]{:S(2)}) %collective-permute-start.43) | collective-permute-done | bytes 262176 | tf_op jit(solution)/shard_map/ppermute | solution.py:28
  158.7 3.0 %collective-permute-done.52.refs_2_ = f32[2,2,64,128]{3,2,1,0:T(8,128)S(1)} collective-permute-done((f32[2,2,64,128]{3,2,1,0:T(8,128)S(1)}, f32[2,2,64,128]{3,2,1,0:T(8,128)S(1)}, u32[]{:S(2)}, u32[]{:S(2)}) %collective-permute-start.52) | collective-permute-done | bytes 131104 | tf_op jit(solution)/shard_map/ppermute | solution.py:28
  164.6 3.9 %collective-permute-start.45 = (f32[8,64,128]{2,1,0:T(8,128)S(1)}, f32[8,64,128]{2,1,0:T(8,128)S(1)}, u32[]{:S(2)}, u32[]{:S(2)}) collective-permute-start(f32[8,64,128]{2,1,0:T(8,128)S(1)} %add.134.mine), channel_id=1, source_target_pairs={{0,8},{8,0},{16,24},{24,16},{1,9},{9,1},{17,25},{25,17},{2,10},{10... | collective-permute-start | bytes 786440 | tf_op jit(solution)/shard_map/ppermute | solution.py:28
  168.5 3.9 %collective-permute-done.54 = f32[8,64,128]{2,1,0:T(8,128)S(1)} collective-permute-done((f32[8,64,128]{2,1,0:T(8,128)S(1)}, f32[8,64,128]{2,1,0:T(8,128)S(1)}, u32[]{:S(2)}, u32[]{:S(2)}) %collective-permute-start.54) | collective-permute-done | bytes 262176 | tf_op jit(solution)/shard_map/ppermute | solution.py:28
  172.5 2.2 collective-permute-start.55
  174.7 2.1 collective-permute-done.45.other
  177.6 4.3 %collective-permute-done.55 = f32[8,64,128]{2,1,0:T(8,128)S(1)} collective-permute-done((f32[8,64,128]{2,1,0:T(8,128)S(1)}, f32[8,64,128]{2,1,0:T(8,128)S(1)}, u32[]{:S(2)}, u32[]{:S(2)}) %collective-permute-start.55) | collective-permute-done | bytes 262176 | tf_op jit(solution)/shard_map/ppermute | solution.py:28
  181.9 1.8 collective-permute-start.56
  183.8 1.6 collective-permute-start.49
  186.4 2.0 collective-permute-done.56.other
  189.2 1.3 collective-permute-start.47
  190.7 1.8 collective-permute-start.60
  195.5 3.4 %collective-permute-done.60.refs_7_ = f32[2,2,64,128]{3,2,1,0:T(8,128)S(1)} collective-permute-done((f32[2,2,64,128]{3,2,1,0:T(8,128)S(1)}, f32[2,2,64,128]{3,2,1,0:T(8,128)S(1)}, u32[]{:S(2)}, u32[]{:S(2)}) %collective-permute-start.60) | collective-permute-done | bytes 131104 | tf_op jit(solution)/shard_map/ppermute | solution.py:28
  198.9 1.7 collective-permute-done.59.refs_6_
  200.8 4.7 %warp_back_and_gradient.3 = (f32[4,192,128]{2,1,0:T(8,128)S(1)}, f32[4,192,128]{2,1,0:T(8,128)S(1)}) custom-call(s32[16]{0:T(128)S(1)} %get-tuple-element.105.source_ref, s32[16]{0:T(128)S(1)} %get-tuple-element.104.valid_ref, s32[2]{0:T(128)S(1)} %pad_add_fusion.me_ref, f32[2048,1536]{1,0:T(8,128)S(1)} %bitcast.96, f32[16,128,128]{2,1,0:T(8,128)S(1)} %gather_fusion, ...), custom_call_target="tpu_custom_call" | custom-call | flops 1 | bytes 1 | tf_op jit(solution)/shard_map/warp_back_and_gradient/pallas_call | solution.py:183
  205.6 1.7 collective-permute-done.61
  207.4 1.3 collective-permute-start.62
  210.9 1.3 collective-permute-done.62
  212.3 3.1 %collective-permute-done.63 = f32[192,128]{1,0:T(8,128)S(1)} collective-permute-done((f32[192,128]{1,0:T(8,128)S(1)}, f32[192,128]{1,0:T(8,128)S(1)}, u32[]{:S(2)}, u32[]{:S(2)}) %collective-permute-start.63) | collective-permute-done | bytes 98336 | tf_op jit(solution)/shard_map/ppermute | solution.py:28
  215.4 1.6 collective-permute-start.65
  217.0 2.8 %collective-permute-start.66 = (f32[48,128]{1,0:T(8,128)S(1)}, f32[48,128]{1,0:T(8,128)S(1)}, u32[]{:S(2)}, u32[]{:S(2)}) collective-permute-start(f32[48,128]{1,0:T(8,128)S(1)} %get-tuple-element.184), channel_id=1, source_target_pairs={{0,24},{8,16},{16,8},{24,0},{1,25},{9,17},{17,9},{25,1},{2,26},{10... | collective-permute-start | bytes 73736 | tf_op jit(solution)/shard_map/ppermute | solution.py:28
  220.9 1.7 collective-permute-done.66
  222.6 1.9 collective-permute-done.67
  (207 shorter events, 55.2 us)
Async XLA Ops:
  0.6 9.5 %collective-permute-start = (f32[48,128]{1,0:T(8,128)}, f32[48,128]{1,0:T(8,128)S(1)}, u32[]{:S(2)}, u32[]{:S(2)}) collective-permute-start(f32[48,128]{1,0:T(8,128)} %param.15), channel_id=1, source_target_pairs={{0,8},{8,0},{16,24},{24,16},{1,9},{9,1},{17,25},{25,17},{2,10},{10... | collective-permute-start | bytes 73736 | tf_op jit(solution)/shard_map/ppermute | solution.py:28
  3.7 6.4 %collective-permute-start.1 = (f32[48,128]{1,0:T(8,128)}, f32[48,128]{1,0:T(8,128)S(1)}, u32[]{:S(2)}, u32[]{:S(2)}) collective-permute-start(f32[48,128]{1,0:T(8,128)} %param.15), channel_id=1, source_target_pairs={{0,24},{8,16},{16,8},{24,0},{1,25},{9,17},{17,9},{25,1},{2,26},{10... | collective-permute-start | bytes 73736 | tf_op jit(solution)/shard_map/ppermute | solution.py:28
  6.2 5.2 %collective-permute-start.2 = (f32[48,128]{1,0:T(8,128)}, f32[48,128]{1,0:T(8,128)S(1)}, u32[]{:S(2)}, u32[]{:S(2)}) collective-permute-start(f32[48,128]{1,0:T(8,128)} %param.15), channel_id=1, source_target_pairs={{0,16},{8,24},{16,0},{24,8},{1,17},{9,25},{17,1},{25,9},{2,18},{10... | collective-permute-start | bytes 73736 | tf_op jit(solution)/shard_map/ppermute | solution.py:28
  11.4 6.3 %collective-permute-start.4 = (f32[208,128]{1,0:T(8,128)S(1)}, f32[208,128]{1,0:T(8,128)S(1)}, u32[]{:S(2)}, u32[]{:S(2)}) collective-permute-start(f32[208,128]{1,0:T(8,128)S(1)} %constant_dynamic-update-slice_fusion), channel_id=1, source_target_pairs={{0,4},{1,5},{2,6},{3,7},{4,0},{5,1},{6,2},{7,3},{8,12},{9,13},{10,... | collective-permute-start | bytes 319496 | tf_op jit(solution)/shard_map/ppermute | solution.py:28
  12.9 5.6 %collective-permute-start.5 = (f32[208,128]{1,0:T(8,128)S(1)}, f32[208,128]{1,0:T(8,128)S(1)}, u32[]{:S(2)}, u32[]{:S(2)}) collective-permute-start(f32[208,128]{1,0:T(8,128)S(1)} %constant_dynamic-update-slice_fusion), channel_id=1, source_target_pairs={{0,6},{1,7},{2,4},{3,5},{4,2},{5,3},{6,0},{7,1},{8,14},{9,15},{10,... | collective-permute-start | bytes 319496 | tf_op jit(solution)/shard_map/ppermute | solution.py:28
  14.4 4.7 %collective-permute-start.3 = (f32[208,128]{1,0:T(8,128)S(1)}, f32[208,128]{1,0:T(8,128)S(1)}, u32[]{:S(2)}, u32[]{:S(2)}) collective-permute-start(f32[208,128]{1,0:T(8,128)S(1)} %constant_dynamic-update-slice_fusion), channel_id=1, source_target_pairs={{0,2},{1,3},{2,0},{3,1},{4,6},{5,7},{6,4},{7,5},{8,10},{9,11},{10,... | collective-permute-start | bytes 319496 | tf_op jit(solution)/shard_map/ppermute | solution.py:28
  19.1 1.8 collective-permute-start.6
  32.0 7.9 %collective-permute-start.9 = (f32[2,2,64,128]{3,2,1,0:T(8,128)S(1)}, f32[2,2,64,128]{3,2,1,0:T(8,128)S(1)}, u32[]{:S(2)}, u32[]{:S(2)}) collective-permute-start(f32[2,2,64,128]{3,2,1,0:T(8,128)S(1)} %pad_maximum_fusion.6), channel_id=1, source_target_pairs={{0,4},{1,5},{2,6},{3,7},{4,0},{5,1},{6,2},{7,3},{8,12},{9,13},{10,... | collective-permute-start | bytes 393224 | tf_op jit(solution)/shard_map/ppermute | solution.py:28
  33.6 7.3 %collective-permute-start.10 = (f32[2,2,64,128]{3,2,1,0:T(8,128)S(1)}, f32[2,2,64,128]{3,2,1,0:T(8,128)S(1)}, u32[]{:S(2)}, u32[]{:S(2)}) collective-permute-start(f32[2,2,64,128]{3,2,1,0:T(8,128)S(1)} %pad_maximum_fusion.7), channel_id=1, source_target_pairs={{0,6},{1,7},{2,4},{3,5},{4,2},{5,3},{6,0},{7,1},{8,14},{9,15},{10,... | collective-permute-start | bytes 393224 | tf_op jit(solution)/shard_map/ppermute | solution.py:28
  34.8 7.0 %collective-permute-start.8 = (f32[2,2,64,128]{3,2,1,0:T(8,128)S(1)}, f32[2,2,64,128]{3,2,1,0:T(8,128)S(1)}, u32[]{:S(2)}, u32[]{:S(2)}) collective-permute-start(f32[2,2,64,128]{3,2,1,0:T(8,128)S(1)} %pad_maximum_fusion.5), channel_id=1, source_target_pairs={{0,2},{1,3},{2,0},{3,1},{4,6},{5,7},{6,4},{7,5},{8,10},{9,11},{10,... | collective-permute-start | bytes 393224 | tf_op jit(solution)/shard_map/ppermute | solution.py:28
  39.9 5.1 %collective-permute-start.14 = (f32[4,2,64,128]{3,2,1,0:T(8,128)S(1)}, f32[4,2,64,128]{3,2,1,0:T(8,128)S(1)}, u32[]{:S(2)}, u32[]{:S(2)}) collective-permute-start(f32[4,2,64,128]{3,2,1,0:T(8,128)S(1)} %get-tuple-element.73), channel_id=1, source_target_pairs={{0,1},{1,0},{2,3},{3,2},{4,5},{5,4},{6,7},{7,6},{8,9},{9,8},{10,11... | collective-permute-start | bytes 786440 | tf_op jit(solution)/shard_map/ppermute | solution.py:28
  42.5 7.3 %collective-permute-start.11 = (f32[8,64,128]{2,1,0:T(8,128)S(1)}, f32[8,64,128]{2,1,0:T(8,128)S(1)}, u32[]{:S(2)}, u32[]{:S(2)}) collective-permute-start(f32[8,64,128]{2,1,0:T(8,128)S(1)} %get-tuple-element.68), channel_id=1, source_target_pairs={{0,8},{8,0},{16,24},{24,16},{1,9},{9,1},{17,25},{25,17},{2,10},{10... | collective-permute-start | bytes 786440 | tf_op jit(solution)/shard_map/ppermute | solution.py:28
  45.1 7.0 %collective-permute-start.17 = (f32[2,2,64,128]{3,2,1,0:T(8,128)S(1)}, f32[2,2,64,128]{3,2,1,0:T(8,128)S(1)}, u32[]{:S(2)}, u32[]{:S(2)}) collective-permute-start(f32[2,2,64,128]{3,2,1,0:T(8,128)S(1)} %pad_maximum_fusion.11), channel_id=1, source_target_pairs={{0,6},{1,7},{2,4},{3,5},{4,2},{5,3},{6,0},{7,1},{8,14},{9,15},{10,... | collective-permute-start | bytes 393224 | tf_op jit(solution)/shard_map/ppermute | solution.py:28
  47.3 5.7 %collective-permute-start.16 = (f32[2,2,64,128]{3,2,1,0:T(8,128)S(1)}, f32[2,2,64,128]{3,2,1,0:T(8,128)S(1)}, u32[]{:S(2)}, u32[]{:S(2)}) collective-permute-start(f32[2,2,64,128]{3,2,1,0:T(8,128)S(1)} %pad_maximum_fusion.10), channel_id=1, source_target_pairs={{0,4},{1,5},{2,6},{3,7},{4,0},{5,1},{6,2},{7,3},{8,12},{9,13},{10,... | collective-permute-start | bytes 393224 | tf_op jit(solution)/shard_map/ppermute | solution.py:28
  47.8 5.5 %collective-permute-start.15 = (f32[2,2,64,128]{3,2,1,0:T(8,128)S(1)}, f32[2,2,64,128]{3,2,1,0:T(8,128)S(1)}, u32[]{:S(2)}, u32[]{:S(2)}) collective-permute-start(f32[2,2,64,128]{3,2,1,0:T(8,128)S(1)} %pad_maximum_fusion.9), channel_id=1, source_target_pairs={{0,2},{1,3},{2,0},{3,1},{4,6},{5,7},{6,4},{7,5},{8,10},{9,11},{10,... | collective-permute-start | bytes 393224 | tf_op jit(solution)/shard_map/ppermute | solution.py:28
  49.9 10.2 %collective-permute-start.12 = (f32[8,64,128]{2,1,0:T(8,128)S(1)}, f32[8,64,128]{2,1,0:T(8,128)S(1)}, u32[]{:S(2)}, u32[]{:S(2)}) collective-permute-start(f32[8,64,128]{2,1,0:T(8,128)S(1)} %add.122), channel_id=1, source_target_pairs={{0,24},{8,16},{16,8},{24,0},{1,25},{9,17},{17,9},{25,1},{2,26},{10... | collective-permute-start | bytes 786440 | tf_op jit(solution)/shard_map/ppermute | solution.py:28
  54.2 10.4 %collective-permute-start.18 = (f32[8,64,128]{2,1,0:T(8,128)S(1)}, f32[8,64,128]{2,1,0:T(8,128)S(1)}, u32[]{:S(2)}, u32[]{:S(2)}) collective-permute-start(f32[8,64,128]{2,1,0:T(8,128)S(1)} %get-tuple-element.75), channel_id=1, source_target_pairs={{0,8},{8,0},{16,24},{24,16},{1,9},{9,1},{17,25},{25,17},{2,10},{10... | collective-permute-start | bytes 786440 | tf_op jit(solution)/shard_map/ppermute | solution.py:28
  60.1 10.7 %collective-permute-start.13 = (f32[8,64,128]{2,1,0:T(8,128)S(1)}, f32[8,64,128]{2,1,0:T(8,128)S(1)}, u32[]{:S(2)}, u32[]{:S(2)}) collective-permute-start(f32[8,64,128]{2,1,0:T(8,128)S(1)} %add.123.mine), channel_id=1, source_target_pairs={{0,8},{8,0},{16,24},{24,16},{1,9},{9,1},{17,25},{25,17},{2,10},{10... | collective-permute-start | bytes 786440 | tf_op jit(solution)/shard_map/ppermute | solution.py:28
  64.7 11.2 %collective-permute-start.23 = (f32[8,64,128]{2,1,0:T(8,128)S(1)}, f32[8,64,128]{2,1,0:T(8,128)S(1)}, u32[]{:S(2)}, u32[]{:S(2)}) collective-permute-start(f32[8,64,128]{2,1,0:T(8,128)S(1)} %add.124.x), channel_id=1, source_target_pairs={{0,24},{8,16},{16,8},{24,0},{1,25},{9,17},{17,9},{25,1},{2,26},{10... | collective-permute-start | bytes 786440 | tf_op jit(solution)/shard_map/ppermute | solution.py:28
  71.7 4.3 %collective-permute-start.19 = (f32[4,2,64,128]{3,2,1,0:T(8,128)S(1)}, f32[4,2,64,128]{3,2,1,0:T(8,128)S(1)}, u32[]{:S(2)}, u32[]{:S(2)}) collective-permute-start(f32[4,2,64,128]{3,2,1,0:T(8,128)S(1)} %get-tuple-element.78), channel_id=1, source_target_pairs={{0,1},{1,0},{2,3},{3,2},{4,5},{5,4},{6,7},{7,6},{8,9},{9,8},{10,11... | collective-permute-start | bytes 786440 | tf_op jit(solution)/shard_map/ppermute | solution.py:28
  75.9 6.4 %collective-permute-start.24 = (f32[8,64,128]{2,1,0:T(8,128)S(1)}, f32[8,64,128]{2,1,0:T(8,128)S(1)}, u32[]{:S(2)}, u32[]{:S(2)}) collective-permute-start(f32[8,64,128]{2,1,0:T(8,128)S(1)} %add.125.mine), channel_id=1, source_target_pairs={{0,8},{8,0},{16,24},{24,16},{1,9},{9,1},{17,25},{25,17},{2,10},{10... | collective-permute-start | bytes 786440 | tf_op jit(solution)/shard_map/ppermute | solution.py:28
  76.1 11.6 %collective-permute-start.22 = (f32[2,2,64,128]{3,2,1,0:T(8,128)S(1)}, f32[2,2,64,128]{3,2,1,0:T(8,128)S(1)}, u32[]{:S(2)}, u32[]{:S(2)}) collective-permute-start(f32[2,2,64,128]{3,2,1,0:T(8,128)S(1)} %pad_maximum_fusion.15), channel_id=1, source_target_pairs={{0,6},{1,7},{2,4},{3,5},{4,2},{5,3},{6,0},{7,1},{8,14},{9,15},{10,... | collective-permute-start | bytes 393224 | tf_op jit(solution)/shard_map/ppermute | solution.py:28
  79.5 9.1 %collective-permute-start.21 = (f32[2,2,64,128]{3,2,1,0:T(8,128)S(1)}, f32[2,2,64,128]{3,2,1,0:T(8,128)S(1)}, u32[]{:S(2)}, u32[]{:S(2)}) collective-permute-start(f32[2,2,64,128]{3,2,1,0:T(8,128)S(1)} %pad_maximum_fusion.14), channel_id=1, source_target_pairs={{0,4},{1,5},{2,6},{3,7},{4,0},{5,1},{6,2},{7,3},{8,12},{9,13},{10,... | collective-permute-start | bytes 393224 | tf_op jit(solution)/shard_map/ppermute | solution.py:28
  83.3 6.1 %collective-permute-start.20 = (f32[2,2,64,128]{3,2,1,0:T(8,128)S(1)}, f32[2,2,64,128]{3,2,1,0:T(8,128)S(1)}, u32[]{:S(2)}, u32[]{:S(2)}) collective-permute-start(f32[2,2,64,128]{3,2,1,0:T(8,128)S(1)} %pad_maximum_fusion.13), channel_id=1, source_target_pairs={{0,2},{1,3},{2,0},{3,1},{4,6},{5,7},{6,4},{7,5},{8,10},{9,11},{10,... | collective-permute-start | bytes 393224 | tf_op jit(solution)/shard_map/ppermute | solution.py:28
  84.9 9.1 %collective-permute-start.28 = (f32[2,2,64,128]{3,2,1,0:T(8,128)S(1)}, f32[2,2,64,128]{3,2,1,0:T(8,128)S(1)}, u32[]{:S(2)}, u32[]{:S(2)}) collective-permute-start(f32[2,2,64,128]{3,2,1,0:T(8,128)S(1)} %pad_maximum_fusion.19), channel_id=1, source_target_pairs={{0,6},{1,7},{2,4},{3,5},{4,2},{5,3},{6,0},{7,1},{8,14},{9,15},{10,... | collective-permute-start | bytes 393224 | tf_op jit(solution)/shard_map/ppermute | solution.py:28
  87.6 8.1 %collective-permute-start.27 = (f32[2,2,64,128]{3,2,1,0:T(8,128)S(1)}, f32[2,2,64,128]{3,2,1,0:T(8,128)S(1)}, u32[]{:S(2)}, u32[]{:S(2)}) collective-permute-start(f32[2,2,64,128]{3,2,1,0:T(8,128)S(1)} %pad_maximum_fusion.18), channel_id=1, source_target_pairs={{0,4},{1,5},{2,6},{3,7},{4,0},{5,1},{6,2},{7,3},{8,12},{9,13},{10,... | collective-permute-start | bytes 393224 | tf_op jit(solution)/shard_map/ppermute | solution.py:28
  87.7 8.0 %collective-permute-start.26 = (f32[2,2,64,128]{3,2,1,0:T(8,128)S(1)}, f32[2,2,64,128]{3,2,1,0:T(8,128)S(1)}, u32[]{:S(2)}, u32[]{:S(2)}) collective-permute-start(f32[2,2,64,128]{3,2,1,0:T(8,128)S(1)} %pad_maximum_fusion.17), channel_id=1, source_target_pairs={{0,2},{1,3},{2,0},{3,1},{4,6},{5,7},{6,4},{7,5},{8,10},{9,11},{10,... | collective-permute-start | bytes 393224 | tf_op jit(solution)/shard_map/ppermute | solution.py:28
  100.4 1.8 collective-permute-start.29
  102.3 5.3 %collective-permute-start.30 = (f32[192,128]{1,0:T(8,128)S(1)}, f32[192,128]{1,0:T(8,128)S(1)}, u32[]{:S(2)}, u32[]{:S(2)}) collective-permute-start(f32[192,128]{1,0:T(8,128)S(1)} %get-tuple-element.115), channel_id=1, source_target_pairs={{0,2},{1,3},{2,0},{3,1},{4,6},{5,7},{6,4},{7,5},{8,10},{9,11},{10,... | collective-permute-start | bytes 294920 | tf_op jit(solution)/shard_map/ppermute | solution.py:28
  103.2 5.8 %collective-permute-start.31 = (f32[192,128]{1,0:T(8,128)S(1)}, f32[192,128]{1,0:T(8,128)S(1)}, u32[]{:S(2)}, u32[]{:S(2)}) collective-permute-start(f32[192,128]{1,0:T(8,128)S(1)} %get-tuple-element.117), channel_id=1, source_target_pairs={{0,4},{1,5},{2,6},{3,7},{4,0},{5,1},{6,2},{7,3},{8,12},{9,13},{10,... | collective-permute-start | bytes 294920 | tf_op jit(solution)/shard_map/ppermute | solution.py:28
  104.8 5.5 %collective-permute-start.32 = (f32[192,128]{1,0:T(8,128)S(1)}, f32[192,128]{1,0:T(8,128)S(1)}, u32[]{:S(2)}, u32[]{:S(2)}) collective-permute-start(f32[192,128]{1,0:T(8,128)S(1)} %get-tuple-element.116), channel_id=1, source_target_pairs={{0,6},{1,7},{2,4},{3,5},{4,2},{5,3},{6,0},{7,1},{8,14},{9,15},{10,... | collective-permute-start | bytes 294920 | tf_op jit(solution)/shard_map/ppermute | solution.py:28
  110.3 4.7 %collective-permute-start.33 = (f32[4,48,128]{2,1,0:T(8,128)S(1)}, f32[4,48,128]{2,1,0:T(8,128)S(1)}, u32[]{:S(2)}, u32[]{:S(2)}) collective-permute-start(f32[4,48,128]{2,1,0:T(8,128)S(1)} %bitcast.102), channel_id=1, source_target_pairs={{0,8},{8,0},{16,24},{24,16},{1,9},{9,1},{17,25},{25,17},{2,10},{10... | collective-permute-start | bytes 294920 | tf_op jit(solution)/shard_map/ppermute | solution.py:28
  115.0 6.5 %collective-permute-start.34 = (f32[4,48,128]{2,1,0:T(8,128)S(1)}, f32[4,48,128]{2,1,0:T(8,128)S(1)}, u32[]{:S(2)}, u32[]{:S(2)}) collective-permute-start(f32[4,48,128]{2,1,0:T(8,128)S(1)} %bitcast_add_fusion.1), channel_id=1, source_target_pairs={{0,24},{8,16},{16,8},{24,0},{1,25},{9,17},{17,9},{25,1},{2,26},{10... | collective-permute-start | bytes 294920 | tf_op jit(solution)/shard_map/ppermute | solution.py:28
  121.6 4.7 %collective-permute-start.35 = (f32[192,128]{1,0:T(8,128)S(1)}, f32[192,128]{1,0:T(8,128)S(1)}, u32[]{:S(2)}, u32[]{:S(2)}) collective-permute-start(f32[192,128]{1,0:T(8,128)S(1)} %fusion.10), channel_id=1, source_target_pairs={{0,2},{1,3},{2,0},{3,1},{4,6},{5,7},{6,4},{7,5},{8,10},{9,11},{10,... | collective-permute-start | bytes 294920 | tf_op jit(solution)/shard_map/ppermute | solution.py:28
  122.5 4.6 %collective-permute-start.36 = (f32[192,128]{1,0:T(8,128)S(1)}, f32[192,128]{1,0:T(8,128)S(1)}, u32[]{:S(2)}, u32[]{:S(2)}) collective-permute-start(f32[192,128]{1,0:T(8,128)S(1)} %fusion.10), channel_id=1, source_target_pairs={{0,4},{1,5},{2,6},{3,7},{4,0},{5,1},{6,2},{7,3},{8,12},{9,13},{10,... | collective-permute-start | bytes 294920 | tf_op jit(solution)/shard_map/ppermute | solution.py:28
  123.8 5.5 %collective-permute-start.37 = (f32[192,128]{1,0:T(8,128)S(1)}, f32[192,128]{1,0:T(8,128)S(1)}, u32[]{:S(2)}, u32[]{:S(2)}) collective-permute-start(f32[192,128]{1,0:T(8,128)S(1)} %fusion.10), channel_id=1, source_target_pairs={{0,6},{1,7},{2,4},{3,5},{4,2},{5,3},{6,0},{7,1},{8,14},{9,15},{10,... | collective-permute-start | bytes 294920 | tf_op jit(solution)/shard_map/ppermute | solution.py:28
  129.3 1.8 collective-permute-start.38
  137.6 8.4 %collective-permute-start.41 = (f32[2,2,64,128]{3,2,1,0:T(8,128)S(1)}, f32[2,2,64,128]{3,2,1,0:T(8,128)S(1)}, u32[]{:S(2)}, u32[]{:S(2)}) collective-permute-start(f32[2,2,64,128]{3,2,1,0:T(8,128)S(1)} %pad_maximum_fusion.22), channel_id=1, source_target_pairs={{0,4},{1,5},{2,6},{3,7},{4,0},{5,1},{6,2},{7,3},{8,12},{9,13},{10,... | collective-permute-start | bytes 393224 | tf_op jit(solution)/shard_map/ppermute | solution.py:28
  138.4 7.6 %collective-permute-start.42 = (f32[2,2,64,128]{3,2,1,0:T(8,128)S(1)}, f32[2,2,64,128]{3,2,1,0:T(8,128)S(1)}, u32[]{:S(2)}, u32[]{:S(2)}) collective-permute-start(f32[2,2,64,128]{3,2,1,0:T(8,128)S(1)} %pad_maximum_fusion.23), channel_id=1, source_target_pairs={{0,6},{1,7},{2,4},{3,5},{4,2},{5,3},{6,0},{7,1},{8,14},{9,15},{10,... | collective-permute-start | bytes 393224 | tf_op jit(solution)/shard_map/ppermute | solution.py:28
  140.3 7.0 %collective-permute-start.40 = (f32[2,2,64,128]{3,2,1,0:T(8,128)S(1)}, f32[2,2,64,128]{3,2,1,0:T(8,128)S(1)}, u32[]{:S(2)}, u32[]{:S(2)}) collective-permute-start(f32[2,2,64,128]{3,2,1,0:T(8,128)S(1)} %pad_maximum_fusion.21), channel_id=1, source_target_pairs={{0,2},{1,3},{2,0},{3,1},{4,6},{5,7},{6,4},{7,5},{8,10},{9,11},{10,... | collective-permute-start | bytes 393224 | tf_op jit(solution)/shard_map/ppermute | solution.py:28
  146.0 2.8 %collective-permute-start.50 = (f32[4,2,64,128]{3,2,1,0:T(8,128)S(1)}, f32[4,2,64,128]{3,2,1,0:T(8,128)S(1)}, u32[]{:S(2)}, u32[]{:S(2)}) collective-permute-start(f32[4,2,64,128]{3,2,1,0:T(8,128)S(1)} %get-tuple-element.93), channel_id=1, source_target_pairs={{0,1},{1,0},{2,3},{3,2},{4,5},{5,4},{6,7},{7,6},{8,9},{9,8},{10,11... | collective-permute-start | bytes 786440 | tf_op jit(solution)/shard_map/ppermute | solution.py:28
  148.1 7.5 %collective-permute-start.43 = (f32[8,64,128]{2,1,0:T(8,128)S(1)}, f32[8,64,128]{2,1,0:T(8,128)S(1)}, u32[]{:S(2)}, u32[]{:S(2)}) collective-permute-start(f32[8,64,128]{2,1,0:T(8,128)S(1)} %get-tuple-element.87), channel_id=1, source_target_pairs={{0,8},{8,0},{16,24},{24,16},{1,9},{9,1},{17,25},{25,17},{2,10},{10... | collective-permute-start | bytes 786440 | tf_op jit(solution)/shard_map/ppermute | solution.py:28
  148.8 9.9 %collective-permute-start.53 = (f32[2,2,64,128]{3,2,1,0:T(8,128)S(1)}, f32[2,2,64,128]{3,2,1,0:T(8,128)S(1)}, u32[]{:S(2)}, u32[]{:S(2)}) collective-permute-start(f32[2,2,64,128]{3,2,1,0:T(8,128)S(1)} %pad_maximum_fusion.31), channel_id=1, source_target_pairs={{0,6},{1,7},{2,4},{3,5},{4,2},{5,3},{6,0},{7,1},{8,14},{9,15},{10,... | collective-permute-start | bytes 393224 | tf_op jit(solution)/shard_map/ppermute | solution.py:28
  155.6 8.9 %collective-permute-start.44 = (f32[8,64,128]{2,1,0:T(8,128)S(1)}, f32[8,64,128]{2,1,0:T(8,128)S(1)}, u32[]{:S(2)}, u32[]{:S(2)}) collective-permute-start(f32[8,64,128]{2,1,0:T(8,128)S(1)} %add.133), channel_id=1, source_target_pairs={{0,24},{8,16},{16,8},{24,0},{1,25},{9,17},{17,9},{25,1},{2,26},{10... | collective-permute-start | bytes 786440 | tf_op jit(solution)/shard_map/ppermute | solution.py:28
  156.6 5.0 %collective-permute-start.52 = (f32[2,2,64,128]{3,2,1,0:T(8,128)S(1)}, f32[2,2,64,128]{3,2,1,0:T(8,128)S(1)}, u32[]{:S(2)}, u32[]{:S(2)}) collective-permute-start(f32[2,2,64,128]{3,2,1,0:T(8,128)S(1)} %pad_maximum_fusion.30), channel_id=1, source_target_pairs={{0,4},{1,5},{2,6},{3,7},{4,0},{5,1},{6,2},{7,3},{8,12},{9,13},{10,... | collective-permute-start | bytes 393224 | tf_op jit(solution)/shard_map/ppermute | solution.py:28
  157.5 5.0 %collective-permute-start.51 = (f32[2,2,64,128]{3,2,1,0:T(8,128)S(1)}, f32[2,2,64,128]{3,2,1,0:T(8,128)S(1)}, u32[]{:S(2)}, u32[]{:S(2)}) collective-permute-start(f32[2,2,64,128]{3,2,1,0:T(8,128)S(1)} %pad_maximum_fusion.29), channel_id=1, source_target_pairs={{0,2},{1,3},{2,0},{3,1},{4,6},{5,7},{6,4},{7,5},{8,10},{9,11},{10,... | collective-permute-start | bytes 393224 | tf_op jit(solution)/shard_map/ppermute | solution.py:28
  163.5 8.9 %collective-permute-start.54 = (f32[8,64,128]{2,1,0:T(8,128)S(1)}, f32[8,64,128]{2,1,0:T(8,128)S(1)}, u32[]{:S(2)}, u32[]{:S(2)}) collective-permute-start(f32[8,64,128]{2,1,0:T(8,128)S(1)} %get-tuple-element.95), channel_id=1, source_target_pairs={{0,8},{8,0},{16,24},{24,16},{1,9},{9,1},{17,25},{25,17},{2,10},{10... | collective-permute-start | bytes 786440 | tf_op jit(solution)/shard_map/ppermute | solution.py:28
  164.6 12.2 %collective-permute-start.45 = (f32[8,64,128]{2,1,0:T(8,128)S(1)}, f32[8,64,128]{2,1,0:T(8,128)S(1)}, u32[]{:S(2)}, u32[]{:S(2)}) collective-permute-start(f32[8,64,128]{2,1,0:T(8,128)S(1)} %add.134.mine), channel_id=1, source_target_pairs={{0,8},{8,0},{16,24},{24,16},{1,9},{9,1},{17,25},{25,17},{2,10},{10... | collective-permute-start | bytes 786440 | tf_op jit(solution)/shard_map/ppermute | solution.py:28
  172.5 9.5 %collective-permute-start.55 = (f32[8,64,128]{2,1,0:T(8,128)S(1)}, f32[8,64,128]{2,1,0:T(8,128)S(1)}, u32[]{:S(2)}, u32[]{:S(2)}) collective-permute-start(f32[8,64,128]{2,1,0:T(8,128)S(1)} %add.135), channel_id=1, source_target_pairs={{0,24},{8,16},{16,8},{24,0},{1,25},{9,17},{17,9},{25,1},{2,26},{10... | collective-permute-start | bytes 786440 | tf_op jit(solution)/shard_map/ppermute | solution.py:28
  177.5 6.3 %collective-permute-start.46 = (f32[4,2,64,128]{3,2,1,0:T(8,128)S(1)}, f32[4,2,64,128]{3,2,1,0:T(8,128)S(1)}, u32[]{:S(2)}, u32[]{:S(2)}) collective-permute-start(f32[4,2,64,128]{3,2,1,0:T(8,128)S(1)} %get-tuple-element.89), channel_id=1, source_target_pairs={{0,1},{1,0},{2,3},{3,2},{4,5},{5,4},{6,7},{7,6},{8,9},{9,8},{10,11... | collective-permute-start | bytes 786440 | tf_op jit(solution)/shard_map/ppermute | solution.py:28
  181.9 6.4 %collective-permute-start.56 = (f32[8,64,128]{2,1,0:T(8,128)S(1)}, f32[8,64,128]{2,1,0:T(8,128)S(1)}, u32[]{:S(2)}, u32[]{:S(2)}) collective-permute-start(f32[8,64,128]{2,1,0:T(8,128)S(1)} %add.136.mine), channel_id=1, source_target_pairs={{0,8},{8,0},{16,24},{24,16},{1,9},{9,1},{17,25},{25,17},{2,10},{10... | collective-permute-start | bytes 786440 | tf_op jit(solution)/shard_map/ppermute | solution.py:28
  183.8 9.7 %collective-permute-start.49 = (f32[2,2,64,128]{3,2,1,0:T(8,128)S(1)}, f32[2,2,64,128]{3,2,1,0:T(8,128)S(1)}, u32[]{:S(2)}, u32[]{:S(2)}) collective-permute-start(f32[2,2,64,128]{3,2,1,0:T(8,128)S(1)} %pad_maximum_fusion.27), channel_id=1, source_target_pairs={{0,6},{1,7},{2,4},{3,5},{4,2},{5,3},{6,0},{7,1},{8,14},{9,15},{10,... | collective-permute-start | bytes 393224 | tf_op jit(solution)/shard_map/ppermute | solution.py:28
  185.4 9.1 %collective-permute-start.48 = (f32[2,2,64,128]{3,2,1,0:T(8,128)S(1)}, f32[2,2,64,128]{3,2,1,0:T(8,128)S(1)}, u32[]{:S(2)}, u32[]{:S(2)}) collective-permute-start(f32[2,2,64,128]{3,2,1,0:T(8,128)S(1)} %pad_maximum_fusion.26), channel_id=1, source_target_pairs={{0,4},{1,5},{2,6},{3,7},{4,0},{5,1},{6,2},{7,3},{8,12},{9,13},{10,... | collective-permute-start | bytes 393224 | tf_op jit(solution)/shard_map/ppermute | solution.py:28
  189.2 6.4 %collective-permute-start.47 = (f32[2,2,64,128]{3,2,1,0:T(8,128)S(1)}, f32[2,2,64,128]{3,2,1,0:T(8,128)S(1)}, u32[]{:S(2)}, u32[]{:S(2)}) collective-permute-start(f32[2,2,64,128]{3,2,1,0:T(8,128)S(1)} %pad_maximum_fusion.25), channel_id=1, source_target_pairs={{0,2},{1,3},{2,0},{3,1},{4,6},{5,7},{6,4},{7,5},{8,10},{9,11},{10,... | collective-permute-start | bytes 393224 | tf_op jit(solution)/shard_map/ppermute | solution.py:28
  190.7 8.2 %collective-permute-start.60 = (f32[2,2,64,128]{3,2,1,0:T(8,128)S(1)}, f32[2,2,64,128]{3,2,1,0:T(8,128)S(1)}, u32[]{:S(2)}, u32[]{:S(2)}) collective-permute-start(f32[2,2,64,128]{3,2,1,0:T(8,128)S(1)} %pad_maximum_fusion.35), channel_id=1, source_target_pairs={{0,6},{1,7},{2,4},{3,5},{4,2},{5,3},{6,0},{7,1},{8,14},{9,15},{10,... | collective-permute-start | bytes 393224 | tf_op jit(solution)/shard_map/ppermute | solution.py:28
  192.5 8.1 %collective-permute-start.59 = (f32[2,2,64,128]{3,2,1,0:T(8,128)S(1)}, f32[2,2,64,128]{3,2,1,0:T(8,128)S(1)}, u32[]{:S(2)}, u32[]{:S(2)}) collective-permute-start(f32[2,2,64,128]{3,2,1,0:T(8,128)S(1)} %pad_maximum_fusion.34), channel_id=1, source_target_pairs={{0,4},{1,5},{2,6},{3,7},{4,0},{5,1},{6,2},{7,3},{8,12},{9,13},{10,... | collective-permute-start | bytes 393224 | tf_op jit(solution)/shard_map/ppermute | solution.py:28
  193.5 7.3 %collective-permute-start.58 = (f32[2,2,64,128]{3,2,1,0:T(8,128)S(1)}, f32[2,2,64,128]{3,2,1,0:T(8,128)S(1)}, u32[]{:S(2)}, u32[]{:S(2)}) collective-permute-start(f32[2,2,64,128]{3,2,1,0:T(8,128)S(1)} %pad_maximum_fusion.33), channel_id=1, source_target_pairs={{0,2},{1,3},{2,0},{3,1},{4,6},{5,7},{6,4},{7,5},{8,10},{9,11},{10,... | collective-permute-start | bytes 393224 | tf_op jit(solution)/shard_map/ppermute | solution.py:28
  205.5 1.8 collective-permute-start.61
  207.4 4.9 %collective-permute-start.62 = (f32[192,128]{1,0:T(8,128)S(1)}, f32[192,128]{1,0:T(8,128)S(1)}, u32[]{:S(2)}, u32[]{:S(2)}) collective-permute-start(f32[192,128]{1,0:T(8,128)S(1)} %get-tuple-element.112), channel_id=1, source_target_pairs={{0,2},{1,3},{2,0},{3,1},{4,6},{5,7},{6,4},{7,5},{8,10},{9,11},{10,... | collective-permute-start | bytes 294920 | tf_op jit(solution)/shard_map/ppermute | solution.py:28
  208.6 6.7 %collective-permute-start.63 = (f32[192,128]{1,0:T(8,128)S(1)}, f32[192,128]{1,0:T(8,128)S(1)}, u32[]{:S(2)}, u32[]{:S(2)}) collective-permute-start(f32[192,128]{1,0:T(8,128)S(1)} %get-tuple-element.114), channel_id=1, source_target_pairs={{0,4},{1,5},{2,6},{3,7},{4,0},{5,1},{6,2},{7,3},{8,12},{9,13},{10,... | collective-permute-start | bytes 294920 | tf_op jit(solution)/shard_map/ppermute | solution.py:28
  209.7 5.6 %collective-permute-start.64 = (f32[192,128]{1,0:T(8,128)S(1)}, f32[192,128]{1,0:T(8,128)S(1)}, u32[]{:S(2)}, u32[]{:S(2)}) collective-permute-start(f32[192,128]{1,0:T(8,128)S(1)} %get-tuple-element.113), channel_id=1, source_target_pairs={{0,6},{1,7},{2,4},{3,5},{4,2},{5,3},{6,0},{7,1},{8,14},{9,15},{10,... | collective-permute-start | bytes 294920 | tf_op jit(solution)/shard_map/ppermute | solution.py:28
  215.4 5.5 %collective-permute-start.65 = (f32[48,128]{1,0:T(8,128)S(1)}, f32[48,128]{1,0:T(8,128)S(1)}, u32[]{:S(2)}, u32[]{:S(2)}) collective-permute-start(f32[48,128]{1,0:T(8,128)S(1)} %get-tuple-element.182), channel_id=1, source_target_pairs={{0,8},{8,0},{16,24},{24,16},{1,9},{9,1},{17,25},{25,17},{2,10},{10... | collective-permute-start | bytes 73736 | tf_op jit(solution)/shard_map/ppermute | solution.py:28
  217.0 5.6 %collective-permute-start.66 = (f32[48,128]{1,0:T(8,128)S(1)}, f32[48,128]{1,0:T(8,128)S(1)}, u32[]{:S(2)}, u32[]{:S(2)}) collective-permute-start(f32[48,128]{1,0:T(8,128)S(1)} %get-tuple-element.184), channel_id=1, source_target_pairs={{0,24},{8,16},{16,8},{24,0},{1,25},{9,17},{17,9},{25,1},{2,26},{10... | collective-permute-start | bytes 73736 | tf_op jit(solution)/shard_map/ppermute | solution.py:28
  219.8 4.7 %collective-permute-start.67 = (f32[48,128]{1,0:T(8,128)S(1)}, f32[48,128]{1,0:T(8,128)S(1)}, u32[]{:S(2)}, u32[]{:S(2)}) collective-permute-start(f32[48,128]{1,0:T(8,128)S(1)} %get-tuple-element.183), channel_id=1, source_target_pairs={{0,16},{8,24},{16,0},{24,8},{1,17},{9,25},{17,1},{25,9},{2,18},{10... | collective-permute-start | bytes 73736 | tf_op jit(solution)/shard_map/ppermute | solution.py:28
  (12 other events, 161.2 us)

commit v8 on v7

--- a/solution.py
+++ b/solution.py
@@ -83,7 +83,8 @@
                     outs[h * cores + c][k, j] = warped[h * part : (h + 1) * part]
 
 
-def forward_body(dims, source_ref, valid_ref, me_ref, matrix, tiles, *refs):
+def forward_body(dims, ahead, source_ref, valid_ref, me_ref, matrix, tiles, *refs):
+    refs = refs[ahead:]
     vox, masks, rows, pieces_n, chunks, cores = dims
     pieces, outs = refs[:pieces_n], refs[pieces_n:-2]
     dose, weights = refs[-2:]
@@ -102,7 +103,7 @@
     warp(chunks, cores, source_ref, valid_ref, tiles, dose, outs)
 
 
-def forward(scalars, matrix, tiles, pieces, rows, vox, masks):
+def forward(scalars, matrix, tiles, pieces, rows, vox, masks, ahead):
     height = tiles.shape[1]
     vox_rows, spots = matrix.shape
     plans = pieces[0].shape[-1]
@@ -110,15 +111,17 @@
     out = jax.ShapeDtypeStruct((vox // cores, CAP, height // CHUNKS, plans), F32)
     outs = [out] * (cores * CHUNKS)
     return pl.pallas_call(
-        functools.partial(forward_body, (vox, masks, rows, len(pieces), CHUNKS, cores)),
-        in_specs=specs(3, pltpu.SMEM) + specs(2 + len(pieces), pltpu.VMEM),
+        functools.partial(
+            forward_body, (vox, masks, rows, len(pieces), CHUNKS, cores), len(ahead)
+        ),
+        in_specs=specs(3, pltpu.SMEM) + specs(2 + len(ahead) + len(pieces), pltpu.VMEM),
         out_specs=specs(len(outs), pltpu.VMEM),
         out_shape=outs,
         scratch_shapes=[pltpu.VMEM((vox_rows, plans), F32), pltpu.VMEM((spots, 2 * plans), BF16)],
         compiler_params=pltpu.CompilerParams(vmem_limit_bytes=LARGE),
         cost_estimate=BRIEF,
         name="dose_and_warp",
-    )(*scalars, matrix, tiles, *pieces)
+    )(*scalars, matrix, tiles, *ahead, *pieces)
 
 
 def piece(arrived, cores, m):
@@ -327,7 +330,7 @@
         in_specs=specs(2, pltpu.VMEM),
         out_specs=pl.BlockSpec(memory_space=pltpu.VMEM),
         out_shape=jax.ShapeDtypeStruct((8, x.shape[-1]), F32),
-        compiler_params=pltpu.CompilerParams(vmem_limit_bytes=SMALL),
+        compiler_params=pltpu.CompilerParams(vmem_limit_bytes=LARGE),
         cost_estimate=BRIEF,
         name="hold",
     )(matrix, x)
@@ -420,7 +423,8 @@
             back_to = jnp.asarray([masks.index(p) for p in range(phases)], jnp.int32)
             every = every[jnp.arange(vox) ^ me_vox][:, back_to[jnp.arange(phases) ^ me_phase]]
             pieces = [every.transpose(1, 0, 2, 3).reshape(spots, plans)]
-        outgoing = forward(scalars, matrix, tiles, pieces, rows, vox, masks)
+        ahead = [hold(matrix, held[None])] if iteration == 0 else []
+        outgoing = forward(scalars, matrix, tiles, pieces, rows, vox, masks, ahead)
         returned, dose = [], []
         incoming, held_halves, seconds = exchange(outgoing[:cores]), [], []
         for h in range(CHUNKS):

time: 225 us -> 224 us (level)
    unnamed x20 -> x15, local copies, waits for them, and re-layouts: 9.95 us -> 9.94 us
  transfers between devices with their start and end apart: 68 -> 68, of which waited for: 51 -> 50; matrix products, arithmetic and copies ran while one was open for 5% -> 6% of each run, Pallas kernels for 3% -> 3%
where the time goes in v8:
time: 224 us
  waiting for transfers between devices  99.2 us (44%)
  starting transfers between devices  76.3 us (34%)
  Pallas kernels  24 us (11%)
  local copies, waits for them, and re-layouts  15.1 us (7%)
  other arithmetic  5.81 us (3%)
    ppermute x68, waiting for transfers between devices, swap(): return lax.ppermute(x, axis, [(i, i ^ mask) for i in range(count)])  99.2 us
    ppermute x68, starting transfers between devices, swap(): return lax.ppermute(x, axis, [(i, i ^ mask) for i in range(count)])  76.3 us
    unnamed x15, local copies, waits for them, and re-layouts  9.94 us
    pallas_call x2, Pallas kernels, forward(): pl.pallas_call(functools.partial(forward_body, (vox, masks, rows, len(pie...  9.54 us
    pallas_call x2, Pallas kernels, gradient_parts(): pl.pallas_call(functools.partial(gradient_body, (vox, masks, rows, cores,...  8.41 us
  transfers between devices with their start and end apart: 68, of which 50 were waited for; matrix products, arithmetic and copies ran while one was open for 6% of the time, Pallas kernels for 3%

profile of v8, /device:TPU:0, one launch (start us, length us, event | category | flops | bytes accessed | tf_op | source)
XLA Modules:
  0.0 223.5 jit_solution(11162919557756598762)
XLA Ops:
  0.6 3.1 %collective-permute-start = (f32[48,128]{1,0:T(8,128)}, f32[48,128]{1,0:T(8,128)S(1)}, u32[]{:S(2)}, u32[]{:S(2)}) collective-permute-start(f32[48,128]{1,0:T(8,128)} %param.15), channel_id=1, source_target_pairs={{0,8},{8,0},{16,24},{24,16},{1,9},{9,1},{17,25},{25,17},{2,10},{10... | collective-permute-start | bytes 73736 | tf_op jit(solution)/shard_map/ppermute | solution.py:28
  3.7 2.5 %collective-permute-start.1 = (f32[48,128]{1,0:T(8,128)}, f32[48,128]{1,0:T(8,128)S(1)}, u32[]{:S(2)}, u32[]{:S(2)}) collective-permute-start(f32[48,128]{1,0:T(8,128)} %param.15), channel_id=1, source_target_pairs={{0,24},{8,16},{16,8},{24,0},{1,25},{9,17},{17,9},{25,1},{2,26},{10... | collective-permute-start | bytes 73736 | tf_op jit(solution)/shard_map/ppermute | solution.py:28
  11.4 1.6 collective-permute-start.4
  13.0 1.4 collective-permute-start.5
  15.0 2.8 %gather_fusion = f32[16,128,128]{2,1,0:T(8,128)S(1)} fusion(f32[64,128,128]{2,1,0:T(8,128)} %param.16, s32[1024]{0:T(1024)S(1)} %pad_clamp_fusion), kind=kCustom, calls=%fused_computation | custom fusion | bytes 2097216 | tf_op jit(solution)/shard_map/gather | solution.py:405
  20.1 4.6 %copy-done.1 = f32[1,2048,1536]{2,1,0:T(8,128)S(1)} copy-done((f32[1,2048,1536]{2,1,0:T(8,128)S(1)}, f32[1,2048,1536]{2,1,0:T(8,128)}, u32[]{:S(2)}) %copy-start.1) | copy-done | bytes 12582936
  24.7 4.8 %dose_and_warp.2 = (f32[4,2,64,128]{3,2,1,0:T(8,128)S(1)}, f32[4,2,64,128]{3,2,1,0:T(8,128)S(1)}, f32[4,2,64,128]{3,2,1,0:T(8,128)S(1)}, f32[4,2,64,128]{3,2,1,0:T(8,128)S(1)}) custom-call(s32[16]{0:T(128)S(1)} %get-tuple-element.105.source_ref, s32[16]{0:T(128)S(1)} %get-tuple-element.104.valid_ref, s32[2]{0:T(128)S(1)} %pad_add_fusion.me_ref, ...), custom_call_target="tpu_custom_call" | custom-call | flops 1 | bytes 1 | tf_op jit(solution)/shard_map/dose_and_warp/pallas_call | solution.py:113
  31.3 1.6 collective-permute-start.9
  35.0 4.6 %collective-permute-done.9.refs_2_ = f32[2,2,64,128]{3,2,1,0:T(8,128)S(1)} collective-permute-done((f32[2,2,64,128]{3,2,1,0:T(8,128)S(1)}, f32[2,2,64,128]{3,2,1,0:T(8,128)S(1)}, u32[]{:S(2)}, u32[]{:S(2)}) %collective-permute-start.9) | collective-permute-done | bytes 131104 | tf_op jit(solution)/shard_map/ppermute | solution.py:28
  44.5 2.2 collective-permute-start.17
  48.2 1.3 collective-permute-done.11
  49.5 1.8 collective-permute-start.12
  53.7 1.5 collective-permute-start.18
  55.2 4.5 %collective-permute-done.12 = f32[8,64,128]{2,1,0:T(8,128)S(1)} collective-permute-done((f32[8,64,128]{2,1,0:T(8,128)S(1)}, f32[8,64,128]{2,1,0:T(8,128)S(1)}, u32[]{:S(2)}, u32[]{:S(2)}) %collective-permute-start.12) | collective-permute-done | bytes 262176 | tf_op jit(solution)/shard_map/ppermute | solution.py:28
  59.7 2.7 %collective-permute-start.13 = (f32[8,64,128]{2,1,0:T(8,128)S(1)}, f32[8,64,128]{2,1,0:T(8,128)S(1)}, u32[]{:S(2)}, u32[]{:S(2)}) collective-permute-start(f32[8,64,128]{2,1,0:T(8,128)S(1)} %add.123.mine), channel_id=1, source_target_pairs={{0,8},{8,0},{16,24},{24,16},{1,9},{9,1},{17,25},{25,17},{2,10},{10... | collective-permute-start | bytes 786440 | tf_op jit(solution)/shard_map/ppermute | solution.py:28
  62.5 1.6 collective-permute-done.18
  64.2 1.8 collective-permute-start.23
  66.1 4.6 %copy-done.2 = f32[1,2048,1536]{2,1,0:T(8,128)S(1)} copy-done((f32[1,2048,1536]{2,1,0:T(8,128)S(1)}, f32[1,2048,1536]{2,1,0:T(8,128)}, u32[]{:S(2)}) %copy-start.2) | copy-done | bytes 12582936
  71.6 4.1 %collective-permute-done.23 = f32[8,64,128]{2,1,0:T(8,128)S(1)} collective-permute-done((f32[8,64,128]{2,1,0:T(8,128)S(1)}, f32[8,64,128]{2,1,0:T(8,128)S(1)}, u32[]{:S(2)}, u32[]{:S(2)}) %collective-permute-start.23) | collective-permute-done | bytes 262176 | tf_op jit(solution)/shard_map/ppermute | solution.py:28
  76.9 2.1 collective-permute-start.22
  79.4 2.8 %collective-permute-done.24.other = f32[8,64,128]{2,1,0:T(8,128)S(1)} collective-permute-done((f32[8,64,128]{2,1,0:T(8,128)S(1)}, f32[8,64,128]{2,1,0:T(8,128)S(1)}, u32[]{:S(2)}, u32[]{:S(2)}) %collective-permute-start.24) | collective-permute-done | bytes 262176 | tf_op jit(solution)/shard_map/ppermute | solution.py:28
  84.7 2.3 %collective-permute-start.28 = (f32[2,2,64,128]{3,2,1,0:T(8,128)S(1)}, f32[2,2,64,128]{3,2,1,0:T(8,128)S(1)}, u32[]{:S(2)}, u32[]{:S(2)}) collective-permute-start(f32[2,2,64,128]{3,2,1,0:T(8,128)S(1)} %pad_maximum_fusion.19), channel_id=1, source_target_pairs={{0,6},{1,7},{2,4},{3,5},{4,2},{5,3},{6,0},{7,1},{8,14},{9,15},{10,... | collective-permute-start | bytes 393224 | tf_op jit(solution)/shard_map/ppermute | solution.py:28
  89.5 3.8 %collective-permute-done.28.refs_7_ = f32[2,2,64,128]{3,2,1,0:T(8,128)S(1)} collective-permute-done((f32[2,2,64,128]{3,2,1,0:T(8,128)S(1)}, f32[2,2,64,128]{3,2,1,0:T(8,128)S(1)}, u32[]{:S(2)}, u32[]{:S(2)}) %collective-permute-start.28) | collective-permute-done | bytes 131104 | tf_op jit(solution)/shard_map/ppermute | solution.py:28
  93.4 1.7 collective-permute-done.27.refs_6_
  95.1 4.2 %warp_back_and_gradient.2 = (f32[4,192,128]{2,1,0:T(8,128)S(1)}, f32[4,192,128]{2,1,0:T(8,128)S(1)}) custom-call(s32[16]{0:T(128)S(1)} %get-tuple-element.105.source_ref, s32[16]{0:T(128)S(1)} %get-tuple-element.104.valid_ref, s32[2]{0:T(128)S(1)} %pad_add_fusion.me_ref, f32[2048,1536]{1,0:T(8,128)S(1)} %bitcast.98, f32[16,128,128]{2,1,0:T(8,128)S(1)} %gather_fusion, ...), custom_call_target="tpu_custom_call" | custom-call | flops 1 | bytes 1 | tf_op jit(solution)/shard_map/warp_back_and_gradient/pallas_call | solution.py:186
  99.4 1.7 collective-permute-done.29
  102.1 1.6 collective-permute-start.31
  104.8 1.7 collective-permute-done.30
  106.5 1.4 collective-permute-done.31
  107.9 1.3 collective-permute-done.32
  110.3 3.7 %collective-permute-done.33 = f32[4,48,128]{2,1,0:T(8,128)S(1)} collective-permute-done((f32[4,48,128]{2,1,0:T(8,128)S(1)}, f32[4,48,128]{2,1,0:T(8,128)S(1)}, u32[]{:S(2)}, u32[]{:S(2)}) %collective-permute-start.33) | collective-permute-done | bytes 98336 | tf_op jit(solution)/shard_map/ppermute | solution.py:28
  114.0 1.5 collective-permute-start.34
  115.4 5.0 %collective-permute-done.34 = f32[4,48,128]{2,1,0:T(8,128)S(1)} collective-permute-done((f32[4,48,128]{2,1,0:T(8,128)S(1)}, f32[4,48,128]{2,1,0:T(8,128)S(1)}, u32[]{:S(2)}, u32[]{:S(2)}) %collective-permute-start.34) | collective-permute-done | bytes 98336 | tf_op jit(solution)/shard_map/ppermute | solution.py:28
  122.7 1.4 collective-permute-start.37
  126.1 2.1 collective-permute-done.37
  128.3 1.7 collective-permute-done.38.refs_1_
  130.0 4.8 %dose_and_warp.3 = (f32[4,2,64,128]{3,2,1,0:T(8,128)S(1)}, f32[4,2,64,128]{3,2,1,0:T(8,128)S(1)}, f32[4,2,64,128]{3,2,1,0:T(8,128)S(1)}, f32[4,2,64,128]{3,2,1,0:T(8,128)S(1)}) custom-call(s32[16]{0:T(128)S(1)} %get-tuple-element.105.source_ref, s32[16]{0:T(128)S(1)} %get-tuple-element.104.valid_ref, s32[2]{0:T(128)S(1)} %pad_add_fusion.me_ref, ...), custom_call_target="tpu_custom_call" | custom-call | flops 1 | bytes 1 | tf_op jit(solution)/shard_map/dose_and_warp/pallas_call | solution.py:113
  135.0 1.4 collective-permute-done.39
  137.3 1.8 collective-permute-start.42
  140.2 4.7 %collective-permute-done.41.refs_2_ = f32[2,2,64,128]{3,2,1,0:T(8,128)S(1)} collective-permute-done((f32[2,2,64,128]{3,2,1,0:T(8,128)S(1)}, f32[2,2,64,128]{3,2,1,0:T(8,128)S(1)}, u32[]{:S(2)}, u32[]{:S(2)}) %collective-permute-start.41) | collective-permute-done | bytes 131104 | tf_op jit(solution)/shard_map/ppermute | solution.py:28
  144.9 1.3 collective-permute-done.40.refs_1_
  147.1 1.5 collective-permute-start.53
  148.5 5.9 %collective-permute-done.43 = f32[8,64,128]{2,1,0:T(8,128)S(1)} collective-permute-done((f32[8,64,128]{2,1,0:T(8,128)S(1)}, f32[8,64,128]{2,1,0:T(8,128)S(1)}, u32[]{:S(2)}, u32[]{:S(2)}) %collective-permute-start.43) | collective-permute-done | bytes 262176 | tf_op jit(solution)/shard_map/ppermute | solution.py:28
  154.5 1.4 collective-permute-start.44
  157.9 3.1 %collective-permute-done.52.refs_2_ = f32[2,2,64,128]{3,2,1,0:T(8,128)S(1)} collective-permute-done((f32[2,2,64,128]{3,2,1,0:T(8,128)S(1)}, f32[2,2,64,128]{3,2,1,0:T(8,128)S(1)}, u32[]{:S(2)}, u32[]{:S(2)}) %collective-permute-start.52) | collective-permute-done | bytes 131104 | tf_op jit(solution)/shard_map/ppermute | solution.py:28
  163.4 3.9 %collective-permute-start.45 = (f32[8,64,128]{2,1,0:T(8,128)S(1)}, f32[8,64,128]{2,1,0:T(8,128)S(1)}, u32[]{:S(2)}, u32[]{:S(2)}) collective-permute-start(f32[8,64,128]{2,1,0:T(8,128)S(1)} %add.134.mine), channel_id=1, source_target_pairs={{0,8},{8,0},{16,24},{24,16},{1,9},{9,1},{17,25},{25,17},{2,10},{10... | collective-permute-start | bytes 786440 | tf_op jit(solution)/shard_map/ppermute | solution.py:28
  167.4 4.4 %collective-permute-done.54 = f32[8,64,128]{2,1,0:T(8,128)S(1)} collective-permute-done((f32[8,64,128]{2,1,0:T(8,128)S(1)}, f32[8,64,128]{2,1,0:T(8,128)S(1)}, u32[]{:S(2)}, u32[]{:S(2)}) %collective-permute-start.54) | collective-permute-done | bytes 262176 | tf_op jit(solution)/shard_map/ppermute | solution.py:28
  171.8 1.7 collective-permute-start.55
  173.5 2.9 %collective-permute-done.45.other = f32[8,64,128]{2,1,0:T(8,128)S(1)} collective-permute-done((f32[8,64,128]{2,1,0:T(8,128)S(1)}, f32[8,64,128]{2,1,0:T(8,128)S(1)}, u32[]{:S(2)}, u32[]{:S(2)}) %collective-permute-start.45) | collective-permute-done | bytes 262176 | tf_op jit(solution)/shard_map/ppermute | solution.py:28
  177.1 3.7 %collective-permute-done.55 = f32[8,64,128]{2,1,0:T(8,128)S(1)} collective-permute-done((f32[8,64,128]{2,1,0:T(8,128)S(1)}, f32[8,64,128]{2,1,0:T(8,128)S(1)}, u32[]{:S(2)}, u32[]{:S(2)}) %collective-permute-start.55) | collective-permute-done | bytes 262176 | tf_op jit(solution)/shard_map/ppermute | solution.py:28
  180.8 2.0 collective-permute-start.56
  182.9 1.6 collective-permute-start.49
  185.7 1.6 collective-permute-done.56.other
  189.6 1.9 collective-permute-start.60
  194.4 3.5 %collective-permute-done.60.refs_7_ = f32[2,2,64,128]{3,2,1,0:T(8,128)S(1)} collective-permute-done((f32[2,2,64,128]{3,2,1,0:T(8,128)S(1)}, f32[2,2,64,128]{3,2,1,0:T(8,128)S(1)}, u32[]{:S(2)}, u32[]{:S(2)}) %collective-permute-start.60) | collective-permute-done | bytes 131104 | tf_op jit(solution)/shard_map/ppermute | solution.py:28
  198.0 1.7 collective-permute-done.59.refs_6_
  199.7 4.2 %warp_back_and_gradient.3 = (f32[4,192,128]{2,1,0:T(8,128)S(1)}, f32[4,192,128]{2,1,0:T(8,128)S(1)}) custom-call(s32[16]{0:T(128)S(1)} %get-tuple-element.105.source_ref, s32[16]{0:T(128)S(1)} %get-tuple-element.104.valid_ref, s32[2]{0:T(128)S(1)} %pad_add_fusion.me_ref, f32[2048,1536]{1,0:T(8,128)S(1)} %bitcast.100, f32[16,128,128]{2,1,0:T(8,128)S(1)} %gather_fusion, ...), custom_call_target="tpu_custom_call" | custom-call | flops 1 | bytes 1 | tf_op jit(solution)/shard_map/warp_back_and_gradient/pallas_call | solution.py:186
  204.0 1.7 collective-permute-done.61
  209.4 1.3 collective-permute-done.62
  210.7 2.0 collective-permute-done.63
  213.9 1.9 collective-permute-start.65
  215.8 2.4 %collective-permute-start.66 = (f32[48,128]{1,0:T(8,128)S(1)}, f32[48,128]{1,0:T(8,128)S(1)}, u32[]{:S(2)}, u32[]{:S(2)}) collective-permute-start(f32[48,128]{1,0:T(8,128)S(1)} %get-tuple-element.184), channel_id=1, source_target_pairs={{0,24},{8,16},{16,8},{24,0},{1,25},{9,17},{17,9},{25,1},{2,26},{10... | collective-permute-start | bytes 73736 | tf_op jit(solution)/shard_map/ppermute | solution.py:28
  219.3 2.1 collective-permute-done.66
  221.4 1.5 collective-permute-done.67
  (204 shorter events, 57.0 us)
Async XLA Ops:
  0.6 9.5 %collective-permute-start = (f32[48,128]{1,0:T(8,128)}, f32[48,128]{1,0:T(8,128)S(1)}, u32[]{:S(2)}, u32[]{:S(2)}) collective-permute-start(f32[48,128]{1,0:T(8,128)} %param.15), channel_id=1, source_target_pairs={{0,8},{8,0},{16,24},{24,16},{1,9},{9,1},{17,25},{25,17},{2,10},{10... | collective-permute-start | bytes 73736 | tf_op jit(solution)/shard_map/ppermute | solution.py:28
  3.7 6.4 %collective-permute-start.1 = (f32[48,128]{1,0:T(8,128)}, f32[48,128]{1,0:T(8,128)S(1)}, u32[]{:S(2)}, u32[]{:S(2)}) collective-permute-start(f32[48,128]{1,0:T(8,128)} %param.15), channel_id=1, source_target_pairs={{0,24},{8,16},{16,8},{24,0},{1,25},{9,17},{17,9},{25,1},{2,26},{10... | collective-permute-start | bytes 73736 | tf_op jit(solution)/shard_map/ppermute | solution.py:28
  6.2 5.2 %collective-permute-start.2 = (f32[48,128]{1,0:T(8,128)}, f32[48,128]{1,0:T(8,128)S(1)}, u32[]{:S(2)}, u32[]{:S(2)}) collective-permute-start(f32[48,128]{1,0:T(8,128)} %param.15), channel_id=1, source_target_pairs={{0,16},{8,24},{16,0},{24,8},{1,17},{9,25},{17,1},{25,9},{2,18},{10... | collective-permute-start | bytes 73736 | tf_op jit(solution)/shard_map/ppermute | solution.py:28
  11.4 6.4 %collective-permute-start.4 = (f32[208,128]{1,0:T(8,128)S(1)}, f32[208,128]{1,0:T(8,128)S(1)}, u32[]{:S(2)}, u32[]{:S(2)}) collective-permute-start(f32[208,128]{1,0:T(8,128)S(1)} %constant_dynamic-update-slice_fusion.4), channel_id=1, source_target_pairs={{0,4},{1,5},{2,6},{3,7},{4,0},{5,1},{6,2},{7,3},{8,12},{9,13},{10,... | collective-permute-start | bytes 319496 | tf_op jit(solution)/shard_map/ppermute | solution.py:28
  13.0 5.6 %collective-permute-start.5 = (f32[208,128]{1,0:T(8,128)S(1)}, f32[208,128]{1,0:T(8,128)S(1)}, u32[]{:S(2)}, u32[]{:S(2)}) collective-permute-start(f32[208,128]{1,0:T(8,128)S(1)} %constant_dynamic-update-slice_fusion.4), channel_id=1, source_target_pairs={{0,6},{1,7},{2,4},{3,5},{4,2},{5,3},{6,0},{7,1},{8,14},{9,15},{10,... | collective-permute-start | bytes 319496 | tf_op jit(solution)/shard_map/ppermute | solution.py:28
  14.4 4.7 %collective-permute-start.3 = (f32[208,128]{1,0:T(8,128)S(1)}, f32[208,128]{1,0:T(8,128)S(1)}, u32[]{:S(2)}, u32[]{:S(2)}) collective-permute-start(f32[208,128]{1,0:T(8,128)S(1)} %constant_dynamic-update-slice_fusion.4), channel_id=1, source_target_pairs={{0,2},{1,3},{2,0},{3,1},{4,6},{5,7},{6,4},{7,5},{8,10},{9,11},{10,... | collective-permute-start | bytes 319496 | tf_op jit(solution)/shard_map/ppermute | solution.py:28
  19.2 5.5 %collective-permute-start.6 = (f32[4,208,128]{2,1,0:T(8,128)S(1)}, f32[4,208,128]{2,1,0:T(8,128)S(1)}, u32[]{:S(2)}, u32[]{:S(2)}) collective-permute-start(f32[4,208,128]{2,1,0:T(8,128)S(1)} %get-tuple-element.111.refs_1_), channel_id=1, source_target_pairs={{0,1},{1,0},{2,3},{3,2},{4,5},{5,4},{6,7},{7,6},{8,9},{9,8},{10,11... | collective-permute-start | bytes 1277960 | tf_op jit(solution)/shard_map/ppermute | solution.py:28
  31.3 8.3 %collective-permute-start.9 = (f32[2,2,64,128]{3,2,1,0:T(8,128)S(1)}, f32[2,2,64,128]{3,2,1,0:T(8,128)S(1)}, u32[]{:S(2)}, u32[]{:S(2)}) collective-permute-start(f32[2,2,64,128]{3,2,1,0:T(8,128)S(1)} %pad_maximum_fusion.6), channel_id=1, source_target_pairs={{0,4},{1,5},{2,6},{3,7},{4,0},{5,1},{6,2},{7,3},{8,12},{9,13},{10,... | collective-permute-start | bytes 393224 | tf_op jit(solution)/shard_map/ppermute | solution.py:28
  32.9 7.4 %collective-permute-start.10 = (f32[2,2,64,128]{3,2,1,0:T(8,128)S(1)}, f32[2,2,64,128]{3,2,1,0:T(8,128)S(1)}, u32[]{:S(2)}, u32[]{:S(2)}) collective-permute-start(f32[2,2,64,128]{3,2,1,0:T(8,128)S(1)} %pad_maximum_fusion.7), channel_id=1, source_target_pairs={{0,6},{1,7},{2,4},{3,5},{4,2},{5,3},{6,0},{7,1},{8,14},{9,15},{10,... | collective-permute-start | bytes 393224 | tf_op jit(solution)/shard_map/ppermute | solution.py:28
  34.1 7.2 %collective-permute-start.8 = (f32[2,2,64,128]{3,2,1,0:T(8,128)S(1)}, f32[2,2,64,128]{3,2,1,0:T(8,128)S(1)}, u32[]{:S(2)}, u32[]{:S(2)}) collective-permute-start(f32[2,2,64,128]{3,2,1,0:T(8,128)S(1)} %pad_maximum_fusion.5), channel_id=1, source_target_pairs={{0,2},{1,3},{2,0},{3,1},{4,6},{5,7},{6,4},{7,5},{8,10},{9,11},{10,... | collective-permute-start | bytes 393224 | tf_op jit(solution)/shard_map/ppermute | solution.py:28
  39.6 4.8 %collective-permute-start.14 = (f32[4,2,64,128]{3,2,1,0:T(8,128)S(1)}, f32[4,2,64,128]{3,2,1,0:T(8,128)S(1)}, u32[]{:S(2)}, u32[]{:S(2)}) collective-permute-start(f32[4,2,64,128]{3,2,1,0:T(8,128)S(1)} %get-tuple-element.73), channel_id=1, source_target_pairs={{0,1},{1,0},{2,3},{3,2},{4,5},{5,4},{6,7},{7,6},{8,9},{9,8},{10,11... | collective-permute-start | bytes 786440 | tf_op jit(solution)/shard_map/ppermute | solution.py:28
  42.0 7.5 %collective-permute-start.11 = (f32[8,64,128]{2,1,0:T(8,128)S(1)}, f32[8,64,128]{2,1,0:T(8,128)S(1)}, u32[]{:S(2)}, u32[]{:S(2)}) collective-permute-start(f32[8,64,128]{2,1,0:T(8,128)S(1)} %get-tuple-element.68), channel_id=1, source_target_pairs={{0,8},{8,0},{16,24},{24,16},{1,9},{9,1},{17,25},{25,17},{2,10},{10... | collective-permute-start | bytes 786440 | tf_op jit(solution)/shard_map/ppermute | solution.py:28
  44.5 7.0 %collective-permute-start.17 = (f32[2,2,64,128]{3,2,1,0:T(8,128)S(1)}, f32[2,2,64,128]{3,2,1,0:T(8,128)S(1)}, u32[]{:S(2)}, u32[]{:S(2)}) collective-permute-start(f32[2,2,64,128]{3,2,1,0:T(8,128)S(1)} %pad_maximum_fusion.11), channel_id=1, source_target_pairs={{0,6},{1,7},{2,4},{3,5},{4,2},{5,3},{6,0},{7,1},{8,14},{9,15},{10,... | collective-permute-start | bytes 393224 | tf_op jit(solution)/shard_map/ppermute | solution.py:28
  46.7 5.9 %collective-permute-start.16 = (f32[2,2,64,128]{3,2,1,0:T(8,128)S(1)}, f32[2,2,64,128]{3,2,1,0:T(8,128)S(1)}, u32[]{:S(2)}, u32[]{:S(2)}) collective-permute-start(f32[2,2,64,128]{3,2,1,0:T(8,128)S(1)} %pad_maximum_fusion.10), channel_id=1, source_target_pairs={{0,4},{1,5},{2,6},{3,7},{4,0},{5,1},{6,2},{7,3},{8,12},{9,13},{10,... | collective-permute-start | bytes 393224 | tf_op jit(solution)/shard_map/ppermute | solution.py:28
  47.3 5.5 %collective-permute-start.15 = (f32[2,2,64,128]{3,2,1,0:T(8,128)S(1)}, f32[2,2,64,128]{3,2,1,0:T(8,128)S(1)}, u32[]{:S(2)}, u32[]{:S(2)}) collective-permute-start(f32[2,2,64,128]{3,2,1,0:T(8,128)S(1)} %pad_maximum_fusion.9), channel_id=1, source_target_pairs={{0,2},{1,3},{2,0},{3,1},{4,6},{5,7},{6,4},{7,5},{8,10},{9,11},{10,... | collective-permute-start | bytes 393224 | tf_op jit(solution)/shard_map/ppermute | solution.py:28
  49.5 10.2 %collective-permute-start.12 = (f32[8,64,128]{2,1,0:T(8,128)S(1)}, f32[8,64,128]{2,1,0:T(8,128)S(1)}, u32[]{:S(2)}, u32[]{:S(2)}) collective-permute-start(f32[8,64,128]{2,1,0:T(8,128)S(1)} %add.122), channel_id=1, source_target_pairs={{0,24},{8,16},{16,8},{24,0},{1,25},{9,17},{17,9},{25,1},{2,26},{10... | collective-permute-start | bytes 786440 | tf_op jit(solution)/shard_map/ppermute | solution.py:28
  53.7 10.5 %collective-permute-start.18 = (f32[8,64,128]{2,1,0:T(8,128)S(1)}, f32[8,64,128]{2,1,0:T(8,128)S(1)}, u32[]{:S(2)}, u32[]{:S(2)}) collective-permute-start(f32[8,64,128]{2,1,0:T(8,128)S(1)} %get-tuple-element.75), channel_id=1, source_target_pairs={{0,8},{8,0},{16,24},{24,16},{1,9},{9,1},{17,25},{25,17},{2,10},{10... | collective-permute-start | bytes 786440 | tf_op jit(solution)/shard_map/ppermute | solution.py:28
  59.7 10.9 %collective-permute-start.13 = (f32[8,64,128]{2,1,0:T(8,128)S(1)}, f32[8,64,128]{2,1,0:T(8,128)S(1)}, u32[]{:S(2)}, u32[]{:S(2)}) collective-permute-start(f32[8,64,128]{2,1,0:T(8,128)S(1)} %add.123.mine), channel_id=1, source_target_pairs={{0,8},{8,0},{16,24},{24,16},{1,9},{9,1},{17,25},{25,17},{2,10},{10... | collective-permute-start | bytes 786440 | tf_op jit(solution)/shard_map/ppermute | solution.py:28
  64.2 11.5 %collective-permute-start.23 = (f32[8,64,128]{2,1,0:T(8,128)S(1)}, f32[8,64,128]{2,1,0:T(8,128)S(1)}, u32[]{:S(2)}, u32[]{:S(2)}) collective-permute-start(f32[8,64,128]{2,1,0:T(8,128)S(1)} %add.124.x), channel_id=1, source_target_pairs={{0,24},{8,16},{16,8},{24,0},{1,25},{9,17},{17,9},{25,1},{2,26},{10... | collective-permute-start | bytes 786440 | tf_op jit(solution)/shard_map/ppermute | solution.py:28
  71.5 5.3 %collective-permute-start.19 = (f32[4,2,64,128]{3,2,1,0:T(8,128)S(1)}, f32[4,2,64,128]{3,2,1,0:T(8,128)S(1)}, u32[]{:S(2)}, u32[]{:S(2)}) collective-permute-start(f32[4,2,64,128]{3,2,1,0:T(8,128)S(1)} %get-tuple-element.78), channel_id=1, source_target_pairs={{0,1},{1,0},{2,3},{3,2},{4,5},{5,4},{6,7},{7,6},{8,9},{9,8},{10,11... | collective-permute-start | bytes 786440 | tf_op jit(solution)/shard_map/ppermute | solution.py:28
  75.8 6.4 %collective-permute-start.24 = (f32[8,64,128]{2,1,0:T(8,128)S(1)}, f32[8,64,128]{2,1,0:T(8,128)S(1)}, u32[]{:S(2)}, u32[]{:S(2)}) collective-permute-start(f32[8,64,128]{2,1,0:T(8,128)S(1)} %add.125.mine), channel_id=1, source_target_pairs={{0,8},{8,0},{16,24},{24,16},{1,9},{9,1},{17,25},{25,17},{2,10},{10... | collective-permute-start | bytes 786440 | tf_op jit(solution)/shard_map/ppermute | solution.py:28
  76.9 10.7 %collective-permute-start.22 = (f32[2,2,64,128]{3,2,1,0:T(8,128)S(1)}, f32[2,2,64,128]{3,2,1,0:T(8,128)S(1)}, u32[]{:S(2)}, u32[]{:S(2)}) collective-permute-start(f32[2,2,64,128]{3,2,1,0:T(8,128)S(1)} %pad_maximum_fusion.15), channel_id=1, source_target_pairs={{0,6},{1,7},{2,4},{3,5},{4,2},{5,3},{6,0},{7,1},{8,14},{9,15},{10,... | collective-permute-start | bytes 393224 | tf_op jit(solution)/shard_map/ppermute | solution.py:28
  78.9 9.5 %collective-permute-start.21 = (f32[2,2,64,128]{3,2,1,0:T(8,128)S(1)}, f32[2,2,64,128]{3,2,1,0:T(8,128)S(1)}, u32[]{:S(2)}, u32[]{:S(2)}) collective-permute-start(f32[2,2,64,128]{3,2,1,0:T(8,128)S(1)} %pad_maximum_fusion.14), channel_id=1, source_target_pairs={{0,4},{1,5},{2,6},{3,7},{4,0},{5,1},{6,2},{7,3},{8,12},{9,13},{10,... | collective-permute-start | bytes 393224 | tf_op jit(solution)/shard_map/ppermute | solution.py:28
  83.2 6.4 %collective-permute-start.20 = (f32[2,2,64,128]{3,2,1,0:T(8,128)S(1)}, f32[2,2,64,128]{3,2,1,0:T(8,128)S(1)}, u32[]{:S(2)}, u32[]{:S(2)}) collective-permute-start(f32[2,2,64,128]{3,2,1,0:T(8,128)S(1)} %pad_maximum_fusion.13), channel_id=1, source_target_pairs={{0,2},{1,3},{2,0},{3,1},{4,6},{5,7},{6,4},{7,5},{8,10},{9,11},{10,... | collective-permute-start | bytes 393224 | tf_op jit(solution)/shard_map/ppermute | solution.py:28
  84.7 8.7 %collective-permute-start.28 = (f32[2,2,64,128]{3,2,1,0:T(8,128)S(1)}, f32[2,2,64,128]{3,2,1,0:T(8,128)S(1)}, u32[]{:S(2)}, u32[]{:S(2)}) collective-permute-start(f32[2,2,64,128]{3,2,1,0:T(8,128)S(1)} %pad_maximum_fusion.19), channel_id=1, source_target_pairs={{0,6},{1,7},{2,4},{3,5},{4,2},{5,3},{6,0},{7,1},{8,14},{9,15},{10,... | collective-permute-start | bytes 393224 | tf_op jit(solution)/shard_map/ppermute | solution.py:28
  87.0 8.1 %collective-permute-start.27 = (f32[2,2,64,128]{3,2,1,0:T(8,128)S(1)}, f32[2,2,64,128]{3,2,1,0:T(8,128)S(1)}, u32[]{:S(2)}, u32[]{:S(2)}) collective-permute-start(f32[2,2,64,128]{3,2,1,0:T(8,128)S(1)} %pad_maximum_fusion.18), channel_id=1, source_target_pairs={{0,4},{1,5},{2,6},{3,7},{4,0},{5,1},{6,2},{7,3},{8,12},{9,13},{10,... | collective-permute-start | bytes 393224 | tf_op jit(solution)/shard_map/ppermute | solution.py:28
  87.5 7.6 %collective-permute-start.26 = (f32[2,2,64,128]{3,2,1,0:T(8,128)S(1)}, f32[2,2,64,128]{3,2,1,0:T(8,128)S(1)}, u32[]{:S(2)}, u32[]{:S(2)}) collective-permute-start(f32[2,2,64,128]{3,2,1,0:T(8,128)S(1)} %pad_maximum_fusion.17), channel_id=1, source_target_pairs={{0,2},{1,3},{2,0},{3,1},{4,6},{5,7},{6,4},{7,5},{8,10},{9,11},{10,... | collective-permute-start | bytes 393224 | tf_op jit(solution)/shard_map/ppermute | solution.py:28
  99.4 1.8 collective-permute-start.29
  101.2 5.3 %collective-permute-start.30 = (f32[192,128]{1,0:T(8,128)S(1)}, f32[192,128]{1,0:T(8,128)S(1)}, u32[]{:S(2)}, u32[]{:S(2)}) collective-permute-start(f32[192,128]{1,0:T(8,128)S(1)} %get-tuple-element.115), channel_id=1, source_target_pairs={{0,2},{1,3},{2,0},{3,1},{4,6},{5,7},{6,4},{7,5},{8,10},{9,11},{10,... | collective-permute-start | bytes 294920 | tf_op jit(solution)/shard_map/ppermute | solution.py:28
  102.1 5.8 %collective-permute-start.31 = (f32[192,128]{1,0:T(8,128)S(1)}, f32[192,128]{1,0:T(8,128)S(1)}, u32[]{:S(2)}, u32[]{:S(2)}) collective-permute-start(f32[192,128]{1,0:T(8,128)S(1)} %get-tuple-element.117), channel_id=1, source_target_pairs={{0,4},{1,5},{2,6},{3,7},{4,0},{5,1},{6,2},{7,3},{8,12},{9,13},{10,... | collective-permute-start | bytes 294920 | tf_op jit(solution)/shard_map/ppermute | solution.py:28
  103.7 5.5 %collective-permute-start.32 = (f32[192,128]{1,0:T(8,128)S(1)}, f32[192,128]{1,0:T(8,128)S(1)}, u32[]{:S(2)}, u32[]{:S(2)}) collective-permute-start(f32[192,128]{1,0:T(8,128)S(1)} %get-tuple-element.116), channel_id=1, source_target_pairs={{0,6},{1,7},{2,4},{3,5},{4,2},{5,3},{6,0},{7,1},{8,14},{9,15},{10,... | collective-permute-start | bytes 294920 | tf_op jit(solution)/shard_map/ppermute | solution.py:28
  109.2 4.7 %collective-permute-start.33 = (f32[4,48,128]{2,1,0:T(8,128)S(1)}, f32[4,48,128]{2,1,0:T(8,128)S(1)}, u32[]{:S(2)}, u32[]{:S(2)}) collective-permute-start(f32[4,48,128]{2,1,0:T(8,128)S(1)} %bitcast.107), channel_id=1, source_target_pairs={{0,8},{8,0},{16,24},{24,16},{1,9},{9,1},{17,25},{25,17},{2,10},{10... | collective-permute-start | bytes 294920 | tf_op jit(solution)/shard_map/ppermute | solution.py:28
  114.0 6.5 %collective-permute-start.34 = (f32[4,48,128]{2,1,0:T(8,128)S(1)}, f32[4,48,128]{2,1,0:T(8,128)S(1)}, u32[]{:S(2)}, u32[]{:S(2)}) collective-permute-start(f32[4,48,128]{2,1,0:T(8,128)S(1)} %bitcast_add_fusion.1), channel_id=1, source_target_pairs={{0,24},{8,16},{16,8},{24,0},{1,25},{9,17},{17,9},{25,1},{2,26},{10... | collective-permute-start | bytes 294920 | tf_op jit(solution)/shard_map/ppermute | solution.py:28
  120.5 4.7 %collective-permute-start.35 = (f32[192,128]{1,0:T(8,128)S(1)}, f32[192,128]{1,0:T(8,128)S(1)}, u32[]{:S(2)}, u32[]{:S(2)}) collective-permute-start(f32[192,128]{1,0:T(8,128)S(1)} %fusion.12), channel_id=1, source_target_pairs={{0,2},{1,3},{2,0},{3,1},{4,6},{5,7},{6,4},{7,5},{8,10},{9,11},{10,... | collective-permute-start | bytes 294920 | tf_op jit(solution)/shard_map/ppermute | solution.py:28
  121.5 4.6 %collective-permute-start.36 = (f32[192,128]{1,0:T(8,128)S(1)}, f32[192,128]{1,0:T(8,128)S(1)}, u32[]{:S(2)}, u32[]{:S(2)}) collective-permute-start(f32[192,128]{1,0:T(8,128)S(1)} %fusion.12), channel_id=1, source_target_pairs={{0,4},{1,5},{2,6},{3,7},{4,0},{5,1},{6,2},{7,3},{8,12},{9,13},{10,... | collective-permute-start | bytes 294920 | tf_op jit(solution)/shard_map/ppermute | solution.py:28
  122.7 5.5 %collective-permute-start.37 = (f32[192,128]{1,0:T(8,128)S(1)}, f32[192,128]{1,0:T(8,128)S(1)}, u32[]{:S(2)}, u32[]{:S(2)}) collective-permute-start(f32[192,128]{1,0:T(8,128)S(1)} %fusion.12), channel_id=1, source_target_pairs={{0,6},{1,7},{2,4},{3,5},{4,2},{5,3},{6,0},{7,1},{8,14},{9,15},{10,... | collective-permute-start | bytes 294920 | tf_op jit(solution)/shard_map/ppermute | solution.py:28
  128.2 1.8 collective-permute-start.38
  136.5 8.4 %collective-permute-start.41 = (f32[2,2,64,128]{3,2,1,0:T(8,128)S(1)}, f32[2,2,64,128]{3,2,1,0:T(8,128)S(1)}, u32[]{:S(2)}, u32[]{:S(2)}) collective-permute-start(f32[2,2,64,128]{3,2,1,0:T(8,128)S(1)} %pad_maximum_fusion.22), channel_id=1, source_target_pairs={{0,4},{1,5},{2,6},{3,7},{4,0},{5,1},{6,2},{7,3},{8,12},{9,13},{10,... | collective-permute-start | bytes 393224 | tf_op jit(solution)/shard_map/ppermute | solution.py:28
  137.3 7.6 %collective-permute-start.42 = (f32[2,2,64,128]{3,2,1,0:T(8,128)S(1)}, f32[2,2,64,128]{3,2,1,0:T(8,128)S(1)}, u32[]{:S(2)}, u32[]{:S(2)}) collective-permute-start(f32[2,2,64,128]{3,2,1,0:T(8,128)S(1)} %pad_maximum_fusion.23), channel_id=1, source_target_pairs={{0,6},{1,7},{2,4},{3,5},{4,2},{5,3},{6,0},{7,1},{8,14},{9,15},{10,... | collective-permute-start | bytes 393224 | tf_op jit(solution)/shard_map/ppermute | solution.py:28
  139.2 7.0 %collective-permute-start.40 = (f32[2,2,64,128]{3,2,1,0:T(8,128)S(1)}, f32[2,2,64,128]{3,2,1,0:T(8,128)S(1)}, u32[]{:S(2)}, u32[]{:S(2)}) collective-permute-start(f32[2,2,64,128]{3,2,1,0:T(8,128)S(1)} %pad_maximum_fusion.21), channel_id=1, source_target_pairs={{0,2},{1,3},{2,0},{3,1},{4,6},{5,7},{6,4},{7,5},{8,10},{9,11},{10,... | collective-permute-start | bytes 393224 | tf_op jit(solution)/shard_map/ppermute | solution.py:28
  144.9 2.2 collective-permute-start.50
  146.9 7.5 %collective-permute-start.43 = (f32[8,64,128]{2,1,0:T(8,128)S(1)}, f32[8,64,128]{2,1,0:T(8,128)S(1)}, u32[]{:S(2)}, u32[]{:S(2)}) collective-permute-start(f32[8,64,128]{2,1,0:T(8,128)S(1)} %get-tuple-element.87), channel_id=1, source_target_pairs={{0,8},{8,0},{16,24},{24,16},{1,9},{9,1},{17,25},{25,17},{2,10},{10... | collective-permute-start | bytes 786440 | tf_op jit(solution)/shard_map/ppermute | solution.py:28
  147.1 10.8 %collective-permute-start.53 = (f32[2,2,64,128]{3,2,1,0:T(8,128)S(1)}, f32[2,2,64,128]{3,2,1,0:T(8,128)S(1)}, u32[]{:S(2)}, u32[]{:S(2)}) collective-permute-start(f32[2,2,64,128]{3,2,1,0:T(8,128)S(1)} %pad_maximum_fusion.31), channel_id=1, source_target_pairs={{0,6},{1,7},{2,4},{3,5},{4,2},{5,3},{6,0},{7,1},{8,14},{9,15},{10,... | collective-permute-start | bytes 393224 | tf_op jit(solution)/shard_map/ppermute | solution.py:28
  154.5 8.9 %collective-permute-start.44 = (f32[8,64,128]{2,1,0:T(8,128)S(1)}, f32[8,64,128]{2,1,0:T(8,128)S(1)}, u32[]{:S(2)}, u32[]{:S(2)}) collective-permute-start(f32[8,64,128]{2,1,0:T(8,128)S(1)} %add.133), channel_id=1, source_target_pairs={{0,24},{8,16},{16,8},{24,0},{1,25},{9,17},{17,9},{25,1},{2,26},{10... | collective-permute-start | bytes 786440 | tf_op jit(solution)/shard_map/ppermute | solution.py:28
  155.9 5.0 %collective-permute-start.52 = (f32[2,2,64,128]{3,2,1,0:T(8,128)S(1)}, f32[2,2,64,128]{3,2,1,0:T(8,128)S(1)}, u32[]{:S(2)}, u32[]{:S(2)}) collective-permute-start(f32[2,2,64,128]{3,2,1,0:T(8,128)S(1)} %pad_maximum_fusion.30), channel_id=1, source_target_pairs={{0,4},{1,5},{2,6},{3,7},{4,0},{5,1},{6,2},{7,3},{8,12},{9,13},{10,... | collective-permute-start | bytes 393224 | tf_op jit(solution)/shard_map/ppermute | solution.py:28
  156.6 5.0 %collective-permute-start.51 = (f32[2,2,64,128]{3,2,1,0:T(8,128)S(1)}, f32[2,2,64,128]{3,2,1,0:T(8,128)S(1)}, u32[]{:S(2)}, u32[]{:S(2)}) collective-permute-start(f32[2,2,64,128]{3,2,1,0:T(8,128)S(1)} %pad_maximum_fusion.29), channel_id=1, source_target_pairs={{0,2},{1,3},{2,0},{3,1},{4,6},{5,7},{6,4},{7,5},{8,10},{9,11},{10,... | collective-permute-start | bytes 393224 | tf_op jit(solution)/shard_map/ppermute | solution.py:28
  162.6 9.1 %collective-permute-start.54 = (f32[8,64,128]{2,1,0:T(8,128)S(1)}, f32[8,64,128]{2,1,0:T(8,128)S(1)}, u32[]{:S(2)}, u32[]{:S(2)}) collective-permute-start(f32[8,64,128]{2,1,0:T(8,128)S(1)} %get-tuple-element.95), channel_id=1, source_target_pairs={{0,8},{8,0},{16,24},{24,16},{1,9},{9,1},{17,25},{25,17},{2,10},{10... | collective-permute-start | bytes 786440 | tf_op jit(solution)/shard_map/ppermute | solution.py:28
  163.4 12.9 %collective-permute-start.45 = (f32[8,64,128]{2,1,0:T(8,128)S(1)}, f32[8,64,128]{2,1,0:T(8,128)S(1)}, u32[]{:S(2)}, u32[]{:S(2)}) collective-permute-start(f32[8,64,128]{2,1,0:T(8,128)S(1)} %add.134.mine), channel_id=1, source_target_pairs={{0,8},{8,0},{16,24},{24,16},{1,9},{9,1},{17,25},{25,17},{2,10},{10... | collective-permute-start | bytes 786440 | tf_op jit(solution)/shard_map/ppermute | solution.py:28
  171.8 9.0 %collective-permute-start.55 = (f32[8,64,128]{2,1,0:T(8,128)S(1)}, f32[8,64,128]{2,1,0:T(8,128)S(1)}, u32[]{:S(2)}, u32[]{:S(2)}) collective-permute-start(f32[8,64,128]{2,1,0:T(8,128)S(1)} %add.135), channel_id=1, source_target_pairs={{0,24},{8,16},{16,8},{24,0},{1,25},{9,17},{17,9},{25,1},{2,26},{10... | collective-permute-start | bytes 786440 | tf_op jit(solution)/shard_map/ppermute | solution.py:28
  177.0 5.8 %collective-permute-start.46 = (f32[4,2,64,128]{3,2,1,0:T(8,128)S(1)}, f32[4,2,64,128]{3,2,1,0:T(8,128)S(1)}, u32[]{:S(2)}, u32[]{:S(2)}) collective-permute-start(f32[4,2,64,128]{3,2,1,0:T(8,128)S(1)} %get-tuple-element.89), channel_id=1, source_target_pairs={{0,1},{1,0},{2,3},{3,2},{4,5},{5,4},{6,7},{7,6},{8,9},{9,8},{10,11... | collective-permute-start | bytes 786440 | tf_op jit(solution)/shard_map/ppermute | solution.py:28
  180.8 6.4 %collective-permute-start.56 = (f32[8,64,128]{2,1,0:T(8,128)S(1)}, f32[8,64,128]{2,1,0:T(8,128)S(1)}, u32[]{:S(2)}, u32[]{:S(2)}) collective-permute-start(f32[8,64,128]{2,1,0:T(8,128)S(1)} %add.136.mine), channel_id=1, source_target_pairs={{0,8},{8,0},{16,24},{24,16},{1,9},{9,1},{17,25},{25,17},{2,10},{10... | collective-permute-start | bytes 786440 | tf_op jit(solution)/shard_map/ppermute | solution.py:28
  182.9 9.6 %collective-permute-start.49 = (f32[2,2,64,128]{3,2,1,0:T(8,128)S(1)}, f32[2,2,64,128]{3,2,1,0:T(8,128)S(1)}, u32[]{:S(2)}, u32[]{:S(2)}) collective-permute-start(f32[2,2,64,128]{3,2,1,0:T(8,128)S(1)} %pad_maximum_fusion.27), channel_id=1, source_target_pairs={{0,6},{1,7},{2,4},{3,5},{4,2},{5,3},{6,0},{7,1},{8,14},{9,15},{10,... | collective-permute-start | bytes 393224 | tf_op jit(solution)/shard_map/ppermute | solution.py:28
  184.4 9.0 %collective-permute-start.48 = (f32[2,2,64,128]{3,2,1,0:T(8,128)S(1)}, f32[2,2,64,128]{3,2,1,0:T(8,128)S(1)}, u32[]{:S(2)}, u32[]{:S(2)}) collective-permute-start(f32[2,2,64,128]{3,2,1,0:T(8,128)S(1)} %pad_maximum_fusion.26), channel_id=1, source_target_pairs={{0,4},{1,5},{2,6},{3,7},{4,0},{5,1},{6,2},{7,3},{8,12},{9,13},{10,... | collective-permute-start | bytes 393224 | tf_op jit(solution)/shard_map/ppermute | solution.py:28
  188.1 6.4 %collective-permute-start.47 = (f32[2,2,64,128]{3,2,1,0:T(8,128)S(1)}, f32[2,2,64,128]{3,2,1,0:T(8,128)S(1)}, u32[]{:S(2)}, u32[]{:S(2)}) collective-permute-start(f32[2,2,64,128]{3,2,1,0:T(8,128)S(1)} %pad_maximum_fusion.25), channel_id=1, source_target_pairs={{0,2},{1,3},{2,0},{3,1},{4,6},{5,7},{6,4},{7,5},{8,10},{9,11},{10,... | collective-permute-start | bytes 393224 | tf_op jit(solution)/shard_map/ppermute | solution.py:28
  189.6 8.4 %collective-permute-start.60 = (f32[2,2,64,128]{3,2,1,0:T(8,128)S(1)}, f32[2,2,64,128]{3,2,1,0:T(8,128)S(1)}, u32[]{:S(2)}, u32[]{:S(2)}) collective-permute-start(f32[2,2,64,128]{3,2,1,0:T(8,128)S(1)} %pad_maximum_fusion.35), channel_id=1, source_target_pairs={{0,6},{1,7},{2,4},{3,5},{4,2},{5,3},{6,0},{7,1},{8,14},{9,15},{10,... | collective-permute-start | bytes 393224 | tf_op jit(solution)/shard_map/ppermute | solution.py:28
  191.6 8.1 %collective-permute-start.59 = (f32[2,2,64,128]{3,2,1,0:T(8,128)S(1)}, f32[2,2,64,128]{3,2,1,0:T(8,128)S(1)}, u32[]{:S(2)}, u32[]{:S(2)}) collective-permute-start(f32[2,2,64,128]{3,2,1,0:T(8,128)S(1)} %pad_maximum_fusion.34), channel_id=1, source_target_pairs={{0,4},{1,5},{2,6},{3,7},{4,0},{5,1},{6,2},{7,3},{8,12},{9,13},{10,... | collective-permute-start | bytes 393224 | tf_op jit(solution)/shard_map/ppermute | solution.py:28
  192.4 7.3 %collective-permute-start.58 = (f32[2,2,64,128]{3,2,1,0:T(8,128)S(1)}, f32[2,2,64,128]{3,2,1,0:T(8,128)S(1)}, u32[]{:S(2)}, u32[]{:S(2)}) collective-permute-start(f32[2,2,64,128]{3,2,1,0:T(8,128)S(1)} %pad_maximum_fusion.33), channel_id=1, source_target_pairs={{0,2},{1,3},{2,0},{3,1},{4,6},{5,7},{6,4},{7,5},{8,10},{9,11},{10,... | collective-permute-start | bytes 393224 | tf_op jit(solution)/shard_map/ppermute | solution.py:28
  203.9 1.8 collective-permute-start.61
  205.8 4.9 %collective-permute-start.62 = (f32[192,128]{1,0:T(8,128)S(1)}, f32[192,128]{1,0:T(8,128)S(1)}, u32[]{:S(2)}, u32[]{:S(2)}) collective-permute-start(f32[192,128]{1,0:T(8,128)S(1)} %get-tuple-element.112), channel_id=1, source_target_pairs={{0,2},{1,3},{2,0},{3,1},{4,6},{5,7},{6,4},{7,5},{8,10},{9,11},{10,... | collective-permute-start | bytes 294920 | tf_op jit(solution)/shard_map/ppermute | solution.py:28
  207.0 5.7 %collective-permute-start.63 = (f32[192,128]{1,0:T(8,128)S(1)}, f32[192,128]{1,0:T(8,128)S(1)}, u32[]{:S(2)}, u32[]{:S(2)}) collective-permute-start(f32[192,128]{1,0:T(8,128)S(1)} %get-tuple-element.114), channel_id=1, source_target_pairs={{0,4},{1,5},{2,6},{3,7},{4,0},{5,1},{6,2},{7,3},{8,12},{9,13},{10,... | collective-permute-start | bytes 294920 | tf_op jit(solution)/shard_map/ppermute | solution.py:28
  208.3 5.5 %collective-permute-start.64 = (f32[192,128]{1,0:T(8,128)S(1)}, f32[192,128]{1,0:T(8,128)S(1)}, u32[]{:S(2)}, u32[]{:S(2)}) collective-permute-start(f32[192,128]{1,0:T(8,128)S(1)} %get-tuple-element.113), channel_id=1, source_target_pairs={{0,6},{1,7},{2,4},{3,5},{4,2},{5,3},{6,0},{7,1},{8,14},{9,15},{10,... | collective-permute-start | bytes 294920 | tf_op jit(solution)/shard_map/ppermute | solution.py:28
  213.9 5.4 %collective-permute-start.65 = (f32[48,128]{1,0:T(8,128)S(1)}, f32[48,128]{1,0:T(8,128)S(1)}, u32[]{:S(2)}, u32[]{:S(2)}) collective-permute-start(f32[48,128]{1,0:T(8,128)S(1)} %get-tuple-element.182), channel_id=1, source_target_pairs={{0,8},{8,0},{16,24},{24,16},{1,9},{9,1},{17,25},{25,17},{2,10},{10... | collective-permute-start | bytes 73736 | tf_op jit(solution)/shard_map/ppermute | solution.py:28
  215.8 5.6 %collective-permute-start.66 = (f32[48,128]{1,0:T(8,128)S(1)}, f32[48,128]{1,0:T(8,128)S(1)}, u32[]{:S(2)}, u32[]{:S(2)}) collective-permute-start(f32[48,128]{1,0:T(8,128)S(1)} %get-tuple-element.184), channel_id=1, source_target_pairs={{0,24},{8,16},{16,8},{24,0},{1,25},{9,17},{17,9},{25,1},{2,26},{10... | collective-permute-start | bytes 73736 | tf_op jit(solution)/shard_map/ppermute | solution.py:28
  218.2 4.7 %collective-permute-start.67 = (f32[48,128]{1,0:T(8,128)S(1)}, f32[48,128]{1,0:T(8,128)S(1)}, u32[]{:S(2)}, u32[]{:S(2)}) collective-permute-start(f32[48,128]{1,0:T(8,128)S(1)} %get-tuple-element.183), channel_id=1, source_target_pairs={{0,16},{8,24},{16,0},{24,8},{1,17},{9,25},{17,1},{25,9},{2,18},{10... | collective-permute-start | bytes 73736 | tf_op jit(solution)/shard_map/ppermute | solution.py:28
  (10 other events, 110.1 us)

commit v9 on v8

--- a/solution.py
+++ b/solution.py
@@ -437,8 +437,6 @@
             if h + 1 < CHUNKS:
                 later = outgoing[(h + 1) * cores : (h + 2) * cores]
                 incoming = exchange([tie(x, incoming[2]) for x in later])
-            if h > 0:
-                got = tie(got, seconds[-1])
             half, second = phase_stages(keep + got)
             held_halves.append(half)
             seconds.append(second)

time: 224 us -> 224 us (level)
  no operation moved by 1% of the time
where the time goes in v9:
time: 224 us
  waiting for transfers between devices  99.2 us (44%)
  starting transfers between devices  76.3 us (34%)
  Pallas kernels  24 us (11%)
  local copies, waits for them, and re-layouts  15.1 us (7%)
  other arithmetic  5.81 us (3%)
    ppermute x68, waiting for transfers between devices, swap(): return lax.ppermute(x, axis, [(i, i ^ mask) for i in range(count)])  99.2 us
    ppermute x68, starting transfers between devices, swap(): return lax.ppermute(x, axis, [(i, i ^ mask) for i in range(count)])  76.3 us
    unnamed x15, local copies, waits for them, and re-layouts  9.94 us
    pallas_call x2, Pallas kernels, forward(): pl.pallas_call(functools.partial(forward_body, (vox, masks, rows, len(pie...  9.54 us
    pallas_call x2, Pallas kernels, gradient_parts(): pl.pallas_call(functools.partial(gradient_body, (vox, masks, rows, cores,...  8.41 us
  transfers between devices with their start and end apart: 68, of which 50 were waited for; matrix products, arithmetic and copies ran while one was open for 6% of the time, Pallas kernels for 3%

profile of v9, /device:TPU:0, one launch (start us, length us, event | category | flops | bytes accessed | tf_op | source)
XLA Modules:
  0.0 223.5 jit_solution(11162919557756598762)
XLA Ops:
  0.6 3.1 %collective-permute-start = (f32[48,128]{1,0:T(8,128)}, f32[48,128]{1,0:T(8,128)S(1)}, u32[]{:S(2)}, u32[]{:S(2)}) collective-permute-start(f32[48,128]{1,0:T(8,128)} %param.15), channel_id=1, source_target_pairs={{0,8},{8,0},{16,24},{24,16},{1,9},{9,1},{17,25},{25,17},{2,10},{10... | collective-permute-start | bytes 73736 | tf_op jit(solution)/shard_map/ppermute | solution.py:28
  3.7 2.5 %collective-permute-start.1 = (f32[48,128]{1,0:T(8,128)}, f32[48,128]{1,0:T(8,128)S(1)}, u32[]{:S(2)}, u32[]{:S(2)}) collective-permute-start(f32[48,128]{1,0:T(8,128)} %param.15), channel_id=1, source_target_pairs={{0,24},{8,16},{16,8},{24,0},{1,25},{9,17},{17,9},{25,1},{2,26},{10... | collective-permute-start | bytes 73736 | tf_op jit(solution)/shard_map/ppermute | solution.py:28
  11.4 1.6 collective-permute-start.4
  13.0 1.4 collective-permute-start.5
  15.0 2.8 %gather_fusion = f32[16,128,128]{2,1,0:T(8,128)S(1)} fusion(f32[64,128,128]{2,1,0:T(8,128)} %param.16, s32[1024]{0:T(1024)S(1)} %pad_clamp_fusion), kind=kCustom, calls=%fused_computation | custom fusion | bytes 2097216 | tf_op jit(solution)/shard_map/gather | solution.py:405
  20.1 4.6 %copy-done.1 = f32[1,2048,1536]{2,1,0:T(8,128)S(1)} copy-done((f32[1,2048,1536]{2,1,0:T(8,128)S(1)}, f32[1,2048,1536]{2,1,0:T(8,128)}, u32[]{:S(2)}) %copy-start.1) | copy-done | bytes 12582936
  24.7 4.8 %dose_and_warp.2 = (f32[4,2,64,128]{3,2,1,0:T(8,128)S(1)}, f32[4,2,64,128]{3,2,1,0:T(8,128)S(1)}, f32[4,2,64,128]{3,2,1,0:T(8,128)S(1)}, f32[4,2,64,128]{3,2,1,0:T(8,128)S(1)}) custom-call(s32[16]{0:T(128)S(1)} %get-tuple-element.101.source_ref, s32[16]{0:T(128)S(1)} %get-tuple-element.100.valid_ref, s32[2]{0:T(128)S(1)} %pad_add_fusion.me_ref, ...), custom_call_target="tpu_custom_call" | custom-call | flops 1 | bytes 1 | tf_op jit(solution)/shard_map/dose_and_warp/pallas_call | solution.py:113
  31.3 1.6 collective-permute-start.9
  35.0 4.6 %collective-permute-done.9.refs_2_ = f32[2,2,64,128]{3,2,1,0:T(8,128)S(1)} collective-permute-done((f32[2,2,64,128]{3,2,1,0:T(8,128)S(1)}, f32[2,2,64,128]{3,2,1,0:T(8,128)S(1)}, u32[]{:S(2)}, u32[]{:S(2)}) %collective-permute-start.9) | collective-permute-done | bytes 131104 | tf_op jit(solution)/shard_map/ppermute | solution.py:28
  44.5 2.2 collective-permute-start.17
  48.2 1.3 collective-permute-done.11
  49.5 1.8 collective-permute-start.12
  53.7 1.5 collective-permute-start.18
  55.2 4.5 %collective-permute-done.12 = f32[8,64,128]{2,1,0:T(8,128)S(1)} collective-permute-done((f32[8,64,128]{2,1,0:T(8,128)S(1)}, f32[8,64,128]{2,1,0:T(8,128)S(1)}, u32[]{:S(2)}, u32[]{:S(2)}) %collective-permute-start.12) | collective-permute-done | bytes 262176 | tf_op jit(solution)/shard_map/ppermute | solution.py:28
  59.7 2.7 %collective-permute-start.13 = (f32[8,64,128]{2,1,0:T(8,128)S(1)}, f32[8,64,128]{2,1,0:T(8,128)S(1)}, u32[]{:S(2)}, u32[]{:S(2)}) collective-permute-start(f32[8,64,128]{2,1,0:T(8,128)S(1)} %add.123.mine), channel_id=1, source_target_pairs={{0,8},{8,0},{16,24},{24,16},{1,9},{9,1},{17,25},{25,17},{2,10},{10... | collective-permute-start | bytes 786440 | tf_op jit(solution)/shard_map/ppermute | solution.py:28
  62.5 1.6 collective-permute-done.18
  64.2 1.8 collective-permute-start.23
  66.1 4.6 %copy-done.2 = f32[1,2048,1536]{2,1,0:T(8,128)S(1)} copy-done((f32[1,2048,1536]{2,1,0:T(8,128)S(1)}, f32[1,2048,1536]{2,1,0:T(8,128)}, u32[]{:S(2)}) %copy-start.2) | copy-done | bytes 12582936
  71.6 4.1 %collective-permute-done.23 = f32[8,64,128]{2,1,0:T(8,128)S(1)} collective-permute-done((f32[8,64,128]{2,1,0:T(8,128)S(1)}, f32[8,64,128]{2,1,0:T(8,128)S(1)}, u32[]{:S(2)}, u32[]{:S(2)}) %collective-permute-start.23) | collective-permute-done | bytes 262176 | tf_op jit(solution)/shard_map/ppermute | solution.py:28
  76.9 2.1 collective-permute-start.22
  79.4 2.8 %collective-permute-done.24.other = f32[8,64,128]{2,1,0:T(8,128)S(1)} collective-permute-done((f32[8,64,128]{2,1,0:T(8,128)S(1)}, f32[8,64,128]{2,1,0:T(8,128)S(1)}, u32[]{:S(2)}, u32[]{:S(2)}) %collective-permute-start.24) | collective-permute-done | bytes 262176 | tf_op jit(solution)/shard_map/ppermute | solution.py:28
  84.7 2.3 %collective-permute-start.28 = (f32[2,2,64,128]{3,2,1,0:T(8,128)S(1)}, f32[2,2,64,128]{3,2,1,0:T(8,128)S(1)}, u32[]{:S(2)}, u32[]{:S(2)}) collective-permute-start(f32[2,2,64,128]{3,2,1,0:T(8,128)S(1)} %pad_maximum_fusion.19), channel_id=1, source_target_pairs={{0,6},{1,7},{2,4},{3,5},{4,2},{5,3},{6,0},{7,1},{8,14},{9,15},{10,... | collective-permute-start | bytes 393224 | tf_op jit(solution)/shard_map/ppermute | solution.py:28
  89.5 3.8 %collective-permute-done.28.refs_7_ = f32[2,2,64,128]{3,2,1,0:T(8,128)S(1)} collective-permute-done((f32[2,2,64,128]{3,2,1,0:T(8,128)S(1)}, f32[2,2,64,128]{3,2,1,0:T(8,128)S(1)}, u32[]{:S(2)}, u32[]{:S(2)}) %collective-permute-start.28) | collective-permute-done | bytes 131104 | tf_op jit(solution)/shard_map/ppermute | solution.py:28
  93.4 1.7 collective-permute-done.27.refs_6_
  95.1 4.2 %warp_back_and_gradient.2 = (f32[4,192,128]{2,1,0:T(8,128)S(1)}, f32[4,192,128]{2,1,0:T(8,128)S(1)}) custom-call(s32[16]{0:T(128)S(1)} %get-tuple-element.101.source_ref, s32[16]{0:T(128)S(1)} %get-tuple-element.100.valid_ref, s32[2]{0:T(128)S(1)} %pad_add_fusion.me_ref, f32[2048,1536]{1,0:T(8,128)S(1)} %bitcast.98, f32[16,128,128]{2,1,0:T(8,128)S(1)} %gather_fusion, ...), custom_call_target="tpu_custom_call" | custom-call | flops 1 | bytes 1 | tf_op jit(solution)/shard_map/warp_back_and_gradient/pallas_call | solution.py:186
  99.4 1.7 collective-permute-done.29
  102.1 1.6 collective-permute-start.31
  104.8 1.7 collective-permute-done.30
  106.5 1.4 collective-permute-done.31
  107.9 1.3 collective-permute-done.32
  110.3 3.7 %collective-permute-done.33 = f32[4,48,128]{2,1,0:T(8,128)S(1)} collective-permute-done((f32[4,48,128]{2,1,0:T(8,128)S(1)}, f32[4,48,128]{2,1,0:T(8,128)S(1)}, u32[]{:S(2)}, u32[]{:S(2)}) %collective-permute-start.33) | collective-permute-done | bytes 98336 | tf_op jit(solution)/shard_map/ppermute | solution.py:28
  114.0 1.5 collective-permute-start.34
  115.4 5.0 %collective-permute-done.34 = f32[4,48,128]{2,1,0:T(8,128)S(1)} collective-permute-done((f32[4,48,128]{2,1,0:T(8,128)S(1)}, f32[4,48,128]{2,1,0:T(8,128)S(1)}, u32[]{:S(2)}, u32[]{:S(2)}) %collective-permute-start.34) | collective-permute-done | bytes 98336 | tf_op jit(solution)/shard_map/ppermute | solution.py:28
  122.7 1.4 collective-permute-start.37
  126.1 2.1 collective-permute-done.37
  128.3 1.7 collective-permute-done.38.refs_1_
  130.0 4.8 %dose_and_warp.3 = (f32[4,2,64,128]{3,2,1,0:T(8,128)S(1)}, f32[4,2,64,128]{3,2,1,0:T(8,128)S(1)}, f32[4,2,64,128]{3,2,1,0:T(8,128)S(1)}, f32[4,2,64,128]{3,2,1,0:T(8,128)S(1)}) custom-call(s32[16]{0:T(128)S(1)} %get-tuple-element.101.source_ref, s32[16]{0:T(128)S(1)} %get-tuple-element.100.valid_ref, s32[2]{0:T(128)S(1)} %pad_add_fusion.me_ref, ...), custom_call_target="tpu_custom_call" | custom-call | flops 1 | bytes 1 | tf_op jit(solution)/shard_map/dose_and_warp/pallas_call | solution.py:113
  135.0 1.4 collective-permute-done.39
  137.3 1.8 collective-permute-start.42
  140.2 4.7 %collective-permute-done.41.refs_2_ = f32[2,2,64,128]{3,2,1,0:T(8,128)S(1)} collective-permute-done((f32[2,2,64,128]{3,2,1,0:T(8,128)S(1)}, f32[2,2,64,128]{3,2,1,0:T(8,128)S(1)}, u32[]{:S(2)}, u32[]{:S(2)}) %collective-permute-start.41) | collective-permute-done | bytes 131104 | tf_op jit(solution)/shard_map/ppermute | solution.py:28
  144.9 1.3 collective-permute-done.40.refs_1_
  147.1 1.5 collective-permute-start.53
  148.5 5.9 %collective-permute-done.43 = f32[8,64,128]{2,1,0:T(8,128)S(1)} collective-permute-done((f32[8,64,128]{2,1,0:T(8,128)S(1)}, f32[8,64,128]{2,1,0:T(8,128)S(1)}, u32[]{:S(2)}, u32[]{:S(2)}) %collective-permute-start.43) | collective-permute-done | bytes 262176 | tf_op jit(solution)/shard_map/ppermute | solution.py:28
  154.5 1.4 collective-permute-start.44
  157.9 3.1 %collective-permute-done.52.refs_2_ = f32[2,2,64,128]{3,2,1,0:T(8,128)S(1)} collective-permute-done((f32[2,2,64,128]{3,2,1,0:T(8,128)S(1)}, f32[2,2,64,128]{3,2,1,0:T(8,128)S(1)}, u32[]{:S(2)}, u32[]{:S(2)}) %collective-permute-start.52) | collective-permute-done | bytes 131104 | tf_op jit(solution)/shard_map/ppermute | solution.py:28
  163.4 3.9 %collective-permute-start.45 = (f32[8,64,128]{2,1,0:T(8,128)S(1)}, f32[8,64,128]{2,1,0:T(8,128)S(1)}, u32[]{:S(2)}, u32[]{:S(2)}) collective-permute-start(f32[8,64,128]{2,1,0:T(8,128)S(1)} %add.134.mine), channel_id=1, source_target_pairs={{0,8},{8,0},{16,24},{24,16},{1,9},{9,1},{17,25},{25,17},{2,10},{10... | collective-permute-start | bytes 786440 | tf_op jit(solution)/shard_map/ppermute | solution.py:28
  167.4 4.4 %collective-permute-done.54 = f32[8,64,128]{2,1,0:T(8,128)S(1)} collective-permute-done((f32[8,64,128]{2,1,0:T(8,128)S(1)}, f32[8,64,128]{2,1,0:T(8,128)S(1)}, u32[]{:S(2)}, u32[]{:S(2)}) %collective-permute-start.54) | collective-permute-done | bytes 262176 | tf_op jit(solution)/shard_map/ppermute | solution.py:28
  171.8 1.7 collective-permute-start.55
  173.5 2.9 %collective-permute-done.45.other = f32[8,64,128]{2,1,0:T(8,128)S(1)} collective-permute-done((f32[8,64,128]{2,1,0:T(8,128)S(1)}, f32[8,64,128]{2,1,0:T(8,128)S(1)}, u32[]{:S(2)}, u32[]{:S(2)}) %collective-permute-start.45) | collective-permute-done | bytes 262176 | tf_op jit(solution)/shard_map/ppermute | solution.py:28
  177.1 3.7 %collective-permute-done.55 = f32[8,64,128]{2,1,0:T(8,128)S(1)} collective-permute-done((f32[8,64,128]{2,1,0:T(8,128)S(1)}, f32[8,64,128]{2,1,0:T(8,128)S(1)}, u32[]{:S(2)}, u32[]{:S(2)}) %collective-permute-start.55) | collective-permute-done | bytes 262176 | tf_op jit(solution)/shard_map/ppermute | solution.py:28
  180.8 2.0 collective-permute-start.56
  182.9 1.6 collective-permute-start.49
  185.7 1.6 collective-permute-done.56.other
  189.6 1.9 collective-permute-start.60
  194.4 3.5 %collective-permute-done.60.refs_7_ = f32[2,2,64,128]{3,2,1,0:T(8,128)S(1)} collective-permute-done((f32[2,2,64,128]{3,2,1,0:T(8,128)S(1)}, f32[2,2,64,128]{3,2,1,0:T(8,128)S(1)}, u32[]{:S(2)}, u32[]{:S(2)}) %collective-permute-start.60) | collective-permute-done | bytes 131104 | tf_op jit(solution)/shard_map/ppermute | solution.py:28
  198.0 1.7 collective-permute-done.59.refs_6_
  199.7 4.2 %warp_back_and_gradient.3 = (f32[4,192,128]{2,1,0:T(8,128)S(1)}, f32[4,192,128]{2,1,0:T(8,128)S(1)}) custom-call(s32[16]{0:T(128)S(1)} %get-tuple-element.101.source_ref, s32[16]{0:T(128)S(1)} %get-tuple-element.100.valid_ref, s32[2]{0:T(128)S(1)} %pad_add_fusion.me_ref, f32[2048,1536]{1,0:T(8,128)S(1)} %bitcast.100, f32[16,128,128]{2,1,0:T(8,128)S(1)} %gather_fusion, ...), custom_call_target="tpu_custom_call" | custom-call | flops 1 | bytes 1 | tf_op jit(solution)/shard_map/warp_back_and_gradient/pallas_call | solution.py:186
  204.0 1.7 collective-permute-done.61
  209.4 1.3 collective-permute-done.62
  210.7 2.0 collective-permute-done.63
  213.9 1.9 collective-permute-start.65
  215.8 2.4 %collective-permute-start.66 = (f32[48,128]{1,0:T(8,128)S(1)}, f32[48,128]{1,0:T(8,128)S(1)}, u32[]{:S(2)}, u32[]{:S(2)}) collective-permute-start(f32[48,128]{1,0:T(8,128)S(1)} %get-tuple-element.180), channel_id=1, source_target_pairs={{0,24},{8,16},{16,8},{24,0},{1,25},{9,17},{17,9},{25,1},{2,26},{10... | collective-permute-start | bytes 73736 | tf_op jit(solution)/shard_map/ppermute | solution.py:28
  219.3 2.1 collective-permute-done.66
  221.4 1.5 collective-permute-done.67
  (204 shorter events, 57.0 us)
Async XLA Ops:
  0.6 9.5 %collective-permute-start = (f32[48,128]{1,0:T(8,128)}, f32[48,128]{1,0:T(8,128)S(1)}, u32[]{:S(2)}, u32[]{:S(2)}) collective-permute-start(f32[48,128]{1,0:T(8,128)} %param.15), channel_id=1, source_target_pairs={{0,8},{8,0},{16,24},{24,16},{1,9},{9,1},{17,25},{25,17},{2,10},{10... | collective-permute-start | bytes 73736 | tf_op jit(solution)/shard_map/ppermute | solution.py:28
  3.7 6.4 %collective-permute-start.1 = (f32[48,128]{1,0:T(8,128)}, f32[48,128]{1,0:T(8,128)S(1)}, u32[]{:S(2)}, u32[]{:S(2)}) collective-permute-start(f32[48,128]{1,0:T(8,128)} %param.15), channel_id=1, source_target_pairs={{0,24},{8,16},{16,8},{24,0},{1,25},{9,17},{17,9},{25,1},{2,26},{10... | collective-permute-start | bytes 73736 | tf_op jit(solution)/shard_map/ppermute | solution.py:28
  6.2 5.2 %collective-permute-start.2 = (f32[48,128]{1,0:T(8,128)}, f32[48,128]{1,0:T(8,128)S(1)}, u32[]{:S(2)}, u32[]{:S(2)}) collective-permute-start(f32[48,128]{1,0:T(8,128)} %param.15), channel_id=1, source_target_pairs={{0,16},{8,24},{16,0},{24,8},{1,17},{9,25},{17,1},{25,9},{2,18},{10... | collective-permute-start | bytes 73736 | tf_op jit(solution)/shard_map/ppermute | solution.py:28
  11.4 6.4 %collective-permute-start.4 = (f32[208,128]{1,0:T(8,128)S(1)}, f32[208,128]{1,0:T(8,128)S(1)}, u32[]{:S(2)}, u32[]{:S(2)}) collective-permute-start(f32[208,128]{1,0:T(8,128)S(1)} %constant_dynamic-update-slice_fusion.4), channel_id=1, source_target_pairs={{0,4},{1,5},{2,6},{3,7},{4,0},{5,1},{6,2},{7,3},{8,12},{9,13},{10,... | collective-permute-start | bytes 319496 | tf_op jit(solution)/shard_map/ppermute | solution.py:28
  13.0 5.6 %collective-permute-start.5 = (f32[208,128]{1,0:T(8,128)S(1)}, f32[208,128]{1,0:T(8,128)S(1)}, u32[]{:S(2)}, u32[]{:S(2)}) collective-permute-start(f32[208,128]{1,0:T(8,128)S(1)} %constant_dynamic-update-slice_fusion.4), channel_id=1, source_target_pairs={{0,6},{1,7},{2,4},{3,5},{4,2},{5,3},{6,0},{7,1},{8,14},{9,15},{10,... | collective-permute-start | bytes 319496 | tf_op jit(solution)/shard_map/ppermute | solution.py:28
  14.4 4.7 %collective-permute-start.3 = (f32[208,128]{1,0:T(8,128)S(1)}, f32[208,128]{1,0:T(8,128)S(1)}, u32[]{:S(2)}, u32[]{:S(2)}) collective-permute-start(f32[208,128]{1,0:T(8,128)S(1)} %constant_dynamic-update-slice_fusion.4), channel_id=1, source_target_pairs={{0,2},{1,3},{2,0},{3,1},{4,6},{5,7},{6,4},{7,5},{8,10},{9,11},{10,... | collective-permute-start | bytes 319496 | tf_op jit(solution)/shard_map/ppermute | solution.py:28
  19.2 5.5 %collective-permute-start.6 = (f32[4,208,128]{2,1,0:T(8,128)S(1)}, f32[4,208,128]{2,1,0:T(8,128)S(1)}, u32[]{:S(2)}, u32[]{:S(2)}) collective-permute-start(f32[4,208,128]{2,1,0:T(8,128)S(1)} %get-tuple-element.107.refs_1_), channel_id=1, source_target_pairs={{0,1},{1,0},{2,3},{3,2},{4,5},{5,4},{6,7},{7,6},{8,9},{9,8},{10,11... | collective-permute-start | bytes 1277960 | tf_op jit(solution)/shard_map/ppermute | solution.py:28
  31.3 8.3 %collective-permute-start.9 = (f32[2,2,64,128]{3,2,1,0:T(8,128)S(1)}, f32[2,2,64,128]{3,2,1,0:T(8,128)S(1)}, u32[]{:S(2)}, u32[]{:S(2)}) collective-permute-start(f32[2,2,64,128]{3,2,1,0:T(8,128)S(1)} %pad_maximum_fusion.6), channel_id=1, source_target_pairs={{0,4},{1,5},{2,6},{3,7},{4,0},{5,1},{6,2},{7,3},{8,12},{9,13},{10,... | collective-permute-start | bytes 393224 | tf_op jit(solution)/shard_map/ppermute | solution.py:28
  32.9 7.4 %collective-permute-start.10 = (f32[2,2,64,128]{3,2,1,0:T(8,128)S(1)}, f32[2,2,64,128]{3,2,1,0:T(8,128)S(1)}, u32[]{:S(2)}, u32[]{:S(2)}) collective-permute-start(f32[2,2,64,128]{3,2,1,0:T(8,128)S(1)} %pad_maximum_fusion.7), channel_id=1, source_target_pairs={{0,6},{1,7},{2,4},{3,5},{4,2},{5,3},{6,0},{7,1},{8,14},{9,15},{10,... | collective-permute-start | bytes 393224 | tf_op jit(solution)/shard_map/ppermute | solution.py:28
  34.1 7.2 %collective-permute-start.8 = (f32[2,2,64,128]{3,2,1,0:T(8,128)S(1)}, f32[2,2,64,128]{3,2,1,0:T(8,128)S(1)}, u32[]{:S(2)}, u32[]{:S(2)}) collective-permute-start(f32[2,2,64,128]{3,2,1,0:T(8,128)S(1)} %pad_maximum_fusion.5), channel_id=1, source_target_pairs={{0,2},{1,3},{2,0},{3,1},{4,6},{5,7},{6,4},{7,5},{8,10},{9,11},{10,... | collective-permute-start | bytes 393224 | tf_op jit(solution)/shard_map/ppermute | solution.py:28
  39.6 4.8 %collective-permute-start.14 = (f32[4,2,64,128]{3,2,1,0:T(8,128)S(1)}, f32[4,2,64,128]{3,2,1,0:T(8,128)S(1)}, u32[]{:S(2)}, u32[]{:S(2)}) collective-permute-start(f32[4,2,64,128]{3,2,1,0:T(8,128)S(1)} %get-tuple-element.71), channel_id=1, source_target_pairs={{0,1},{1,0},{2,3},{3,2},{4,5},{5,4},{6,7},{7,6},{8,9},{9,8},{10,11... | collective-permute-start | bytes 786440 | tf_op jit(solution)/shard_map/ppermute | solution.py:28
  42.0 7.5 %collective-permute-start.11 = (f32[8,64,128]{2,1,0:T(8,128)S(1)}, f32[8,64,128]{2,1,0:T(8,128)S(1)}, u32[]{:S(2)}, u32[]{:S(2)}) collective-permute-start(f32[8,64,128]{2,1,0:T(8,128)S(1)} %get-tuple-element.66), channel_id=1, source_target_pairs={{0,8},{8,0},{16,24},{24,16},{1,9},{9,1},{17,25},{25,17},{2,10},{10... | collective-permute-start | bytes 786440 | tf_op jit(solution)/shard_map/ppermute | solution.py:28
  44.5 7.0 %collective-permute-start.17 = (f32[2,2,64,128]{3,2,1,0:T(8,128)S(1)}, f32[2,2,64,128]{3,2,1,0:T(8,128)S(1)}, u32[]{:S(2)}, u32[]{:S(2)}) collective-permute-start(f32[2,2,64,128]{3,2,1,0:T(8,128)S(1)} %pad_maximum_fusion.11), channel_id=1, source_target_pairs={{0,6},{1,7},{2,4},{3,5},{4,2},{5,3},{6,0},{7,1},{8,14},{9,15},{10,... | collective-permute-start | bytes 393224 | tf_op jit(solution)/shard_map/ppermute | solution.py:28
  46.7 5.9 %collective-permute-start.16 = (f32[2,2,64,128]{3,2,1,0:T(8,128)S(1)}, f32[2,2,64,128]{3,2,1,0:T(8,128)S(1)}, u32[]{:S(2)}, u32[]{:S(2)}) collective-permute-start(f32[2,2,64,128]{3,2,1,0:T(8,128)S(1)} %pad_maximum_fusion.10), channel_id=1, source_target_pairs={{0,4},{1,5},{2,6},{3,7},{4,0},{5,1},{6,2},{7,3},{8,12},{9,13},{10,... | collective-permute-start | bytes 393224 | tf_op jit(solution)/shard_map/ppermute | solution.py:28
  47.3 5.5 %collective-permute-start.15 = (f32[2,2,64,128]{3,2,1,0:T(8,128)S(1)}, f32[2,2,64,128]{3,2,1,0:T(8,128)S(1)}, u32[]{:S(2)}, u32[]{:S(2)}) collective-permute-start(f32[2,2,64,128]{3,2,1,0:T(8,128)S(1)} %pad_maximum_fusion.9), channel_id=1, source_target_pairs={{0,2},{1,3},{2,0},{3,1},{4,6},{5,7},{6,4},{7,5},{8,10},{9,11},{10,... | collective-permute-start | bytes 393224 | tf_op jit(solution)/shard_map/ppermute | solution.py:28
  49.5 10.2 %collective-permute-start.12 = (f32[8,64,128]{2,1,0:T(8,128)S(1)}, f32[8,64,128]{2,1,0:T(8,128)S(1)}, u32[]{:S(2)}, u32[]{:S(2)}) collective-permute-start(f32[8,64,128]{2,1,0:T(8,128)S(1)} %add.122), channel_id=1, source_target_pairs={{0,24},{8,16},{16,8},{24,0},{1,25},{9,17},{17,9},{25,1},{2,26},{10... | collective-permute-start | bytes 786440 | tf_op jit(solution)/shard_map/ppermute | solution.py:28
  53.7 10.5 %collective-permute-start.18 = (f32[8,64,128]{2,1,0:T(8,128)S(1)}, f32[8,64,128]{2,1,0:T(8,128)S(1)}, u32[]{:S(2)}, u32[]{:S(2)}) collective-permute-start(f32[8,64,128]{2,1,0:T(8,128)S(1)} %get-tuple-element.73), channel_id=1, source_target_pairs={{0,8},{8,0},{16,24},{24,16},{1,9},{9,1},{17,25},{25,17},{2,10},{10... | collective-permute-start | bytes 786440 | tf_op jit(solution)/shard_map/ppermute | solution.py:28
  59.7 10.9 %collective-permute-start.13 = (f32[8,64,128]{2,1,0:T(8,128)S(1)}, f32[8,64,128]{2,1,0:T(8,128)S(1)}, u32[]{:S(2)}, u32[]{:S(2)}) collective-permute-start(f32[8,64,128]{2,1,0:T(8,128)S(1)} %add.123.mine), channel_id=1, source_target_pairs={{0,8},{8,0},{16,24},{24,16},{1,9},{9,1},{17,25},{25,17},{2,10},{10... | collective-permute-start | bytes 786440 | tf_op jit(solution)/shard_map/ppermute | solution.py:28
  64.2 11.5 %collective-permute-start.23 = (f32[8,64,128]{2,1,0:T(8,128)S(1)}, f32[8,64,128]{2,1,0:T(8,128)S(1)}, u32[]{:S(2)}, u32[]{:S(2)}) collective-permute-start(f32[8,64,128]{2,1,0:T(8,128)S(1)} %add.124.x), channel_id=1, source_target_pairs={{0,24},{8,16},{16,8},{24,0},{1,25},{9,17},{17,9},{25,1},{2,26},{10... | collective-permute-start | bytes 786440 | tf_op jit(solution)/shard_map/ppermute | solution.py:28
  71.5 5.3 %collective-permute-start.19 = (f32[4,2,64,128]{3,2,1,0:T(8,128)S(1)}, f32[4,2,64,128]{3,2,1,0:T(8,128)S(1)}, u32[]{:S(2)}, u32[]{:S(2)}) collective-permute-start(f32[4,2,64,128]{3,2,1,0:T(8,128)S(1)} %get-tuple-element.75), channel_id=1, source_target_pairs={{0,1},{1,0},{2,3},{3,2},{4,5},{5,4},{6,7},{7,6},{8,9},{9,8},{10,11... | collective-permute-start | bytes 786440 | tf_op jit(solution)/shard_map/ppermute | solution.py:28
  75.8 6.4 %collective-permute-start.24 = (f32[8,64,128]{2,1,0:T(8,128)S(1)}, f32[8,64,128]{2,1,0:T(8,128)S(1)}, u32[]{:S(2)}, u32[]{:S(2)}) collective-permute-start(f32[8,64,128]{2,1,0:T(8,128)S(1)} %add.125.mine), channel_id=1, source_target_pairs={{0,8},{8,0},{16,24},{24,16},{1,9},{9,1},{17,25},{25,17},{2,10},{10... | collective-permute-start | bytes 786440 | tf_op jit(solution)/shard_map/ppermute | solution.py:28
  76.9 10.7 %collective-permute-start.22 = (f32[2,2,64,128]{3,2,1,0:T(8,128)S(1)}, f32[2,2,64,128]{3,2,1,0:T(8,128)S(1)}, u32[]{:S(2)}, u32[]{:S(2)}) collective-permute-start(f32[2,2,64,128]{3,2,1,0:T(8,128)S(1)} %pad_maximum_fusion.15), channel_id=1, source_target_pairs={{0,6},{1,7},{2,4},{3,5},{4,2},{5,3},{6,0},{7,1},{8,14},{9,15},{10,... | collective-permute-start | bytes 393224 | tf_op jit(solution)/shard_map/ppermute | solution.py:28
  78.9 9.5 %collective-permute-start.21 = (f32[2,2,64,128]{3,2,1,0:T(8,128)S(1)}, f32[2,2,64,128]{3,2,1,0:T(8,128)S(1)}, u32[]{:S(2)}, u32[]{:S(2)}) collective-permute-start(f32[2,2,64,128]{3,2,1,0:T(8,128)S(1)} %pad_maximum_fusion.14), channel_id=1, source_target_pairs={{0,4},{1,5},{2,6},{3,7},{4,0},{5,1},{6,2},{7,3},{8,12},{9,13},{10,... | collective-permute-start | bytes 393224 | tf_op jit(solution)/shard_map/ppermute | solution.py:28
  83.2 6.4 %collective-permute-start.20 = (f32[2,2,64,128]{3,2,1,0:T(8,128)S(1)}, f32[2,2,64,128]{3,2,1,0:T(8,128)S(1)}, u32[]{:S(2)}, u32[]{:S(2)}) collective-permute-start(f32[2,2,64,128]{3,2,1,0:T(8,128)S(1)} %pad_maximum_fusion.13), channel_id=1, source_target_pairs={{0,2},{1,3},{2,0},{3,1},{4,6},{5,7},{6,4},{7,5},{8,10},{9,11},{10,... | collective-permute-start | bytes 393224 | tf_op jit(solution)/shard_map/ppermute | solution.py:28
  84.7 8.7 %collective-permute-start.28 = (f32[2,2,64,128]{3,2,1,0:T(8,128)S(1)}, f32[2,2,64,128]{3,2,1,0:T(8,128)S(1)}, u32[]{:S(2)}, u32[]{:S(2)}) collective-permute-start(f32[2,2,64,128]{3,2,1,0:T(8,128)S(1)} %pad_maximum_fusion.19), channel_id=1, source_target_pairs={{0,6},{1,7},{2,4},{3,5},{4,2},{5,3},{6,0},{7,1},{8,14},{9,15},{10,... | collective-permute-start | bytes 393224 | tf_op jit(solution)/shard_map/ppermute | solution.py:28
  87.0 8.1 %collective-permute-start.27 = (f32[2,2,64,128]{3,2,1,0:T(8,128)S(1)}, f32[2,2,64,128]{3,2,1,0:T(8,128)S(1)}, u32[]{:S(2)}, u32[]{:S(2)}) collective-permute-start(f32[2,2,64,128]{3,2,1,0:T(8,128)S(1)} %pad_maximum_fusion.18), channel_id=1, source_target_pairs={{0,4},{1,5},{2,6},{3,7},{4,0},{5,1},{6,2},{7,3},{8,12},{9,13},{10,... | collective-permute-start | bytes 393224 | tf_op jit(solution)/shard_map/ppermute | solution.py:28
  87.5 7.6 %collective-permute-start.26 = (f32[2,2,64,128]{3,2,1,0:T(8,128)S(1)}, f32[2,2,64,128]{3,2,1,0:T(8,128)S(1)}, u32[]{:S(2)}, u32[]{:S(2)}) collective-permute-start(f32[2,2,64,128]{3,2,1,0:T(8,128)S(1)} %pad_maximum_fusion.17), channel_id=1, source_target_pairs={{0,2},{1,3},{2,0},{3,1},{4,6},{5,7},{6,4},{7,5},{8,10},{9,11},{10,... | collective-permute-start | bytes 393224 | tf_op jit(solution)/shard_map/ppermute | solution.py:28
  99.4 1.8 collective-permute-start.29
  101.2 5.3 %collective-permute-start.30 = (f32[192,128]{1,0:T(8,128)S(1)}, f32[192,128]{1,0:T(8,128)S(1)}, u32[]{:S(2)}, u32[]{:S(2)}) collective-permute-start(f32[192,128]{1,0:T(8,128)S(1)} %get-tuple-element.111), channel_id=1, source_target_pairs={{0,2},{1,3},{2,0},{3,1},{4,6},{5,7},{6,4},{7,5},{8,10},{9,11},{10,... | collective-permute-start | bytes 294920 | tf_op jit(solution)/shard_map/ppermute | solution.py:28
  102.1 5.8 %collective-permute-start.31 = (f32[192,128]{1,0:T(8,128)S(1)}, f32[192,128]{1,0:T(8,128)S(1)}, u32[]{:S(2)}, u32[]{:S(2)}) collective-permute-start(f32[192,128]{1,0:T(8,128)S(1)} %get-tuple-element.113), channel_id=1, source_target_pairs={{0,4},{1,5},{2,6},{3,7},{4,0},{5,1},{6,2},{7,3},{8,12},{9,13},{10,... | collective-permute-start | bytes 294920 | tf_op jit(solution)/shard_map/ppermute | solution.py:28
  103.7 5.5 %collective-permute-start.32 = (f32[192,128]{1,0:T(8,128)S(1)}, f32[192,128]{1,0:T(8,128)S(1)}, u32[]{:S(2)}, u32[]{:S(2)}) collective-permute-start(f32[192,128]{1,0:T(8,128)S(1)} %get-tuple-element.112), channel_id=1, source_target_pairs={{0,6},{1,7},{2,4},{3,5},{4,2},{5,3},{6,0},{7,1},{8,14},{9,15},{10,... | collective-permute-start | bytes 294920 | tf_op jit(solution)/shard_map/ppermute | solution.py:28
  109.2 4.7 %collective-permute-start.33 = (f32[4,48,128]{2,1,0:T(8,128)S(1)}, f32[4,48,128]{2,1,0:T(8,128)S(1)}, u32[]{:S(2)}, u32[]{:S(2)}) collective-permute-start(f32[4,48,128]{2,1,0:T(8,128)S(1)} %bitcast.107), channel_id=1, source_target_pairs={{0,8},{8,0},{16,24},{24,16},{1,9},{9,1},{17,25},{25,17},{2,10},{10... | collective-permute-start | bytes 294920 | tf_op jit(solution)/shard_map/ppermute | solution.py:28
  114.0 6.5 %collective-permute-start.34 = (f32[4,48,128]{2,1,0:T(8,128)S(1)}, f32[4,48,128]{2,1,0:T(8,128)S(1)}, u32[]{:S(2)}, u32[]{:S(2)}) collective-permute-start(f32[4,48,128]{2,1,0:T(8,128)S(1)} %bitcast_add_fusion.1), channel_id=1, source_target_pairs={{0,24},{8,16},{16,8},{24,0},{1,25},{9,17},{17,9},{25,1},{2,26},{10... | collective-permute-start | bytes 294920 | tf_op jit(solution)/shard_map/ppermute | solution.py:28
  120.5 4.7 %collective-permute-start.35 = (f32[192,128]{1,0:T(8,128)S(1)}, f32[192,128]{1,0:T(8,128)S(1)}, u32[]{:S(2)}, u32[]{:S(2)}) collective-permute-start(f32[192,128]{1,0:T(8,128)S(1)} %fusion.12), channel_id=1, source_target_pairs={{0,2},{1,3},{2,0},{3,1},{4,6},{5,7},{6,4},{7,5},{8,10},{9,11},{10,... | collective-permute-start | bytes 294920 | tf_op jit(solution)/shard_map/ppermute | solution.py:28
  121.5 4.6 %collective-permute-start.36 = (f32[192,128]{1,0:T(8,128)S(1)}, f32[192,128]{1,0:T(8,128)S(1)}, u32[]{:S(2)}, u32[]{:S(2)}) collective-permute-start(f32[192,128]{1,0:T(8,128)S(1)} %fusion.12), channel_id=1, source_target_pairs={{0,4},{1,5},{2,6},{3,7},{4,0},{5,1},{6,2},{7,3},{8,12},{9,13},{10,... | collective-permute-start | bytes 294920 | tf_op jit(solution)/shard_map/ppermute | solution.py:28
  122.7 5.5 %collective-permute-start.37 = (f32[192,128]{1,0:T(8,128)S(1)}, f32[192,128]{1,0:T(8,128)S(1)}, u32[]{:S(2)}, u32[]{:S(2)}) collective-permute-start(f32[192,128]{1,0:T(8,128)S(1)} %fusion.12), channel_id=1, source_target_pairs={{0,6},{1,7},{2,4},{3,5},{4,2},{5,3},{6,0},{7,1},{8,14},{9,15},{10,... | collective-permute-start | bytes 294920 | tf_op jit(solution)/shard_map/ppermute | solution.py:28
  128.2 1.8 collective-permute-start.38
  136.5 8.4 %collective-permute-start.41 = (f32[2,2,64,128]{3,2,1,0:T(8,128)S(1)}, f32[2,2,64,128]{3,2,1,0:T(8,128)S(1)}, u32[]{:S(2)}, u32[]{:S(2)}) collective-permute-start(f32[2,2,64,128]{3,2,1,0:T(8,128)S(1)} %pad_maximum_fusion.22), channel_id=1, source_target_pairs={{0,4},{1,5},{2,6},{3,7},{4,0},{5,1},{6,2},{7,3},{8,12},{9,13},{10,... | collective-permute-start | bytes 393224 | tf_op jit(solution)/shard_map/ppermute | solution.py:28
  137.3 7.6 %collective-permute-start.42 = (f32[2,2,64,128]{3,2,1,0:T(8,128)S(1)}, f32[2,2,64,128]{3,2,1,0:T(8,128)S(1)}, u32[]{:S(2)}, u32[]{:S(2)}) collective-permute-start(f32[2,2,64,128]{3,2,1,0:T(8,128)S(1)} %pad_maximum_fusion.23), channel_id=1, source_target_pairs={{0,6},{1,7},{2,4},{3,5},{4,2},{5,3},{6,0},{7,1},{8,14},{9,15},{10,... | collective-permute-start | bytes 393224 | tf_op jit(solution)/shard_map/ppermute | solution.py:28
  139.2 7.0 %collective-permute-start.40 = (f32[2,2,64,128]{3,2,1,0:T(8,128)S(1)}, f32[2,2,64,128]{3,2,1,0:T(8,128)S(1)}, u32[]{:S(2)}, u32[]{:S(2)}) collective-permute-start(f32[2,2,64,128]{3,2,1,0:T(8,128)S(1)} %pad_maximum_fusion.21), channel_id=1, source_target_pairs={{0,2},{1,3},{2,0},{3,1},{4,6},{5,7},{6,4},{7,5},{8,10},{9,11},{10,... | collective-permute-start | bytes 393224 | tf_op jit(solution)/shard_map/ppermute | solution.py:28
  144.9 2.2 collective-permute-start.50
  146.9 7.5 %collective-permute-start.43 = (f32[8,64,128]{2,1,0:T(8,128)S(1)}, f32[8,64,128]{2,1,0:T(8,128)S(1)}, u32[]{:S(2)}, u32[]{:S(2)}) collective-permute-start(f32[8,64,128]{2,1,0:T(8,128)S(1)} %get-tuple-element.84), channel_id=1, source_target_pairs={{0,8},{8,0},{16,24},{24,16},{1,9},{9,1},{17,25},{25,17},{2,10},{10... | collective-permute-start | bytes 786440 | tf_op jit(solution)/shard_map/ppermute | solution.py:28
  147.1 10.8 %collective-permute-start.53 = (f32[2,2,64,128]{3,2,1,0:T(8,128)S(1)}, f32[2,2,64,128]{3,2,1,0:T(8,128)S(1)}, u32[]{:S(2)}, u32[]{:S(2)}) collective-permute-start(f32[2,2,64,128]{3,2,1,0:T(8,128)S(1)} %pad_maximum_fusion.31), channel_id=1, source_target_pairs={{0,6},{1,7},{2,4},{3,5},{4,2},{5,3},{6,0},{7,1},{8,14},{9,15},{10,... | collective-permute-start | bytes 393224 | tf_op jit(solution)/shard_map/ppermute | solution.py:28
  154.5 8.9 %collective-permute-start.44 = (f32[8,64,128]{2,1,0:T(8,128)S(1)}, f32[8,64,128]{2,1,0:T(8,128)S(1)}, u32[]{:S(2)}, u32[]{:S(2)}) collective-permute-start(f32[8,64,128]{2,1,0:T(8,128)S(1)} %add.133), channel_id=1, source_target_pairs={{0,24},{8,16},{16,8},{24,0},{1,25},{9,17},{17,9},{25,1},{2,26},{10... | collective-permute-start | bytes 786440 | tf_op jit(solution)/shard_map/ppermute | solution.py:28
  155.9 5.0 %collective-permute-start.52 = (f32[2,2,64,128]{3,2,1,0:T(8,128)S(1)}, f32[2,2,64,128]{3,2,1,0:T(8,128)S(1)}, u32[]{:S(2)}, u32[]{:S(2)}) collective-permute-start(f32[2,2,64,128]{3,2,1,0:T(8,128)S(1)} %pad_maximum_fusion.30), channel_id=1, source_target_pairs={{0,4},{1,5},{2,6},{3,7},{4,0},{5,1},{6,2},{7,3},{8,12},{9,13},{10,... | collective-permute-start | bytes 393224 | tf_op jit(solution)/shard_map/ppermute | solution.py:28
  156.6 5.0 %collective-permute-start.51 = (f32[2,2,64,128]{3,2,1,0:T(8,128)S(1)}, f32[2,2,64,128]{3,2,1,0:T(8,128)S(1)}, u32[]{:S(2)}, u32[]{:S(2)}) collective-permute-start(f32[2,2,64,128]{3,2,1,0:T(8,128)S(1)} %pad_maximum_fusion.29), channel_id=1, source_target_pairs={{0,2},{1,3},{2,0},{3,1},{4,6},{5,7},{6,4},{7,5},{8,10},{9,11},{10,... | collective-permute-start | bytes 393224 | tf_op jit(solution)/shard_map/ppermute | solution.py:28
  162.6 9.1 %collective-permute-start.54 = (f32[8,64,128]{2,1,0:T(8,128)S(1)}, f32[8,64,128]{2,1,0:T(8,128)S(1)}, u32[]{:S(2)}, u32[]{:S(2)}) collective-permute-start(f32[8,64,128]{2,1,0:T(8,128)S(1)} %get-tuple-element.92), channel_id=1, source_target_pairs={{0,8},{8,0},{16,24},{24,16},{1,9},{9,1},{17,25},{25,17},{2,10},{10... | collective-permute-start | bytes 786440 | tf_op jit(solution)/shard_map/ppermute | solution.py:28
  163.4 12.9 %collective-permute-start.45 = (f32[8,64,128]{2,1,0:T(8,128)S(1)}, f32[8,64,128]{2,1,0:T(8,128)S(1)}, u32[]{:S(2)}, u32[]{:S(2)}) collective-permute-start(f32[8,64,128]{2,1,0:T(8,128)S(1)} %add.134.mine), channel_id=1, source_target_pairs={{0,8},{8,0},{16,24},{24,16},{1,9},{9,1},{17,25},{25,17},{2,10},{10... | collective-permute-start | bytes 786440 | tf_op jit(solution)/shard_map/ppermute | solution.py:28
  171.8 9.0 %collective-permute-start.55 = (f32[8,64,128]{2,1,0:T(8,128)S(1)}, f32[8,64,128]{2,1,0:T(8,128)S(1)}, u32[]{:S(2)}, u32[]{:S(2)}) collective-permute-start(f32[8,64,128]{2,1,0:T(8,128)S(1)} %add.135), channel_id=1, source_target_pairs={{0,24},{8,16},{16,8},{24,0},{1,25},{9,17},{17,9},{25,1},{2,26},{10... | collective-permute-start | bytes 786440 | tf_op jit(solution)/shard_map/ppermute | solution.py:28
  177.0 5.8 %collective-permute-start.46 = (f32[4,2,64,128]{3,2,1,0:T(8,128)S(1)}, f32[4,2,64,128]{3,2,1,0:T(8,128)S(1)}, u32[]{:S(2)}, u32[]{:S(2)}) collective-permute-start(f32[4,2,64,128]{3,2,1,0:T(8,128)S(1)} %get-tuple-element.86), channel_id=1, source_target_pairs={{0,1},{1,0},{2,3},{3,2},{4,5},{5,4},{6,7},{7,6},{8,9},{9,8},{10,11... | collective-permute-start | bytes 786440 | tf_op jit(solution)/shard_map/ppermute | solution.py:28
  180.8 6.4 %collective-permute-start.56 = (f32[8,64,128]{2,1,0:T(8,128)S(1)}, f32[8,64,128]{2,1,0:T(8,128)S(1)}, u32[]{:S(2)}, u32[]{:S(2)}) collective-permute-start(f32[8,64,128]{2,1,0:T(8,128)S(1)} %add.136.mine), channel_id=1, source_target_pairs={{0,8},{8,0},{16,24},{24,16},{1,9},{9,1},{17,25},{25,17},{2,10},{10... | collective-permute-start | bytes 786440 | tf_op jit(solution)/shard_map/ppermute | solution.py:28
  182.9 9.6 %collective-permute-start.49 = (f32[2,2,64,128]{3,2,1,0:T(8,128)S(1)}, f32[2,2,64,128]{3,2,1,0:T(8,128)S(1)}, u32[]{:S(2)}, u32[]{:S(2)}) collective-permute-start(f32[2,2,64,128]{3,2,1,0:T(8,128)S(1)} %pad_maximum_fusion.27), channel_id=1, source_target_pairs={{0,6},{1,7},{2,4},{3,5},{4,2},{5,3},{6,0},{7,1},{8,14},{9,15},{10,... | collective-permute-start | bytes 393224 | tf_op jit(solution)/shard_map/ppermute | solution.py:28
  184.4 9.0 %collective-permute-start.48 = (f32[2,2,64,128]{3,2,1,0:T(8,128)S(1)}, f32[2,2,64,128]{3,2,1,0:T(8,128)S(1)}, u32[]{:S(2)}, u32[]{:S(2)}) collective-permute-start(f32[2,2,64,128]{3,2,1,0:T(8,128)S(1)} %pad_maximum_fusion.26), channel_id=1, source_target_pairs={{0,4},{1,5},{2,6},{3,7},{4,0},{5,1},{6,2},{7,3},{8,12},{9,13},{10,... | collective-permute-start | bytes 393224 | tf_op jit(solution)/shard_map/ppermute | solution.py:28
  188.1 6.4 %collective-permute-start.47 = (f32[2,2,64,128]{3,2,1,0:T(8,128)S(1)}, f32[2,2,64,128]{3,2,1,0:T(8,128)S(1)}, u32[]{:S(2)}, u32[]{:S(2)}) collective-permute-start(f32[2,2,64,128]{3,2,1,0:T(8,128)S(1)} %pad_maximum_fusion.25), channel_id=1, source_target_pairs={{0,2},{1,3},{2,0},{3,1},{4,6},{5,7},{6,4},{7,5},{8,10},{9,11},{10,... | collective-permute-start | bytes 393224 | tf_op jit(solution)/shard_map/ppermute | solution.py:28
  189.6 8.4 %collective-permute-start.60 = (f32[2,2,64,128]{3,2,1,0:T(8,128)S(1)}, f32[2,2,64,128]{3,2,1,0:T(8,128)S(1)}, u32[]{:S(2)}, u32[]{:S(2)}) collective-permute-start(f32[2,2,64,128]{3,2,1,0:T(8,128)S(1)} %pad_maximum_fusion.35), channel_id=1, source_target_pairs={{0,6},{1,7},{2,4},{3,5},{4,2},{5,3},{6,0},{7,1},{8,14},{9,15},{10,... | collective-permute-start | bytes 393224 | tf_op jit(solution)/shard_map/ppermute | solution.py:28
  191.6 8.1 %collective-permute-start.59 = (f32[2,2,64,128]{3,2,1,0:T(8,128)S(1)}, f32[2,2,64,128]{3,2,1,0:T(8,128)S(1)}, u32[]{:S(2)}, u32[]{:S(2)}) collective-permute-start(f32[2,2,64,128]{3,2,1,0:T(8,128)S(1)} %pad_maximum_fusion.34), channel_id=1, source_target_pairs={{0,4},{1,5},{2,6},{3,7},{4,0},{5,1},{6,2},{7,3},{8,12},{9,13},{10,... | collective-permute-start | bytes 393224 | tf_op jit(solution)/shard_map/ppermute | solution.py:28
  192.4 7.3 %collective-permute-start.58 = (f32[2,2,64,128]{3,2,1,0:T(8,128)S(1)}, f32[2,2,64,128]{3,2,1,0:T(8,128)S(1)}, u32[]{:S(2)}, u32[]{:S(2)}) collective-permute-start(f32[2,2,64,128]{3,2,1,0:T(8,128)S(1)} %pad_maximum_fusion.33), channel_id=1, source_target_pairs={{0,2},{1,3},{2,0},{3,1},{4,6},{5,7},{6,4},{7,5},{8,10},{9,11},{10,... | collective-permute-start | bytes 393224 | tf_op jit(solution)/shard_map/ppermute | solution.py:28
  203.9 1.8 collective-permute-start.61
  205.8 4.9 %collective-permute-start.62 = (f32[192,128]{1,0:T(8,128)S(1)}, f32[192,128]{1,0:T(8,128)S(1)}, u32[]{:S(2)}, u32[]{:S(2)}) collective-permute-start(f32[192,128]{1,0:T(8,128)S(1)} %get-tuple-element.108), channel_id=1, source_target_pairs={{0,2},{1,3},{2,0},{3,1},{4,6},{5,7},{6,4},{7,5},{8,10},{9,11},{10,... | collective-permute-start | bytes 294920 | tf_op jit(solution)/shard_map/ppermute | solution.py:28
  207.0 5.7 %collective-permute-start.63 = (f32[192,128]{1,0:T(8,128)S(1)}, f32[192,128]{1,0:T(8,128)S(1)}, u32[]{:S(2)}, u32[]{:S(2)}) collective-permute-start(f32[192,128]{1,0:T(8,128)S(1)} %get-tuple-element.110), channel_id=1, source_target_pairs={{0,4},{1,5},{2,6},{3,7},{4,0},{5,1},{6,2},{7,3},{8,12},{9,13},{10,... | collective-permute-start | bytes 294920 | tf_op jit(solution)/shard_map/ppermute | solution.py:28
  208.3 5.5 %collective-permute-start.64 = (f32[192,128]{1,0:T(8,128)S(1)}, f32[192,128]{1,0:T(8,128)S(1)}, u32[]{:S(2)}, u32[]{:S(2)}) collective-permute-start(f32[192,128]{1,0:T(8,128)S(1)} %get-tuple-element.109), channel_id=1, source_target_pairs={{0,6},{1,7},{2,4},{3,5},{4,2},{5,3},{6,0},{7,1},{8,14},{9,15},{10,... | collective-permute-start | bytes 294920 | tf_op jit(solution)/shard_map/ppermute | solution.py:28
  213.9 5.4 %collective-permute-start.65 = (f32[48,128]{1,0:T(8,128)S(1)}, f32[48,128]{1,0:T(8,128)S(1)}, u32[]{:S(2)}, u32[]{:S(2)}) collective-permute-start(f32[48,128]{1,0:T(8,128)S(1)} %get-tuple-element.178), channel_id=1, source_target_pairs={{0,8},{8,0},{16,24},{24,16},{1,9},{9,1},{17,25},{25,17},{2,10},{10... | collective-permute-start | bytes 73736 | tf_op jit(solution)/shard_map/ppermute | solution.py:28
  215.8 5.6 %collective-permute-start.66 = (f32[48,128]{1,0:T(8,128)S(1)}, f32[48,128]{1,0:T(8,128)S(1)}, u32[]{:S(2)}, u32[]{:S(2)}) collective-permute-start(f32[48,128]{1,0:T(8,128)S(1)} %get-tuple-element.180), channel_id=1, source_target_pairs={{0,24},{8,16},{16,8},{24,0},{1,25},{9,17},{17,9},{25,1},{2,26},{10... | collective-permute-start | bytes 73736 | tf_op jit(solution)/shard_map/ppermute | solution.py:28
  218.2 4.7 %collective-permute-start.67 = (f32[48,128]{1,0:T(8,128)S(1)}, f32[48,128]{1,0:T(8,128)S(1)}, u32[]{:S(2)}, u32[]{:S(2)}) collective-permute-start(f32[48,128]{1,0:T(8,128)S(1)} %get-tuple-element.179), channel_id=1, source_target_pairs={{0,16},{8,24},{16,0},{24,8},{1,17},{9,25},{17,1},{25,9},{2,18},{10... | collective-permute-start | bytes 73736 | tf_op jit(solution)/shard_map/ppermute | solution.py:28
  (10 other events, 110.1 us)
